TPU v7x, 32 devices: a whole 2x2x4 slice. The times are simulated.
32 devices in a mesh: seq: 16 (over z, y, x), head: 2 (over core).
Axes of the slice: x: 2, y: 2, z: 4, core: 2. Of those that a mesh axis runs over, the one named last changes fastest.
Arguments:
- tokens: bfloat16 [4, 4096, 2048], P(None, 'seq'), may hold values from -6 to 6
- norm_gain: float32 [2048], replicated, may hold values from 0.1 to 1.9
- in_weight: bfloat16 [2048, 2, 4096], P(None, None, 'head'), may hold values from -0.125 to 0.125
- bc_weight: bfloat16 [2048, 256], replicated, may hold values from -0.125 to 0.125
- dt_weight: bfloat16 [2048, 64], P(None, 'head'), may hold values from -0.125 to 0.125
- dt_bias: float32 [64], P('head'), may hold values from -1 to 0.5
- a_log: float32 [64], P('head'), may hold values from -14 to -2
- conv_weight: float32 [4, 4096], P(None, 'head'), may hold values from -3 to 3
- conv_bias: float32 [4096], P('head'), may hold values from -0.5 to 0.5
- bc_conv_weight: float32 [4, 256], replicated, may hold values from -3 to 3
- bc_conv_bias: float32 [256], replicated, may hold values from -0.5 to 0.5
- d_skip: float32 [64], P('head'), may hold values from 0.5 to 1.5
- gate_gain: float32 [4096], P('head'), may hold values from 0.1 to 1.9
- out_weight: bfloat16 [2048, 4096], P(None, 'head'), may hold values from -0.09375 to 0.09375
- cotangent: bfloat16 [4, 4096, 2048], P(None, 'seq'), may hold values from -6 to 6
- seq_lengths: int32 [2, 3], replicated, may hold values from 1 to 2048, 4096 in all within a row
Outputs:
- block_out: bfloat16 [4, 4096, 2048], P(None, 'seq', 'head')
- grad_tokens: float32 [4, 4096, 2048], P(None, 'seq')
- grad_norm_gain: float32 [2048], replicated
- grad_in_weight: float32 [2048, 2, 4096], P('seq', None, 'head')
- grad_bc_weight: float32 [2048, 256], replicated
- grad_dt_weight: float32 [2048, 64], P(None, 'head')
- grad_dt_bias: float32 [64], P('head')
- grad_a_log: float32 [64], P('head')
- grad_d_skip: float32 [64], P('head')
- grad_conv_weight: float32 [4, 4096], P(None, 'head')
- grad_conv_bias: float32 [4096], P('head')
- grad_bc_conv_weight: float32 [4, 256], replicated
- grad_bc_conv_bias: float32 [256], replicated
- grad_gate_gain: float32 [4096], P('head')
- grad_out_weight: float32 [2048, 4096], P('seq', 'head')
Inputs may be any that keep to these rules, and one draw needn't show every extreme that they name: `seq_lengths`: row m lists, in order, the lengths of the sequences packed into micro-batch m; each row sums to 4096 and its largest entry is 2048.
All inputs are finite; a program needn't handle non-finite values.
Results may differ from a plain program's by a relative error of at most 0.006.
The roundings to bfloat16 on the way count: a program that leaves them out, or rounds other values in their place, can miss the bound.
Values sent between devices are 32-bit elements; how exact they have to be, the bound alone decides.
A program may use at most 384 MiB of HBM per device.

v0:
```python
import jax
import jax.numpy as jnp
from jax import lax
from jax.sharding import PartitionSpec as P

BLOCK = 256


EPSILON = 1e-05
HIGHEST = lax.Precision.HIGHEST


def shifted(shard, axis, by):
    length = lax.axis_size(axis)
    pairs = [(i, i + by) for i in range(length) if 0 <= i + by < length]
    return lax.ppermute(shard, axis, pairs)


def segment_ids(seq_lengths, first, count, micro):
    places = first + jnp.arange(count, dtype=jnp.int32)
    starts = jnp.cumsum(seq_lengths, axis=-1) - seq_lengths
    short_ids = (
        jnp.sum((starts[:, None, :] <= places[None, :, None]).astype(jnp.int32), axis=-1) - 1
    )
    long_ids = jnp.zeros((micro - seq_lengths.shape[0], count), jnp.int32)
    labels = jnp.concatenate([short_ids, long_ids], axis=0)
    return jnp.where(places[None, :] >= 0, labels, -1)


def rms_scale(values, gain):
    return values * lax.rsqrt(jnp.mean(values * values, axis=-1, keepdims=True) + EPSILON) * gain


def conv_silu(extended, weight, bias, labels):
    taps = weight.shape[0]
    count = extended.shape[0] - taps + 1
    own = labels[taps - 1 :]
    total = bias + weight[0] * extended[taps - 1 :]
    for shift in range(1, taps):
        first = taps - 1 - shift
        mask = (labels[first : first + count] == own).astype(extended.dtype)
        total = total + weight[shift] * extended[first : first + count] * mask[:, None]
    return jax.nn.silu(total)


def step_sizes(delta_pre, dt_bias, a_log):
    delta = jax.nn.softplus(delta_pre + dt_bias)
    return (delta, -jnp.exp(a_log) * delta)


def decay_tables(decays, own_labels, label_before):
    running = jnp.cumsum(decays, axis=0)
    by_head = running.T
    order = jnp.arange(decays.shape[0])
    causal = ((own_labels[:, None] == own_labels[None, :]) & (order[:, None] >= order[None, :]))[
        None
    ]
    spread = by_head[:, :, None] - by_head[:, None, :]
    inside = jnp.where(causal, jnp.exp(jnp.where(causal, spread, 0.0)), 0.0)
    living = (own_labels == label_before).astype(decays.dtype)
    carried = jnp.exp(running) * living[:, None]
    return (running, inside, carried)


def block_output(values, c_rows, steps, decays, skip, carry_in, scores, own_labels, label_before):
    running, inside, carried = decay_tables(decays, own_labels, label_before)
    weights = inside * scores[None, :, :] * steps.T[:, None, :]
    result = jnp.einsum("hij,jhp->ihp", weights, values, precision=HIGHEST)
    result = result + carried[:, :, None] * jnp.einsum(
        "hpn,in->ihp", carry_in, c_rows, precision=HIGHEST
    )
    return result + skip[None, :, None] * values


def block_state(values, b_rows, steps, decays, carry_in, own_labels, label_before):
    running = jnp.cumsum(decays, axis=0)
    living = (own_labels[-1] == label_before).astype(decays.dtype)
    tail = (own_labels == own_labels[-1]).astype(decays.dtype)
    weights = jnp.exp(running[-1][None, :] - running) * tail[:, None] * steps
    kept = (jnp.exp(running[-1]) * living)[:, None, None] * carry_in
    return kept + jnp.einsum("jh,jhp,jn->hpn", weights, values, b_rows, precision=HIGHEST)


def running_totals(logs, lives):
    log_prefix = jnp.concatenate([jnp.zeros_like(logs[:1]), jnp.cumsum(logs, axis=0)], axis=0)
    break_prefix = jnp.concatenate(
        [jnp.zeros_like(lives[:1]), jnp.cumsum(1.0 - lives, axis=0)], axis=0
    )
    return (log_prefix, break_prefix)


def masked_exp(valid, gap):
    return jnp.where(valid[:, :, None], jnp.exp(jnp.where(valid[:, :, None], gap, 0.0)), 0.0)


def earlier_states(device_state, device_log, device_live):
    states, logs, lives = (
        lax.all_gather(device_state[None], "seq", axis=0, tiled=True),
        lax.all_gather(device_log[None], "seq", axis=0, tiled=True),
        lax.all_gather(device_live[None], "seq", axis=0, tiled=True),
    )
    log_prefix, break_prefix = running_totals(logs, lives)
    own_index = lax.axis_index("seq")
    here_log = lax.dynamic_index_in_dim(log_prefix, own_index, 0, keepdims=True)
    here_break = lax.dynamic_index_in_dim(break_prefix, own_index, 0, keepdims=True)
    order = jnp.arange(states.shape[0])[:, None]
    valid = (order < own_index) & (here_break - break_prefix[1:] == 0.0)
    weight = masked_exp(valid, here_log - log_prefix[1:])
    incoming = jnp.einsum("jmh,jmhpn->mhpn", weight, states, precision=HIGHEST)
    return (incoming, log_prefix, break_prefix)


def later_grads(device_grad, log_prefix, break_prefix):
    grads = lax.all_gather(device_grad[None], "seq", axis=0, tiled=True)
    own_index = lax.axis_index("seq")
    next_log = lax.dynamic_index_in_dim(log_prefix, own_index + 1, 0, keepdims=True)
    next_break = lax.dynamic_index_in_dim(break_prefix, own_index + 1, 0, keepdims=True)
    order = jnp.arange(grads.shape[0])[:, None]
    valid = (order > own_index) & (break_prefix[:-1] - next_break == 0.0)
    weight = masked_exp(valid, log_prefix[:-1] - next_log)
    return jnp.einsum("jmh,jmhpn->mhpn", weight, grads, precision=HIGHEST)


def out_term(cot_flat, normed_gate):
    return lax.dot_general(
        cot_flat, normed_gate, (((0,), (0,)), ((), ())), preferred_element_type=jnp.float32
    )


def in_term(normed_low, grad_gate_x):
    return jnp.einsum("tr,tkc->rkc", normed_low, grad_gate_x, preferred_element_type=jnp.float32)


def body(
    tokens,
    norm_gain,
    in_weight,
    bc_weight,
    dt_weight,
    dt_bias,
    a_log,
    conv_weight,
    conv_bias,
    bc_conv_weight,
    bc_conv_bias,
    d_skip,
    gate_gain,
    out_weight,
    cotangent,
    seq_lengths,
):
    micro, length, width = tokens.shape
    heads = dt_bias.shape[0]
    inner = conv_bias.shape[0]
    head_dim = inner // heads
    state_size = bc_weight.shape[1] // 2
    taps = conv_weight.shape[0]
    span = min(BLOCK, length)
    pieces = length // span
    groups = micro * pieces
    total = micro * length
    full_inner = inner * lax.axis_size("head")
    labels = segment_ids(
        seq_lengths, lax.axis_index("seq") * length - (taps - 1), length + taps - 1, micro
    )
    own_labels = labels[:, taps - 1 :]
    before_labels = labels[:, taps - 2 :: span][:, :pieces].reshape(groups)
    flat = tokens.reshape(total, width).astype(jnp.float32)
    normed, norm_back = jax.vjp(rms_scale, flat, norm_gain)
    normed_low = normed.astype(jnp.bfloat16)
    gate_x = jnp.einsum("td,dkc->tkc", normed_low, in_weight, preferred_element_type=jnp.float32)
    gate_pre = gate_x[:, 0].reshape(micro, length, inner)
    x_pre = gate_x[:, 1].reshape(micro, length, inner)
    bc_pre = jnp.dot(normed_low, bc_weight, preferred_element_type=jnp.float32).reshape(
        micro, length, 2 * state_size
    )
    delta_pre = jnp.dot(normed_low, dt_weight, preferred_element_type=jnp.float32)
    left_x, left_bc = shifted(
        (x_pre[:, length - taps + 1 :], bc_pre[:, length - taps + 1 :]), "seq", 1
    )
    conv_many = jax.vmap(conv_silu, in_axes=(0, None, None, 0))
    x_act, x_conv_back = jax.vjp(
        lambda extended, weight, bias: conv_many(extended, weight, bias, labels),
        jnp.concatenate([left_x, x_pre], axis=1),
        conv_weight,
        conv_bias,
    )
    bc_act, bc_conv_back = jax.vjp(
        lambda extended, weight, bias: conv_many(extended, weight, bias, labels),
        jnp.concatenate([left_bc, bc_pre], axis=1),
        bc_conv_weight,
        bc_conv_bias,
    )
    x_low = x_act.astype(jnp.bfloat16)
    bc_low = bc_act.astype(jnp.bfloat16)
    (delta, decay), rate_back = jax.vjp(step_sizes, delta_pre, dt_bias, a_log)
    values = x_low.astype(jnp.float32).reshape(groups, span, heads, head_dim)
    b_low = bc_low[..., :state_size]
    c_low = bc_low[..., state_size:]
    b_rows = b_low.astype(jnp.float32)
    c_rows = c_low.astype(jnp.float32)
    scores = jnp.einsum("gin,gjn->gij", c_low, b_low, preferred_element_type=jnp.float32)
    steps = delta.reshape(groups, span, heads)
    decays = decay.reshape(groups, span, heads)
    zero_state = jnp.zeros((groups, heads, head_dim, state_size), jnp.float32)
    state_many = jax.vmap(block_state)
    own_states, state_back = jax.vjp(
        lambda block_values, block_b, block_steps, block_decays: state_many(
            block_values, block_b, block_steps, block_decays, zero_state, own_labels, before_labels
        ),
        values,
        b_rows,
        steps,
        decays,
    )
    living = (own_labels[:, -1] == before_labels).astype(jnp.float32)
    block_logs = jnp.sum(decays, axis=1)
    factor = (jnp.exp(block_logs) * living[:, None]).reshape(micro, pieces, heads)
    own_states = own_states.reshape(micro, pieces, heads, head_dim, state_size)
    device_state = jnp.zeros((micro, heads, head_dim, state_size), jnp.float32)
    piece = 0
    device_state = factor[:, piece, :, None, None] * device_state + own_states[:, piece]
    device_log = jnp.sum(block_logs.reshape(micro, pieces, heads), axis=1)
    device_live = jnp.prod(living.reshape(micro, pieces), axis=1)
    incoming, log_prefix, break_prefix = earlier_states(device_state, device_log, device_live)
    current = incoming
    piece = 0
    starts = [current]
    block_starts = jnp.stack(starts, axis=1).reshape(groups, heads, head_dim, state_size)
    output_many = jax.vmap(block_output, in_axes=(0, 0, 0, 0, None, 0, 0, 0, 0))
    mixed, output_back = jax.vjp(
        lambda block_values, block_c, block_steps, block_decays, skip, carry, block_scores: output_many(
            block_values,
            block_c,
            block_steps,
            block_decays,
            skip,
            carry,
            block_scores,
            own_labels,
            before_labels,
        ),
        values,
        c_rows,
        steps,
        decays,
        d_skip,
        block_starts,
        scores,
    )
    mixed = mixed.reshape(micro, length, inner)
    gate_act = jax.nn.silu(gate_pre)
    gated = mixed * gate_act
    square_sum = lax.psum(jnp.sum(gated * gated, axis=-1), "head")
    scale = lax.rsqrt(square_sum / full_inner + EPSILON)[:, :, None]
    normed_gate = (gated * scale * gate_gain).astype(jnp.bfloat16).reshape(total, inner)
    head_terms = lax.dot_general(
        normed_gate, out_weight, (((1,), (1,)), ((), ())), preferred_element_type=jnp.float32
    )
    summed = lax.psum_scatter(head_terms, "head", scatter_dimension=1, tiled=True)
    share = summed.shape[1]
    residual = lax.dynamic_slice_in_dim(flat, lax.axis_index("head") * share, share, 1)
    block_out = (residual + summed).astype(jnp.bfloat16).reshape(micro, length, share)
    cot_flat = cotangent.reshape(total, width)
    grad_gate_n = jnp.dot(cot_flat, out_weight, preferred_element_type=jnp.float32).reshape(
        micro, length, inner
    )
    grad_out_weight = lax.psum_scatter(
        out_term(cot_flat, normed_gate), "seq", scatter_dimension=0, tiled=True
    )
    grad_gate_gain = jnp.sum(grad_gate_n * gated * scale, axis=(0, 1))
    dot_total = lax.psum(jnp.sum(grad_gate_n * gate_gain * gated, axis=-1), "head")
    grad_gated = (
        grad_gate_n * gate_gain * scale - gated * scale**3 * dot_total[:, :, None] / full_inner
    )
    sigma = jax.nn.sigmoid(gate_pre)
    grad_gate_pre = grad_gated * mixed * sigma * (1.0 + gate_pre * (1.0 - sigma))
    grad_mixed = (grad_gated * gate_act).astype(jnp.bfloat16).astype(jnp.float32)
    grad_rows = grad_mixed.reshape(groups, span, heads, head_dim)
    out_values, out_c, out_steps, out_decays, grad_d_skip, grad_starts, grad_scores = output_back(
        grad_rows
    )
    out_c = out_c + jnp.einsum("gij,gjn->gin", grad_scores, b_rows, precision=HIGHEST)
    out_b = jnp.einsum("gij,gin->gjn", grad_scores, c_rows, precision=HIGHEST)
    grad_starts = grad_starts.reshape(micro, pieces, heads, head_dim, state_size)
    device_grad = jnp.zeros_like(device_state)
    for piece in reversed(range(pieces)):
        device_grad = grad_starts[:, piece] + factor[:, piece, :, None, None] * device_grad
    outgoing = later_grads(device_grad, log_prefix, break_prefix)
    ends = [outgoing] * pieces
    current = outgoing
    for piece in reversed(range(pieces)):
        ends[piece] = current
        current = grad_starts[:, piece] + factor[:, piece, :, None, None] * current
    end_grads = jnp.stack(ends, axis=1).reshape(groups, heads, head_dim, state_size)
    own_values, own_b, own_steps, own_decays = state_back(end_grads)
    carry_weight = jnp.sum(end_grads * block_starts, axis=(2, 3)) * factor.reshape(groups, heads)
    grad_values = (out_values + own_values).reshape(micro, length, inner)
    grad_bc_act = jnp.concatenate([out_b + own_b, out_c], axis=-1)
    grad_delta = (out_steps + own_steps).reshape(total, heads)
    grad_decay = (out_decays + own_decays + carry_weight[:, None, :]).reshape(total, heads)
    grad_delta_pre, grad_dt_bias, grad_a_log = rate_back((grad_delta, grad_decay))
    grad_x_ext, grad_conv_weight, grad_conv_bias = x_conv_back(grad_values)
    grad_bc_ext, grad_bc_conv_weight, grad_bc_conv_bias = bc_conv_back(grad_bc_act)
    right_x, right_bc = shifted((grad_x_ext[:, : taps - 1], grad_bc_ext[:, : taps - 1]), "seq", -1)
    grad_x_pre = grad_x_ext[:, taps - 1 :].at[:, length - taps + 1 :].add(right_x)
    grad_bc_pre = grad_bc_ext[:, taps - 1 :].at[:, length - taps + 1 :].add(right_bc)
    grad_gate_x = (
        jnp.stack([grad_gate_pre, grad_x_pre], axis=2).reshape(total, 2, inner).astype(jnp.bfloat16)
    )
    bc_flat = grad_bc_pre.reshape(total, 2 * state_size)
    row_part = jnp.einsum("tkc,dkc->td", grad_gate_x, in_weight, preferred_element_type=jnp.float32)
    row_part = row_part + jnp.einsum(
        "tc,dc->td", bc_flat, bc_weight, precision=HIGHEST, preferred_element_type=jnp.float32
    )
    row_part = row_part + jnp.einsum(
        "th,dh->td",
        grad_delta_pre,
        dt_weight,
        precision=HIGHEST,
        preferred_element_type=jnp.float32,
    )
    row_grads = lax.psum(row_part, "head")
    grad_flat, grad_norm_gain = norm_back(row_grads)
    grad_tokens = (cot_flat.astype(jnp.float32) + grad_flat).reshape(micro, length, width)
    grad_in_weight = lax.psum_scatter(
        in_term(normed_low, grad_gate_x), "seq", scatter_dimension=0, tiled=True
    )
    grad_bc_weight = jnp.einsum(
        "td,tc->dc", normed_low, bc_flat, precision=HIGHEST, preferred_element_type=jnp.float32
    )
    grad_dt_weight = jnp.einsum(
        "td,th->dh",
        normed_low,
        grad_delta_pre,
        precision=HIGHEST,
        preferred_element_type=jnp.float32,
    )
    grad_bc_weight, grad_bc_conv_weight, grad_bc_conv_bias = lax.psum(
        (grad_bc_weight, grad_bc_conv_weight, grad_bc_conv_bias), ("seq", "head")
    )
    (
        grad_norm_gain,
        grad_dt_weight,
        grad_dt_bias,
        grad_a_log,
        grad_d_skip,
        grad_conv_weight,
        grad_conv_bias,
        grad_gate_gain,
    ) = lax.psum(
        (
            grad_norm_gain,
            grad_dt_weight,
            grad_dt_bias,
            grad_a_log,
            grad_d_skip,
            grad_conv_weight,
            grad_conv_bias,
            grad_gate_gain,
        ),
        "seq",
    )
    return (
        block_out,
        grad_tokens,
        grad_norm_gain,
        grad_in_weight,
        grad_bc_weight,
        grad_dt_weight,
        grad_dt_bias,
        grad_a_log,
        grad_d_skip,
        grad_conv_weight,
        grad_conv_bias,
        grad_bc_conv_weight,
        grad_bc_conv_bias,
        grad_gate_gain,
        grad_out_weight,
    )


def solution(mesh):
    return jax.shard_map(
        body,
        mesh=mesh,
        in_specs=(
            P(None, "seq", None),
            P(),
            P(None, None, "head"),
            P(),
            P(None, "head"),
            P("head"),
            P("head"),
            P(None, "head"),
            P("head"),
            P(),
            P(),
            P("head"),
            P("head"),
            P(None, "head"),
            P(None, "seq", None),
            P(),
        ),
        out_specs=(
            P(None, "seq", "head"),
            P(None, "seq", None),
            P(),
            P("seq", None, "head"),
            P(),
            P(None, "head"),
            P("head"),
            P("head"),
            P("head"),
            P(None, "head"),
            P("head"),
            P(),
            P(),
            P("head"),
            P("seq", "head"),
        ),
        check_vma=False,
    )
```

profile of v0, /device:TPU:1, one launch (start us, length us, event | category | flops | bytes accessed | tf_op | source)
XLA Modules:
  0.0 3021.1 jit_solution(9589570245245134429)
XLA Ops:
  7.2 3.2 multiply_reduce_fusion.13
  11.0 3.2 multiply_convert_fusion.5
  16.2 22.8 fusion.27
  39.0 10.2 fusion.142
  49.9 4.1 collective-permute-start
  56.0 3.9 collective-permute-start.1
  62.0 4.2 compare_select_fusion.2
  81.4 19.4 multiply_convert_fusion.4
  100.9 6.2 copy.512
  107.1 8.4 add_add_fusion.1
  115.7 14.8 reshape.604
  130.6 15.2 copy.532
  147.3 31.7 %all-reduce.21 = f32[64]{0:T(128)S(1)} all-reduce(f32[64]{0:T(128)S(1)} %dynamic-update-slice.7), channel_id=2, replica_groups=mesh['seq'=16,'head'=2] {'seq'}, use_global_device_ids=true, to_apply=%add.21 | all-reduce | flops 64 | bytes 512
  179.1 31.1 %all-gather.4 = f32[16,4,32]{2,1,0:T(4,128)S(1)} all-gather(f32[1,4,32]{2,1,0:T(4,128)S(1)} %bitcast.308), channel_id=3, replica_groups=mesh['seq'=16,'head'=2] {'seq'}, dimensions={0}, use_global_device_ids=true | all-gather | bytes 8704 | tf_op jit(solution)/shard_map/all_gather | solution.py:99
  212.0 7.4 copy.527
  219.3 565.9 %all-gather.8.cloned.1.call-done = f32[64,32,64,128]{3,2,1,0:T(8,128)} async-done(((f32[4,32,64,128]{3,2,1,0:T(8,128)}), f32[64,32,64,128]{3,2,1,0:T(8,128)}) %all-gather.8.cloned.1.call-update) | async-done | bytes 67108880 | tf_op jit(solution)/shard_map/all_gather | solution.py:98
  785.2 87.1 %fusion.2 = f32[4,32,1,64,128]{4,2,3,1,0:T(1,128)S(1)} fusion(f32[16,4,32,1,1]{0,3,4,2,1:T(1,128)S(1)} %copy.568, f32[16,4,32,64,128]{4,3,2,1,0:T(8,128)} %bitcast.28), kind=kOutput, calls=%fused_computation.2 | convolution fusion | flops 201326592 | bytes 71311360 | tf_op jit(solution)/shard_map/jmh,jmhpn->mhpn/dot_general | solution.py:109
  872.4 3.4 fusion.87
  876.1 5.5 copy-done.16
  881.6 30.4 %multiply_reduce_fusion.12 = (f32[4,256]{1,0:T(4,128)S(1)}, f32[4,256,32,64]{1,3,2,0:T(8,128)}) fusion(f32[4,256,32,64]{1,3,2,0:T(8,128)} %copy.532, f32[4,256,32,64]{1,3,2,0:T(8,128)S(1)} %bitcast.274, f32[32]{0:T(128)S(1)} %copy-done.101, f32[4,256,32,64]{1,3,2,0:T(8,128)S(1)} %fusion.87, f32[4,256,32]{1,2,0:T(8,128)S(1)} %copy.521, ...), kind=kOutput, calls=%fused_computation.82 | convolution fusion | flops 6507461632 | bytes 39456896 | tf_op jit(solution)/shard_map/jvp(vmap(hij,jhp->ihp))/dot_general | solution.py:68
  912.0 3.2 psum.98
  915.2 8.8 copy.533
  924.0 20.1 multiply_reduce_fusion.2
  946.5 15.9 multiply_reduce_fusion.7
  962.4 6.9 copy.535
  969.3 9.5 fusion.72
  978.9 16.4 copy.589
  995.3 14.9 reshape.603
  1010.2 17.9 fusion.63
  1028.2 18.4 convolution_bitcast_fusion
  1048.0 6.4 copy.536
  1054.4 26.9 fusion.12
  1083.3 8.2 multiply_reduce_fusion.10
  1098.5 10.0 reduce-window.24
  1108.6 16.6 fusion.76
  1126.6 518.5 %all-gather.10.cloned.1.call-done = f32[64,32,64,128]{3,2,1,0:T(8,128)} async-done(((f32[4,32,64,128]{3,2,1,0:T(8,128)}), f32[64,32,64,128]{3,2,1,0:T(8,128)}) %all-gather.10.cloned.1.call-update) | async-done | bytes 67108880 | tf_op jit(solution)/shard_map/all_gather | solution.py:114
  1645.2 87.4 %fusion = f32[4,32,1,64,128]{4,2,3,1,0:T(1,128)S(1)} fusion(f32[16,4,32,1,1]{0,3,4,2,1:T(1,128)S(1)} %copy-done.43, f32[16,4,32,64,128]{4,3,2,1,0:T(8,128)} %bitcast.48), kind=kOutput, calls=%fused_computation | convolution fusion | flops 201326592 | bytes 71311360 | tf_op jit(solution)/shard_map/jmh,jmhpn->mhpn/dot_general | solution.py:121
  1732.6 7.3 fusion.31
  1745.8 5.0 multiply_reduce_fusion.14
  1751.8 10.0 reduce-window.26
  1762.9 26.9 fusion.38
  1789.8 8.8 copy.537
  1798.7 16.1 fusion.79
  1821.3 13.2 multiply_reduce_fusion.6
  1834.5 12.1 multiply_multiply_fusion.2
  1850.2 12.8 pad_add_fusion
  1862.9 5.7 fusion.146
  1876.8 5.9 collective-permute-done.2
  1885.7 26.6 fusion.25
  1912.3 8.8 fusion.37
  1921.2 25.9 fusion.54
  1947.2 6.7 bitcast_convert_fusion
  1954.2 5.5 add_convert_fusion
  1959.7 56.3 %reduce-scatter.8.cloned.1.call-done = f32[128,2048]{0,1:T(8,128)} async-done(((f32[2048,2048]{0,1:T(8,128)}), f32[128,2048]{0,1:T(8,128)}) %reduce-scatter.8.cloned.1.call-update) | async-done | bytes 1048592 | tf_op jit(solution)/shard_map/reduce_scatter | solution.py:268
  2018.6 5.0 fusion.147
  2023.8 44.2 %all-reduce.22 = (f32[4,256]{1,0:T(4,128)}, f32[256]{0:T(256)}) all-reduce(f32[4,256]{1,0:T(4,128)S(1)} %pad_add_fusion.6, f32[256]{0:T(256)S(1)} %copy-done.90), channel_id=1, replica_groups=mesh['seq'=16,'head'=2] {'seq','head'}, use_global_device_ids=true, to_apply=%region_50.51 | all-reduce | flops 1280 | bytes 10240 | tf_op jit(solution)/shard_map/psum | solution.py:339
  2068.1 8.6 fusion.71
  2076.7 6.1 multiply_reduce_fusion.8
  2082.9 67.5 %all-reduce.23 = (f32[2048]{0:T(1024)}, f32[32]{0:T(128)}, f32[32]{0:T(128)}, f32[32]{0:T(128)}, f32[4,2048]{1,0:T(4,128)}, /*index=5*/f32[2048]{0:T(1024)}, f32[2048]{0:T(1024)}) all-reduce(f32[2048]{0:T(1024)S(1)} %get-tuple-element.199, f32[32]{0:T(128)S(1)} %copy-done.98, ...), channel_id=1, replica_groups=mesh['seq'=16,'head'=2] {'seq'}, use_global_device_ids=true, to_apply=%region_28.29 | all-reduce | flops 14432 | bytes 115456 | tf_op jit(solution)/shard_map/psum | solution.py:351
  2150.4 9.6 fusion.36
  2160.0 592.7 %reduce-scatter.6.cloned.1.call-done = f32[128,2,2048]{2,0,1:T(8,128)} async-done(((f32[2048,2,2048]{2,0,1:T(8,128)}), f32[128,2,2048]{2,0,1:T(8,128)}) %reduce-scatter.6.cloned.1.call-update) | async-done | bytes 2097168 | tf_op jit(solution)/shard_map/reduce_scatter | solution.py:326
  2752.7 4.5 copy.565
  2757.2 112.6 %all-reduce.32.cloned.1.call-done = f32[2048,32]{0,1:T(8,128)} async-done(((f32[2048,32]{0,1:T(8,128)}), f32[2048,32]{0,1:T(8,128)}) %all-reduce.32.cloned.1.call-update) | async-done | bytes 262160 | tf_op jit(solution)/shard_map/psum | solution.py:351
  2869.8 139.5 %all-reduce.30.cloned.1.call-done = f32[2048,256]{1,0:T(8,128)} async-done(((f32[2048,256]{1,0:T(8,128)}), f32[2048,256]{1,0:T(8,128)}) %all-reduce.30.cloned.1.call-update) | async-done | bytes 2097168 | tf_op jit(solution)/shard_map/psum | solution.py:339
  (360 shorter events, 76.6 us)
Async XLA Ops:
  7.2 46.8 %copy-start = (bf16[2048,256]{1,0:T(8,128)(2,1)S(1)}, bf16[2048,256]{1,0:T(8,128)(2,1)}, u32[]{:S(2)}) copy-start(bf16[2048,256]{1,0:T(8,128)(2,1)} %param.23) | copy-start | bytes 3145732
  7.2 778.0 %all-gather.8.cloned.1.call-start = ((), (), s32[]{:S(2)}) async-start(), calls=%async_computation.9 | async-start | bytes 71303168 | tf_op jit(solution)/shard_map/all_gather | solution.py:98
  10.4 43.6 %copy-start.95 = (f32[4,256]{1,0:T(4,128)}, f32[4,256]{1,0:T(4,128)S(1)}, u32[]{:S(2)}) copy-start(f32[4,256]{1,0:T(4,128)S(1)} %get-tuple-element.271) | copy-start | bytes 12292
  49.9 31.5 %collective-permute-start = (f32[4,3,2048]{2,1,0:T(4,128)}, f32[4,3,2048]{2,1,0:T(4,128)S(1)}, u32[]{:S(2)}, u32[]{:S(2)}) collective-permute-start(f32[4,3,2048]{2,1,0:T(4,128)} %slice.222), channel_id=1, source_target_pairs={{0,2},{2,4},{4,6},{6,8},{8,10},{10,12},{12,14},{14,16},{16,18},{18... | collective-permute-start | bytes 294920 | tf_op jit(solution)/shard_map/ppermute | solution.py:16
  55.4 45.4 %copy-start.19 = (f32[4,256,256]{2,1,0:T(8,128)}, f32[4,256,256]{2,1,0:T(8,128)S(1)}, u32[]{:S(2)}) copy-start(f32[4,256,256]{2,1,0:T(8,128)S(1)} %fusion.70) | copy-start | bytes 3145732
  56.0 22.8 collective-permute-start.1
  66.5 112.6 %copy-start.74 = (f32[4,32]{1,0:T(4,128)}, f32[4,32]{1,0:T(4,128)S(1)}, u32[]{:S(2)}) copy-start(f32[4,32]{1,0:T(4,128)S(1)} %copy.522) | copy-start | bytes 1540
  67.2 33.7 %copy-start.46 = (f32[4,256]{1,0:T(4,128)}, f32[4,256]{1,0:T(4,128)S(1)}, u32[]{:S(2)}) copy-start(f32[4,256]{1,0:T(4,128)S(1)} %get-tuple-element.261) | copy-start | bytes 12292
  67.2 33.7 %copy-start.48 = (f32[4,256]{1,0:T(4,128)}, f32[4,256]{1,0:T(4,128)S(1)}, u32[]{:S(2)}) copy-start(f32[4,256]{1,0:T(4,128)S(1)} %get-tuple-element.262) | copy-start | bytes 12292
  67.2 33.7 %copy-start.50 = (f32[4,256]{1,0:T(4,128)}, f32[4,256]{1,0:T(4,128)S(1)}, u32[]{:S(2)}) copy-start(f32[4,256]{1,0:T(4,128)S(1)} %get-tuple-element.263) | copy-start | bytes 12292
  71.6 29.2 copy-start.17
  78.8 28.3 copy-start.29
  81.4 887.9 %copy-start.12 = (bf16[4,256,256]{2,1,0:T(8,128)(2,1)}, bf16[4,256,256]{2,1,0:T(8,128)(2,1)S(1)}, u32[]{:S(2)}) copy-start(bf16[4,256,256]{2,1,0:T(8,128)(2,1)S(1)} %get-tuple-element.226) | copy-start | bytes 1572868
  81.4 19.5 copy-start.36
  115.6 1529.6 %all-gather.10.cloned.1.call-start = ((), (), s32[]{:S(2)}) async-start(), calls=%async_computation.10 | async-start | bytes 71303168 | tf_op jit(solution)/shard_map/all_gather | solution.py:114
  130.6 16.5 copy-start.86
  130.6 80.6 %copy-start.27 = (f32[4,256,32]{2,0,1:T(4,128)S(1)}, f32[4,256,32]{2,0,1:T(4,128)}, u32[]{:S(2)}) copy-start(f32[4,256,32]{2,0,1:T(4,128)} %get-tuple-element.242) | copy-start | bytes 393220
  211.4 664.5 %copy-start.57 = (f32[4,32,256]{2,1,0:T(8,128)}, f32[4,32,256]{2,1,0:T(8,128)S(1)}, u32[]{:S(2)}) copy-start(f32[4,32,256]{2,1,0:T(8,128)S(1)} %copy.518) | copy-start | bytes 393220
  211.7 664.2 %copy-start.44 = (pred[4,256,256]{2,1,0:T(8,128)(4,1)}, pred[4,256,256]{2,1,0:T(8,128)(4,1)S(1)}, u32[]{:S(2)}) copy-start(pred[4,256,256]{2,1,0:T(8,128)(4,1)S(1)} %compare_and_fusion) | copy-start | bytes 786436
  212.0 663.9 %copy-start.33 = (f32[4,256,256]{2,1,0:T(8,128)}, f32[4,256,256]{2,1,0:T(8,128)S(1)}, u32[]{:S(2)}) copy-start(f32[4,256,256]{2,1,0:T(8,128)S(1)} %fusion.95) | copy-start | bytes 3145732
  872.4 39.6 %copy-start.4 = (f32[4,32,1,64,128]{4,2,3,1,0:T(1,128)}, f32[4,32,1,64,128]{4,2,3,1,0:T(1,128)S(1)}, u32[]{:S(2)}) copy-start(f32[4,32,1,64,128]{4,2,3,1,0:T(1,128)S(1)} %fusion.2) | copy-start | bytes 12582916
  875.9 36.2 %copy-start.9 = (f32[4,256,32,64]{1,3,2,0:T(8,128)}, f32[4,256,32,64]{1,3,2,0:T(8,128)S(1)}, u32[]{:S(2)}) copy-start(f32[4,256,32,64]{1,3,2,0:T(8,128)S(1)} %fusion.87) | copy-start | bytes 25165828
  978.8 975.3 %reduce-scatter.4.cloned.1.call-start = ((), (), s32[]{:S(2)}) async-start(), calls=%async_computation.3 | async-start | bytes 12582912 | tf_op jit(solution)/shard_map/reduce_scatter | solution.py:260
  1028.1 987.9 %reduce-scatter.8.cloned.1.call-start = ((), (), s32[]{:S(2)}) async-start(), calls=%async_computation.8 | async-start | bytes 17825792 | tf_op jit(solution)/shard_map/reduce_scatter | solution.py:268
  1046.6 1030.1 %all-reduce.28.cloned.1.call-start = ((), (), s32[]{:S(2)}) async-start(), calls=%async_computation.4 | async-start | bytes 16777216 | tf_op jit(solution)/shard_map/psum | solution.py:323
  1081.3 43.9 %copy-start.22 = (f32[4,256,256]{2,1,0:T(8,128)}, f32[4,256,256]{2,1,0:T(8,128)S(1)}, u32[]{:S(2)}) copy-start(f32[4,256,256]{2,1,0:T(8,128)S(1)} %get-tuple-element.192) | copy-start | bytes 3145732
  1094.6 30.6 %copy-start.13 = (bf16[4,256,256]{2,1,0:T(8,128)(2,1)S(1)}, bf16[4,256,256]{2,1,0:T(8,128)(2,1)}, u32[]{:S(2)}) copy-start(bf16[4,256,256]{2,1,0:T(8,128)(2,1)} %copy-done.12) | copy-start | bytes 1572868
  1108.5 536.7 %copy-start.43 = (f32[16,4,32,1,1]{0,3,4,2,1:T(1,128)S(1)}, f32[16,4,32,1,1]{0,3,4,2,1:T(1,128)}, u32[]{:S(2)}) copy-start(f32[16,4,32,1,1]{0,3,4,2,1:T(1,128)} %copy.572) | copy-start | bytes 24580
  1645.2 87.4 %copy-start.8 = (bf16[4,256,2048]{1,2,0:T(8,128)(2,1)S(1)}, bf16[4,256,2048]{1,2,0:T(8,128)(2,1)}, u32[]{:S(2)}) copy-start(bf16[4,256,2048]{1,2,0:T(8,128)(2,1)} %copy.512) | copy-start | bytes 12582916
  1739.9 22.0 copy-start.75
  1739.9 23.0 copy-start.30
  1744.4 18.5 copy-start.42
  1744.4 18.5 copy-start.45
  1798.6 16.2 copy-start.23
  1798.6 17.2 copy-start.20
  1798.6 17.2 copy-start.21
  1798.7 17.2 copy-start.28
  1798.7 17.3 copy-start.47
  1798.7 17.3 copy-start.49
  1798.7 17.3 copy-start.51
  1798.7 19.9 copy-start.80
  1798.7 19.9 copy-start.81
  1798.7 19.9 copy-start.82
  1798.7 19.9 copy-start.83
  1798.7 22.5 slice-start.2
  1819.1 15.4 copy-start.10
  1819.8 54.7 %collective-permute-start.3 = (f32[4,3,256]{2,1,0:T(4,128)}, f32[4,3,256]{2,1,0:T(4,128)}, u32[]{:S(2)}, u32[]{:S(2)}) collective-permute-start(f32[4,3,256]{2,1,0:T(4,128)} %pad_add_fusion.5), channel_id=1, source_target_pairs={{2,0},{4,2},{6,4},{8,6},{10,8},{12,10},{14,12},{16,14},{18,16},{20... | collective-permute-start | bytes 36872 | tf_op jit(solution)/shard_map/ppermute | solution.py:16
  1872.1 10.7 collective-permute-start.2
  1885.6 26.6 copy-start.24
  1921.1 831.5 %reduce-scatter.6.cloned.1.call-start = ((), (), s32[]{:S(2)}) async-start(), calls=%async_computation.5 | async-start | bytes 35651584 | tf_op jit(solution)/shard_map/reduce_scatter | solution.py:326
  1947.1 922.7 %all-reduce.32.cloned.1.call-start = ((), (), s32[]{:S(2)}) async-start(), calls=%async_computation.7 | async-start | bytes 524288 | tf_op jit(solution)/shard_map/psum | solution.py:351
  1953.9 64.7 %copy-start.100 = (f32[32]{0:T(128)S(1)}, f32[32]{0:T(128)}, u32[]{:S(2)}) copy-start(f32[32]{0:T(128)} %get-tuple-element.244) | copy-start | bytes 388
  1953.9 64.7 %copy-start.103 = (f32[32]{0:T(128)S(1)}, f32[32]{0:T(128)}, u32[]{:S(2)}) copy-start(f32[32]{0:T(128)} %param.26) | copy-start | bytes 388
  1954.1 69.6 %copy-start.91 = (f32[256]{0:T(256)S(1)}, f32[256]{0:T(256)}, u32[]{:S(2)}) copy-start(f32[256]{0:T(256)} %get-tuple-element.204) | copy-start | bytes 3076
  1954.1 69.6 %copy-start.92 = (f32[256]{0:T(256)S(1)}, f32[256]{0:T(256)}, u32[]{:S(2)}) copy-start(f32[256]{0:T(256)} %get-tuple-element.205) | copy-start | bytes 3076
  1954.1 69.6 %copy-start.93 = (f32[256]{0:T(256)S(1)}, f32[256]{0:T(256)}, u32[]{:S(2)}) copy-start(f32[256]{0:T(256)} %get-tuple-element.206) | copy-start | bytes 3076
  1954.1 69.6 %copy-start.94 = (f32[256]{0:T(256)S(1)}, f32[256]{0:T(256)}, u32[]{:S(2)}) copy-start(f32[256]{0:T(256)} %get-tuple-element.207) | copy-start | bytes 3076
  1954.1 69.7 %copy-start.90 = (f32[256]{0:T(256)S(1)}, f32[256]{0:T(256)}, u32[]{:S(2)}) copy-start(f32[256]{0:T(256)} %get-tuple-element.208) | copy-start | bytes 3076
  1954.1 113.9 %copy-start.71 = (f32[2048]{0:T(1024)S(1)}, f32[2048]{0:T(1024)}, u32[]{:S(2)}) copy-start(f32[2048]{0:T(1024)} %get-tuple-element.196) | copy-start | bytes 24580
  1954.1 113.9 %copy-start.72 = (f32[2048]{0:T(1024)S(1)}, f32[2048]{0:T(1024)}, u32[]{:S(2)}) copy-start(f32[2048]{0:T(1024)} %get-tuple-element.197) | copy-start | bytes 24580
  1954.1 113.9 %copy-start.73 = (f32[2048]{0:T(1024)S(1)}, f32[2048]{0:T(1024)}, u32[]{:S(2)}) copy-start(f32[2048]{0:T(1024)} %get-tuple-element.198) | copy-start | bytes 24580
  1954.1 113.9 %copy-start.59 = (f32[2048]{0:T(1024)S(1)}, f32[2048]{0:T(1024)}, u32[]{:S(2)}) copy-start(f32[2048]{0:T(1024)} %param.21) | copy-start | bytes 24580
  1954.2 113.9 %copy-start.96 = (f32[4,256]{1,0:T(4,128)S(1)}, f32[4,256]{1,0:T(4,128)}, u32[]{:S(2)}) copy-start(f32[4,256]{1,0:T(4,128)} %copy-done.95) | copy-start | bytes 12292
  2023.6 985.7 %all-reduce.30.cloned.1.call-start = ((), (), s32[]{:S(2)}) async-start(), calls=%async_computation.6 | async-start | bytes 4194304 | tf_op jit(solution)/shard_map/psum | solution.py:339
  (59 other events, 452.9 us)
Sparse Core Ops, SparseCore 0:
  115.7 669.4 all-gather.7
  979.0 666.1 all-gather.9
  1647.5 15.8 reduce-scatter.3
  1665.6 350.3 reduce-scatter.7
  2018.5 44.8 all-reduce.27
  2065.7 686.9 reduce-scatter.5
  2759.3 110.4 all-reduce.31
  2875.7 133.5 all-reduce.29
where the time goes:
time: 3030 us; the launch traced here: 3020 us
  waiting for transfers between devices  1990 us (66%)
  matrix products  488 us (16%)
  blocking collectives  180 us (6%)
  other arithmetic  169 us (6%)
  local copies, waits for them, and re-layouts  165 us (5%)
    reduce_scatter x1, waiting for transfers between devices, body(): lax.psum_scatter(in_term(normed_low, grad_gate_x), 'seq', scatter_dimensi...  593 us
    all_gather x1, waiting for transfers between devices, earlier_states(): lax.all_gather(device_state[None], 'seq', axis=0, tiled=True)  566 us
    all_gather x1, waiting for transfers between devices, later_grads(): grads = lax.all_gather(device_grad[None], 'seq', axis=0, tiled=True)  519 us
    psum x1, waiting for transfers between devices, body(): lax.psum((grad_bc_weight, grad_bc_conv_weight, grad_bc_conv_bias), ('seq'...  140 us
    psum x1, waiting for transfers between devices, body(): lax.psum((grad_norm_gain, grad_dt_weight, grad_dt_bias, grad_a_log, grad_...  113 us
    dot_general x1, matrix products, later_grads(): return jnp.einsum('jmh,jmhpn->mhpn', weight, grads, precision=HIGHEST)  87.4 us
    dot_general x1, matrix products, earlier_states(): incoming = jnp.einsum('jmh,jmhpn->mhpn', weight, states, precision=HIGHEST)  87.1 us
    dot_general x3, matrix products, block_output(): result = jnp.einsum('hij,jhp->ihp', weights, values, precision=HIGHEST)  84.2 us
  transfers between devices with their start and end apart: 12, of which 7 were waited for; matrix products, arithmetic and copies ran while one was open for 18% of the time, Pallas kernels for 0%

commit v1 on v0

--- a/solution.py
+++ b/solution.py
@@ -1,6 +1,10 @@
+import functools
+
 import jax
 import jax.numpy as jnp
 from jax import lax
+from jax.experimental import pallas as pl
+from jax.experimental.pallas import tpu as pltpu
 from jax.sharding import PartitionSpec as P
 
 BLOCK = 256
@@ -81,44 +85,276 @@
     return kept + jnp.einsum("jh,jhp,jn->hpn", weights, values, b_rows, precision=HIGHEST)
 
 
-def running_totals(logs, lives):
-    log_prefix = jnp.concatenate([jnp.zeros_like(logs[:1]), jnp.cumsum(logs, axis=0)], axis=0)
-    break_prefix = jnp.concatenate(
-        [jnp.zeros_like(lives[:1]), jnp.cumsum(1.0 - lives, axis=0)], axis=0
-    )
-    return (log_prefix, break_prefix)
-
-
-def masked_exp(valid, gap):
-    return jnp.where(valid[:, :, None], jnp.exp(jnp.where(valid[:, :, None], gap, 0.0)), 0.0)
-
-
-def earlier_states(device_state, device_log, device_live):
-    states, logs, lives = (
-        lax.all_gather(device_state[None], "seq", axis=0, tiled=True),
-        lax.all_gather(device_log[None], "seq", axis=0, tiled=True),
-        lax.all_gather(device_live[None], "seq", axis=0, tiled=True),
-    )
-    log_prefix, break_prefix = running_totals(logs, lives)
-    own_index = lax.axis_index("seq")
-    here_log = lax.dynamic_index_in_dim(log_prefix, own_index, 0, keepdims=True)
-    here_break = lax.dynamic_index_in_dim(break_prefix, own_index, 0, keepdims=True)
-    order = jnp.arange(states.shape[0])[:, None]
-    valid = (order < own_index) & (here_break - break_prefix[1:] == 0.0)
-    weight = masked_exp(valid, here_log - log_prefix[1:])
-    incoming = jnp.einsum("jmh,jmhpn->mhpn", weight, states, precision=HIGHEST)
-    return (incoming, log_prefix, break_prefix)
-
-
-def later_grads(device_grad, log_prefix, break_prefix):
-    grads = lax.all_gather(device_grad[None], "seq", axis=0, tiled=True)
-    own_index = lax.axis_index("seq")
-    next_log = lax.dynamic_index_in_dim(log_prefix, own_index + 1, 0, keepdims=True)
-    next_break = lax.dynamic_index_in_dim(break_prefix, own_index + 1, 0, keepdims=True)
-    order = jnp.arange(grads.shape[0])[:, None]
-    valid = (order > own_index) & (break_prefix[:-1] - next_break == 0.0)
-    weight = masked_exp(valid, log_prefix[:-1] - next_log)
-    return jnp.einsum("jmh,jmhpn->mhpn", weight, grads, precision=HIGHEST)
+DEAD = -1e30
+GROUP = 4
+
+
+def exchange_kernel(
+    length,
+    reverse,
+    part_ref,
+    log_ref,
+    out_ref,
+    parts,
+    logs,
+    edge_in,
+    edge_out,
+    given,
+    part_send,
+    part_recv,
+    log_send,
+    log_recv,
+    edge_send,
+    edge_recv,
+    given_send,
+    given_recv,
+):
+    me = lax.axis_index("seq")
+    rank = lax.rem(me, GROUP)
+    plane = me // GROUP
+    first = me - rank
+    mates = (
+        rank + 1 - 2 * lax.rem(rank, 2),
+        rank + 2 - 4 * (rank // 2),
+        3 - rank,
+    )
+    micro = part_ref.shape[0]
+    planes = length // GROUP
+    begins, ends = plane == 0, plane == planes - 1
+    if reverse:
+        begins, ends = ends, begins
+    step = -GROUP if reverse else GROUP
+
+    barrier = pltpu.get_barrier_semaphore()
+    for mate in mates:
+        pl.semaphore_signal(
+            barrier, inc=1, device_id={"seq": first + mate}, device_id_type=pl.DeviceIdType.MESH
+        )
+
+    @pl.when(plane > 0)
+    def _():
+        pl.semaphore_signal(
+            barrier, inc=1, device_id={"seq": me - GROUP}, device_id_type=pl.DeviceIdType.MESH
+        )
+
+    @pl.when(plane < planes - 1)
+    def _():
+        pl.semaphore_signal(
+            barrier, inc=1, device_id={"seq": me + GROUP}, device_id_type=pl.DeviceIdType.MESH
+        )
+
+    above = jnp.where(plane < planes - 1, 1, 0)
+    below = jnp.where(plane > 0, 1, 0)
+    pl.semaphore_wait(barrier, 3 + above + below)
+
+    def remote(src, dst, send, recv, target):
+        return pltpu.make_async_remote_copy(
+            src_ref=src,
+            dst_ref=dst,
+            send_sem=send,
+            recv_sem=recv,
+            device_id={"seq": target},
+            device_id_type=pl.DeviceIdType.MESH,
+        )
+
+    def log_copy(slot):
+        mate = mates[slot]
+        return remote(
+            log_ref.at[mate], logs.at[rank], log_send.at[slot], log_recv.at[slot], first + mate
+        )
+
+    def part_copy(m, slot):
+        mate = mates[slot]
+        return remote(
+            part_ref.at[m, mate],
+            parts.at[m, rank],
+            part_send.at[m, slot],
+            part_recv.at[m, slot],
+            first + mate,
+        )
+
+    def edge_copy(m):
+        return remote(edge_out.at[m], edge_in.at[m], edge_send.at[m], edge_recv.at[m], me + step)
+
+    def given_copy(m, slot):
+        mate = mates[slot]
+        return remote(
+            given.at[m, mate],
+            out_ref.at[m, rank],
+            given_send.at[m, slot],
+            given_recv.at[m, slot],
+            first + mate,
+        )
+
+    for slot in range(3):
+        log_copy(slot).start()
+    for m in range(micro):
+        for slot in range(3):
+            part_copy(m, slot).start()
+    logs[rank] = log_ref[rank]
+    for m in range(micro):
+        parts[m, rank] = part_ref[m, rank]
+
+    @pl.when(begins)
+    def _():
+        edge_in[...] = jnp.zeros_like(edge_in)
+
+    for slot in range(3):
+        log_copy(slot).wait()
+    order = tuple(reversed(range(GROUP))) if reverse else tuple(range(GROUP))
+    for m in range(micro):
+        for slot in range(3):
+            part_copy(m, slot).wait()
+        factors = [jnp.exp(logs[t, m])[:, None, :] for t in order]
+        whole = jnp.exp(logs[0, m] + logs[1, m] + logs[2, m] + logs[3, m])[:, None, :]
+        total = parts[m, order[0]]
+        for t, factor in zip(order[1:], factors[1:]):
+            total = total * factor + parts[m, t]
+
+        @pl.when(jnp.logical_not(begins))
+        def _():
+            edge_copy(m).wait_recv()
+
+        @pl.when(jnp.logical_not(ends))
+        def _():
+            edge_out[m] = total + whole * edge_in[m]
+            edge_copy(m).start()
+
+        running = edge_in[m]
+        for place, (t, factor) in enumerate(zip(order, factors)):
+            given[m, t] = running
+            if place < GROUP - 1:
+                running = running * factor + parts[m, t]
+        for slot in range(3):
+            given_copy(m, slot).start()
+        out_ref[m, rank] = given[m, rank]
+    for m in range(micro):
+        for slot in range(3):
+            given_copy(m, slot).wait()
+
+        @pl.when(jnp.logical_not(ends))
+        def _():
+            edge_copy(m).wait_send()
+
+
+def exchange(parts, logs, reverse):
+    micro, heads, rows, columns = parts.shape
+    quarter = heads // GROUP
+    length = lax.axis_size("seq")
+    spread = jnp.broadcast_to(logs[:, :, None], (micro, heads, columns))
+    spread = spread.reshape(micro, GROUP, quarter, columns).transpose(1, 0, 2, 3)
+    shape = (micro, GROUP, quarter, rows, columns)
+    out = pl.pallas_call(
+        functools.partial(exchange_kernel, length, reverse),
+        out_shape=jax.ShapeDtypeStruct(shape, jnp.float32),
+        in_specs=[pl.BlockSpec(memory_space=pltpu.VMEM)] * 2,
+        out_specs=pl.BlockSpec(memory_space=pltpu.VMEM),
+        scratch_shapes=[
+            pltpu.VMEM(shape, jnp.float32),
+            pltpu.VMEM((GROUP, micro, quarter, columns), jnp.float32),
+            pltpu.VMEM((micro, quarter, rows, columns), jnp.float32),
+            pltpu.VMEM((micro, quarter, rows, columns), jnp.float32),
+            pltpu.VMEM(shape, jnp.float32),
+            pltpu.SemaphoreType.DMA((micro, 3)),
+            pltpu.SemaphoreType.DMA((micro, 3)),
+            pltpu.SemaphoreType.DMA((3,)),
+            pltpu.SemaphoreType.DMA((3,)),
+            pltpu.SemaphoreType.DMA((micro,)),
+            pltpu.SemaphoreType.DMA((micro,)),
+            pltpu.SemaphoreType.DMA((micro, 3)),
+            pltpu.SemaphoreType.DMA((micro, 3)),
+        ],
+        compiler_params=pltpu.CompilerParams(
+            collective_id=1 if reverse else 0,
+            has_side_effects=True,
+            vmem_limit_bytes=40 * 1024 * 1024,
+        ),
+        name="exchange_back" if reverse else "exchange",
+    )(parts.reshape(shape), spread)
+    return out.reshape(micro, heads, rows, columns)
+
+
+def xor_permute(value, axis, bit):
+    size = lax.axis_size(axis)
+    return lax.ppermute(value, axis, [(i, i ^ (1 << bit)) for i in range(size)])
+
+
+def axis_bits(axis):
+    return (lax.axis_size(axis) - 1).bit_length()
+
+
+def own_bit(axis, bit):
+    return lax.rem(lax.axis_index(axis) // (1 << bit), 2)
+
+
+def pick(array, dim, index):
+    return lax.dynamic_index_in_dim(array, index, dim, keepdims=False)
+
+
+def all_sum(value, axis):
+    for bit in range(axis_bits(axis)):
+        value = value + xor_permute(value, axis, bit)
+    return value
+
+
+def scatter_product(left, right, order):
+    bits = axis_bits("seq")
+    tokens, rows = left.shape
+    block = rows >> bits
+    names = list(range(bits - 1, -1, -1))
+    view = left.reshape((tokens,) + (2,) * bits + (block,))
+    total = None
+    for place, bit in enumerate(order):
+        dim = names.index(bit)
+        names.remove(bit)
+        mine = own_bit("seq", bit)
+        if place == 0:
+            def product(index):
+                chosen = pick(view, dim + 1, index).reshape(tokens, rows // 2)
+                return lax.dot_general(
+                    chosen, right, (((0,), (0,)), ((), ())), preferred_element_type=jnp.float32
+                )
+
+            arrived = xor_permute(product(1 - mine), "seq", bit)
+            total = product(mine) + arrived
+        else:
+            cut = total.reshape((2,) * (len(names) + 1) + (block, right.shape[1]))
+            arrived = xor_permute(pick(cut, dim, 1 - mine), "seq", bit)
+            total = pick(cut, dim, mine) + arrived
+        total = total.reshape((2,) * len(names) + (block, right.shape[1]))
+    return total.reshape(block, right.shape[1])
+
+
+def scatter_orders():
+    bits = axis_bits("seq")
+    if bits < 3:
+        return [tuple(range(bits))]
+    rest = tuple(range(3, bits))
+    return [(0, 1, 2) + rest, (1, 0, 2) + rest, (2, 0, 1) + rest]
+
+
+def scatter_all(left, right):
+    orders = scatter_orders()
+    columns = right.shape[1]
+    unit = max(columns // 16, 128)
+    shares = [5 * unit, 6 * unit, columns - 11 * unit] if columns >= 16 * 128 else [columns]
+    if len(shares) > len(orders):
+        shares = [columns]
+    parts, first = [], 0
+    for share, order in zip(shares, orders):
+        parts.append(scatter_product(left, right[:, first : first + share], order))
+        first += share
+    return jnp.concatenate(parts, axis=1) if len(parts) > 1 else parts[0]
+
+
+def gather_rows(block, axis):
+    for bit in range(axis_bits(axis)):
+        other = xor_permute(block, axis, bit)
+        mine = own_bit(axis, bit)
+        low = jnp.where(mine == 0, block, other)
+        high = jnp.where(mine == 0, other, block)
+        block = jnp.concatenate([low, high], axis=0)
+    return block
 
 
 def out_term(cot_flat, normed_gate):
@@ -222,7 +458,8 @@
     device_state = factor[:, piece, :, None, None] * device_state + own_states[:, piece]
     device_log = jnp.sum(block_logs.reshape(micro, pieces, heads), axis=1)
     device_live = jnp.prod(living.reshape(micro, pieces), axis=1)
-    incoming, log_prefix, break_prefix = earlier_states(device_state, device_log, device_live)
+    exchange_log = jnp.where(device_live[:, None] > 0.0, device_log, DEAD)
+    incoming = exchange(device_state, exchange_log, False)
     current = incoming
     piece = 0
     starts = [current]
@@ -251,7 +488,7 @@
     mixed = mixed.reshape(micro, length, inner)
     gate_act = jax.nn.silu(gate_pre)
     gated = mixed * gate_act
-    square_sum = lax.psum(jnp.sum(gated * gated, axis=-1), "head")
+    square_sum = all_sum(jnp.sum(gated * gated, axis=-1), "head")
     scale = lax.rsqrt(square_sum / full_inner + EPSILON)[:, :, None]
     normed_gate = (gated * scale * gate_gain).astype(jnp.bfloat16).reshape(total, inner)
     head_terms = lax.dot_general(
@@ -265,11 +502,9 @@
     grad_gate_n = jnp.dot(cot_flat, out_weight, preferred_element_type=jnp.float32).reshape(
         micro, length, inner
     )
-    grad_out_weight = lax.psum_scatter(
-        out_term(cot_flat, normed_gate), "seq", scatter_dimension=0, tiled=True
-    )
+    grad_out_weight = scatter_all(cot_flat, normed_gate)
     grad_gate_gain = jnp.sum(grad_gate_n * gated * scale, axis=(0, 1))
-    dot_total = lax.psum(jnp.sum(grad_gate_n * gate_gain * gated, axis=-1), "head")
+    dot_total = all_sum(jnp.sum(grad_gate_n * gate_gain * gated, axis=-1), "head")
     grad_gated = (
         grad_gate_n * gate_gain * scale - gated * scale**3 * dot_total[:, :, None] / full_inner
     )
@@ -286,7 +521,7 @@
     device_grad = jnp.zeros_like(device_state)
     for piece in reversed(range(pieces)):
         device_grad = grad_starts[:, piece] + factor[:, piece, :, None, None] * device_grad
-    outgoing = later_grads(device_grad, log_prefix, break_prefix)
+    outgoing = exchange(device_grad, exchange_log, True)
     ends = [outgoing] * pieces
     current = outgoing
     for piece in reversed(range(pieces)):
@@ -320,11 +555,12 @@
         precision=HIGHEST,
         preferred_element_type=jnp.float32,
     )
-    row_grads = lax.psum(row_part, "head")
+    row_grads = all_sum(row_part, "head")
     grad_flat, grad_norm_gain = norm_back(row_grads)
     grad_tokens = (cot_flat.astype(jnp.float32) + grad_flat).reshape(micro, length, width)
-    grad_in_weight = lax.psum_scatter(
-        in_term(normed_low, grad_gate_x), "seq", scatter_dimension=0, tiled=True
+    grad_in_weight = jnp.stack(
+        [scatter_all(normed_low, grad_gate_x[:, 0]), scatter_all(normed_low, grad_gate_x[:, 1])],
+        axis=1,
     )
     grad_bc_weight = jnp.einsum(
         "td,tc->dc", normed_low, bc_flat, precision=HIGHEST, preferred_element_type=jnp.float32
@@ -336,31 +572,45 @@
         precision=HIGHEST,
         preferred_element_type=jnp.float32,
     )
-    grad_bc_weight, grad_bc_conv_weight, grad_bc_conv_bias = lax.psum(
-        (grad_bc_weight, grad_bc_conv_weight, grad_bc_conv_bias), ("seq", "head")
-    )
-    (
+    bits = axis_bits("seq")
+    rows = width >> bits
+    narrow = jnp.concatenate([all_sum(grad_bc_weight, "head"), grad_dt_weight], axis=1)
+    across = narrow.shape[1]
+    for bit in range(bits):
+        cut = narrow.reshape((2,) * (bits - bit) + (rows, across))
+        mine = own_bit("seq", bit)
+        dim = bits - bit - 1
+        narrow = pick(cut, dim, mine) + xor_permute(pick(cut, dim, 1 - mine), "seq", bit)
+    narrow = gather_rows(narrow.reshape(rows, across), "seq")
+    grad_bc_weight = narrow[:, : 2 * state_size]
+    grad_dt_weight = narrow[:, 2 * state_size :]
+    shared = [grad_bc_conv_weight, grad_bc_conv_bias]
+    shared_row = all_sum(jnp.concatenate([item.reshape(-1) for item in shared]), "head")
+    small = [
         grad_norm_gain,
-        grad_dt_weight,
         grad_dt_bias,
         grad_a_log,
         grad_d_skip,
         grad_conv_weight,
         grad_conv_bias,
         grad_gate_gain,
-    ) = lax.psum(
-        (
-            grad_norm_gain,
-            grad_dt_weight,
-            grad_dt_bias,
-            grad_a_log,
-            grad_d_skip,
-            grad_conv_weight,
-            grad_conv_bias,
-            grad_gate_gain,
-        ),
-        "seq",
-    )
+    ]
+    row = all_sum(jnp.concatenate([shared_row] + [item.reshape(-1) for item in small]), "seq")
+    pieces_out, first = [], 0
+    for item in shared + small:
+        pieces_out.append(row[first : first + item.size].reshape(item.shape))
+        first += item.size
+    (
+        grad_bc_conv_weight,
+        grad_bc_conv_bias,
+        grad_norm_gain,
+        grad_dt_bias,
+        grad_a_log,
+        grad_d_skip,
+        grad_conv_weight,
+        grad_conv_bias,
+        grad_gate_gain,
+    ) = pieces_out
     return (
         block_out,
         grad_tokens,

time: 3030 us -> 1640 us (0.54)
  waiting for transfers between devices: 1990 us -> 462 us
  Pallas kernels: 0 us -> 205 us
  blocking collectives: 180 us -> 0 us
  matrix products: 488 us -> 314 us
  local copies, waits for them, and re-layouts: 165 us -> 337 us
  other arithmetic: 169 us -> 231 us
  starting transfers between devices: 11 us -> 59.2 us
    all_gather x2 -> x0, waiting for transfers between devices: 1080 us -> none  [the longest x1 566 us: earlier_states(): lax.all_gather(device_state[None], 'seq', axis=0, tiled=True)]
    reduce_scatter x2 -> x0, waiting for transfers between devices: 649 us -> none  [the longest x1 593 us: body(): lax.psum_scatter(in_term(normed_low, grad_gate_x), 'seq', scatter_dimensi...]
    ppermute x0 -> x53, waiting for transfers between devices: none -> 462 us  [xor_permute(): return lax.ppermute(value, axis, [(i, i ^ 1 << bit) for i in range(size)])]
    psum x3 -> x0, waiting for transfers between devices: 252 us -> none  [the longest x1 140 us: body(): lax.psum((grad_bc_weight, grad_bc_conv_weight, grad_bc_conv_bias), ('seq'...]
    pallas_call x0 -> x2, Pallas kernels: none -> 205 us  [exchange(): pl.pallas_call(functools.partial(exchange_kernel, length, reverse), out_s...]
    dot_general x4 -> x18, matrix products: 219 us -> 67.6 us  [product(): lax.dot_general(chosen, right, (((0,), (0,)), ((), ())), preferred_elemen...]
    dynamic_slice x0 -> x20, local copies, waits for them, and re-layouts: none -> 133 us  [pick(): return lax.dynamic_index_in_dim(array, index, dim, keepdims=False)]
    psum x4 -> x0, blocking collectives: 117 us -> none  [the longest x1 67.5 us: body(): lax.psum((grad_norm_gain, grad_dt_weight, grad_dt_bias, grad_a_log, grad_...]
  transfers between devices with their start and end apart: 12 -> 58, of which waited for: 7 -> 27; matrix products, arithmetic and copies ran while one was open for 18% -> 45% of each run, Pallas kernels for 0% -> 7%
where the time goes in v1:
time: 1640 us; the launch traced here: 1630 us
  waiting for transfers between devices  462 us (28%)
  local copies, waits for them, and re-layouts  337 us (21%)
  matrix products  314 us (19%)
  other arithmetic  231 us (14%)
  Pallas kernels  205 us (12%)
  starting transfers between devices  59.2 us (4%)
  between operations  16.8 us (1%)
    ppermute x53, waiting for transfers between devices, xor_permute(): return lax.ppermute(value, axis, [(i, i ^ 1 << bit) for i in range(size)])  462 us
    pallas_call x2, Pallas kernels, exchange(): pl.pallas_call(functools.partial(exchange_kernel, length, reverse), out_s...  205 us
    dynamic_slice x20, local copies, waits for them, and re-layouts, pick(): return lax.dynamic_index_in_dim(array, index, dim, keepdims=False)  133 us
    dot_general x3, matrix products, block_output(): result = jnp.einsum('hij,jhp->ihp', weights, values, precision=HIGHEST)  86.6 us
    dot_general x18, matrix products, product(): lax.dot_general(chosen, right, (((0,), (0,)), ((), ())), preferred_elemen...  67.6 us
    ppermute x53, starting transfers between devices, xor_permute(): return lax.ppermute(value, axis, [(i, i ^ 1 << bit) for i in range(size)])  48.8 us
    reshape x3, local copies, waits for them, and re-layouts, body(): mixed = mixed.reshape(micro, length, inner)  39.9 us
    another operation x7, other arithmetic  35.2 us
  transfers between devices with their start and end apart: 58, of which 27 were waited for; matrix products, arithmetic and copies ran while one was open for 45% of the time, Pallas kernels for 7%

profile of v1, /device:TPU:1, one launch (start us, length us, event | category | flops | bytes accessed | tf_op | source)
XLA Modules:
  0.0 1625.5 jit_solution(3666529543554435108)
XLA Ops:
  13.9 22.8 %fusion.23 = f32[1024,2,2048]{2,0,1:T(8,128)} fusion(bf16[2048,2,2048]{2,1,0:T(2,128)(2,1)} %param.22, bf16[1024,2048]{1,0:T(8,128)(2,1)S(1)} %multiply_convert_fusion.5), kind=kOutput, calls=%fused_computation.25 | convolution fusion | flops 17179869184 | bytes 37748736 | tf_op jit(solution)/shard_map/td,dkc->tkc/dot_general | solution.py:407
  36.7 10.0 fusion.151
  59.0 11.9 reshape.709
  70.9 7.7 reshape_reshape.2
  78.6 7.5 multiply_convert_fusion
  86.2 7.3 constant_dynamic-slice_fusion.9
  98.4 11.4 constant_dynamic-slice_fusion.13
  109.9 9.9 constant_dynamic-slice_fusion.5
  126.9 14.4 reduce-window.20
  150.3 7.1 constant_dynamic-slice_fusion.11
  158.9 14.4 reshape.723
  173.4 14.3 copy.550
  192.7 19.5 %multiply_convert_fusion.4 = (bf16[4,256,2048]{2,1,0:T(8,128)(2,1)}, f32[4,256,2048]{2,1,0:T(8,128)}) fusion(f32[4,256]{1,0:T(4,128)S(1)} %get-tuple-element.261, f32[4,256,2048]{2,1,0:T(8,128)} %bitcast.405, f32[4,3,2048]{2,1,0:T(4,128)} %collective-permute-done, f32[2048]{0:T(1024)S(1)} %bitcast.499, f32[4,256]{1,0:T(4,128)S(1)} %get-tuple-element.262, ...), kind=kLoop, calls=%fused_computation.81 | loop fusion | flops 39845888 | bytes 21123072 | tf_op jit(solution)/shard_map/convert_element_type | solution.py:430
  212.2 6.9 copy.545
  231.4 93.9 %exchange.1 = f32[4,4,8,64,128]{4,3,2,1,0:T(8,128)S(1)} custom-call(f32[4,4,8,64,128]{4,3,2,1,0:T(8,128)S(1)} %bitcast.398, f32[4,4,8,128]{3,2,1,0:T(8,128)S(1)} %broadcast_bitcast_fusion.log_ref), custom_call_target="tpu_custom_call" | custom-call | tf_op jit(solution)/shard_map/exchange/pallas_call | solution.py:247
  329.1 34.9 %multiply_reduce_fusion.12 = (f32[4,256]{1,0:T(4,128)S(1)}, f32[4,256,32,64]{1,3,2,0:T(8,128)}) fusion(f32[4,256,32,64]{1,3,2,0:T(8,128)} %copy.550, f32[4,256,32,64]{1,3,2,0:T(8,128)} %bitcast.426, f32[32]{0:T(128)S(1)} %copy-done.157, f32[4,256,32,64]{1,3,2,0:T(8,128)S(1)} %fusion.108, f32[4,256,32]{1,2,0:T(8,128)S(1)} %copy.538, ...), kind=kOutput, calls=%fused_computation.79 | convolution fusion | flops 6507461632 | bytes 39456896 | tf_op jit(solution)/shard_map/jvp(vmap(hij,jhp->ihp))/dot_general | solution.py:72
  397.4 10.6 copy.581
  408.0 10.7 copy.580
  440.5 9.0 copy.590
  449.5 10.5 copy.589
  460.0 16.2 copy.612
  476.2 14.8 reshape.722
  491.1 8.9 copy.551
  500.0 7.8 fusion.48
  509.8 13.3 fusion.156
  523.2 19.3 %multiply_reduce_fusion.2 = (f32[2048]{0:T(1024)}, f32[4,256]{1,0:T(4,128)S(1)}, f32[4,256,2048]{2,1,0:T(8,128)S(1)}) fusion(f32[4,256]{1,0:T(4,128)S(1)} %get-tuple-element.203, f32[4,256,2048]{2,1,0:T(8,128)} %copy.551, f32[4,256,2048]{2,1,0:T(8,128)} %bitcast.407, f32[2048]{0:T(1024)S(1)} %copy-done.116, bf16[4,256,2048]{2,1,0:T(8,128)(2,1)} %param.34, ...), kind=kOutput, calls=%fused_computation.64 | convolution fusion | flops 8613000192 | bytes 37773312 | tf_op jit(solution)/shard_map/dot_general | solution.py:502
  557.3 9.5 multiply_reduce_fusion.7
  566.8 6.9 copy.553
  573.7 6.5 copy.554
  580.2 9.0 multiply_reduce_fusion.10
  593.5 111.4 %exchange_back.1 = f32[4,4,8,64,128]{4,3,2,1,0:T(8,128)S(1)} custom-call(f32[4,4,8,64,128]{4,3,2,1,0:T(8,128)S(1)} %bitcast.397, f32[4,4,8,128]{3,2,1,0:T(8,128)S(1)} %broadcast_bitcast_fusion.log_ref), custom_call_target="tpu_custom_call" | custom-call | tf_op jit(solution)/shard_map/exchange_back/pallas_call | solution.py:247
  713.6 26.9 %fusion.8 = (f32[4,32,256]{2,1,0:T(8,128)}, f32[4,32,256]{2,1,0:T(8,128)}, f32[4,32,256]{2,1,0:T(8,128)}, f32[4,256,256]{2,1,0:T(8,128)S(1)}) fusion(f32[4,32,256]{2,1,0:T(8,128)} %copy.535, f32[4,256,256]{2,1,0:T(8,128)S(1)} %copy-done.78, f32[4,32,256]{2,1,0:T(8,128)S(1)} %copy-done.84, pred[4,256,256]{2,1,0:T(8,128)(4,1)S(1)} %copy-done.88, ...), kind=kOutput, calls=%fused_computation.10 | convolution fusion | flops 1199210496 | bytes 11403264 | tf_op jit(solution)/shard_map/transpose(jvp(vmap(hij,jhp->ihp)))/dot_general | solution.py:72
  740.5 24.8 %fusion.37 = f32[4,256,32,64]{1,3,2,0:T(8,128)} fusion(f32[4,256,32,64]{1,3,2,0:T(8,128)S(1)} %get-tuple-element.277, f32[4,256,32,64]{1,3,2,0:T(8,128)S(1)} %bitcast.400, f32[32]{0:T(128)S(1)} %copy-done.158, f32[4,256,32]{1,2,0:T(8,128)S(1)} %copy-done.71, bf16[4,32,64,256]{3,2,1,0:T(8,128)(2,1)S(1)} %bitcast.444, f32[4,32,256]{2,1,0:T(8,128)S(1)} %copy-done.98, ...), kind=kOutput, calls=%fused_computation.50 | convolution fusion | flops 6492782592 | bytes 31064192 | tf_op jit(solution)/shard_map/transpose(jvp(vmap(hij,jhp->ihp)))/dot_general | solution.py:72
  765.3 8.7 copy.555
  774.1 23.5 %multiply_reduce_fusion.6 = (f32[2048]{0:T(1024)}, f32[2048]{0:T(1024)}, f32[2048]{0:T(1024)}, f32[2048]{0:T(1024)}, f32[2048]{0:T(1024)}, /*index=5*/f32[4,256,2048]{2,1,0:T(8,128)}) fusion(f32[4,256,2048]{2,1,0:T(8,128)} %bitcast.406, f32[4,3,2048]{2,1,0:T(4,128)} %collective-permute-done, f32[4,256]{1,0:T(4,128)S(1)} %copy-done.90, ...), kind=kLoop, calls=%fused_computation.68 | loop fusion | flops 50321408 | bytes 33705984 | tf_op jit(solution)/shard_map/transpose(jvp(vmap()))/reduce_sum | solution.py:46
  797.6 14.8 multiply_multiply_fusion.2
  812.4 15.2 pad_add_fusion
  830.1 13.7 fusion.79
  843.8 13.5 fusion.82
  876.6 10.0 reduce-window.26
  896.8 10.7 reduce-window.24
  909.8 7.0 fusion.157
  963.5 26.6 %fusion.21 = f32[1024,2048,1]{1,0,2:T(8,128)S(1)} fusion(bf16[2048,2,2048]{2,1,0:T(2,128)(2,1)} %param.22, bf16[1024,1,2048]{2,0,1:T(8,128)(2,1)} %bitcast.436, bf16[1024,1,2048]{2,0,1:T(8,128)(2,1)} %bitcast.429), kind=kOutput, calls=%fused_computation.23 | convolution fusion | flops 17184063488 | bytes 33554432 | tf_op jit(solution)/shard_map/tkc,dkc->td/dot_general | solution.py:547
  990.1 9.5 fusion.36
  1044.1 34.6 %collective-permute-done.32 = f32[1024,640]{1,0:T(8,128)S(1)} collective-permute-done((f32[1024,640]{1,0:T(8,128)}, f32[1024,640]{1,0:T(8,128)S(1)}, u32[]{:S(2)}, u32[]{:S(2)}) %collective-permute-start.32) | collective-permute-done | bytes 2621472 | tf_op jit(solution)/shard_map/ppermute | solution.py:279
  1099.3 48.0 %collective-permute-done.16 = f32[1024,768]{1,0:T(8,128)} collective-permute-done((f32[1024,768]{1,0:T(8,128)}, f32[1024,768]{1,0:T(8,128)}, u32[]{:S(2)}, u32[]{:S(2)}) %collective-permute-start.16) | collective-permute-done | bytes 3145760 | tf_op jit(solution)/shard_map/ppermute | solution.py:279
  1155.3 59.3 %collective-permute-done.28 = f32[1024,768]{1,0:T(8,128)} collective-permute-done((f32[1024,768]{1,0:T(8,128)}, f32[1024,768]{1,0:T(8,128)}, u32[]{:S(2)}, u32[]{:S(2)}) %collective-permute-start.28) | collective-permute-done | bytes 3145760 | tf_op jit(solution)/shard_map/ppermute | solution.py:279
  1219.8 35.5 %collective-permute-done.38 = f32[2,2,128,288]{2,3,1,0:T(8,128)S(1)} collective-permute-done((f32[2,2,128,288]{2,3,1,0:T(8,128)S(1)}, f32[2,2,128,288]{2,3,1,0:T(8,128)S(1)}, u32[]{:S(2)}, u32[]{:S(2)}) %collective-permute-start.38) | collective-permute-done | bytes 589856 | tf_op jit(solution)/shard_map/ppermute | solution.py:279
  1262.5 22.6 %collective-permute-done.13 = f32[2,2,128,640]{3,2,1,0:T(8,128)S(1)} collective-permute-done((f32[2,2,128,640]{3,2,1,0:T(8,128)}, f32[2,2,128,640]{3,2,1,0:T(8,128)S(1)}, u32[]{:S(2)}, u32[]{:S(2)}) %collective-permute-start.13) | collective-permute-done | bytes 1310752 | tf_op jit(solution)/shard_map/ppermute | solution.py:279
  1291.0 22.0 %collective-permute-done.25 = f32[2,2,128,640]{3,2,1,0:T(8,128)S(1)} collective-permute-done((f32[2,2,128,640]{3,2,1,0:T(8,128)}, f32[2,2,128,640]{3,2,1,0:T(8,128)S(1)}, u32[]{:S(2)}, u32[]{:S(2)}) %collective-permute-start.25) | collective-permute-done | bytes 1310752 | tf_op jit(solution)/shard_map/ppermute | solution.py:279
  1328.7 10.5 collective-permute-done.22
  1343.2 9.2 collective-permute-done.34
  1363.1 30.8 %collective-permute-done.29 = f32[2,2,128,768]{3,2,1,0:T(8,128)S(1)} collective-permute-done((f32[2,2,128,768]{3,2,1,0:T(8,128)}, f32[2,2,128,768]{3,2,1,0:T(8,128)S(1)}, u32[]{:S(2)}, u32[]{:S(2)}) %collective-permute-start.29) | collective-permute-done | bytes 1572896 | tf_op jit(solution)/shard_map/ppermute | solution.py:279
  1398.9 21.7 %collective-permute-done.23 = f32[128,640]{1,0:T(8,128)S(1)} collective-permute-done((f32[128,640]{1,0:T(8,128)}, f32[128,640]{1,0:T(8,128)S(1)}, u32[]{:S(2)}, u32[]{:S(2)}) %collective-permute-start.23) | collective-permute-done | bytes 327712 | tf_op jit(solution)/shard_map/ppermute | solution.py:279
  1420.7 7.0 collective-permute-done.15
  1427.7 7.0 collective-permute-done.35
  1434.8 7.0 collective-permute-done.27
  1441.8 30.9 %collective-permute-done.43 = f32[512,288]{0,1:T(8,128)S(1)} collective-permute-done((f32[512,288]{0,1:T(8,128)S(1)}, f32[512,288]{0,1:T(8,128)S(1)}, u32[]{:S(2)}, u32[]{:S(2)}) %collective-permute-start.43) | collective-permute-done | bytes 589856 | tf_op jit(solution)/shard_map/ppermute | solution.py:279
  1475.8 22.6 %collective-permute-done.18 = f32[2,128,768]{2,1,0:T(8,128)S(1)} collective-permute-done((f32[2,128,768]{2,1,0:T(8,128)S(1)}, f32[2,128,768]{2,1,0:T(8,128)S(1)}, u32[]{:S(2)}, u32[]{:S(2)}) %collective-permute-start.18) | collective-permute-done | bytes 786464 | tf_op jit(solution)/shard_map/ppermute | solution.py:279
  1499.4 15.9 collective-permute-done.30
  1516.3 43.9 %collective-permute-done.52 = f32[128,768]{1,0:T(8,128)S(1)} collective-permute-done((f32[128,768]{1,0:T(8,128)S(1)}, f32[128,768]{1,0:T(8,128)S(1)}, u32[]{:S(2)}, u32[]{:S(2)}) %collective-permute-start.52) | collective-permute-done | bytes 393248 | tf_op jit(solution)/shard_map/ppermute | solution.py:279
  1561.3 7.3 collective-permute-done.19
  1568.7 8.3 collective-permute-done.31
  1596.5 13.1 fusion.32
  (686 shorter events, 388.3 us)
Async XLA Ops:
  7.2 1605.5 %reduce-scatter.2.cloned.1.call-start = ((), (), s32[]{:S(2)}) async-start(), calls=%async_computation.1 | async-start | bytes 12582912 | tf_op jit(solution)/shard_map/reduce_scatter | solution.py:497
  47.4 145.2 %collective-permute-start = (f32[4,3,2048]{2,1,0:T(4,128)}, f32[4,3,2048]{2,1,0:T(4,128)}, u32[]{:S(2)}, u32[]{:S(2)}) collective-permute-start(f32[4,3,2048]{2,1,0:T(4,128)} %slice.296), channel_id=1, source_target_pairs={{0,2},{2,4},{4,6},{6,8},{8,10},{10,12},{12,14},{14,16},{16,18},{18... | collective-permute-start | bytes 294920 | tf_op jit(solution)/shard_map/ppermute | solution.py:20
  53.3 136.4 %copy-start.33 = (f32[4,256,256]{2,1,0:T(8,128)}, f32[4,256,256]{2,1,0:T(8,128)S(1)}, u32[]{:S(2)}) copy-start(f32[4,256,256]{2,1,0:T(8,128)S(1)} %fusion.63) | copy-start | bytes 3145732
  54.0 135.8 %collective-permute-start.1 = (f32[4,3,256]{2,1,0:T(4,128)}, f32[4,3,256]{2,1,0:T(4,128)}, u32[]{:S(2)}, u32[]{:S(2)}) collective-permute-start(f32[4,3,256]{2,1,0:T(4,128)} %slice.307), channel_id=1, source_target_pairs={{0,2},{2,4},{4,6},{6,8},{8,10},{10,12},{12,14},{14,16},{16,18},{18... | collective-permute-start | bytes 36872 | tf_op jit(solution)/shard_map/ppermute | solution.py:20
  121.1 71.5 %copy-start.93 = (f32[4,256]{1,0:T(4,128)}, f32[4,256]{1,0:T(4,128)S(1)}, u32[]{:S(2)}) copy-start(f32[4,256]{1,0:T(4,128)S(1)} %get-tuple-element.263) | copy-start | bytes 12292
  188.1 401.2 %copy-start.72 = (f32[4,256,32]{1,2,0:T(8,128)}, f32[4,256,32]{1,2,0:T(8,128)S(1)}, u32[]{:S(2)}) copy-start(f32[4,256,32]{1,2,0:T(8,128)S(1)} %copy.538) | copy-start | bytes 393220
  192.3 133.0 %copy-start.24 = (bf16[4,256,256]{2,1,0:T(8,128)(2,1)}, bf16[4,256,256]{2,1,0:T(8,128)(2,1)S(1)}, u32[]{:S(2)}) copy-start(bf16[4,256,256]{2,1,0:T(8,128)(2,1)S(1)} %get-tuple-element.206) | copy-start | bytes 1572868
  192.6 136.2 %copy-start.77 = (f32[4,256,256]{2,1,0:T(8,128)}, f32[4,256,256]{2,1,0:T(8,128)S(1)}, u32[]{:S(2)}) copy-start(f32[4,256,256]{2,1,0:T(8,128)S(1)} %fusion.116) | copy-start | bytes 3145732
  364.0 136.0 %collective-permute-start.2 = (f32[4,256]{1,0:T(4,128)S(1)}, f32[4,256]{1,0:T(4,128)S(1)}, u32[]{:S(2)}, u32[]{:S(2)}) collective-permute-start(f32[4,256]{1,0:T(4,128)S(1)} %get-tuple-element.273), channel_id=1, source_target_pairs={{0,1},{1,0},{2,3},{3,2},{4,5},{5,4},{6,7},{7,6},{8,9},{9,8},{10,11... | collective-permute-start | bytes 12296 | tf_op jit(solution)/shard_map/ppermute | solution.py:279
  542.5 13.6 collective-permute-start.3
  547.9 472.1 %collective-permute-start.53 = (f32[1024,640]{1,0:T(8,128)}, f32[1024,640]{1,0:T(8,128)}, u32[]{:S(2)}, u32[]{:S(2)}) collective-permute-start(f32[1024,640]{1,0:T(8,128)} %fusion.83), channel_id=1, source_target_pairs={{0,8},{2,10},{4,12},{6,14},{8,0},{10,2},{12,4},{14,6},{16,24},{18,... | collective-permute-start | bytes 7864328 | tf_op jit(solution)/shard_map/ppermute | solution.py:279
  555.9 470.4 %collective-permute-start.45 = (f32[1024,640]{1,0:T(8,128)}, f32[1024,640]{1,0:T(8,128)}, u32[]{:S(2)}, u32[]{:S(2)}) collective-permute-start(f32[1024,640]{1,0:T(8,128)} %fusion.86), channel_id=1, source_target_pairs={{0,2},{2,0},{4,6},{6,4},{8,10},{10,8},{12,14},{14,12},{16,18},{18,... | collective-permute-start | bytes 7864328 | tf_op jit(solution)/shard_map/ppermute | solution.py:279
  593.5 111.4 %copy-start.2 = (f32[4,4,8,64,128]{4,3,2,1,0:T(8,128)S(1)}, f32[4,4,8,64,128]{4,3,2,1,0:T(8,128)}, u32[]{:S(2)}) copy-start(f32[4,4,8,64,128]{4,3,2,1,0:T(8,128)} %copy-done.1) | copy-start | bytes 12582916
  922.3 37.6 %collective-permute-start.4 = (f32[4,3,2048]{2,1,0:T(4,128)S(1)}, f32[4,3,2048]{2,1,0:T(4,128)}, u32[]{:S(2)}, u32[]{:S(2)}) collective-permute-start(f32[4,3,2048]{2,1,0:T(4,128)S(1)} %copy-done.95), channel_id=1, source_target_pairs={{2,0},{4,2},{6,4},{8,6},{10,8},{12,10},{14,12},{16,14},{18,16},{20... | collective-permute-start | bytes 294920 | tf_op jit(solution)/shard_map/ppermute | solution.py:20
  923.8 26.9 %collective-permute-start.5 = (f32[4,3,256]{2,1,0:T(4,128)}, f32[4,3,256]{2,1,0:T(4,128)}, u32[]{:S(2)}, u32[]{:S(2)}) collective-permute-start(f32[4,3,256]{2,1,0:T(4,128)} %pad_add_fusion.4), channel_id=1, source_target_pairs={{2,0},{4,2},{6,4},{8,6},{10,8},{12,10},{14,12},{16,14},{18,16},{20... | collective-permute-start | bytes 36872 | tf_op jit(solution)/shard_map/ppermute | solution.py:20
  925.7 18.1 %collective-permute-start.7 = (f32[1280]{0:T(1024)}, f32[1280]{0:T(1024)}, u32[]{:S(2)}, u32[]{:S(2)}) collective-permute-start(f32[1280]{0:T(1024)} %pad_maximum_fusion.10), channel_id=1, source_target_pairs={{0,1},{1,0},{2,3},{3,2},{4,5},{5,4},{6,7},{7,6},{8,9},{9,8},{10,11... | collective-permute-start | bytes 15368 | tf_op jit(solution)/shard_map/ppermute | solution.py:279
  943.9 88.0 %collective-permute-start.20 = (f32[1024,640]{1,0:T(8,128)}, f32[1024,640]{1,0:T(8,128)}, u32[]{:S(2)}, u32[]{:S(2)}) collective-permute-start(f32[1024,640]{1,0:T(8,128)} %fusion.95), channel_id=1, source_target_pairs={{0,8},{2,10},{4,12},{6,14},{8,0},{10,2},{12,4},{14,6},{16,24},{18,... | collective-permute-start | bytes 7864328 | tf_op jit(solution)/shard_map/ppermute | solution.py:279
  950.6 87.6 %collective-permute-start.12 = (f32[1024,640]{1,0:T(8,128)}, f32[1024,640]{1,0:T(8,128)}, u32[]{:S(2)}, u32[]{:S(2)}) collective-permute-start(f32[1024,640]{1,0:T(8,128)} %fusion.98), channel_id=1, source_target_pairs={{0,2},{2,0},{4,6},{6,4},{8,10},{10,8},{12,14},{14,12},{16,18},{18,... | collective-permute-start | bytes 7864328 | tf_op jit(solution)/shard_map/ppermute | solution.py:279
  959.9 49.9 %collective-permute-start.36 = (f32[2048,256]{0,1:T(8,128)S(1)}, f32[2048,256]{0,1:T(8,128)}, u32[]{:S(2)}, u32[]{:S(2)}) collective-permute-start(f32[2048,256]{0,1:T(8,128)S(1)} %fusion.64), channel_id=1, source_target_pairs={{0,1},{1,0},{2,3},{3,2},{4,5},{5,4},{6,7},{7,6},{8,9},{9,8},{10,11... | collective-permute-start | bytes 6291464 | tf_op jit(solution)/shard_map/ppermute | solution.py:279
  1009.8 83.5 %collective-permute-start.49 = (f32[1024,768]{1,0:T(8,128)}, f32[1024,768]{1,0:T(8,128)}, u32[]{:S(2)}, u32[]{:S(2)}) collective-permute-start(f32[1024,768]{1,0:T(8,128)} %fusion.70), channel_id=1, source_target_pairs={{0,4},{2,6},{4,0},{6,2},{8,12},{10,14},{12,8},{14,10},{16,20},{18,... | collective-permute-start | bytes 9437192 | tf_op jit(solution)/shard_map/ppermute | solution.py:279
  1020.1 58.6 %collective-permute-start.32 = (f32[1024,640]{1,0:T(8,128)}, f32[1024,640]{1,0:T(8,128)S(1)}, u32[]{:S(2)}, u32[]{:S(2)}) collective-permute-start(f32[1024,640]{1,0:T(8,128)} %fusion.89), channel_id=1, source_target_pairs={{0,8},{2,10},{4,12},{6,14},{8,0},{10,2},{12,4},{14,6},{16,24},{18,... | collective-permute-start | bytes 7864328 | tf_op jit(solution)/shard_map/ppermute | solution.py:279
  1026.3 60.7 %collective-permute-start.24 = (f32[1024,640]{1,0:T(8,128)}, f32[1024,640]{1,0:T(8,128)}, u32[]{:S(2)}, u32[]{:S(2)}) collective-permute-start(f32[1024,640]{1,0:T(8,128)} %fusion.92), channel_id=1, source_target_pairs={{0,2},{2,0},{4,6},{6,4},{8,10},{10,8},{12,14},{14,12},{16,18},{18,... | collective-permute-start | bytes 7864328 | tf_op jit(solution)/shard_map/ppermute | solution.py:279
  1031.8 115.4 %collective-permute-start.16 = (f32[1024,768]{1,0:T(8,128)}, f32[1024,768]{1,0:T(8,128)}, u32[]{:S(2)}, u32[]{:S(2)}) collective-permute-start(f32[1024,768]{1,0:T(8,128)} %fusion.76), channel_id=1, source_target_pairs={{0,4},{2,6},{4,0},{6,2},{8,12},{10,14},{12,8},{14,10},{16,20},{18,... | collective-permute-start | bytes 9437192 | tf_op jit(solution)/shard_map/ppermute | solution.py:279
  1038.2 542.4 %collective-permute-start.6 = (f32[1024,2048]{1,0:T(8,128)S(1)}, f32[1024,2048]{1,0:T(8,128)S(1)}, u32[]{:S(2)}, u32[]{:S(2)}) collective-permute-start(f32[1024,2048]{1,0:T(8,128)S(1)} %bitcast.412), channel_id=1, source_target_pairs={{0,1},{1,0},{2,3},{3,2},{4,5},{5,4},{6,7},{7,6},{8,9},{9,8},{10,11... | collective-permute-start | bytes 25165832 | tf_op jit(solution)/shard_map/ppermute | solution.py:279
  1080.3 134.4 %collective-permute-start.28 = (f32[1024,768]{1,0:T(8,128)}, f32[1024,768]{1,0:T(8,128)}, u32[]{:S(2)}, u32[]{:S(2)}) collective-permute-start(f32[1024,768]{1,0:T(8,128)} %fusion.73), channel_id=1, source_target_pairs={{0,4},{2,6},{4,0},{6,2},{8,12},{10,14},{12,8},{14,10},{16,20},{18,... | collective-permute-start | bytes 9437192 | tf_op jit(solution)/shard_map/ppermute | solution.py:279
  1087.0 65.4 %collective-permute-start.37 = (f32[2,2,2,128,288]{3,4,2,1,0:T(8,128)}, f32[2,2,2,128,288]{3,4,2,1,0:T(8,128)}, u32[]{:S(2)}, u32[]{:S(2)}) collective-permute-start(f32[2,2,2,128,288]{3,4,2,1,0:T(8,128)} %bitcast.390), channel_id=1, source_target_pairs={{0,2},{2,0},{4,6},{6,4},{8,10},{10,8},{12,14},{14,12},{16,18},{18,... | collective-permute-start | bytes 3538952 | tf_op jit(solution)/shard_map/ppermute | solution.py:279
  1093.3 162.3 %collective-permute-start.54 = (f32[2,2,128,640]{3,2,1,0:T(8,128)}, f32[2,2,128,640]{3,2,1,0:T(8,128)S(1)}, u32[]{:S(2)}, u32[]{:S(2)}) collective-permute-start(f32[2,2,128,640]{3,2,1,0:T(8,128)} %dynamic-slice_bitcast_fusion.3), channel_id=1, source_target_pairs={{0,2},{2,0},{4,6},{6,4},{8,10},{10,8},{12,14},{14,12},{16,18},{18,... | collective-permute-start | bytes 3932168 | tf_op jit(solution)/shard_map/ppermute | solution.py:279
  1147.2 109.9 %collective-permute-start.46 = (f32[2,2,128,640]{3,2,1,0:T(8,128)}, f32[2,2,128,640]{3,2,1,0:T(8,128)}, u32[]{:S(2)}, u32[]{:S(2)}) collective-permute-start(f32[2,2,128,640]{3,2,1,0:T(8,128)} %dynamic-slice_bitcast_fusion.4), channel_id=1, source_target_pairs={{0,4},{2,6},{4,0},{6,2},{8,12},{10,14},{12,8},{14,10},{16,20},{18,... | collective-permute-start | bytes 3932168 | tf_op jit(solution)/shard_map/ppermute | solution.py:279
  1152.4 107.7 %collective-permute-start.21 = (f32[2,2,128,640]{3,2,1,0:T(8,128)}, f32[2,2,128,640]{3,2,1,0:T(8,128)}, u32[]{:S(2)}, u32[]{:S(2)}) collective-permute-start(f32[2,2,128,640]{3,2,1,0:T(8,128)} %dynamic-slice_bitcast_fusion.7), channel_id=1, source_target_pairs={{0,2},{2,0},{4,6},{6,4},{8,10},{10,8},{12,14},{14,12},{16,18},{18,... | collective-permute-start | bytes 3932168 | tf_op jit(solution)/shard_map/ppermute | solution.py:279
  1214.7 40.6 %collective-permute-start.38 = (f32[2,2,128,288]{2,3,1,0:T(8,128)S(1)}, f32[2,2,128,288]{2,3,1,0:T(8,128)S(1)}, u32[]{:S(2)}, u32[]{:S(2)}) collective-permute-start(f32[2,2,128,288]{2,3,1,0:T(8,128)S(1)} %dynamic-slice_bitcast_fusion.18), channel_id=1, source_target_pairs={{0,4},{2,6},{4,0},{6,2},{8,12},{10,14},{12,8},{14,10},{16,20},{18,... | collective-permute-start | bytes 1769480 | tf_op jit(solution)/shard_map/ppermute | solution.py:279
  1255.3 29.8 %collective-permute-start.13 = (f32[2,2,128,640]{3,2,1,0:T(8,128)}, f32[2,2,128,640]{3,2,1,0:T(8,128)S(1)}, u32[]{:S(2)}, u32[]{:S(2)}) collective-permute-start(f32[2,2,128,640]{3,2,1,0:T(8,128)} %dynamic-slice_bitcast_fusion.8), channel_id=1, source_target_pairs={{0,4},{2,6},{4,0},{6,2},{8,12},{10,14},{12,8},{14,10},{16,20},{18,... | collective-permute-start | bytes 3932168 | tf_op jit(solution)/shard_map/ppermute | solution.py:279
  1255.5 29.8 %collective-permute-start.33 = (f32[2,2,128,640]{3,2,1,0:T(8,128)}, f32[2,2,128,640]{3,2,1,0:T(8,128)}, u32[]{:S(2)}, u32[]{:S(2)}) collective-permute-start(f32[2,2,128,640]{3,2,1,0:T(8,128)} %dynamic-slice_bitcast_fusion.5), channel_id=1, source_target_pairs={{0,2},{2,0},{4,6},{6,4},{8,10},{10,8},{12,14},{14,12},{16,18},{18,... | collective-permute-start | bytes 3932168 | tf_op jit(solution)/shard_map/ppermute | solution.py:279
  1257.2 55.9 %collective-permute-start.25 = (f32[2,2,128,640]{3,2,1,0:T(8,128)}, f32[2,2,128,640]{3,2,1,0:T(8,128)S(1)}, u32[]{:S(2)}, u32[]{:S(2)}) collective-permute-start(f32[2,2,128,640]{3,2,1,0:T(8,128)} %dynamic-slice_bitcast_fusion.6), channel_id=1, source_target_pairs={{0,4},{2,6},{4,0},{6,2},{8,12},{10,14},{12,8},{14,10},{16,20},{18,... | collective-permute-start | bytes 3932168 | tf_op jit(solution)/shard_map/ppermute | solution.py:279
  1260.1 94.6 %collective-permute-start.50 = (f32[2,2,128,768]{3,2,1,0:T(8,128)}, f32[2,2,128,768]{3,2,1,0:T(8,128)S(1)}, u32[]{:S(2)}, u32[]{:S(2)}) collective-permute-start(f32[2,2,128,768]{3,2,1,0:T(8,128)} %dynamic-slice_bitcast_fusion), channel_id=1, source_target_pairs={{0,2},{2,0},{4,6},{6,4},{8,10},{10,8},{12,14},{14,12},{16,18},{18,... | collective-permute-start | bytes 4718600 | tf_op jit(solution)/shard_map/ppermute | solution.py:279
  1285.1 5.9 collective-permute-start.39
  1285.3 41.8 %collective-permute-start.55 = (f32[2,128,640]{2,1,0:T(8,128)S(1)}, f32[2,128,640]{2,1,0:T(8,128)S(1)}, u32[]{:S(2)}, u32[]{:S(2)}) collective-permute-start(f32[2,128,640]{2,1,0:T(8,128)S(1)} %dynamic-slice_bitcast_fusion.12), channel_id=1, source_target_pairs={{0,4},{2,6},{4,0},{6,2},{8,12},{10,14},{12,8},{14,10},{16,20},{18,... | collective-permute-start | bytes 1966088 | tf_op jit(solution)/shard_map/ppermute | solution.py:279
  1291.0 36.3 %collective-permute-start.47 = (f32[2,128,640]{2,1,0:T(8,128)S(1)}, f32[2,128,640]{2,1,0:T(8,128)S(1)}, u32[]{:S(2)}, u32[]{:S(2)}) collective-permute-start(f32[2,128,640]{2,1,0:T(8,128)S(1)} %dynamic-slice_bitcast_fusion.13), channel_id=1, source_target_pairs={{0,8},{2,10},{4,12},{6,14},{8,0},{10,2},{12,4},{14,6},{16,24},{18,... | collective-permute-start | bytes 1966088 | tf_op jit(solution)/shard_map/ppermute | solution.py:279
  1313.1 6.0 collective-permute-start.40
  1319.1 4.4 collective-permute-start.41
  1323.4 15.8 collective-permute-start.22
  1327.1 13.3 collective-permute-start.14
  1327.3 32.9 %collective-permute-start.17 = (f32[2,2,128,768]{3,2,1,0:T(8,128)S(1)}, f32[2,2,128,768]{3,2,1,0:T(8,128)S(1)}, u32[]{:S(2)}, u32[]{:S(2)}) collective-permute-start(f32[2,2,128,768]{3,2,1,0:T(8,128)S(1)} %copy-done.69), channel_id=1, source_target_pairs={{0,2},{2,0},{4,6},{6,4},{8,10},{10,8},{12,14},{14,12},{16,18},{18,... | collective-permute-start | bytes 4718600 | tf_op jit(solution)/shard_map/ppermute | solution.py:279
  1339.2 13.2 collective-permute-start.34
  1340.4 14.1 collective-permute-start.26
  1352.4 41.5 %collective-permute-start.29 = (f32[2,2,128,768]{3,2,1,0:T(8,128)}, f32[2,2,128,768]{3,2,1,0:T(8,128)S(1)}, u32[]{:S(2)}, u32[]{:S(2)}) collective-permute-start(f32[2,2,128,768]{3,2,1,0:T(8,128)} %dynamic-slice_bitcast_fusion.1), channel_id=1, source_target_pairs={{0,2},{2,0},{4,6},{6,4},{8,10},{10,8},{12,14},{14,12},{16,18},{18,... | collective-permute-start | bytes 4718600 | tf_op jit(solution)/shard_map/ppermute | solution.py:279
  1354.5 8.1 collective-permute-start.42
  1354.7 41.7 %collective-permute-start.56 = (f32[128,640]{1,0:T(8,128)S(1)}, f32[128,640]{1,0:T(8,128)S(1)}, u32[]{:S(2)}, u32[]{:S(2)}) collective-permute-start(f32[128,640]{1,0:T(8,128)S(1)} %dynamic-slice_bitcast_fusion.22), channel_id=1, source_target_pairs={{0,16},{2,18},{4,20},{6,22},{8,24},{10,26},{12,28},{14,30},{16,0},... | collective-permute-start | bytes 983048 | tf_op jit(solution)/shard_map/ppermute | solution.py:279
  1360.2 36.5 %collective-permute-start.48 = (f32[128,640]{1,0:T(8,128)S(1)}, f32[128,640]{1,0:T(8,128)S(1)}, u32[]{:S(2)}, u32[]{:S(2)}) collective-permute-start(f32[128,640]{1,0:T(8,128)S(1)} %dynamic-slice_bitcast_fusion.23), channel_id=1, source_target_pairs={{0,16},{2,18},{4,20},{6,22},{8,24},{10,26},{12,28},{14,30},{16,0},... | collective-permute-start | bytes 983048 | tf_op jit(solution)/shard_map/ppermute | solution.py:279
  1362.7 58.0 %collective-permute-start.23 = (f32[128,640]{1,0:T(8,128)}, f32[128,640]{1,0:T(8,128)S(1)}, u32[]{:S(2)}, u32[]{:S(2)}) collective-permute-start(f32[128,640]{1,0:T(8,128)} %dynamic-slice_bitcast_fusion.26), channel_id=1, source_target_pairs={{0,16},{2,18},{4,20},{6,22},{8,24},{10,26},{12,28},{14,30},{16,0},... | collective-permute-start | bytes 983048 | tf_op jit(solution)/shard_map/ppermute | solution.py:279
  1393.9 33.8 %collective-permute-start.15 = (f32[128,640]{1,0:T(8,128)}, f32[128,640]{1,0:T(8,128)S(1)}, u32[]{:S(2)}, u32[]{:S(2)}) collective-permute-start(f32[128,640]{1,0:T(8,128)} %dynamic-slice_bitcast_fusion.27), channel_id=1, source_target_pairs={{0,16},{2,18},{4,20},{6,22},{8,24},{10,26},{12,28},{14,30},{16,0},... | collective-permute-start | bytes 983048 | tf_op jit(solution)/shard_map/ppermute | solution.py:279
  1396.4 38.4 %collective-permute-start.35 = (f32[128,640]{1,0:T(8,128)S(1)}, f32[128,640]{1,0:T(8,128)S(1)}, u32[]{:S(2)}, u32[]{:S(2)}) collective-permute-start(f32[128,640]{1,0:T(8,128)S(1)} %copy-done.86), channel_id=1, source_target_pairs={{0,16},{2,18},{4,20},{6,22},{8,24},{10,26},{12,28},{14,30},{16,0},... | collective-permute-start | bytes 983048 | tf_op jit(solution)/shard_map/ppermute | solution.py:279
  1396.6 45.1 %collective-permute-start.27 = (f32[128,640]{1,0:T(8,128)S(1)}, f32[128,640]{1,0:T(8,128)S(1)}, u32[]{:S(2)}, u32[]{:S(2)}) collective-permute-start(f32[128,640]{1,0:T(8,128)S(1)} %dynamic-slice_bitcast_fusion.25), channel_id=1, source_target_pairs={{0,16},{2,18},{4,20},{6,22},{8,24},{10,26},{12,28},{14,30},{16,0},... | collective-permute-start | bytes 983048 | tf_op jit(solution)/shard_map/ppermute | solution.py:279
  1420.6 52.6 %collective-permute-start.51 = (f32[2,128,768]{2,1,0:T(8,128)S(1)}, f32[2,128,768]{2,1,0:T(8,128)S(1)}, u32[]{:S(2)}, u32[]{:S(2)}) collective-permute-start(f32[2,128,768]{2,1,0:T(8,128)S(1)} %dynamic-slice_bitcast_fusion.9), channel_id=1, source_target_pairs={{0,8},{2,10},{4,12},{6,14},{8,0},{10,2},{12,4},{14,6},{16,24},{18,... | collective-permute-start | bytes 2359304 | tf_op jit(solution)/shard_map/ppermute | solution.py:279
  1427.7 45.0 %collective-permute-start.43 = (f32[512,288]{0,1:T(8,128)S(1)}, f32[512,288]{0,1:T(8,128)S(1)}, u32[]{:S(2)}, u32[]{:S(2)}) collective-permute-start(f32[512,288]{0,1:T(8,128)S(1)} %pad_maximum_fusion.7), channel_id=1, source_target_pairs={{0,8},{2,10},{4,12},{6,14},{8,0},{10,2},{12,4},{14,6},{16,24},{18,... | collective-permute-start | bytes 1769480 | tf_op jit(solution)/shard_map/ppermute | solution.py:279
  1434.7 63.7 %collective-permute-start.18 = (f32[2,128,768]{2,1,0:T(8,128)S(1)}, f32[2,128,768]{2,1,0:T(8,128)S(1)}, u32[]{:S(2)}, u32[]{:S(2)}) collective-permute-start(f32[2,128,768]{2,1,0:T(8,128)S(1)} %dynamic-slice_bitcast_fusion.11), channel_id=1, source_target_pairs={{0,8},{2,10},{4,12},{6,14},{8,0},{10,2},{12,4},{14,6},{16,24},{18,... | collective-permute-start | bytes 2359304 | tf_op jit(solution)/shard_map/ppermute | solution.py:279
  1441.7 73.5 %collective-permute-start.30 = (f32[2,128,768]{2,1,0:T(8,128)S(1)}, f32[2,128,768]{2,1,0:T(8,128)S(1)}, u32[]{:S(2)}, u32[]{:S(2)}) collective-permute-start(f32[2,128,768]{2,1,0:T(8,128)S(1)} %dynamic-slice_bitcast_fusion.10), channel_id=1, source_target_pairs={{0,8},{2,10},{4,12},{6,14},{8,0},{10,2},{12,4},{14,6},{16,24},{18,... | collective-permute-start | bytes 2359304 | tf_op jit(solution)/shard_map/ppermute | solution.py:279
  1473.1 107.2 %collective-permute-start.44 = (f32[1024,288]{0,1:T(8,128)S(1)}, f32[1024,288]{0,1:T(8,128)S(1)}, u32[]{:S(2)}, u32[]{:S(2)}) collective-permute-start(f32[1024,288]{0,1:T(8,128)S(1)} %pad_maximum_fusion.3), channel_id=1, source_target_pairs={{0,16},{2,18},{4,20},{6,22},{8,24},{10,26},{12,28},{14,30},{16,0},... | collective-permute-start | bytes 3538952 | tf_op jit(solution)/shard_map/ppermute | solution.py:279
  1473.4 86.7 %collective-permute-start.52 = (f32[128,768]{1,0:T(8,128)S(1)}, f32[128,768]{1,0:T(8,128)S(1)}, u32[]{:S(2)}, u32[]{:S(2)}) collective-permute-start(f32[128,768]{1,0:T(8,128)S(1)} %dynamic-slice_bitcast_fusion.19), channel_id=1, source_target_pairs={{0,16},{2,18},{4,20},{6,22},{8,24},{10,26},{12,28},{14,30},{16,0},... | collective-permute-start | bytes 1179656 | tf_op jit(solution)/shard_map/ppermute | solution.py:279
  1498.5 70.0 %collective-permute-start.19 = (f32[128,768]{1,0:T(8,128)S(1)}, f32[128,768]{1,0:T(8,128)S(1)}, u32[]{:S(2)}, u32[]{:S(2)}) collective-permute-start(f32[128,768]{1,0:T(8,128)S(1)} %dynamic-slice_bitcast_fusion.21), channel_id=1, source_target_pairs={{0,16},{2,18},{4,20},{6,22},{8,24},{10,26},{12,28},{14,30},{16,0},... | collective-permute-start | bytes 1179656 | tf_op jit(solution)/shard_map/ppermute | solution.py:279
  1515.4 61.6 %collective-permute-start.31 = (f32[128,768]{1,0:T(8,128)S(1)}, f32[128,768]{1,0:T(8,128)S(1)}, u32[]{:S(2)}, u32[]{:S(2)}) collective-permute-start(f32[128,768]{1,0:T(8,128)S(1)} %dynamic-slice_bitcast_fusion.20), channel_id=1, source_target_pairs={{0,16},{2,18},{4,20},{6,22},{8,24},{10,26},{12,28},{14,30},{16,0},... | collective-permute-start | bytes 1179656 | tf_op jit(solution)/shard_map/ppermute | solution.py:279
  1585.4 3.2 collective-permute-start.8
  1588.6 4.6 collective-permute-start.9
  1593.2 3.2 collective-permute-start.10
  1596.4 13.2 collective-permute-start.11
  (165 other events, 2151.1 us)
Sparse Core Ops, SparseCore 0:
  523.3 15.9 reduce-scatter.1

commit v2 on v1

v2 whole, which is shorter than its diff:
```python
import functools
import math

import jax
import jax.numpy as jnp
from jax import lax
from jax.experimental import pallas as pl
from jax.experimental.pallas import tpu as pltpu
from jax.sharding import PartitionSpec as P

EPSILON = 1e-05
HIGHEST = lax.Precision.HIGHEST


def shifted(shard, axis, by):
    length = lax.axis_size(axis)
    pairs = [(i, i + by) for i in range(length) if 0 <= i + by < length]
    return lax.ppermute(shard, axis, pairs)


def segment_ids(seq_lengths, first, count, micro):
    places = first + jnp.arange(count, dtype=jnp.int32)
    starts = jnp.cumsum(seq_lengths, axis=-1) - seq_lengths
    short_ids = (
        jnp.sum((starts[:, None, :] <= places[None, :, None]).astype(jnp.int32), axis=-1) - 1
    )
    long_ids = jnp.zeros((micro - seq_lengths.shape[0], count), jnp.int32)
    labels = jnp.concatenate([short_ids, long_ids], axis=0)
    return jnp.where(places[None, :] >= 0, labels, -1)


def rms_scale(values, gain):
    return values * lax.rsqrt(jnp.mean(values * values, axis=-1, keepdims=True) + EPSILON) * gain


def conv_silu(extended, weight, bias, labels):
    taps = weight.shape[0]
    count = extended.shape[0] - taps + 1
    own = labels[taps - 1 :]
    total = bias + weight[0] * extended[taps - 1 :]
    for shift in range(1, taps):
        first = taps - 1 - shift
        mask = (labels[first : first + count] == own).astype(extended.dtype)
        total = total + weight[shift] * extended[first : first + count] * mask[:, None]
    return jax.nn.silu(total)


def step_sizes(delta_pre, dt_bias, a_log):
    delta = jax.nn.softplus(delta_pre + dt_bias[:, None])
    return (delta, -jnp.exp(a_log)[:, None] * delta)


DEAD = -1e30
EXCHANGE_COST = 100_000_000_000
FINISH_LIMIT = 60 * 1024 * 1024
GROUP = 4


def exchange_kernel(length, reverse, orders, part_ref, log_ref, *refs):
    refs = list(refs)
    sources = [refs.pop(0) for _ in range(2 if orders else 0)]
    out_ref = refs.pop(0)
    targets = [refs.pop(0) for _ in range(4 * len(orders))]
    (
        parts,
        logs,
        edge_in,
        edge_out,
        given,
        part_send,
        part_recv,
        log_send,
        log_recv,
        edge_send,
        edge_recv,
        given_send,
        given_recv,
        stage_sem,
        place_sem,
        staged,
    ) = refs
    me = lax.axis_index("seq")
    bits = (length - 1).bit_length()
    placed = arrange_copies(bits, orders, me, staged, targets, place_sem)
    stages = [
        pltpu.make_async_copy(source, staged.at[k], stage_sem.at[k])
        for k, source in enumerate(sources)
    ]
    for copy in stages:
        copy.start()
    rank = lax.rem(me, GROUP)
    plane = me // GROUP
    first = me - rank
    mates = (
        rank + 1 - 2 * lax.rem(rank, 2),
        rank + 2 - 4 * (rank // 2),
        3 - rank,
    )
    micro = part_ref.shape[0]
    planes = length // GROUP
    begins, ends = plane == 0, plane == planes - 1
    if reverse:
        begins, ends = ends, begins
    step = -GROUP if reverse else GROUP

    barrier = pltpu.get_barrier_semaphore()
    for mate in mates:
        pl.semaphore_signal(
            barrier, inc=1, device_id={"seq": first + mate}, device_id_type=pl.DeviceIdType.MESH
        )

    @pl.when(plane > 0)
    def _():
        pl.semaphore_signal(
            barrier, inc=1, device_id={"seq": me - GROUP}, device_id_type=pl.DeviceIdType.MESH
        )

    @pl.when(plane < planes - 1)
    def _():
        pl.semaphore_signal(
            barrier, inc=1, device_id={"seq": me + GROUP}, device_id_type=pl.DeviceIdType.MESH
        )

    above = jnp.where(plane < planes - 1, 1, 0)
    below = jnp.where(plane > 0, 1, 0)
    pl.semaphore_wait(barrier, 3 + above + below)

    def remote(src, dst, send, recv, target):
        return pltpu.make_async_remote_copy(
            src_ref=src,
            dst_ref=dst,
            send_sem=send,
            recv_sem=recv,
            device_id={"seq": target},
            device_id_type=pl.DeviceIdType.MESH,
        )

    def log_copy(slot):
        mate = mates[slot]
        return remote(
            log_ref.at[mate], logs.at[rank], log_send.at[slot], log_recv.at[slot], first + mate
        )

    def part_copy(m, slot):
        mate = mates[slot]
        return remote(
            part_ref.at[m, mate],
            parts.at[m, rank],
            part_send.at[m, slot],
            part_recv.at[m, slot],
            first + mate,
        )

    def edge_copy(m):
        return remote(edge_out.at[m], edge_in.at[m], edge_send.at[m], edge_recv.at[m], me + step)

    def given_copy(m, slot):
        mate = mates[slot]
        return remote(
            given.at[m, mate],
            out_ref.at[m, rank],
            given_send.at[m, slot],
            given_recv.at[m, slot],
            first + mate,
        )

    for slot in range(3):
        log_copy(slot).start()
    for m in range(micro):
        for slot in range(3):
            part_copy(m, slot).start()
    logs[rank] = log_ref[rank]
    for m in range(micro):
        parts[m, rank] = part_ref[m, rank]

    @pl.when(begins)
    def _():
        edge_in[...] = jnp.zeros_like(edge_in)

    for copy in stages:
        copy.wait()
    for copy in placed:
        copy.start()
    for slot in range(3):
        log_copy(slot).wait()
    order = tuple(reversed(range(GROUP))) if reverse else tuple(range(GROUP))
    for m in range(micro):
        for slot in range(3):
            part_copy(m, slot).wait()
        factors = [jnp.exp(logs[t, m])[:, None, :] for t in order]
        whole = jnp.exp(logs[0, m] + logs[1, m] + logs[2, m] + logs[3, m])[:, None, :]
        total = parts[m, order[0]]
        for t, factor in zip(order[1:], factors[1:]):
            total = total * factor + parts[m, t]

        @pl.when(jnp.logical_not(begins))
        def _():
            edge_copy(m).wait_recv()

        @pl.when(jnp.logical_not(ends))
        def _():
            edge_out[m] = total + whole * edge_in[m]
            edge_copy(m).start()

        running = edge_in[m]
        for place, (t, factor) in enumerate(zip(order, factors)):
            given[m, t] = running
            if place < GROUP - 1:
                running = running * factor + parts[m, t]
        for slot in range(3):
            given_copy(m, slot).start()
        out_ref[m, rank] = given[m, rank]
    for m in range(micro):
        for slot in range(3):
            given_copy(m, slot).wait()

        @pl.when(jnp.logical_not(ends))
        def _():
            edge_copy(m).wait_send()

    for copy in placed:
        copy.wait()


def exchange(parts, logs, reverse, sources=(), orders=()):
    micro, heads, rows, columns = parts.shape
    quarter = heads // GROUP
    length = lax.axis_size("seq")
    spread = jnp.broadcast_to(logs[:, :, None], (micro, heads, columns))
    spread = spread.reshape(micro, GROUP, quarter, columns).transpose(1, 0, 2, 3)
    shape = (micro, GROUP, quarter, rows, columns)
    arranged = []
    for source in sources:
        half = jax.ShapeDtypeStruct((source.shape[0], source.shape[1] // 2), source.dtype)
        arranged += [half] * (2 * len(orders))
    vmem = pl.BlockSpec(memory_space=pltpu.VMEM)
    hbm = pl.BlockSpec(memory_space=pl.ANY)
    out, *arranged = pl.pallas_call(
        functools.partial(exchange_kernel, length, reverse, orders),
        out_shape=[jax.ShapeDtypeStruct(shape, jnp.float32)] + arranged,
        in_specs=[vmem] * 2 + [hbm] * len(sources),
        out_specs=[vmem] + [hbm] * len(arranged),
        scratch_shapes=[
            pltpu.VMEM(shape, jnp.float32),
            pltpu.VMEM((GROUP, micro, quarter, columns), jnp.float32),
            pltpu.VMEM((micro, quarter, rows, columns), jnp.float32),
            pltpu.VMEM((micro, quarter, rows, columns), jnp.float32),
            pltpu.VMEM(shape, jnp.float32),
            pltpu.SemaphoreType.DMA((micro, 3)),
            pltpu.SemaphoreType.DMA((micro, 3)),
            pltpu.SemaphoreType.DMA((3,)),
            pltpu.SemaphoreType.DMA((3,)),
            pltpu.SemaphoreType.DMA((micro,)),
            pltpu.SemaphoreType.DMA((micro,)),
            pltpu.SemaphoreType.DMA((micro, 3)),
            pltpu.SemaphoreType.DMA((micro, 3)),
            pltpu.SemaphoreType.DMA((2,)),
            pltpu.SemaphoreType.DMA((max(len(arranged), 1) * max(length // 2, 1),)),
            pltpu.VMEM((2,) + sources[0].shape if sources else (2, 16, 128), jnp.bfloat16),
        ],
        compiler_params=pltpu.CompilerParams(
            collective_id=1 if reverse else 0,
            has_side_effects=True,
            vmem_limit_bytes=40 * 1024 * 1024,
        ),
        cost_estimate=pl.CostEstimate(
            flops=EXCHANGE_COST, bytes_accessed=0, transcendentals=0
        ),
        name="exchange_back" if reverse else "exchange",
    )(parts.reshape(shape), spread, *sources)
    return out.reshape(micro, heads, rows, columns), arranged


def xor_permute(value, axis, bit):
    size = lax.axis_size(axis)
    return lax.ppermute(value, axis, [(i, i ^ (1 << bit)) for i in range(size)])


def axis_bits(axis):
    return (lax.axis_size(axis) - 1).bit_length()


def own_bit(axis, bit):
    return lax.rem(lax.axis_index(axis) // (1 << bit), 2)


def all_sum(value, axis):
    for bit in range(axis_bits(axis)):
        value = value + xor_permute(value, axis, bit)
    return value


def scatter_parts(columns, bits):
    if bits < 3 or columns % 2048:
        return [(tuple(range(bits)), (columns,))]
    rest = tuple(range(3, bits))
    unit = columns // 16
    return [
        ((0, 1, 2) + rest, (3 * unit, 2 * unit)),
        ((1, 0, 2) + rest, (2 * unit, 3 * unit)),
        ((2, 0, 1) + rest, (3 * unit, 0)),
        ((2, 1, 0) + rest, (0, 3 * unit)),
    ]


def arranged_place(order, position, bits):
    return [(position >> (bits - 1 - t)) & 1 for t, _ in sorted(enumerate(order), key=lambda p: p[1])]


def arranged_block(order, position, bits, me):
    flips = arranged_place(order, position, bits)
    total = 0
    for bit, flip in enumerate(flips):
        mine = lax.rem(me // (1 << bit), 2)
        total = total + (1 << bit) * ((1 - mine) if flip else mine)
    return total


def arrange(left, orders):
    bits = axis_bits("seq")
    size = 1 << bits
    tokens, width = left.shape
    view = left.reshape(tokens, size, width // size)
    me = lax.axis_index("seq").astype(jnp.int32)
    results = []
    for order in orders:
        table = jnp.stack([arranged_block(order, j, bits, me) for j in range(size)])
        chosen = jnp.take(view, table, axis=1).reshape(tokens, width)
        results += [chosen[:, width // 2 :], chosen[:, : width // 2]]
    return results


def arrange_copies(bits, orders, me, staged, targets, sem):
    copies, number = [], 0
    half = 1 << (bits - 1)
    for source in range(len(targets) // (2 * len(orders)) if orders else 0):
        block = staged.shape[2] >> bits
        for order in orders:
            for begin in (half, 0):
                target = targets[number]
                for j in range(half):
                    place = arranged_block(order, begin + j, bits, me)
                    first = pl.multiple_of(place * block, block)
                    copies.append(
                        pltpu.make_async_copy(
                            staged.at[source, :, pl.ds(first, block)],
                            target.at[:, pl.ds(j * block, block)],
                            sem.at[number * half + j],
                        )
                    )
                number += 1
    return copies


def product(left, right):
    return lax.dot_general(left, right, (TN, ((), ())), preferred_element_type=jnp.float32)


def split_columns(array, parts):
    pieces, first = [], 0
    for _, widths in parts:
        pieces.append(array[:, first : first + sum(widths)])
        first += sum(widths)
    return pieces


def sent_products(lefts, right, parts):
    return [
        product(lefts[2 * k], piece) for k, piece in enumerate(split_columns(right, parts))
    ]


def send_parts(products, parts):
    return [xor_permute(item, "seq", order[0]) for item, (order, _) in zip(products, parts)]


def keep_parts(lefts, right, parts, arrived):
    return [
        product(lefts[2 * k + 1], piece) + arrived[k]
        for k, piece in enumerate(split_columns(right, parts))
    ]


def finish_kernel(parts, mats, bits, blocks, *refs):
    refs = list(refs)
    take = lambda count: [refs.pop(0) for _ in range(count)]
    ins = [take(len(parts)) for _ in range(mats)]
    narrow_ref, vector_ref = take(2)
    outs = take(mats)
    gathered_ref, vector_out_ref = take(2)
    me = lax.axis_index("seq")

    def partner(bit):
        return me + (1 << bit) * (1 - 2 * lax.rem(me // (1 << bit), 2))

    waves = []
    piece_count = len(parts[0][1])
    chain_count = 0
    for mat in range(mats):
        for piece in range(piece_count):
            wave, first = [], 0
            for k, (order, widths) in enumerate(parts):
                if widths[piece]:
                    within = sum(widths[:piece])
                    keep = refs.pop(0)
                    recvs = take(bits - 1)
                    wave.append(
                        (chain_count, ins[mat][k], within, outs[mat], first + within, order[1:], keep, recvs)
                    )
                    chain_count += 1
                first += sum(widths)
            waves.append(wave)
    narrow_order = parts[0][0]
    narrow = (chain_count, narrow_ref, 0, None, 0, narrow_order, refs.pop(0), take(bits))
    vector_sums, vector_recvs, local_sem, send_sem, recv_sem = refs

    barrier = pltpu.get_barrier_semaphore()
    for bit in range(bits):
        pl.semaphore_signal(
            barrier,
            inc=1,
            device_id={"seq": partner(bit)},
            device_id_type=pl.DeviceIdType.MESH,
        )
    pl.semaphore_wait(barrier, bits)

    numbers = {}

    def remote(key, src, dst, bit):
        number = numbers.setdefault(key, len(numbers))
        return pltpu.make_async_remote_copy(
            src_ref=src,
            dst_ref=dst,
            send_sem=send_sem.at[number],
            recv_sem=recv_sem.at[number],
            device_id={"seq": partner(bit)},
            device_id_type=pl.DeviceIdType.MESH,
        )

    def local_copy(chain):
        number, source, first, _, _, _, keep, _ = chain
        rows, columns = keep.shape
        return pltpu.make_async_copy(
            source.at[pl.ds(0, rows), pl.ds(first, columns)], keep, local_sem.at[number]
        )

    def chain_copy(chain, phase):
        number, source, first, _, _, order, keep, recvs = chain
        rows, columns = recvs[phase].shape
        if phase == 0:
            region = source.at[pl.ds(rows, rows), pl.ds(first, columns)]
        else:
            region = keep.at[pl.ds(rows, rows)]
        return remote((number, phase), region, recvs[phase], order[phase])

    def begin(wave):
        for chain in wave:
            chain_copy(chain, 0).start()
            local_copy(chain).start()

    def advance(chain, phase):
        if phase == 0:
            local_copy(chain).wait()
        chain_copy(chain, phase).wait_recv()
        number, _, _, out, place, order, keep, recvs = chain
        recv = recvs[phase]
        rows = recv.shape[0]
        slab = min(rows, 32)

        @pl.loop(0, rows // slab)
        def _(step):
            cut = pl.ds(pl.multiple_of(step * slab, slab), slab)
            keep[cut, :] = keep[cut, :] + recv[cut, :]

        if phase + 1 < len(order):
            chain_copy(chain, phase + 1).start()
        elif out is not None:
            out[:, place : place + keep.shape[1]] = keep[0:blocks, :]

    def vector_copy(phase):
        return remote(("vector", phase), vector_sums.at[phase], vector_recvs.at[phase], phase)

    def advance_vector(phase):
        vector_copy(phase).wait_recv()
        total = vector_sums[phase] + vector_recvs[phase]
        if phase + 1 < bits:
            vector_sums[phase + 1] = total
            vector_copy(phase + 1).start()
        else:
            vector_out_ref[...] = total

    def gather_copies(phase):
        bit = bits - 1 - phase
        copies = []
        for high in range(1 << phase):
            block = lax.rem(me, 2 << bit) + high * (2 << bit)
            region = gathered_ref.at[block]
            copies.append(remote(("gather", phase, high), region, region, bit))
        return copies

    narrow_steps = []

    def narrow_halving(phase):
        advance(narrow, phase)
        if phase + 1 == bits:
            gathered_ref[me] = narrow[6][0 : gathered_ref.shape[1], :]
            for copy in gather_copies(0):
                copy.start()

    def narrow_gather(phase):
        for copy in gather_copies(phase):
            copy.wait_recv()
        if phase + 1 < bits:
            for copy in gather_copies(phase + 1):
                copy.start()

    for phase in range(bits):
        narrow_steps.append(functools.partial(narrow_halving, phase))
    for phase in range(bits):
        narrow_steps.append(functools.partial(narrow_gather, phase))

    vector_sums[0] = vector_ref[...]
    vector_copy(0).start()
    chain_copy(narrow, 0).start()
    local_copy(narrow).start()
    for wave in waves[:2]:
        begin(wave)
    ticks = len(waves) + bits - 2
    for tick in range(max(ticks, 2 * bits)):
        if tick < bits:
            advance_vector(tick)
        if tick < len(narrow_steps):
            narrow_steps[tick]()
        for phase in range(bits - 1):
            number = tick - phase
            if 0 <= number < len(waves):
                for chain in waves[number]:
                    advance(chain, phase)
                if phase == 0 and number + 2 < len(waves):
                    begin(waves[number + 2])
    for wave in waves:
        for chain in wave:
            for phase in range(bits - 1):
                chain_copy(chain, phase).wait_send()
    for phase in range(bits):
        chain_copy(narrow, phase).wait_send()
        vector_copy(phase).wait_send()
        for copy in gather_copies(phase):
            copy.wait_send()


def finish(parts, mats, narrow, vector):
    bits = axis_bits("seq")
    size = 1 << bits
    blocks = mats[0][0].shape[0] // (size // 2)
    columns = sum(sum(widths) for _, widths in parts)
    scratch, copies, chains = [], 0, 0
    for _ in mats:
        for piece in range(len(parts[0][1])):
            for _, widths in parts:
                if widths[piece]:
                    rows = blocks * size // 4
                    scratch.append(pltpu.VMEM((rows, widths[piece]), jnp.float32))
                    for phase in range(bits - 1):
                        scratch.append(pltpu.VMEM((rows >> phase, widths[piece]), jnp.float32))
                    copies += bits - 1
                    chains += 1
    rows = narrow.shape[0] // 2
    scratch.append(pltpu.VMEM((rows, narrow.shape[1]), jnp.float32))
    for phase in range(bits):
        scratch.append(pltpu.VMEM((rows >> phase, narrow.shape[1]), jnp.float32))
    copies += 2 * bits + size - 1
    scratch += [pltpu.VMEM((bits,) + vector.shape, jnp.float32)] * 2
    scratch += [
        pltpu.SemaphoreType.DMA((chains + 1,)),
        pltpu.SemaphoreType.DMA((copies,)),
        pltpu.SemaphoreType.DMA((copies,)),
    ]
    shapes = [jax.ShapeDtypeStruct((blocks, columns), jnp.float32) for _ in mats]
    shapes.append(
        jax.ShapeDtypeStruct((size, narrow.shape[0] // size, narrow.shape[1]), jnp.float32)
    )
    shapes.append(jax.ShapeDtypeStruct(vector.shape, jnp.float32))
    flat = [item for mat in mats for item in mat]
    results = pl.pallas_call(
        functools.partial(finish_kernel, parts, len(mats), bits, blocks),
        out_shape=shapes,
        in_specs=[pl.BlockSpec(memory_space=pl.ANY)] * (len(flat) + 1)
        + [pl.BlockSpec(memory_space=pltpu.VMEM)],
        out_specs=[pl.BlockSpec(memory_space=pltpu.VMEM)] * len(shapes),
        scratch_shapes=scratch,
        compiler_params=pltpu.CompilerParams(
            collective_id=2, has_side_effects=True, vmem_limit_bytes=FINISH_LIMIT
        ),
        name="finish",
    )(*flat, narrow, vector)
    return results[:-2], results[-2], results[-1]


def head_gather(block):
    if lax.axis_size("head") != 2:
        return lax.all_gather(block, "head", axis=1, tiled=True)
    other = xor_permute(block, "head", 0)
    mine = lax.axis_index("head") == 0
    return jnp.concatenate(
        [jnp.where(mine, block, other), jnp.where(mine, other, block)], axis=1
    )


HEAD_GROUP = 8
VMEM_LIMIT = 56 * 1024 * 1024
FAR = 1 << 30
NN = ((1,), (0,))
NT = ((1,), (1,))
TN = ((0,), (0,))


def low_dot(left, right, dims):
    return lax.dot_general(
        left.astype(jnp.bfloat16),
        right.astype(jnp.bfloat16),
        (dims, ((), ())),
        preferred_element_type=jnp.float32,
    )


def halves_of(value):
    high = value.astype(jnp.bfloat16)
    return high, (value - high.astype(jnp.float32)).astype(jnp.bfloat16)


def thirds_of(value):
    first = value.astype(jnp.bfloat16).astype(jnp.float32)
    second = (value - first).astype(jnp.bfloat16).astype(jnp.float32)
    return first, second, value - first - second


def spread_matrix(heads, head_dim):
    shape = (heads, heads * head_dim)
    rows = lax.broadcasted_iota(jnp.int32, shape, 0)
    columns = lax.broadcasted_iota(jnp.int32, shape, 1)
    return (columns // head_dim == rows).astype(jnp.float32)


def turned(rows, matrix):
    return low_dot(
        jnp.concatenate(thirds_of(rows), axis=0), jnp.concatenate([matrix] * 3, axis=0), TN
    )


def head_sums(spread, value):
    high, low = halves_of(value)
    return low_dot(spread, high, NT) + low_dot(spread, low, NT)


def map_dot(left, right):
    high, low = halves_of(right)
    return low_dot(
        jnp.concatenate([left, left], axis=1), jnp.concatenate([high, low], axis=1), NT
    )


def fine_dot(left, right):
    left_high, left_low = halves_of(left)
    right_high, right_low = halves_of(right)
    return (
        low_dot(left_high, right_high, NN)
        + low_dot(left_high, right_low, NN)
        + low_dot(left_low, right_high, NN)
    )


def sigmoid(value):
    return 1.0 / (1.0 + jnp.exp(-value))


def segment_of(places, starts_ref, micro):
    label = jnp.zeros_like(places)
    for number in range(starts_ref.shape[1]):
        label = label + jnp.where(places >= starts_ref[micro, number], 1, 0)
    return label


def same_segment(count, base_ref, starts_ref, taps):
    micro = pl.program_id(0)
    places = base_ref[0] + lax.broadcasted_iota(jnp.int32, (count, 1), 0)
    own = segment_of(places, starts_ref, micro)
    return [
        jnp.where(segment_of(places - shift, starts_ref, micro) == own, 1.0, 0.0)
        for shift in range(1, taps)
    ]


def pair_labels(count, base_ref, starts_ref):
    micro = pl.program_id(0)
    column = base_ref[0] + lax.broadcasted_iota(jnp.int32, (count, 1), 0)
    row = base_ref[0] + lax.broadcasted_iota(jnp.int32, (1, count), 1)
    return segment_of(column, starts_ref, micro) == segment_of(row, starts_ref, micro)


def conv_sum(ext, value, halo, weight, bias, masks):
    count = value.shape[0]
    ext[0:8, :] = halo
    ext[8 : 8 + count, :] = value
    total = bias + weight[0:1] * value
    for shift in range(1, weight.shape[0]):
        total = (
            total
            + weight[shift : shift + 1]
            * ext[8 - shift : 8 - shift + count, :]
            * masks[shift - 1]
        )
    return total


def front_kernel(
    head_dim,
    base_ref,
    starts_ref,
    x_ref,
    halo_ref,
    weight_ref,
    bias_ref,
    b_ref,
    tail_ref,
    low_ref,
    state_ref,
    ext,
):
    heads = tail_ref.shape[1]
    weight = weight_ref[...]
    masks = same_segment(x_ref.shape[2], base_ref, starts_ref, weight.shape[0])
    total = conv_sum(ext, x_ref[0, 0], halo_ref[0], weight, bias_ref[...], masks)
    act = (total * sigmoid(total)).astype(jnp.bfloat16)
    low_ref[0] = act
    scale = turned(tail_ref[0], spread_matrix(heads, head_dim))
    high, low = halves_of(act.astype(jnp.float32) * scale)
    state_ref[0] = low_dot(high, b_ref[0], TN) + low_dot(low, b_ref[0], TN)


def mix_kernel(
    head_dim,
    base_ref,
    starts_ref,
    x_ref,
    b_ref,
    c_ref,
    run_ref,
    step_ref,
    carry_ref,
    start_ref,
    gate_ref,
    cot_ref,
    gain_ref,
    skip_ref,
    mixed_ref,
    sums_ref,
):
    heads = step_ref.shape[1]
    count = x_ref.shape[1]
    spread = spread_matrix(heads, head_dim)
    x = x_ref[0]
    b, c = b_ref[0], c_ref[0]
    rows = lax.broadcasted_iota(jnp.int32, (count, count), 0)
    columns = lax.broadcasted_iota(jnp.int32, (count, count), 1)
    valid = pair_labels(count, base_ref, starts_ref) & (rows >= columns)
    scores = jnp.where(valid, low_dot(c, b, NT), 0.0)
    wide = x.astype(jnp.float32)
    scaled = (wide * turned(step_ref[0], spread)).astype(jnp.bfloat16)
    inter = map_dot(c, start_ref[0]) * turned(carry_ref[0], spread)
    run_row = run_ref[0]
    run = turned(run_row, spread_matrix(heads, 1))
    pair = 2 * head_dim
    middle = count // 2
    lane = lax.broadcasted_iota(jnp.int32, (count, pair), 1)
    results = []
    for first in range(0, heads, 2):
        block = scaled[:, first * head_dim : first * head_dim + pair]
        halves = []
        for head in (first, first + 1):
            strips = []
            for top, cut in ((0, middle), (middle, count)):
                gap = run[top:cut, head : head + 1] - run_row[head : head + 1, :cut]
                weights = jnp.exp(jnp.minimum(gap, 0.0)) * scores[top:cut, :cut]
                strips.append(low_dot(weights, block[:cut], NN))
            halves.append(jnp.concatenate(strips, axis=0))
        results.append(jnp.where(lane < head_dim, halves[0], halves[1]))
    mixed = jnp.concatenate(results, axis=1) + inter + skip_ref[...] * wide
    mixed_ref[0] = mixed
    gate = gate_ref[0, 0]
    gated = mixed * (gate * sigmoid(gate))
    square = jnp.sum(gated * gated, axis=1, keepdims=True)
    cross = jnp.sum(cot_ref[0] * gain_ref[...] * gated, axis=1, keepdims=True)
    both = jnp.concatenate([square, cross], axis=1)

    @pl.when(pl.program_id(1) == 0)
    def _():
        sums_ref[0] = both

    @pl.when(pl.program_id(1) > 0)
    def _():
        sums_ref[0] = sums_ref[0] + both


def gate_kernel(
    head_dim,
    full,
    mixed_ref,
    gate_ref,
    cot_ref,
    sums_ref,
    gain_ref,
    carry_ref,
    c_ref,
    norm_ref,
    grad_gate_ref,
    both_ref,
    grad_mixed_ref,
    start_ref,
    rows_ref,
):
    heads = carry_ref.shape[1]
    mixed, gate, cot, gain = mixed_ref[0], gate_ref[0, 0], cot_ref[0], gain_ref[...]
    scale = lax.rsqrt(sums_ref[0, :, 0:1] / full + EPSILON)
    sigma = sigmoid(gate)
    act = gate * sigma
    gated = mixed * act
    unit = gated * scale
    norm_ref[0] = (unit * gain).astype(jnp.bfloat16)
    pull = scale * scale * scale * sums_ref[0, :, 1:2] / full
    grad_gated = cot * gain * scale - gated * pull
    grad_gate = (grad_gated * mixed * sigma * (1.0 + gate * (1.0 - sigma))).astype(jnp.bfloat16)
    grad_gate_ref[0] = grad_gate
    both_ref[0, 0] = grad_gate
    grad_mixed = (grad_gated * act).astype(jnp.bfloat16)
    grad_mixed_ref[0] = grad_mixed
    carried = grad_mixed.astype(jnp.float32) * turned(
        carry_ref[0], spread_matrix(heads, head_dim)
    )
    high, low = halves_of(carried)
    start_ref[0] = low_dot(high, c_ref[0], TN) + low_dot(low, c_ref[0], TN)
    gains = jnp.sum(cot * unit, axis=0, keepdims=True)
    rows_ref[0] = jnp.concatenate([gains, jnp.zeros((7, gains.shape[1]), jnp.float32)], axis=0)


def back_kernel(
    head_dim,
    base_ref,
    starts_ref,
    x_ref,
    g_ref,
    b_ref,
    c_ref,
    run_ref,
    step_ref,
    carry_ref,
    tail_ref,
    start_ref,
    end_ref,
    pre_ref,
    halo_ref,
    weight_ref,
    bias_ref,
    skip_ref,
    both_in_ref,
    both_ref,
    edge_ref,
    halo_out_ref,
    rows_ref,
    direct_ref,
    decay_ref,
    pair_ref,
    grad_b_ref,
    grad_c_ref,
    ext,
    moved,
):
    heads = step_ref.shape[1]
    count = x_ref.shape[1]
    spread = spread_matrix(heads, head_dim)
    x, g, b, c = x_ref[0], g_ref[0], b_ref[0], c_ref[0]
    x_wide, g_wide = x.astype(jnp.float32), g.astype(jnp.float32)
    rows = lax.broadcasted_iota(jnp.int32, (count, count), 0)
    columns = lax.broadcasted_iota(jnp.int32, (count, count), 1)
    valid = pair_labels(count, base_ref, starts_ref) & (columns >= rows)
    scores = jnp.where(valid, low_dot(b, c, NT), 0.0)
    upto = (rows >= columns).astype(jnp.bfloat16)
    before = (rows < columns).astype(jnp.float32)
    step = turned(step_ref[0], spread)
    carry = turned(carry_ref[0], spread)
    tail = turned(tail_ref[0], spread)
    scaled_wide = x_wide * step
    scaled, scaled_rest = halves_of(scaled_wide)
    start, end = start_ref[0], end_ref[0]
    run_row = run_ref[0]
    run = turned(run_row, spread_matrix(heads, 1))
    pair = 2 * head_dim
    lane = lax.broadcasted_iota(jnp.int32, (count, pair), 1)
    middle = count // 2
    score_grads = [
        jnp.zeros((middle, count), jnp.float32),
        jnp.zeros((count - middle, count - middle), jnp.float32),
    ]
    results, straddles = [], []
    for first in range(0, heads, 2):
        cut = slice(first * head_dim, first * head_dim + pair)
        g_block = g[:, cut]
        g_swap = jnp.concatenate([g_block[:, head_dim:], g_block[:, :head_dim]], axis=1)
        x_block, x_rest = scaled[:, cut], scaled_rest[:, cut]
        x_rest = jnp.concatenate([x_rest[:, head_dim:], x_rest[:, :head_dim]], axis=1)
        halves = []
        for head in (first, first + 1):
            own = (lane < head_dim) if head == first else (lane >= head_dim)
            x_own, g_own = jnp.where(own, x_block, x_rest), jnp.where(own, g_block, g_swap)
            strips, straddle = [], None
            for part, (top, cut) in enumerate(((0, middle), (middle, count))):
                gap = run_row[head : head + 1, top:] - run[top:cut, head : head + 1]
                fade = jnp.exp(jnp.minimum(gap, 0.0))
                weights = fade * scores[top:cut, top:]
                strips.append(low_dot(weights, g_block[top:], NN))
                inner = low_dot(x_own[top:cut], g_own[top:], NT)
                score_grads[part] = score_grads[part] + fade * inner
                sums = low_dot(weights * inner, upto[top:, top:], NN)
                sums = jnp.sum(sums * before[top:cut, top:], axis=0, keepdims=True)
                if part == 0:
                    straddle = sums
                else:
                    straddle = jnp.concatenate(
                        [straddle[:, :middle], straddle[:, middle:] + sums], axis=1
                    )
            straddles.append(straddle)
            halves.append(jnp.concatenate(strips, axis=0))
        results.append(jnp.where(lane < head_dim, halves[0], halves[1]))
    score_grad = jnp.concatenate(
        [
            score_grads[0],
            jnp.concatenate([jnp.zeros((count - middle, middle), jnp.float32), score_grads[1]], axis=1),
        ],
        axis=0,
    )
    score_grad = jnp.where(valid, score_grad, 0.0)
    later = map_dot(b, end) * tail
    values = jnp.concatenate(results, axis=1) + later
    inter = map_dot(c, start) * carry
    direct_ref[0] = head_sums(spread, x_wide * values)
    given = head_sums(spread, scaled_wide * later)
    taken = head_sums(spread, g_wide * inter)
    flows = jnp.concatenate([given, taken], axis=0)
    flow_pieces = [item.astype(jnp.bfloat16) for item in thirds_of(flows)]
    after = (rows < columns).astype(jnp.bfloat16)
    flow_later = sum(low_dot(item, after, NN) for item in flow_pieces)
    flow_sooner = sum(low_dot(item, upto, NN) for item in flow_pieces)
    decay_ref[0] = (
        jnp.concatenate(straddles, axis=0) + flow_later[:heads] + flow_sooner[heads:]
    )
    pair_high, pair_low = halves_of(start * end)
    pair_ref[0] = low_dot(spread, pair_high, NN) + low_dot(spread, pair_low, NN)
    grads_high, grads_low = halves_of(score_grad)
    grad_c = fine_dot(g_wide * carry, start) + low_dot(grads_high, b, TN) + low_dot(grads_low, b, TN)
    grad_b = fine_dot(scaled_wide * tail, end) + low_dot(grads_high, c, NN) + low_dot(grads_low, c, NN)

    @pl.when(pl.program_id(1) == 0)
    def _():
        grad_b_ref[0] = grad_b
        grad_c_ref[0] = grad_c

    @pl.when(pl.program_id(1) > 0)
    def _():
        grad_b_ref[0] = grad_b_ref[0] + grad_b
        grad_c_ref[0] = grad_c_ref[0] + grad_c

    weight, pre = weight_ref[...], pre_ref[0, 0]
    masks = same_segment(count, base_ref, starts_ref, weight.shape[0])
    total = conv_sum(ext, pre, halo_ref[0], weight, bias_ref[...], masks)
    sigma = sigmoid(total)
    grad_conv = (values * step + skip_ref[...] * g_wide) * (
        sigma * (1.0 + total * (1.0 - sigma))
    )
    moved[0:8, :] = jnp.zeros_like(moved[0:8, :])
    moved[8 + count :, :] = jnp.zeros_like(moved[8 + count :, :])
    sums = [jnp.sum(grad_conv * pre, axis=0, keepdims=True)]
    back = jnp.concatenate(
        [jnp.zeros((8, pre.shape[1]), jnp.float32), grad_conv * weight[0:1]], axis=0
    )
    for shift in range(1, weight.shape[0]):
        part = grad_conv * masks[shift - 1]
        sums.append(
            jnp.sum(part * ext[8 - shift : 8 - shift + count, :], axis=0, keepdims=True)
        )
        moved[8 : 8 + count, :] = part * weight[shift : shift + 1]
        back = back + moved[shift : shift + 8 + count, :]
    halo_out_ref[0] = back[:8]
    both_ref[0, 0] = back[8:].astype(jnp.bfloat16)
    edge_ref[0] = back[count:]
    sums.append(jnp.sum(grad_conv, axis=0, keepdims=True))
    sums.append(jnp.sum(g_wide * x_wide, axis=0, keepdims=True))
    sums.append(jnp.zeros((8 - len(sums), pre.shape[1]), jnp.float32))
    rows_ref[0] = jnp.concatenate(sums, axis=0)


def blocked(kernel, name, grid, ins, outs, scratch=(), micros=0, aliases=None):
    moved = sum(item[0].size * item[0].dtype.itemsize for item in ins if item[1] != "any")
    moved += sum(math.prod(item[2]) * grid[0] * grid[1] * jnp.dtype(item[1]).itemsize for item in outs)

    def spec(item):
        if item[1] is None:
            return pl.BlockSpec(memory_space=pltpu.SMEM)
        if item[1] == "any":
            return pl.BlockSpec(memory_space=pl.ANY)
        return pl.BlockSpec(item[1], item[2])

    return pl.pallas_call(
        kernel,
        grid=grid,
        in_specs=[spec(item) for item in ins],
        out_specs=[pl.BlockSpec(item[2], item[3]) for item in outs],
        out_shape=[jax.ShapeDtypeStruct(item[0], item[1]) for item in outs],
        scratch_shapes=list(scratch),
        input_output_aliases=aliases or {},
        compiler_params=pltpu.CompilerParams(
            dimension_semantics=("arbitrary",) * len(grid), vmem_limit_bytes=VMEM_LIMIT
        ),
        cost_estimate=pl.CostEstimate(
            flops=micros * 1_000_000_000, bytes_accessed=moved, transcendentals=0
        ),
        name=name,
    )(*[item[0] for item in ins])


def body(
    tokens,
    norm_gain,
    in_weight,
    bc_weight,
    dt_weight,
    dt_bias,
    a_log,
    conv_weight,
    conv_bias,
    bc_conv_weight,
    bc_conv_bias,
    d_skip,
    gate_gain,
    out_weight,
    cotangent,
    seq_lengths,
):
    micro, length, width = tokens.shape
    heads = dt_bias.shape[0]
    inner = conv_bias.shape[0]
    head_dim = inner // heads
    state_size = bc_weight.shape[1] // 2
    taps = conv_weight.shape[0]
    total = micro * length
    head_count = lax.axis_size("head")
    full_inner = inner * head_count
    group = min(HEAD_GROUP, heads)
    groups = heads // group
    wide = group * head_dim
    base = lax.axis_index("seq").astype(jnp.int32) * length
    labels = segment_ids(seq_lengths, base - (taps - 1), length + taps - 1, micro)
    own_labels = labels[:, taps - 1 :]
    before_labels = labels[:, taps - 2]
    starts = jnp.cumsum(seq_lengths, axis=-1).astype(jnp.int32) - seq_lengths
    long_starts = jnp.full((micro - starts.shape[0], starts.shape[1]), FAR, jnp.int32)
    starts = jnp.concatenate([starts, long_starts.at[:, 0].set(0)], axis=0)
    base_item, starts_item = (base[None], None), (starts, None)

    flat = tokens.reshape(total, width).astype(jnp.float32)
    cot_flat = cotangent.reshape(total, width)
    normed, norm_back = jax.vjp(rms_scale, flat, norm_gain)
    normed_low = normed.astype(jnp.bfloat16)
    gate_x = jnp.einsum(
        "td,dkc->ktc", normed_low, in_weight, preferred_element_type=jnp.float32
    ).reshape(2, micro, length, inner)
    bc_pre = jnp.dot(normed_low, bc_weight, preferred_element_type=jnp.float32).reshape(
        micro, length, 2 * state_size
    )
    delta_pre = lax.dot_general(
        dt_weight, normed_low, (((0,), (1,)), ((), ())), preferred_element_type=jnp.float32
    )
    left = shifted(
        jnp.concatenate(
            [gate_x[1, :, length - taps + 1 :], bc_pre[:, length - taps + 1 :]], axis=-1
        ),
        "seq",
        1,
    )
    left_x, left_bc = left[..., :inner], left[..., inner:]
    halo = jnp.pad(left_x, ((0, 0), (9 - taps, 0), (0, 0)))
    conv_many = jax.vmap(conv_silu, in_axes=(0, None, None, 0))
    bc_act, bc_conv_back = jax.vjp(
        lambda extended, weight, bias: conv_many(extended, weight, bias, labels),
        jnp.concatenate([left_bc, bc_pre], axis=1),
        bc_conv_weight,
        bc_conv_bias,
    )
    bc_low = bc_act.astype(jnp.bfloat16)
    b_low, c_low = bc_low[..., :state_size], bc_low[..., state_size:]
    (delta, decay), rate_back = jax.vjp(step_sizes, delta_pre, dt_bias, a_log)

    def by_micro(array):
        return array.reshape(heads, micro, length).transpose(1, 0, 2)

    def by_head(array):
        return array.transpose(1, 0, 2).reshape(heads, total)

    delta, decay = by_micro(delta), by_micro(decay)
    order = jnp.arange(length)
    running = jnp.einsum(
        "mhj,ji->mhi",
        decay,
        (order[:, None] <= order[None, :]).astype(jnp.float32),
        precision=HIGHEST,
    )
    device_log = running[:, :, -1]
    live = (own_labels == before_labels[:, None]).astype(jnp.float32)
    last = (own_labels == own_labels[:, -1:]).astype(jnp.float32)
    carried = jnp.exp(running) * live[:, None]
    tail = jnp.exp(device_log[:, :, None] - running) * last[:, None]
    device_live = live[:, -1]
    gain_row, skip_row = gate_gain[None], jnp.repeat(d_skip, head_dim)[None]
    conv_row = conv_bias[None]

    grid = (micro, groups)
    token_block = (1, length, wide)
    in_token = lambda m, k: (m, 0, k)
    half_block = (1, 1, length, wide)
    in_gate, in_x = lambda m, k: (0, m, 0, k), lambda m, k: (1, m, 0, k)
    row_block, in_row = (1, group, length), lambda m, k: (m, k, 0)
    map_block, in_map = (1, length, state_size), lambda m, k: (m, 0, 0)
    state_block, in_state = (1, wide, state_size), lambda m, k: (m, k, 0)
    halo_block = (1, 8, wide)
    flat_block, in_flat = (1, wide), lambda m, k: (0, k)
    conv_item = (conv_weight, (taps, wide), in_flat)
    whole = (micro, length, inner)
    state_shape = (micro, inner, state_size)
    row_shape = (micro, heads, length)

    x_low, device_state = blocked(
        functools.partial(front_kernel, head_dim),
        "front",
        grid,
        [
            base_item,
            starts_item,
            (gate_x, half_block, in_x),
            (halo, halo_block, in_token),
            conv_item,
            (conv_row, flat_block, in_flat),
            (b_low, map_block, in_map),
            (tail * delta, row_block, in_row),
        ],
        [
            (whole, jnp.bfloat16, token_block, in_token),
            (state_shape, jnp.float32, state_block, in_state),
        ],
        [pltpu.VMEM((length + 8, wide), jnp.float32)],
        20,
    )
    exchange_log = jnp.where(device_live[:, None] > 0.0, device_log, DEAD)
    exchange_shape = (micro, heads, head_dim, state_size)
    parts = scatter_parts(inner, axis_bits("seq"))
    orders = tuple(order for order, _ in parts)
    tiled = (width >> axis_bits("seq")) % 128 == 0
    incoming, arranged = exchange(
        device_state.reshape(exchange_shape),
        exchange_log,
        False,
        (cot_flat, normed_low) if tiled else (),
        orders if tiled else (),
    )
    if not tiled:
        arranged = arrange(cot_flat, orders) + arrange(normed_low, orders)
    cot_parts, normed_parts = arranged[: 2 * len(parts)], arranged[2 * len(parts) :]
    incoming = incoming.reshape(state_shape)

    grad_gate_n = jnp.dot(cot_flat, out_weight, preferred_element_type=jnp.float32).reshape(whole)
    mixed, sums = blocked(
        functools.partial(mix_kernel, head_dim),
        "mix",
        grid,
        [
            base_item,
            starts_item,
            (x_low, token_block, in_token),
            (b_low, map_block, in_map),
            (c_low, map_block, in_map),
            (running, row_block, in_row),
            (delta, row_block, in_row),
            (carried, row_block, in_row),
            (incoming, state_block, in_state),
            (gate_x, half_block, in_gate),
            (grad_gate_n, token_block, in_token),
            (gain_row, flat_block, in_flat),
            (skip_row, flat_block, in_flat),
        ],
        [
            (whole, jnp.float32, token_block, in_token),
            ((micro, length, 2), jnp.float32, (1, length, 2), in_map),
        ],
        (),
        25,
    )
    sums = all_sum(sums, "head")
    normed_gate, grad_gate_pre, grad_gate_x, grad_mixed, device_grad, gate_rows = blocked(
        functools.partial(gate_kernel, head_dim, float(full_inner)),
        "gate",
        grid,
        [
            (mixed, token_block, in_token),
            (gate_x, half_block, in_gate),
            (grad_gate_n, token_block, in_token),
            (sums, (1, length, 2), in_map),
            (gain_row, flat_block, in_flat),
            (carried, row_block, in_row),
            (c_low, map_block, in_map),
        ],
        [
            (whole, jnp.bfloat16, token_block, in_token),
            (whole, jnp.bfloat16, token_block, in_token),
            ((2,) + whole, jnp.bfloat16, half_block, in_gate),
            (whole, jnp.bfloat16, token_block, in_token),
            (state_shape, jnp.float32, state_block, in_state),
            ((micro, 8, inner), jnp.float32, halo_block, in_token),
        ],
        (),
        20,
    )
    normed_gate = normed_gate.reshape(total, inner)
    grad_gate_pre = grad_gate_pre.reshape(total, inner)
    grad_gate_gain = jnp.sum(gate_rows[:, 0], axis=0)

    out_sent = sent_products(cot_parts, normed_gate, parts)
    gate_sent = sent_products(normed_parts, grad_gate_pre, parts)
    outgoing, _ = exchange(device_grad.reshape(exchange_shape), exchange_log, True)
    outgoing, out_sent, gate_sent = lax.optimization_barrier((outgoing, out_sent, gate_sent))
    out_arrived = send_parts(out_sent, parts)
    gate_arrived = send_parts(gate_sent, parts)
    outgoing = outgoing.reshape(state_shape)
    grad_gate_x, edge, halo_grad, conv_rows, direct, fading, pairs, grad_b, grad_c = blocked(
        functools.partial(back_kernel, head_dim),
        "back",
        grid,
        [
            base_item,
            starts_item,
            (x_low, token_block, in_token),
            (grad_mixed, token_block, in_token),
            (b_low, map_block, in_map),
            (c_low, map_block, in_map),
            (running, row_block, in_row),
            (delta, row_block, in_row),
            (carried, row_block, in_row),
            (tail, row_block, in_row),
            (incoming, state_block, in_state),
            (outgoing, state_block, in_state),
            (gate_x, half_block, in_x),
            (halo, halo_block, in_token),
            conv_item,
            (conv_row, flat_block, in_flat),
            (skip_row, flat_block, in_flat),
            (grad_gate_x, "any"),
        ],
        [
            ((2,) + whole, jnp.bfloat16, half_block, in_x),
            ((micro, 8, inner), jnp.float32, halo_block, in_token),
            ((micro, 8, inner), jnp.float32, halo_block, in_token),
            ((micro, 8, inner), jnp.float32, halo_block, in_token),
            (row_shape, jnp.float32, row_block, in_row),
            (row_shape, jnp.float32, row_block, in_row),
            ((micro, heads, state_size), jnp.float32, (1, group, state_size), in_state),
            ((micro, length, state_size), jnp.float32, map_block, in_map),
            ((micro, length, state_size), jnp.float32, map_block, in_map),
        ],
        [
            pltpu.VMEM((length + 8, wide), jnp.float32),
            pltpu.VMEM((length + 16, wide), jnp.float32),
        ],
        80,
        {17: 0},
    )
    halo_grad, grad_b, grad_gate_x, out_arrived, gate_arrived = lax.optimization_barrier(
        (halo_grad, grad_b, grad_gate_x, out_arrived, gate_arrived)
    )
    grad_bc = all_sum(jnp.concatenate([grad_b, grad_c], axis=-1), "head")
    kept = jnp.sum(pairs, axis=-1) * jnp.exp(device_log) * device_live[:, None]
    grad_decay = by_head(fading + kept[:, :, None])
    grad_delta_pre, grad_dt_bias, grad_a_log = rate_back((by_head(direct), grad_decay))
    conv_rows = jnp.sum(conv_rows, axis=0)
    grad_conv_weight, grad_conv_bias = conv_rows[:taps], conv_rows[taps]
    grad_d_skip = jnp.sum(conv_rows[taps + 1].reshape(heads, head_dim), axis=-1)
    grad_bc_ext, grad_bc_conv_weight, grad_bc_conv_bias = bc_conv_back(grad_bc)
    right = shifted(
        jnp.concatenate([halo_grad[:, 9 - taps :], grad_bc_ext[:, : taps - 1]], axis=-1), "seq", -1
    )
    right_x, right_bc = right[..., :inner], right[..., inner:]
    grad_gate_x = lax.dynamic_update_slice(
        grad_gate_x,
        (edge[:, 9 - taps :] + right_x).astype(jnp.bfloat16)[None],
        (1, 0, length - taps + 1, 0),
    )
    grad_bc_pre = grad_bc_ext[:, taps - 1 :].at[:, length - taps + 1 :].add(right_bc)
    bc_flat = grad_bc_pre.reshape(total, 2 * state_size)
    grad_gate_x = grad_gate_x.reshape(2, total, inner)
    x_sent = sent_products(normed_parts, grad_gate_x[1], parts)
    grad_gate_x, x_sent = lax.optimization_barrier((grad_gate_x, x_sent))
    x_arrived = send_parts(x_sent, parts)

    row_part = jnp.einsum(
        "ktc,dkc->td", grad_gate_x, in_weight, preferred_element_type=jnp.float32
    )
    bc_high, bc_rest = halves_of(bc_flat * (1.0 / head_count))
    delta_high, delta_rest = halves_of(grad_delta_pre.T)
    narrow_left = jnp.concatenate([bc_high, bc_rest, delta_high, delta_rest], axis=1)
    narrow_right = jnp.concatenate([bc_weight, bc_weight, dt_weight, dt_weight], axis=1)
    row_part = row_part + lax.dot_general(
        narrow_left, narrow_right, (NT, ((), ())), preferred_element_type=jnp.float32
    )
    row_grads = all_sum(row_part, "head")
    grad_flat, grad_norm_gain = norm_back(row_grads)
    grad_tokens = (cot_flat.astype(jnp.float32) + grad_flat).reshape(micro, length, width)

    share_bc = 2 * state_size // head_count
    own_bc = lax.dynamic_slice_in_dim(bc_flat, lax.axis_index("head") * share_bc, share_bc, 1)
    across = share_bc + heads
    narrow_high, narrow_rest = halves_of(jnp.concatenate([own_bc, grad_delta_pre.T], axis=1))
    both = jnp.concatenate([narrow_high, narrow_rest], axis=1)
    narrow = jnp.concatenate(
        [product(normed_parts[1], both), product(normed_parts[0], both)], axis=0
    )
    narrow = narrow[:, :across] + narrow[:, across:]
    size = lax.axis_size("seq")
    row_count = width // size
    narrow = narrow.reshape(size, row_count, across)
    beside = 128 // heads
    narrow_bc = jnp.pad(narrow[:, :, :share_bc], ((0, 0), (0, 0), (0, -share_bc % 128)))
    narrow_steps = narrow[:, :, share_bc:].reshape(size, row_count // beside, 128)
    narrow_steps = jnp.pad(narrow_steps, ((0, 0), (0, 0), (0, narrow_bc.shape[2] - 128)))
    narrow = jnp.concatenate([narrow_bc, narrow_steps], axis=1)
    narrow_rows = narrow.shape[1]
    narrow = jnp.pad(narrow, ((0, 0), (0, -narrow_rows % 8), (0, 0)))
    narrow = narrow.reshape(-1, narrow.shape[2])

    small = [
        grad_bc_conv_weight,
        grad_bc_conv_bias,
        grad_norm_gain,
        grad_dt_bias,
        grad_a_log,
        grad_d_skip,
        grad_conv_weight,
        grad_conv_bias,
        grad_gate_gain,
    ]
    row = jnp.concatenate([item.reshape(-1) for item in small])
    count = row.size
    row = jnp.pad(row, (0, -count % 1024)).reshape(-1, 128)

    mats = [
        keep_parts(cot_parts, normed_gate, parts, out_arrived),
        keep_parts(normed_parts, grad_gate_pre, parts, gate_arrived),
        keep_parts(normed_parts, grad_gate_x[1], parts, x_arrived),
    ]
    (grad_out_weight, gate_block, x_block), gathered, row = finish(parts, mats, narrow, row)
    grad_in_weight = jnp.stack([gate_block, x_block], axis=1)
    grad_bc_weight = head_gather(gathered[:, :row_count, :share_bc].reshape(width, share_bc))
    grad_dt_weight = gathered[:, row_count:narrow_rows, :128].reshape(width, heads)
    row = row.reshape(-1)
    sizes, first = [], 0
    for item in small:
        sizes.append(row[first : first + item.size].reshape(item.shape))
        first += item.size
    (
        grad_bc_conv_weight,
        grad_bc_conv_bias,
        grad_norm_gain,
        grad_dt_bias,
        grad_a_log,
        grad_d_skip,
        grad_conv_weight,
        grad_conv_bias,
        grad_gate_gain,
    ) = sizes

    share = width // head_count
    if head_count == 2:
        first = lax.axis_index("head") * share
        own_rows = lax.dynamic_slice_in_dim(out_weight, first, share, 0)
        other_rows = lax.dynamic_slice_in_dim(out_weight, share - first, share, 0)
        summed = lax.dot_general(
            normed_gate, own_rows, (NT, ((), ())), preferred_element_type=jnp.float32
        ) + xor_permute(
            lax.dot_general(
                normed_gate, other_rows, (NT, ((), ())), preferred_element_type=jnp.float32
            ),
            "head",
            0,
        )
    else:
        head_terms = lax.dot_general(
            normed_gate, out_weight, (NT, ((), ())), preferred_element_type=jnp.float32
        )
        summed = lax.psum_scatter(head_terms, "head", scatter_dimension=1, tiled=True)
    residual = lax.dynamic_slice_in_dim(flat, lax.axis_index("head") * share, share, 1)
    block_out = (residual + summed).astype(jnp.bfloat16).reshape(micro, length, share)
    return (
        block_out,
        grad_tokens,
        grad_norm_gain,
        grad_in_weight,
        grad_bc_weight,
        grad_dt_weight,
        grad_dt_bias,
        grad_a_log,
        grad_d_skip,
        grad_conv_weight,
        grad_conv_bias,
        grad_bc_conv_weight,
        grad_bc_conv_bias,
        grad_gate_gain,
        grad_out_weight,
    )


def solution(mesh):
    return jax.shard_map(
        body,
        mesh=mesh,
        in_specs=(
            P(None, "seq", None),
            P(),
            P(None, None, "head"),
            P(),
            P(None, "head"),
            P("head"),
            P("head"),
            P(None, "head"),
            P("head"),
            P(),
            P(),
            P("head"),
            P("head"),
            P(None, "head"),
            P(None, "seq", None),
            P(),
        ),
        out_specs=(
            P(None, "seq", "head"),
            P(None, "seq", None),
            P(),
            P("seq", None, "head"),
            P(),
            P(None, "head"),
            P("head"),
            P("head"),
            P("head"),
            P(None, "head"),
            P("head"),
            P(),
            P(),
            P("head"),
            P("seq", "head"),
        ),
        check_vma=False,
    )
```

time: 1640 us -> 1060 us (0.65)
  Pallas kernels: 205 us -> 605 us
  waiting for transfers between devices: 462 us -> 135 us
  local copies, waits for them, and re-layouts: 337 us -> 49.3 us
  other arithmetic: 231 us -> 54.9 us
  matrix products: 314 us -> 184 us
  starting transfers between devices: 59.2 us -> 23.2 us
    pallas_call x2 -> x7, Pallas kernels: 205 us -> 605 us  [the longest x1 223 us: finish(): pl.pallas_call(functools.partial(finish_kernel, parts, len(mats), bits, b...]
    ppermute x53 -> x17, waiting for transfers between devices: 462 us -> 131 us  [xor_permute(): return lax.ppermute(value, axis, [(i, i ^ 1 << bit) for i in range(size)])]
    dynamic_slice x20 -> x1, local copies, waits for them, and re-layouts: 133 us -> 0.04 us  [body(): lax.dynamic_slice_in_dim(bc_flat, lax.axis_index('head') * share_bc, shar...]
    dot_general x38 -> x33, matrix products: 293 us -> 169 us  [the longest x26 87.5 us: product(): lax.dot_general(left, right, (TN, ((), ())), preferred_element_type=jnp.f...]
    reshape x11 -> x9, local copies, waits for them, and re-layouts: 54.4 us -> 5.01 us  [the longest x2 1.23 us: body(): sizes.append(row[first:first + item.size].reshape(item.shape))]
    another operation x18 -> x2, local copies, waits for them, and re-layouts: 43.5 us -> 0.75 us  [the longest x1 0.68 us: body(): gain_row, skip_row = (gate_gain[None], jnp.repeat(d_skip, head_dim)[None])]
    convert_element_type x7 -> x2, local copies, waits for them, and re-layouts: 40 us -> 1.68 us  [the longest x1 0.84 us: halves_of(): high = value.astype(jnp.bfloat16)]
    another operation x12 -> x3, other arithmetic: 37 us -> 0.95 us
  transfers between devices with their start and end apart: 58 -> 19, of which waited for: 27 -> 7; matrix products, arithmetic and copies ran while one was open for 45% -> 19% of each run, Pallas kernels for 7% -> 11%
where the time goes in v2:
time: 1060 us; the launch traced here: 1050 us
  Pallas kernels  605 us (57%)
  matrix products  184 us (17%)
  waiting for transfers between devices  135 us (13%)
  other arithmetic  54.9 us (5%)
  local copies, waits for them, and re-layouts  49.3 us (5%)
  starting transfers between devices  23.2 us (2%)
    pallas_call x1, Pallas kernels, finish(): pl.pallas_call(functools.partial(finish_kernel, parts, len(mats), bits, b...  223 us
    pallas_call x2, Pallas kernels, exchange(): pl.pallas_call(functools.partial(exchange_kernel, length, reverse, orders...  195 us
    pallas_call x4, Pallas kernels, blocked(): pl.pallas_call(kernel, grid=grid, in_specs=[spec(item) for item in ins],...  187 us
    ppermute x17, waiting for transfers between devices, xor_permute(): return lax.ppermute(value, axis, [(i, i ^ 1 << bit) for i in range(size)])  131 us
    dot_general x26, matrix products, product(): lax.dot_general(left, right, (TN, ((), ())), preferred_element_type=jnp.f...  87.5 us
    dot_general x1, matrix products, body(): jnp.einsum('ktc,dkc->td', grad_gate_x, in_weight, preferred_element_type=...  26.1 us
    dot_general x1, matrix products, body(): jnp.einsum('td,dkc->ktc', normed_low, in_weight, preferred_element_type=j...  22.4 us
  transfers between devices with their start and end apart: 19, of which 7 were waited for; matrix products, arithmetic and copies ran while one was open for 19% of the time, Pallas kernels for 11%

profile of v2, /device:TPU:1, one launch (start us, length us, event | category | flops | bytes accessed | tf_op | source)
XLA Modules:
  0.0 1054.8 jit_solution(2280184576113083738)
XLA Ops:
  0.7 3.2 multiply_reduce_fusion.2
  5.2 22.4 %fusion.2 = f32[1024,2,2048]{2,0,1:T(8,128)S(1)} fusion(bf16[2048,2,2048]{2,1,0:T(2,128)(2,1)} %param.22, bf16[1024,2048]{1,0:T(8,128)(2,1)S(1)} %multiply_convert_fusion.1.refs_1_), kind=kOutput, calls=%fused_computation.2 | convolution fusion | flops 17179869184 | bytes 37748736 | tf_op jit(solution)/shard_map/td,dkc->ktc/dot_general | solution.py:1073
  29.0 4.3 copy-done.79
  33.4 4.2 collective-permute-start
  39.0 4.2 broadcast_multiply_fusion.1
  47.1 14.5 %fusion.5.cot_ref = f32[4,256,2048]{2,1,0:T(8,128)} fusion(bf16[4,256,2048]{2,1,0:T(8,128)(2,1)} %param.34, bf16[2048,2048]{1,0:T(8,128)(2,1)} %param.33), kind=kOutput, calls=%fused_computation.7 | convolution fusion | flops 8589934592 | bytes 20971520 | tf_op jit(solution)/shard_map/dot_general | solution.py:1178
  62.3 1.7 multiply_convert_fusion.3
  65.6 21.1 %front.1 = (bf16[4,256,2048]{2,1,0:T(8,128)(2,1)}, f32[4,2048,128]{2,1,0:T(8,128)}) custom-call(s32[1]{0:T(128)} %bitcast.1.base_ref, s32[4,3]{1,0:T(4,128)} %pad_add_fusion.2.starts_ref, f32[2,4,256,2048]{3,2,1,0:T(8,128)} %bitcast.209, f32[4,8,2048]{2,1,0:T(8,128)} %pad.38.halo_ref, f32[4,2048]{1,0:T(4,128)} %weight_ref.3, f32[1,2048]{1,0:T(1,128)} %bitcast.215, ...), custom_call_target="tpu_custom_call" | custom-call | flops 20000000000 | bytes 25862196 | tf_op jit(solution)/shard_map/front/pallas_call | solution.py:1012
  86.7 100.4 %exchange.1 = (f32[4,4,8,64,128]{4,3,2,1,0:T(8,128)}, bf16[1024,1024]{1,0:T(8,128)(2,1)S(1)}, bf16[1024,1024]{1,0:T(8,128)(2,1)S(1)}, bf16[1024,1024]{1,0:T(8,12...) custom-call(f32[4,4,8,64,128]{4,3,2,1,0:T(8,128)} %bitcast.237, ...), custom_call_target="tpu_custom_call" | custom-call | flops 99999997952 | tf_op jit(solution)/shard_map/exchange/pallas_call | solution.py:238
  191.1 26.2 %mix.1 = (f32[4,256,2048]{2,1,0:T(8,128)}, f32[4,256,2]{2,1,0:T(8,128)}) custom-call(s32[1]{0:T(128)} %bitcast.1.base_ref, s32[4,3]{1,0:T(4,128)} %pad_add_fusion.2.starts_ref, bf16[4,256,2048]{2,1,0:T(8,128)(2,1)} %get-tuple-element.105.x_ref, bf16[4,256,128]{2,1,0:T(8,128)(2,1)} %get-tuple-element.271.b_ref, ...), custom_call_target="tpu_custom_call" | custom-call | flops 24999999488 | bytes 42909748 | tf_op jit(solution)/shard_map/mix/pallas_call | solution.py:1012
  217.3 1.9 collective-permute-start.1
  219.2 1.7 collective-permute-done.1
  221.0 1.9 add.202.sums_ref
  222.8 22.8 %gate.1 = (bf16[4,256,2048]{2,1,0:T(8,128)(2,1)}, bf16[4,256,2048]{2,1,0:T(8,128)(2,1)}, bf16[2,4,256,2048]{3,2,1,0:T(8,128)(2,1)}, bf16[4,256,2048]{2,1,0:T(8,1...) custom-call(f32[4,256,2048]{2,1,0:T(8,128)} %get-tuple-element.108.mixed_ref, f32[2,4,256,2048]{3,2,1,0:T(8,128)} %bitcast.211, ...), custom_call_target="tpu_custom_call" | custom-call | flops 20000000000 | bytes 55197696 | tf_op jit(solution)/shard_map/gate/pallas_call | solution.py:1012
  245.7 3.7 fusion.86
  249.4 2.5 fusion.93
  251.8 3.3 fusion.45
  255.2 3.4 fusion.52
  258.6 2.4 fusion.100
  261.0 2.5 fusion.107
  263.5 3.4 fusion.59
  266.9 3.4 fusion.66
  270.3 94.3 %exchange_back.1 = f32[4,4,8,64,128]{4,3,2,1,0:T(8,128)S(1)} custom-call(f32[4,4,8,64,128]{4,3,2,1,0:T(8,128)S(1)} %bitcast.160, f32[4,4,8,128]{3,2,1,0:T(8,128)S(1)} %broadcast_bitcast_fusion.log_ref), custom_call_target="tpu_custom_call" | custom-call | flops 99999997952 | tf_op jit(solution)/shard_map/exchange_back/pallas_call | solution.py:238
  364.7 2.0 copy-done
  369.3 6.7 bitcast_convert_fusion.1
  377.8 23.8 %collective-permute-done.10 = f32[1024,384]{1,0:T(8,128)} collective-permute-done((f32[1024,384]{1,0:T(8,128)}, f32[1024,384]{1,0:T(8,128)}, u32[]{:S(2)}, u32[]{:S(2)}) %collective-permute-start.10) | collective-permute-done | bytes 1572896 | tf_op jit(solution)/shard_map/ppermute | solution.py:276
  402.0 33.3 %collective-permute-done.5 = f32[1024,384]{1,0:T(8,128)} collective-permute-done((f32[1024,384]{1,0:T(8,128)}, f32[1024,384]{1,0:T(8,128)}, u32[]{:S(2)}, u32[]{:S(2)}) %collective-permute-start.5) | collective-permute-done | bytes 1572896 | tf_op jit(solution)/shard_map/ppermute | solution.py:276
  436.6 117.0 %back.1 = (bf16[2,4,256,2048]{3,2,1,0:T(8,128)(2,1)}, f32[4,8,2048]{2,1,0:T(8,128)}, f32[4,8,2048]{2,1,0:T(8,128)}, f32[4,8,2048]{2,1,0:T(8,128)}, f32[4,32,256]...) custom-call(s32[1]{0:T(128)} %bitcast.1.base_ref, ...), custom_call_target="tpu_custom_call", output_to_operand_aliasing={{0}: (17, {})} | custom-call | flops 80000000000 | bytes 44417076 | tf_op jit(solution)/shard_map/back/pallas_call | solution.py:1012
  559.1 10.0 fusion.12
  569.2 22.8 %collective-permute-done.9 = f32[1024,384]{1,0:T(8,128)S(1)} collective-permute-done((f32[1024,384]{1,0:T(8,128)}, f32[1024,384]{1,0:T(8,128)S(1)}, u32[]{:S(2)}, u32[]{:S(2)}) %collective-permute-start.9) | collective-permute-done | bytes 1572896 | tf_op jit(solution)/shard_map/ppermute | solution.py:276
  593.1 3.3 collective-permute-start.11
  596.5 1.6 slice_reduce_fusion
  603.6 4.9 fusion.88.refs_7_
  608.5 3.8 fusion.95.refs_6_
  612.4 2.8 multiply_reduce_fusion.6
  618.7 4.0 collective-permute-done.12
  622.8 2.1 dynamic_update_slice.3
  624.9 2.6 slice.343
  627.7 2.4 fusion.80
  630.2 2.5 fusion.82
  632.6 3.4 fusion.32
  636.1 3.4 fusion.34
  641.5 1.5 multiply_convert_fusion.4
  643.0 8.8 fusion.18
  651.8 26.1 %bitcast_add_fusion = f32[1024,2048]{1,0:T(8,128)} fusion(f32[1024,2048]{1,0:T(8,128)} %fusion.18, bf16[2,1024,2048]{2,1,0:T(8,128)(2,1)S(1)} %bitcast.164, bf16[2048,2,2048]{2,1,0:T(2,128)(2,1)} %param.22), kind=kOutput, calls=%fused_computation.6 | convolution fusion | flops 17181966336 | bytes 41943040 | tf_op jit(solution)/shard_map/ktc,dkc->td/dot_general | solution.py:1310
  679.4 3.8 fusion.102.refs_3_
  683.3 4.0 fusion.109.refs_2_
  687.3 5.2 fusion.47.refs_5_
  692.5 5.3 fusion.54.refs_4_
  697.8 5.3 fusion.61.refs_1_
  703.1 5.2 fusion.68.refs_0_
  716.4 3.1 slice_bitcast_fusion
  720.7 2.5 collective-permute-start.14
  723.2 9.2 add_convert_fusion
  732.4 18.3 %collective-permute-done.17 = f32[1024,384]{1,0:T(8,128)S(1)} collective-permute-done((f32[1024,384]{1,0:T(8,128)}, f32[1024,384]{1,0:T(8,128)S(1)}, u32[]{:S(2)}, u32[]{:S(2)}) %collective-permute-start.17) | collective-permute-done | bytes 1572896 | tf_op jit(solution)/shard_map/ppermute | solution.py:276
  750.8 2.5 convolution_add_fusion.2.refs_11_
  753.3 31.2 %collective-permute-done.16 = f32[1024,384]{1,0:T(8,128)S(1)} collective-permute-done((f32[1024,384]{1,0:T(8,128)}, f32[1024,384]{1,0:T(8,128)S(1)}, u32[]{:S(2)}, u32[]{:S(2)}) %collective-permute-start.16) | collective-permute-done | bytes 1572896 | tf_op jit(solution)/shard_map/ppermute | solution.py:276
  784.5 2.5 convolution_add_fusion.3.refs_10_
  786.9 3.4 convolution_add_fusion.refs_9_
  790.4 3.4 convolution_add_fusion.1.refs_8_
  793.9 7.7 multiply_reduce_fusion
  802.4 222.9 %finish.1 = (f32[128,2048]{1,0:T(8,128)}, f32[128,2048]{1,0:T(8,128)}, f32[128,2048]{1,0:T(8,128)}, f32[16,160,128]{2,1,0:T(8,128)}, f32[128,128]{1,0:T(8,128)}) custom-call(f32[1024,640]{1,0:T(8,128)} %fusion.68.refs_0_, f32[1024,640]{1,0:T(8,128)} %fusion.61.refs_1_, f32[1024,384]{1,0:T(8,128)} %fusion.109.refs_2_, f32[1024,384]{1,0:T(8,128)} %fusion.102.refs_3_, ...), custom_call_target="tpu_custom_call" | custom-call | tf_op jit(solution)/shard_map/finish/pallas_call | solution.py:585
  1031.8 2.9 copy.125
  1037.3 13.1 %fusion.4 = f32[1024,2048]{1,0:T(8,128)} fusion(f32[1024]{0:T(1024)S(1)} %multiply_multiply_fusion.3, f32[2048]{0:T(1024)S(1)} %copy-done.39, f32[1024]{0:T(1024)S(1)} %copy-done.48, bf16[4,256,2048]{2,1,0:T(8,128)(2,1)} %param.34, bf16[4,256,2048]{2,1,0:T(8,128)(2,1)} %param.20, f32[1024,2048]{1,0:T(8,128)} %bitcast_add_fusion, ...), kind=kLoop, calls=%fused_computation.5 | loop fusion | flops 18874368 | bytes 33570816 | tf_op jit(solution)/shard_map/add | solution.py:1322
  (355 shorter events, 62.0 us)
Async XLA Ops:
  5.2 22.4 %copy-start.12 = (bf16[1024,2048]{1,0:T(8,128)(2,1)}, bf16[1024,2048]{1,0:T(8,128)(2,1)S(1)}, u32[]{:S(2)}) copy-start(bf16[1024,2048]{1,0:T(8,128)(2,1)S(1)} %multiply_convert_fusion.1.refs_1_) | copy-start | bytes 12582916
  5.2 22.5 %copy-start.85 = (bf16[2048,256]{1,0:T(8,128)(2,1)S(1)}, bf16[2048,256]{1,0:T(8,128)(2,1)}, u32[]{:S(2)}) copy-start(bf16[2048,256]{1,0:T(8,128)(2,1)} %param.23) | copy-start | bytes 3145732
  27.6 10.6 %copy-start.68 = (s32[2,3]{1,0:T(2,128)S(1)}, s32[2,3]{1,0:T(2,128)}, u32[]{:S(2)}) copy-start(s32[2,3]{1,0:T(2,128)} %param.35) | copy-start | bytes 76
  27.6 11.2 %copy-start.69 = (f32[4,256]{1,0:T(4,128)S(1)}, f32[4,256]{1,0:T(4,128)}, u32[]{:S(2)}) copy-start(f32[4,256]{1,0:T(4,128)} %param.29) | copy-start | bytes 12292
  27.7 11.2 %copy-start.86 = (f32[32]{0:T(128)S(1)}, f32[32]{0:T(128)}, u32[]{:S(2)}) copy-start(f32[32]{0:T(128)} %param.26) | copy-start | bytes 388
  27.7 11.2 %copy-start.30 = (bf16[2048,32]{0,1:T(8,128)(2,1)S(1)}, bf16[2048,32]{0,1:T(8,128)(2,1)}, u32[]{:S(2)}) copy-start(bf16[2048,32]{0,1:T(8,128)(2,1)} %param.24) | copy-start | bytes 393220
  27.7 11.2 %copy-start.77 = (f32[32]{0:T(128)S(1)}, f32[32]{0:T(128)}, u32[]{:S(2)}) copy-start(f32[32]{0:T(128)} %param.25) | copy-start | bytes 388
  33.3 28.9 %copy-start.21 = (f32[4,256,256]{2,1,0:T(8,128)}, f32[4,256,256]{2,1,0:T(8,128)S(1)}, u32[]{:S(2)}) copy-start(f32[4,256,256]{2,1,0:T(8,128)S(1)} %fusion.9) | copy-start | bytes 3145732
  33.4 28.8 %collective-permute-start = (f32[4,3,2304]{2,1,0:T(4,128)S(1)}, f32[4,3,2304]{2,1,0:T(4,128)S(1)}, u32[]{:S(2)}, u32[]{:S(2)}) collective-permute-start(f32[4,3,2304]{2,1,0:T(4,128)S(1)} %pad_maximum_fusion.9), channel_id=1, source_target_pairs={{0,2},{2,4},{4,6},{6,8},{8,10},{10,12},{12,14},{14,16},{16,18},{18... | collective-permute-start | bytes 331784 | tf_op jit(solution)/shard_map/ppermute | solution.py:18
  38.9 23.4 %copy-start.58 = (f32[1,256]{1,0:T(1,128)}, f32[1,256]{1,0:T(1,128)S(1)}, u32[]{:S(2)}) copy-start(f32[1,256]{1,0:T(1,128)S(1)} %get-tuple-element.288) | copy-start | bytes 3076
  38.9 23.4 %copy-start.60 = (f32[1,256]{1,0:T(1,128)}, f32[1,256]{1,0:T(1,128)S(1)}, u32[]{:S(2)}) copy-start(f32[1,256]{1,0:T(1,128)S(1)} %get-tuple-element.289) | copy-start | bytes 3076
  38.9 23.4 %copy-start.62 = (f32[1,256]{1,0:T(1,128)}, f32[1,256]{1,0:T(1,128)S(1)}, u32[]{:S(2)}) copy-start(f32[1,256]{1,0:T(1,128)S(1)} %get-tuple-element.290) | copy-start | bytes 3076
  38.9 23.4 %copy-start.64 = (f32[1,256]{1,0:T(1,128)}, f32[1,256]{1,0:T(1,128)S(1)}, u32[]{:S(2)}) copy-start(f32[1,256]{1,0:T(1,128)S(1)} %get-tuple-element.291) | copy-start | bytes 3076
  43.4 18.2 %copy-start.28 = (f32[4,32,256]{2,1,0:T(8,128)}, f32[4,32,256]{2,1,0:T(8,128)S(1)}, u32[]{:S(2)}) copy-start(f32[4,32,256]{2,1,0:T(8,128)S(1)} %fusion.115.run_ref) | copy-start | bytes 393220
  43.6 18.0 %copy-start.54 = (f32[4,32,1]{1,0,2:T(4,128)}, f32[4,32,1]{1,0,2:T(4,128)S(1)}, u32[]{:S(2)}) copy-start(f32[4,32,1]{1,0,2:T(4,128)S(1)} %copy.128) | copy-start | bytes 1540
  44.4 17.2 %copy-start.52 = (f32[4,256]{1,0:T(4,128)}, f32[4,256]{1,0:T(4,128)S(1)}, u32[]{:S(2)}) copy-start(f32[4,256]{1,0:T(4,128)S(1)} %get-tuple-element.283) | copy-start | bytes 12292
  44.4 17.9 %copy-start.41 = (f32[4,256]{1,0:T(4,128)}, f32[4,256]{1,0:T(4,128)S(1)}, u32[]{:S(2)}) copy-start(f32[4,256]{1,0:T(4,128)S(1)} %get-tuple-element.284) | copy-start | bytes 12292
  44.4 17.9 %copy-start.43 = (f32[4,256]{1,0:T(4,128)}, f32[4,256]{1,0:T(4,128)S(1)}, u32[]{:S(2)}) copy-start(f32[4,256]{1,0:T(4,128)S(1)} %get-tuple-element.285) | copy-start | bytes 12292
  44.4 17.9 %copy-start.45 = (f32[4,256]{1,0:T(4,128)}, f32[4,256]{1,0:T(4,128)S(1)}, u32[]{:S(2)}) copy-start(f32[4,256]{1,0:T(4,128)S(1)} %get-tuple-element.287) | copy-start | bytes 12292
  47.1 15.2 %copy-start.78 = (f32[256]{0:T(256)S(1)}, f32[256]{0:T(256)}, u32[]{:S(2)}) copy-start(f32[256]{0:T(256)} %param.30) | copy-start | bytes 3076
  62.2 24.5 %copy-start.35 = (f32[4,3,256]{2,1,0:T(4,128)}, f32[4,3,256]{2,1,0:T(4,128)S(1)}, u32[]{:S(2)}) copy-start(f32[4,3,256]{2,1,0:T(4,128)S(1)} %slice.319) | copy-start | bytes 36868
  191.1 26.2 %copy-start.4 = (bf16[1024,1024]{1,0:T(8,128)(2,1)}, bf16[1024,1024]{1,0:T(8,128)(2,1)S(1)}, u32[]{:S(2)}) copy-start(bf16[1024,1024]{1,0:T(8,128)(2,1)S(1)} %get-tuple-element.146) | copy-start | bytes 6291460
  217.3 3.7 collective-permute-start.1
  222.8 22.8 %copy-start.104 = (bf16[1024,1024]{1,0:T(8,128)(2,1)S(1)}, bf16[1024,1024]{1,0:T(8,128)(2,1)}, u32[]{:S(2)}) copy-start(bf16[1024,1024]{1,0:T(8,128)(2,1)} %get-tuple-element.121) | copy-start | bytes 6291460
  270.3 97.8 %copy-start.31 = (bf16[2048,32]{0,1:T(8,128)(2,1)S(1)}, bf16[2048,32]{0,1:T(8,128)(2,1)}, u32[]{:S(2)}) copy-start(bf16[2048,32]{0,1:T(8,128)(2,1)} %param.24) | copy-start | bytes 393220
  270.3 98.8 %copy-start.53 = (f32[4,256]{1,0:T(4,128)S(1)}, f32[4,256]{1,0:T(4,128)}, u32[]{:S(2)}) copy-start(f32[4,256]{1,0:T(4,128)} %copy-done.52) | copy-start | bytes 12292
  366.6 35.0 %collective-permute-start.10 = (f32[1024,384]{1,0:T(8,128)}, f32[1024,384]{1,0:T(8,128)}, u32[]{:S(2)}, u32[]{:S(2)}) collective-permute-start(f32[1024,384]{1,0:T(8,128)} %fusion.86), channel_id=1, source_target_pairs={{0,8},{2,10},{4,12},{6,14},{8,0},{10,2},{12,4},{14,6},{16,24},{18,... | collective-permute-start | bytes 4718600 | tf_op jit(solution)/shard_map/ppermute | solution.py:276
  367.9 67.4 %collective-permute-start.5 = (f32[1024,384]{1,0:T(8,128)}, f32[1024,384]{1,0:T(8,128)}, u32[]{:S(2)}, u32[]{:S(2)}) collective-permute-start(f32[1024,384]{1,0:T(8,128)} %fusion.107), channel_id=1, source_target_pairs={{0,8},{2,10},{4,12},{6,14},{8,0},{10,2},{12,4},{14,6},{16,24},{18,... | collective-permute-start | bytes 4718600 | tf_op jit(solution)/shard_map/ppermute | solution.py:276
  376.0 216.0 %collective-permute-start.3 = (f32[1024,640]{1,0:T(8,128)}, f32[1024,640]{1,0:T(8,128)}, u32[]{:S(2)}, u32[]{:S(2)}) collective-permute-start(f32[1024,640]{1,0:T(8,128)} %fusion.66), channel_id=1, source_target_pairs={{0,2},{2,0},{4,6},{6,4},{8,10},{10,8},{12,14},{14,12},{16,18},{18,... | collective-permute-start | bytes 7864328 | tf_op jit(solution)/shard_map/ppermute | solution.py:276
  376.3 215.7 %collective-permute-start.4 = (f32[1024,640]{1,0:T(8,128)}, f32[1024,640]{1,0:T(8,128)}, u32[]{:S(2)}, u32[]{:S(2)}) collective-permute-start(f32[1024,640]{1,0:T(8,128)} %fusion.59), channel_id=1, source_target_pairs={{0,4},{2,6},{4,0},{6,2},{8,12},{10,14},{12,8},{14,10},{16,20},{18,... | collective-permute-start | bytes 7864328 | tf_op jit(solution)/shard_map/ppermute | solution.py:276
  377.6 214.4 %collective-permute-start.7 = (f32[1024,640]{1,0:T(8,128)}, f32[1024,640]{1,0:T(8,128)}, u32[]{:S(2)}, u32[]{:S(2)}) collective-permute-start(f32[1024,640]{1,0:T(8,128)} %fusion.52), channel_id=1, source_target_pairs={{0,2},{2,0},{4,6},{6,4},{8,10},{10,8},{12,14},{14,12},{16,18},{18,... | collective-permute-start | bytes 7864328 | tf_op jit(solution)/shard_map/ppermute | solution.py:276
  401.6 190.4 %collective-permute-start.8 = (f32[1024,640]{1,0:T(8,128)}, f32[1024,640]{1,0:T(8,128)}, u32[]{:S(2)}, u32[]{:S(2)}) collective-permute-start(f32[1024,640]{1,0:T(8,128)} %fusion.45), channel_id=1, source_target_pairs={{0,4},{2,6},{4,0},{6,2},{8,12},{10,14},{12,8},{14,10},{16,20},{18,... | collective-permute-start | bytes 7864328 | tf_op jit(solution)/shard_map/ppermute | solution.py:276
  435.3 123.0 %collective-permute-start.6 = (f32[1024,384]{1,0:T(8,128)}, f32[1024,384]{1,0:T(8,128)}, u32[]{:S(2)}, u32[]{:S(2)}) collective-permute-start(f32[1024,384]{1,0:T(8,128)} %fusion.100), channel_id=1, source_target_pairs={{0,8},{2,10},{4,12},{6,14},{8,0},{10,2},{12,4},{14,6},{16,24},{18,... | collective-permute-start | bytes 4718600 | tf_op jit(solution)/shard_map/ppermute | solution.py:276
  436.6 117.9 %copy-start.55 = (f32[4,32,1]{1,0,2:T(4,128)S(1)}, f32[4,32,1]{1,0,2:T(4,128)}, u32[]{:S(2)}) copy-start(f32[4,32,1]{1,0,2:T(4,128)} %copy-done.54) | copy-start | bytes 1540
  436.6 120.9 %copy-start.29 = (f32[32,1024]{1,0:T(8,128)S(1)}, f32[32,1024]{1,0:T(8,128)}, u32[]{:S(2)}) copy-start(f32[32,1024]{1,0:T(8,128)} %get-tuple-element.294) | copy-start | bytes 393220
  436.6 120.9 %copy-start.67 = (f32[32]{0:T(128)S(1)}, f32[32]{0:T(128)}, u32[]{:S(2)}) copy-start(f32[32]{0:T(128)} %copy-done.66) | copy-start | bytes 388
  558.3 33.7 %collective-permute-start.9 = (f32[1024,384]{1,0:T(8,128)}, f32[1024,384]{1,0:T(8,128)S(1)}, u32[]{:S(2)}, u32[]{:S(2)}) collective-permute-start(f32[1024,384]{1,0:T(8,128)} %fusion.93), channel_id=1, source_target_pairs={{0,8},{2,10},{4,12},{6,14},{8,0},{10,2},{12,4},{14,6},{16,24},{18,... | collective-permute-start | bytes 4718600 | tf_op jit(solution)/shard_map/ppermute | solution.py:276
  559.1 32.9 %copy-start.33 = (f32[4,256,128]{2,1,0:T(8,128)S(1)}, f32[4,256,128]{2,1,0:T(8,128)}, u32[]{:S(2)}) copy-start(f32[4,256,128]{2,1,0:T(8,128)} %get-tuple-element.138) | copy-start | bytes 1572868
  559.1 32.9 %copy-start.32 = (f32[4,256,128]{2,1,0:T(8,128)S(1)}, f32[4,256,128]{2,1,0:T(8,128)}, u32[]{:S(2)}) copy-start(f32[4,256,128]{2,1,0:T(8,128)} %get-tuple-element.139) | copy-start | bytes 1572868
  569.2 32.9 %copy-start.87 = (f32[32]{0:T(128)S(1)}, f32[32]{0:T(128)}, u32[]{:S(2)}) copy-start(f32[32]{0:T(128)} %param.26) | copy-start | bytes 388
  593.1 19.2 %collective-permute-start.11 = (f32[4,256,256]{2,1,0:T(8,128)S(1)}, f32[4,256,256]{2,1,0:T(8,128)}, u32[]{:S(2)}, u32[]{:S(2)}) collective-permute-start(f32[4,256,256]{2,1,0:T(8,128)S(1)} %constant_dynamic-update-slice_fusion), channel_id=1, source_target_pairs={{0,1},{1,0},{2,3},{3,2},{4,5},{5,4},{6,7},{7,6},{8,9},{9,8},{10,11... | collective-permute-start | bytes 3145736 | tf_op jit(solution)/shard_map/ppermute | solution.py:276
  602.0 118.7 %collective-permute-start.2 = (f32[1024,1024]{1,0:T(8,128)}, f32[1024,1024]{1,0:T(8,128)}, u32[]{:S(2)}, u32[]{:S(2)}) collective-permute-start(f32[1024,1024]{1,0:T(8,128)} %fusion.12), channel_id=1, source_target_pairs={{0,1},{1,0},{2,3},{3,2},{4,5},{5,4},{6,7},{7,6},{8,9},{9,8},{10,11... | collective-permute-start | bytes 12582920 | tf_op jit(solution)/shard_map/ppermute | solution.py:276
  615.8 6.9 collective-permute-start.12
  641.5 10.3 slice-start
  643.0 8.8 slice-start.1
  651.8 27.6 %copy-start.89 = (bf16[4,256,2048]{2,1,0:T(8,128)(2,1)S(1)}, bf16[4,256,2048]{2,1,0:T(8,128)(2,1)}, u32[]{:S(2)}) copy-start(bf16[4,256,2048]{2,1,0:T(8,128)(2,1)} %get-tuple-element.110) | copy-start | bytes 12582916
  651.8 27.6 %copy-start.96 = (bf16[1024,1024]{1,0:T(8,128)(2,1)S(1)}, bf16[1024,1024]{1,0:T(8,128)(2,1)}, u32[]{:S(2)}) copy-start(bf16[1024,1024]{1,0:T(8,128)(2,1)} %get-tuple-element.150) | copy-start | bytes 6291460
  678.0 115.9 %collective-permute-start.13 = (f32[1024,2048]{1,0:T(8,128)}, f32[1024,2048]{1,0:T(8,128)}, u32[]{:S(2)}, u32[]{:S(2)}) collective-permute-start(f32[1024,2048]{1,0:T(8,128)} %bitcast_add_fusion), channel_id=1, source_target_pairs={{0,1},{1,0},{2,3},{3,2},{4,5},{5,4},{6,7},{7,6},{8,9},{9,8},{10,11... | collective-permute-start | bytes 25165832 | tf_op jit(solution)/shard_map/ppermute | solution.py:276
  714.5 8.8 copy-start.90
  714.5 36.3 %collective-permute-start.17 = (f32[1024,384]{1,0:T(8,128)}, f32[1024,384]{1,0:T(8,128)S(1)}, u32[]{:S(2)}, u32[]{:S(2)}) collective-permute-start(f32[1024,384]{1,0:T(8,128)} %fusion.80), channel_id=1, source_target_pairs={{0,8},{2,10},{4,12},{6,14},{8,0},{10,2},{12,4},{14,6},{16,24},{18,... | collective-permute-start | bytes 4718600 | tf_op jit(solution)/shard_map/ppermute | solution.py:276
  714.7 69.7 %collective-permute-start.16 = (f32[1024,384]{1,0:T(8,128)}, f32[1024,384]{1,0:T(8,128)S(1)}, u32[]{:S(2)}, u32[]{:S(2)}) collective-permute-start(f32[1024,384]{1,0:T(8,128)} %fusion.82), channel_id=1, source_target_pairs={{0,8},{2,10},{4,12},{6,14},{8,0},{10,2},{12,4},{14,6},{16,24},{18,... | collective-permute-start | bytes 4718600 | tf_op jit(solution)/shard_map/ppermute | solution.py:276
  716.0 70.9 %collective-permute-start.15 = (f32[1024,640]{1,0:T(8,128)}, f32[1024,640]{1,0:T(8,128)S(1)}, u32[]{:S(2)}, u32[]{:S(2)}) collective-permute-start(f32[1024,640]{1,0:T(8,128)} %fusion.32), channel_id=1, source_target_pairs={{0,4},{2,6},{4,0},{6,2},{8,12},{10,14},{12,8},{14,10},{16,20},{18,... | collective-permute-start | bytes 7864328 | tf_op jit(solution)/shard_map/ppermute | solution.py:276
  720.7 30.0 %copy-start.95 = (bf16[1024,1024]{1,0:T(8,128)(2,1)S(1)}, bf16[1024,1024]{1,0:T(8,128)(2,1)}, u32[]{:S(2)}) copy-start(bf16[1024,1024]{1,0:T(8,128)(2,1)} %get-tuple-element.158) | copy-start | bytes 6291460
  720.7 69.6 %collective-permute-start.14 = (f32[1024,640]{1,0:T(8,128)S(1)}, f32[1024,640]{1,0:T(8,128)S(1)}, u32[]{:S(2)}, u32[]{:S(2)}) collective-permute-start(f32[1024,640]{1,0:T(8,128)S(1)} %copy-done.82), channel_id=1, source_target_pairs={{0,2},{2,0},{4,6},{6,4},{8,10},{10,8},{12,14},{14,12},{16,18},{18,... | collective-permute-start | bytes 7864328 | tf_op jit(solution)/shard_map/ppermute | solution.py:276
  732.4 52.0 %copy-start.94 = (bf16[1024,1024]{1,0:T(8,128)(2,1)S(1)}, bf16[1024,1024]{1,0:T(8,128)(2,1)}, u32[]{:S(2)}) copy-start(bf16[1024,1024]{1,0:T(8,128)(2,1)} %get-tuple-element.156) | copy-start | bytes 6291460
  753.3 33.7 %copy-start.108 = (bf16[1024,1024]{1,0:T(8,128)(2,1)S(1)}, bf16[1024,1024]{1,0:T(8,128)(2,1)}, u32[]{:S(2)}) copy-start(bf16[1024,1024]{1,0:T(8,128)(2,1)} %get-tuple-element.154) | copy-start | bytes 6291460
  793.8 7.7 copy-start.37
  793.8 7.8 copy-start.56
  793.8 7.8 copy-start.57
  793.8 7.8 copy-start.70
  793.8 7.8 copy-start.75
  793.8 7.8 copy-start.76
  793.8 7.8 copy-start.80
  1030.3 20.1 %collective-permute-start.18 = (f32[2048,128]{1,0:T(8,128)S(1)}, f32[2048,128]{1,0:T(8,128)}, u32[]{:S(2)}, u32[]{:S(2)}) collective-permute-start(f32[2048,128]{1,0:T(8,128)S(1)} %bitcast.170), channel_id=1, source_target_pairs={{0,1},{1,0},{2,3},{3,2},{4,5},{5,4},{6,7},{7,6},{8,9},{9,8},{10,11... | collective-permute-start | bytes 3145736 | tf_op jit(solution)/shard_map/ppermute | solution.py:276
  (68 other events, 248.2 us)

commit v3 on v2

--- a/solution.py
+++ b/solution.py
@@ -56,10 +56,14 @@
 GROUP = 4
 
 
-def exchange_kernel(length, reverse, orders, part_ref, log_ref, *refs):
+def exchange_kernel(length, reverse, orders, jobs, part_ref, log_ref, *refs):
     refs = list(refs)
     sources = [refs.pop(0) for _ in range(2 if orders else 0)]
+    job_refs = [[refs.pop(0) for _ in range(count)] for _, _, count in jobs]
     out_ref = refs.pop(0)
+    steps = []
+    for (make, parts, _), inputs in zip(jobs, job_refs):
+        steps += make(inputs, refs.pop(0), parts)
     targets = [refs.pop(0) for _ in range(4 * len(orders))]
     (
         parts,
@@ -101,7 +105,7 @@
     begins, ends = plane == 0, plane == planes - 1
     if reverse:
         begins, ends = ends, begins
-    step = -GROUP if reverse else GROUP
+    onward = -GROUP if reverse else GROUP
 
     barrier = pltpu.get_barrier_semaphore()
     for mate in mates:
@@ -152,7 +156,7 @@
         )
 
     def edge_copy(m):
-        return remote(edge_out.at[m], edge_in.at[m], edge_send.at[m], edge_recv.at[m], me + step)
+        return remote(edge_out.at[m], edge_in.at[m], edge_send.at[m], edge_recv.at[m], me + onward)
 
     def given_copy(m, slot):
         mate = mates[slot]
@@ -185,6 +189,8 @@
         log_copy(slot).wait()
     order = tuple(reversed(range(GROUP))) if reverse else tuple(range(GROUP))
     for m in range(micro):
+        for step in steps[m * len(steps) // micro : (m + 1) * len(steps) // micro]:
+            step()
         for slot in range(3):
             part_copy(m, slot).wait()
         factors = [jnp.exp(logs[t, m])[:, None, :] for t in order]
@@ -222,7 +228,7 @@
         copy.wait()
 
 
-def exchange(parts, logs, reverse, sources=(), orders=()):
+def exchange(parts, logs, reverse, sources=(), orders=(), jobs=()):
     micro, heads, rows, columns = parts.shape
     quarter = heads // GROUP
     length = lax.axis_size("seq")
@@ -235,10 +241,15 @@
         arranged += [half] * (2 * len(orders))
     vmem = pl.BlockSpec(memory_space=pltpu.VMEM)
     hbm = pl.BlockSpec(memory_space=pl.ANY)
+    made = [jax.ShapeDtypeStruct(job[3], jnp.float32) for job in jobs]
+    count = len(arranged)
+    arranged = made + arranged
+    job_inputs = [item for job in jobs for item in job[2]]
+    plans = tuple((job[0], job[1], len(job[2])) for job in jobs)
     out, *arranged = pl.pallas_call(
-        functools.partial(exchange_kernel, length, reverse, orders),
+        functools.partial(exchange_kernel, length, reverse, orders, plans),
         out_shape=[jax.ShapeDtypeStruct(shape, jnp.float32)] + arranged,
-        in_specs=[vmem] * 2 + [hbm] * len(sources),
+        in_specs=[vmem] * 2 + [hbm] * (len(sources) + len(job_inputs)),
         out_specs=[vmem] + [hbm] * len(arranged),
         scratch_shapes=[
             pltpu.VMEM(shape, jnp.float32),
@@ -255,20 +266,21 @@
             pltpu.SemaphoreType.DMA((micro, 3)),
             pltpu.SemaphoreType.DMA((micro, 3)),
             pltpu.SemaphoreType.DMA((2,)),
-            pltpu.SemaphoreType.DMA((max(len(arranged), 1) * max(length // 2, 1),)),
+            pltpu.SemaphoreType.DMA((max(count, 1) * max(length // 2, 1),)),
             pltpu.VMEM((2,) + sources[0].shape if sources else (2, 16, 128), jnp.bfloat16),
         ],
         compiler_params=pltpu.CompilerParams(
             collective_id=1 if reverse else 0,
             has_side_effects=True,
-            vmem_limit_bytes=40 * 1024 * 1024,
+            vmem_limit_bytes=FINISH_LIMIT,
         ),
         cost_estimate=pl.CostEstimate(
             flops=EXCHANGE_COST, bytes_accessed=0, transcendentals=0
         ),
         name="exchange_back" if reverse else "exchange",
-    )(parts.reshape(shape), spread, *sources)
-    return out.reshape(micro, heads, rows, columns), arranged
+    )(parts.reshape(shape), spread, *sources, *job_inputs)
+    out = out.reshape(micro, heads, rows, columns)
+    return out, arranged[: len(jobs)], arranged[len(jobs) :]
 
 
 def xor_permute(value, axis, bit):
@@ -356,6 +368,74 @@
     return lax.dot_general(left, right, (TN, ((), ())), preferred_element_type=jnp.float32)
 
 
+def product_steps(inputs, out_ref, parts):
+    lefts, right_ref, more = inputs[: len(parts)], inputs[len(parts)], inputs[len(parts) + 1 :]
+    steps, first = [], 0
+    for left_ref, (_, widths) in zip(lefts, parts):
+        steps.append(
+            functools.partial(product_step, left_ref, right_ref, more, out_ref, first, sum(widths))
+        )
+        first += sum(widths)
+    return steps
+
+
+def product_step(left_ref, right_ref, more, out_ref, first, width):
+    tokens, rows = left_ref.shape
+    tile = min(rows, 256)
+    columns = pl.ds(first, width)
+
+    def body(left, right, *rest):
+        value = product(left[...], right[...])
+        for item in rest[:-1]:
+            value = value + item[...]
+        rest[-1][...] = value
+
+    tiled = pl.BlockSpec((tile, width), lambda i: (i, 0))
+    pltpu.emit_pipeline(
+        body,
+        grid=(rows // tile,),
+        in_specs=[
+            pl.BlockSpec((tokens, tile), lambda i: (0, i)),
+            pl.BlockSpec((tokens, width), lambda i: (0, 0)),
+        ]
+        + [tiled] * len(more),
+        out_specs=[tiled],
+    )(
+        left_ref,
+        right_ref.at[:, columns],
+        *[item.at[:, columns] for item in more],
+        out_ref.at[:, columns],
+    )
+
+
+def plain_steps(inputs, out_ref, parts):
+    left_ref, right_ref = inputs
+    width = min(right_ref.shape[1], 512)
+    return [
+        functools.partial(plain_step, left_ref, right_ref, out_ref, first, width)
+        for first in range(0, right_ref.shape[1], width)
+    ]
+
+
+def plain_step(left_ref, right_ref, out_ref, first, width):
+    rows, depth = left_ref.shape
+    tile = min(rows, 256)
+    columns = pl.ds(first, width)
+
+    def body(left, right, out):
+        out[...] = low_dot(left[...], right[...], NN)
+
+    pltpu.emit_pipeline(
+        body,
+        grid=(rows // tile,),
+        in_specs=[
+            pl.BlockSpec((tile, depth), lambda i: (i, 0)),
+            pl.BlockSpec((depth, width), lambda i: (0, 0)),
+        ],
+        out_specs=[pl.BlockSpec((tile, width), lambda i: (i, 0))],
+    )(left_ref, right_ref.at[:, columns], out_ref.at[:, columns])
+
+
 def split_columns(array, parts):
     pieces, first = [], 0
     for _, widths in parts:
@@ -381,13 +461,15 @@
     ]
 
 
-def finish_kernel(parts, mats, bits, blocks, *refs):
+def finish_kernel(parts, kinds, bits, blocks, *refs):
     refs = list(refs)
     take = lambda count: [refs.pop(0) for _ in range(count)]
-    ins = [take(len(parts)) for _ in range(mats)]
+    mats = len(kinds)
+    ins = [take(len(parts) + (2 if made else 0)) for made in kinds]
     narrow_ref, vector_ref = take(2)
     outs = take(mats)
     gathered_ref, vector_out_ref = take(2)
+    made_refs = [take(1)[0] if made else None for made in kinds]
     me = lax.axis_index("seq")
 
     def partner(bit):
@@ -404,8 +486,11 @@
                     within = sum(widths[:piece])
                     keep = refs.pop(0)
                     recvs = take(bits - 1)
+                    source, start = ins[mat][k], within
+                    if kinds[mat]:
+                        source, start = made_refs[mat], first + within
                     wave.append(
-                        (chain_count, ins[mat][k], within, outs[mat], first + within, order[1:], keep, recvs)
+                        (chain_count, source, start, outs[mat], first + within, order[1:], keep, recvs)
                     )
                     chain_count += 1
                 first += sum(widths)
@@ -523,9 +608,20 @@
     vector_copy(0).start()
     chain_copy(narrow, 0).start()
     local_copy(narrow).start()
-    for wave in waves[:2]:
-        begin(wave)
+    makes = [
+        product_steps(items, made_refs[mat], parts) if kinds[mat] else []
+        for mat, items in enumerate(ins)
+    ]
+    begun = min(2, len(waves))
+    for number in range(begun):
+        if number % piece_count == 0:
+            for step in makes[number // piece_count]:
+                step()
+        begin(waves[number])
     ticks = len(waves) + bits - 2
+    if len(waves) > begun:
+        for step in makes[begun // piece_count]:
+            step()
     for tick in range(max(ticks, 2 * bits)):
         if tick < bits:
             advance_vector(tick)
@@ -538,6 +634,10 @@
                     advance(chain, phase)
                 if phase == 0 and number + 2 < len(waves):
                     begin(waves[number + 2])
+                    ahead = number + 3
+                    if ahead < len(waves) and ahead % piece_count == 0:
+                        for step in makes[ahead // piece_count]:
+                            step()
     for wave in waves:
         for chain in wave:
             for phase in range(bits - 1):
@@ -552,7 +652,8 @@
 def finish(parts, mats, narrow, vector):
     bits = axis_bits("seq")
     size = 1 << bits
-    blocks = mats[0][0].shape[0] // (size // 2)
+    kinds = tuple(len(mat) > len(parts) for mat in mats)
+    blocks = mats[-1][-1].shape[0] // (size // 2)
     columns = sum(sum(widths) for _, widths in parts)
     scratch, copies, chains = [], 0, 0
     for _ in mats:
@@ -582,19 +683,23 @@
     )
     shapes.append(jax.ShapeDtypeStruct(vector.shape, jnp.float32))
     flat = [item for mat in mats for item in mat]
+    outputs = len(shapes)
+    made = sum(kinds)
+    shapes += [jax.ShapeDtypeStruct((blocks * size // 2, columns), jnp.float32)] * made
     results = pl.pallas_call(
-        functools.partial(finish_kernel, parts, len(mats), bits, blocks),
+        functools.partial(finish_kernel, parts, kinds, bits, blocks),
         out_shape=shapes,
         in_specs=[pl.BlockSpec(memory_space=pl.ANY)] * (len(flat) + 1)
         + [pl.BlockSpec(memory_space=pltpu.VMEM)],
-        out_specs=[pl.BlockSpec(memory_space=pltpu.VMEM)] * len(shapes),
+        out_specs=[pl.BlockSpec(memory_space=pltpu.VMEM)] * outputs
+        + [pl.BlockSpec(memory_space=pl.ANY)] * made,
         scratch_shapes=scratch,
         compiler_params=pltpu.CompilerParams(
             collective_id=2, has_side_effects=True, vmem_limit_bytes=FINISH_LIMIT
         ),
         name="finish",
     )(*flat, narrow, vector)
-    return results[:-2], results[-2], results[-1]
+    return results[: outputs - 2], results[outputs - 2], results[outputs - 1]
 
 
 def head_gather(block):
@@ -845,6 +950,8 @@
 
 def back_kernel(
     head_dim,
+    parts,
+    bits,
     base_ref,
     starts_ref,
     x_ref,
@@ -863,6 +970,8 @@
     bias_ref,
     skip_ref,
     both_in_ref,
+    out_sent_ref,
+    gate_sent_ref,
     both_ref,
     edge_ref,
     halo_out_ref,
@@ -872,9 +981,60 @@
     pair_ref,
     grad_b_ref,
     grad_c_ref,
+    out_arrived_ref,
+    gate_arrived_ref,
     ext,
     moved,
+    send_sem,
+    recv_sem,
 ):
+    me = lax.axis_index("seq")
+
+    def partner(bit):
+        return me + (1 << bit) * (1 - 2 * lax.rem(me // (1 << bit), 2))
+
+    def sends():
+        copies = []
+        for source, target in (
+            (out_sent_ref, out_arrived_ref),
+            (gate_sent_ref, gate_arrived_ref),
+        ):
+            first = 0
+            for order, widths in parts:
+                columns = pl.ds(first, sum(widths))
+                first += sum(widths)
+                copies.append(
+                    pltpu.make_async_remote_copy(
+                        src_ref=source.at[:, columns],
+                        dst_ref=target.at[:, columns],
+                        send_sem=send_sem.at[len(copies)],
+                        recv_sem=recv_sem.at[len(copies)],
+                        device_id={"seq": partner(order[0])},
+                        device_id_type=pl.DeviceIdType.MESH,
+                    )
+                )
+        return copies
+
+    at_first = (pl.program_id(0) == 0) & (pl.program_id(1) == 0)
+    at_last = (pl.program_id(0) == pl.num_programs(0) - 1) & (
+        pl.program_id(1) == pl.num_programs(1) - 1
+    )
+    used = sorted({order[0] for order, _ in parts})
+
+    @pl.when(at_first)
+    def _():
+        barrier = pltpu.get_barrier_semaphore()
+        for bit in used:
+            pl.semaphore_signal(
+                barrier,
+                inc=1,
+                device_id={"seq": partner(bit)},
+                device_id_type=pl.DeviceIdType.MESH,
+            )
+        pl.semaphore_wait(barrier, len(used))
+        for copy in sends():
+            copy.start()
+
     heads = step_ref.shape[1]
     count = x_ref.shape[1]
     spread = spread_matrix(heads, head_dim)
@@ -997,10 +1157,19 @@
     sums.append(jnp.zeros((8 - len(sums), pre.shape[1]), jnp.float32))
     rows_ref[0] = jnp.concatenate(sums, axis=0)
 
-
-def blocked(kernel, name, grid, ins, outs, scratch=(), micros=0, aliases=None):
+    @pl.when(at_last)
+    def _():
+        for copy in sends():
+            copy.wait()
+
+
+def blocked(kernel, name, grid, ins, outs, scratch=(), micros=0, aliases=None, remote=None):
     moved = sum(item[0].size * item[0].dtype.itemsize for item in ins if item[1] != "any")
-    moved += sum(math.prod(item[2]) * grid[0] * grid[1] * jnp.dtype(item[1]).itemsize for item in outs)
+    moved += sum(
+        math.prod(item[2]) * grid[0] * grid[1] * jnp.dtype(item[1]).itemsize
+        for item in outs
+        if item[2] != "any"
+    )
 
     def spec(item):
         if item[1] is None:
@@ -1013,12 +1182,15 @@
         kernel,
         grid=grid,
         in_specs=[spec(item) for item in ins],
-        out_specs=[pl.BlockSpec(item[2], item[3]) for item in outs],
+        out_specs=[spec(item[1:]) for item in outs],
         out_shape=[jax.ShapeDtypeStruct(item[0], item[1]) for item in outs],
         scratch_shapes=list(scratch),
         input_output_aliases=aliases or {},
         compiler_params=pltpu.CompilerParams(
-            dimension_semantics=("arbitrary",) * len(grid), vmem_limit_bytes=VMEM_LIMIT
+            dimension_semantics=("arbitrary",) * len(grid),
+            vmem_limit_bytes=VMEM_LIMIT,
+            collective_id=remote,
+            has_side_effects=remote is not None,
         ),
         cost_estimate=pl.CostEstimate(
             flops=micros * 1_000_000_000, bytes_accessed=moved, transcendentals=0
@@ -1163,19 +1335,20 @@
     parts = scatter_parts(inner, axis_bits("seq"))
     orders = tuple(order for order, _ in parts)
     tiled = (width >> axis_bits("seq")) % 128 == 0
-    incoming, arranged = exchange(
+    incoming, (grad_gate_n,), arranged = exchange(
         device_state.reshape(exchange_shape),
         exchange_log,
         False,
         (cot_flat, normed_low) if tiled else (),
         orders if tiled else (),
-    )
+        [(plain_steps, (), (cot_flat, out_weight), (total, inner))],
+    )
+    grad_gate_n = grad_gate_n.reshape(whole)
     if not tiled:
         arranged = arrange(cot_flat, orders) + arrange(normed_low, orders)
     cot_parts, normed_parts = arranged[: 2 * len(parts)], arranged[2 * len(parts) :]
     incoming = incoming.reshape(state_shape)
 
-    grad_gate_n = jnp.dot(cot_flat, out_weight, preferred_element_type=jnp.float32).reshape(whole)
     mixed, sums = blocked(
         functools.partial(mix_kernel, head_dim),
         "mix",
@@ -1231,15 +1404,31 @@
     grad_gate_pre = grad_gate_pre.reshape(total, inner)
     grad_gate_gain = jnp.sum(gate_rows[:, 0], axis=0)
 
-    out_sent = sent_products(cot_parts, normed_gate, parts)
-    gate_sent = sent_products(normed_parts, grad_gate_pre, parts)
-    outgoing, _ = exchange(device_grad.reshape(exchange_shape), exchange_log, True)
-    outgoing, out_sent, gate_sent = lax.optimization_barrier((outgoing, out_sent, gate_sent))
-    out_arrived = send_parts(out_sent, parts)
-    gate_arrived = send_parts(gate_sent, parts)
+    half_shape = (width // 2, inner)
+    outgoing, (out_sent, gate_sent), _ = exchange(
+        device_grad.reshape(exchange_shape),
+        exchange_log,
+        True,
+        jobs=[
+            (product_steps, parts, cot_parts[::2] + [normed_gate], half_shape),
+            (product_steps, parts, normed_parts[::2] + [grad_gate_pre], half_shape),
+        ],
+    )
     outgoing = outgoing.reshape(state_shape)
-    grad_gate_x, edge, halo_grad, conv_rows, direct, fading, pairs, grad_b, grad_c = blocked(
-        functools.partial(back_kernel, head_dim),
+    (
+        grad_gate_x,
+        edge,
+        halo_grad,
+        conv_rows,
+        direct,
+        fading,
+        pairs,
+        grad_b,
+        grad_c,
+        out_arrived,
+        gate_arrived,
+    ) = blocked(
+        functools.partial(back_kernel, head_dim, parts, axis_bits("seq")),
         "back",
         grid,
         [
@@ -1261,6 +1450,8 @@
             (conv_row, flat_block, in_flat),
             (skip_row, flat_block, in_flat),
             (grad_gate_x, "any"),
+            (out_sent, "any"),
+            (gate_sent, "any"),
         ],
         [
             ((2,) + whole, jnp.bfloat16, half_block, in_x),
@@ -1272,16 +1463,18 @@
             ((micro, heads, state_size), jnp.float32, (1, group, state_size), in_state),
             ((micro, length, state_size), jnp.float32, map_block, in_map),
             ((micro, length, state_size), jnp.float32, map_block, in_map),
+            (half_shape, jnp.float32, "any"),
+            (half_shape, jnp.float32, "any"),
         ],
         [
             pltpu.VMEM((length + 8, wide), jnp.float32),
             pltpu.VMEM((length + 16, wide), jnp.float32),
+            pltpu.SemaphoreType.DMA((2 * len(parts),)),
+            pltpu.SemaphoreType.DMA((2 * len(parts),)),
         ],
         80,
         {17: 0},
-    )
-    halo_grad, grad_b, grad_gate_x, out_arrived, gate_arrived = lax.optimization_barrier(
-        (halo_grad, grad_b, grad_gate_x, out_arrived, gate_arrived)
+        3,
     )
     grad_bc = all_sum(jnp.concatenate([grad_b, grad_c], axis=-1), "head")
     kept = jnp.sum(pairs, axis=-1) * jnp.exp(device_log) * device_live[:, None]
@@ -1358,11 +1551,11 @@
     row = jnp.pad(row, (0, -count % 1024)).reshape(-1, 128)
 
     mats = [
-        keep_parts(cot_parts, normed_gate, parts, out_arrived),
-        keep_parts(normed_parts, grad_gate_pre, parts, gate_arrived),
         keep_parts(normed_parts, grad_gate_x[1], parts, x_arrived),
+        cot_parts[1::2] + [normed_gate, out_arrived],
+        normed_parts[1::2] + [grad_gate_pre, gate_arrived],
     ]
-    (grad_out_weight, gate_block, x_block), gathered, row = finish(parts, mats, narrow, row)
+    (x_block, grad_out_weight, gate_block), gathered, row = finish(parts, mats, narrow, row)
     grad_in_weight = jnp.stack([gate_block, x_block], axis=1)
     grad_bc_weight = head_gather(gathered[:, :row_count, :share_bc].reshape(width, share_bc))
     grad_dt_weight = gathered[:, row_count:narrow_rows, :128].reshape(width, heads)

time: 1060 us -> 951 us (0.90)
  matrix products: 184 us -> 110 us
  waiting for transfers between devices: 135 us -> 66.7 us
  Pallas kernels: 605 us -> 646 us
    ppermute x17 -> x9, waiting for transfers between devices: 131 us -> 62.5 us  [xor_permute(): return lax.ppermute(value, axis, [(i, i ^ 1 << bit) for i in range(size)])]
    dot_general x26 -> x10, matrix products: 87.5 us -> 32.1 us  [product(): lax.dot_general(left, right, (TN, ((), ())), preferred_element_type=jnp.f...]
    pallas_call x4, Pallas kernels: 187 us -> 208 us  [blocked(): pl.pallas_call(kernel, grid=grid, in_specs=[spec(item) for item in ins],...]
    pallas_call x1, Pallas kernels: 223 us -> 239 us  [finish(): pl.pallas_call(functools.partial(finish_kernel, parts, kinds, bits, block...]
    dot_general x1 -> x0, matrix products: 14.5 us -> none  [body(): jnp.dot(cot_flat, out_weight, preferred_element_type=jnp.float32)]
  transfers between devices with their start and end apart: 19 -> 11, of which waited for: 7 -> 4; matrix products, arithmetic and copies ran while one was open for 19% -> 10% of each run, Pallas kernels for 11% -> 0%
where the time goes in v3:
time: 951 us; the launch traced here: 939 us
  Pallas kernels  646 us (68%)
  matrix products  110 us (12%)
  waiting for transfers between devices  66.7 us (7%)
  other arithmetic  53.1 us (6%)
  local copies, waits for them, and re-layouts  42.8 us (5%)
  starting transfers between devices  17.1 us (2%)
    pallas_call x1, Pallas kernels, finish(): pl.pallas_call(functools.partial(finish_kernel, parts, kinds, bits, block...  239 us
    pallas_call x4, Pallas kernels, blocked(): pl.pallas_call(kernel, grid=grid, in_specs=[spec(item) for item in ins],...  208 us
    pallas_call x2, Pallas kernels, exchange(): pl.pallas_call(functools.partial(exchange_kernel, length, reverse, orders...  199 us
    ppermute x9, waiting for transfers between devices, xor_permute(): return lax.ppermute(value, axis, [(i, i ^ 1 << bit) for i in range(size)])  62.5 us
    dot_general x10, matrix products, product(): lax.dot_general(left, right, (TN, ((), ())), preferred_element_type=jnp.f...  32.1 us
    dot_general x1, matrix products, body(): jnp.einsum('ktc,dkc->td', grad_gate_x, in_weight, preferred_element_type=...  25.2 us
    dot_general x1, matrix products, body(): jnp.einsum('td,dkc->ktc', normed_low, in_weight, preferred_element_type=j...  22.4 us
  transfers between devices with their start and end apart: 11, of which 4 were waited for; matrix products, arithmetic and copies ran while one was open for 10% of the time, Pallas kernels for 0%

profile of v3, /device:TPU:1, one launch (start us, length us, event | category | flops | bytes accessed | tf_op | source)
XLA Modules:
  0.0 939.0 jit_solution(14826014319638602647)
XLA Ops:
  0.7 3.2 multiply_reduce_fusion.2
  4.5 1.0 multiply_convert_fusion.1.refs_1_
  5.6 22.4 %fusion.2 = f32[1024,2,2048]{2,0,1:T(8,128)S(1)} fusion(bf16[2048,2,2048]{2,1,0:T(2,128)(2,1)} %param.22, bf16[1024,2048]{1,0:T(8,128)(2,1)S(1)} %multiply_convert_fusion.1.refs_1_), kind=kOutput, calls=%fused_computation.2 | convolution fusion | flops 17179869184 | bytes 37748736 | tf_op jit(solution)/shard_map/td,dkc->ktc/dot_general | solution.py:1245
  28.1 1.3 fusion.7
  29.4 4.4 copy-done.65
  33.9 4.0 collective-permute-start
  39.2 4.2 broadcast_multiply_fusion.1
  48.6 1.7 multiply_convert_fusion.3
  52.0 21.0 %front.1 = (bf16[4,256,2048]{2,1,0:T(8,128)(2,1)}, f32[4,2048,128]{2,1,0:T(8,128)}) custom-call(s32[1]{0:T(128)} %bitcast.1.base_ref, s32[4,3]{1,0:T(4,128)} %pad_add_fusion.2.starts_ref, f32[2,4,256,2048]{3,2,1,0:T(8,128)} %bitcast.196, f32[4,8,2048]{2,1,0:T(8,128)} %pad.38.halo_ref, f32[4,2048]{1,0:T(4,128)} %weight_ref.3, f32[1,2048]{1,0:T(1,128)} %bitcast.202, ...), custom_call_target="tpu_custom_call" | custom-call | flops 20000000000 | bytes 25862196 | tf_op jit(solution)/shard_map/front/pallas_call | solution.py:1181
  73.0 100.3 %exchange.1 = (f32[4,4,8,64,128]{4,3,2,1,0:T(8,128)}, f32[1024,2048]{1,0:T(8,128)}, bf16[1024,1024]{1,0:T(8,128)(2,1)}, bf16[1024,1024]{1,0:T(8,128)(2,1)}, bf16...) custom-call(f32[4,4,8,64,128]{4,3,2,1,0:T(8,128)} %bitcast.209, ...), custom_call_target="tpu_custom_call" | custom-call | flops 99999997952 | tf_op jit(solution)/shard_map/exchange/pallas_call | solution.py:249
  173.3 25.5 %mix.1 = (f32[4,256,2048]{2,1,0:T(8,128)}, f32[4,256,2]{2,1,0:T(8,128)}) custom-call(s32[1]{0:T(128)} %bitcast.1.base_ref, s32[4,3]{1,0:T(4,128)} %pad_add_fusion.2.starts_ref, bf16[4,256,2048]{2,1,0:T(8,128)(2,1)} %get-tuple-element.91.x_ref, bf16[4,256,128]{2,1,0:T(8,128)(2,1)} %get-tuple-element.243.b_ref, bf16[4,256,128]{2,1,0:T(8,128)(2,1)} %get-tuple-element.242.c_ref, ...), custom_call_target="tpu_custom_call" | custom-call | flops 24999999488 | bytes 42909748 | tf_op jit(solution)/shard_map/mix/pallas_call | solution.py:1181
  198.8 1.9 collective-permute-start.1
  201.4 1.0 copy.120
  202.5 1.9 add.178.sums_ref
  204.4 22.4 %gate.1 = (bf16[4,256,2048]{2,1,0:T(8,128)(2,1)}, bf16[4,256,2048]{2,1,0:T(8,128)(2,1)}, bf16[2,4,256,2048]{3,2,1,0:T(8,128)(2,1)}, bf16[4,256,2048]{2,1,0:T(8,1...) custom-call(f32[4,256,2048]{2,1,0:T(8,128)} %get-tuple-element.95.mixed_ref, f32[2,4,256,2048]{3,2,1,0:T(8,128)} %bitcast.198, ...), custom_call_target="tpu_custom_call" | custom-call | flops 20000000000 | bytes 55197696 | tf_op jit(solution)/shard_map/gate/pallas_call | solution.py:1181
  226.8 98.5 %exchange_back.1 = (f32[4,4,8,64,128]{4,3,2,1,0:T(8,128)}, f32[1024,2048]{1,0:T(8,128)}, f32[1024,2048]{1,0:T(8,128)}) custom-call(f32[4,4,8,64,128]{4,3,2,1,0:T(8,128)} %bitcast.210, f32[4,4,8,128]{3,2,1,0:T(8,128)} %broadcast_bitcast_fusion.log_ref, bf16[1024,1024]{1,0:T(8,128)(2,1)} %get-tuple-element.100.refs_0_, ...), custom_call_target="tpu_custom_call" | custom-call | flops 99999997952 | tf_op jit(solution)/shard_map/exchange_back/pallas_call | solution.py:249
  325.3 139.0 %back.1 = (bf16[2,4,256,2048]{3,2,1,0:T(8,128)(2,1)}, f32[4,8,2048]{2,1,0:T(8,128)}, f32[4,8,2048]{2,1,0:T(8,128)}, f32[4,8,2048]{2,1,0:T(8,128)}, f32[4,32,256]...) custom-call(s32[1]{0:T(128)} %bitcast.1.base_ref, ...), custom_call_target="tpu_custom_call", output_to_operand_aliasing={{0}: (17, {})} | custom-call | flops 80000000000 | bytes 44417076 | tf_op jit(solution)/shard_map/back/pallas_call | solution.py:1181
  464.3 1.2 constant_dynamic-update-slice_fusion.1
  465.6 1.1 constant_dynamic-update-slice_fusion
  466.7 2.2 collective-permute-start.3
  470.9 1.0 add_bitcast_fusion
  472.8 1.4 fusion.79
  476.0 2.8 multiply_reduce_fusion.6
  479.5 1.8 collective-permute-start.4
  481.8 1.1 slice.300
  482.8 4.2 collective-permute-done.4
  487.7 1.7 dynamic_update_slice.3
  489.4 2.6 slice.295
  492.2 2.4 fusion.50
  494.6 2.4 fusion.52
  497.1 3.4 fusion.30
  500.4 3.4 fusion.32
  504.6 1.4 scatter-add.4
  506.0 1.5 multiply_convert_fusion.4
  507.6 5.5 fusion.16
  513.1 25.2 %bitcast_add_fusion = f32[1024,2048]{1,0:T(8,128)} fusion(f32[1024,2048]{1,0:T(8,128)S(1)} %fusion.16, bf16[2,1024,2048]{2,1,0:T(8,128)(2,1)S(1)} %bitcast.144, bf16[2048,2,2048]{2,1,0:T(2,128)(2,1)} %param.22), kind=kOutput, calls=%fused_computation.6 | convolution fusion | flops 17181966336 | bytes 41943040 | tf_op jit(solution)/shard_map/ktc,dkc->td/dot_general | solution.py:1503
  539.1 6.7 bitcast_convert_fusion.1
  545.9 10.3 %fusion.10 = f32[1024,1024]{1,0:T(8,128)} fusion(bf16[1024,2048]{1,0:T(8,128)(2,1)} %bitcast.151, bf16[2048,2048]{1,0:T(8,128)(2,1)} %refs_3_.1, s32[]{:T(128)S(6)} %select_n.47), kind=kOutput, calls=%fused_computation.17 | convolution fusion | flops 4294967296 | bytes 12582916 | tf_op jit(solution)/shard_map/dot_general | solution.py:1587
  556.2 1.1 collective-permute-start.9
  557.3 1.0 slice_reduce_fusion
  559.3 2.0 collective-permute-start.6
  561.5 1.0 fusion.54
  562.5 29.3 %collective-permute-done.9 = f32[1024,384]{1,0:T(8,128)} collective-permute-done((f32[1024,384]{1,0:T(8,128)S(1)}, f32[1024,384]{1,0:T(8,128)}, u32[]{:S(2)}, u32[]{:S(2)}) %collective-permute-start.9) | collective-permute-done | bytes 1572896 | tf_op jit(solution)/shard_map/ppermute | solution.py:288
  591.8 1.1 collective-permute-start.7
  592.9 1.0 fusion.55
  594.0 1.0 copy.127
  595.1 1.1 slice.308
  596.5 2.4 pad_maximum_fusion.3
  598.8 2.8 slice_bitcast_fusion
  601.7 4.0 convolution_add_fusion.2.refs_3_
  605.7 19.8 %collective-permute-done.8 = f32[1024,384]{1,0:T(8,128)} collective-permute-done((f32[1024,384]{1,0:T(8,128)}, f32[1024,384]{1,0:T(8,128)}, u32[]{:S(2)}, u32[]{:S(2)}) %collective-permute-start.8) | collective-permute-done | bytes 1572896 | tf_op jit(solution)/shard_map/ppermute | solution.py:288
  625.5 4.0 convolution_add_fusion.3.refs_2_
  629.5 5.2 convolution_add_fusion.1.refs_0_
  634.8 13.4 %collective-permute-done.7 = f32[1024,640]{1,0:T(8,128)} collective-permute-done((f32[1024,640]{1,0:T(8,128)}, f32[1024,640]{1,0:T(8,128)}, u32[]{:S(2)}, u32[]{:S(2)}) %collective-permute-start.7) | collective-permute-done | bytes 2621472 | tf_op jit(solution)/shard_map/ppermute | solution.py:288
  648.2 5.2 convolution_add_fusion.refs_1_
  653.5 8.8 add_convert_fusion
  662.3 7.6 multiply_reduce_fusion
  670.7 239.4 %finish.1 = (f32[128,2048]{1,0:T(8,128)}, f32[128,2048]{1,0:T(8,128)}, f32[128,2048]{1,0:T(8,128)}, f32[16,160,128]{2,1,0:T(8,128)}, f32[128,128]{1,0:T(8,128)},...) custom-call(f32[1024,640]{1,0:T(8,128)} %convolution_add_fusion.1.refs_0_, f32[1024,640]{1,0:T(8,128)} %convolution_add_fusion.refs_1_, ...), custom_call_target="tpu_custom_call" | custom-call | tf_op jit(solution)/shard_map/finish/pallas_call | solution.py:689
  910.2 1.5 slice.265
  915.2 1.8 collective-permute-start.10
  917.2 2.9 copy.125
  920.4 1.0 copy.126
  922.7 13.1 %fusion.4 = f32[1024,2048]{1,0:T(8,128)} fusion(f32[1024]{0:T(1024)S(1)} %multiply_multiply_fusion.3, f32[2048]{0:T(1024)S(1)} %copy-done.28, f32[1024]{0:T(1024)S(1)} %copy-done.37, bf16[4,256,2048]{2,1,0:T(8,128)(2,1)} %param.34, bf16[4,256,2048]{2,1,0:T(8,128)(2,1)} %param.20, f32[1024,2048]{1,0:T(8,128)} %bitcast_add_fusion, ...), kind=kLoop, calls=%fused_computation.5 | loop fusion | flops 18874368 | bytes 33570816 | tf_op jit(solution)/shard_map/add | solution.py:1515
  936.0 1.5 pad_maximum_fusion.1
  (259 shorter events, 25.8 us)
Async XLA Ops:
  5.6 22.4 %copy-start.2 = (bf16[1024,2048]{1,0:T(8,128)(2,1)}, bf16[1024,2048]{1,0:T(8,128)(2,1)S(1)}, u32[]{:S(2)}) copy-start(bf16[1024,2048]{1,0:T(8,128)(2,1)S(1)} %multiply_convert_fusion.1.refs_1_) | copy-start | bytes 12582916
  5.6 22.4 %copy-start.69 = (bf16[2048,256]{1,0:T(8,128)(2,1)S(1)}, bf16[2048,256]{1,0:T(8,128)(2,1)}, u32[]{:S(2)}) copy-start(bf16[2048,256]{1,0:T(8,128)(2,1)} %param.23) | copy-start | bytes 3145732
  28.0 5.8 copy-start.65
  28.0 10.5 %copy-start.54 = (s32[2,3]{1,0:T(2,128)S(1)}, s32[2,3]{1,0:T(2,128)}, u32[]{:S(2)}) copy-start(s32[2,3]{1,0:T(2,128)} %param.35) | copy-start | bytes 76
  28.0 11.1 %copy-start.55 = (f32[4,256]{1,0:T(4,128)S(1)}, f32[4,256]{1,0:T(4,128)}, u32[]{:S(2)}) copy-start(f32[4,256]{1,0:T(4,128)} %param.29) | copy-start | bytes 12292
  28.1 11.1 %copy-start.70 = (f32[32]{0:T(128)S(1)}, f32[32]{0:T(128)}, u32[]{:S(2)}) copy-start(f32[32]{0:T(128)} %param.26) | copy-start | bytes 388
  28.1 11.1 %copy-start.20 = (bf16[2048,32]{0,1:T(8,128)(2,1)S(1)}, bf16[2048,32]{0,1:T(8,128)(2,1)}, u32[]{:S(2)}) copy-start(bf16[2048,32]{0,1:T(8,128)(2,1)} %param.24) | copy-start | bytes 393220
  28.1 11.1 %copy-start.63 = (f32[32]{0:T(128)S(1)}, f32[32]{0:T(128)}, u32[]{:S(2)}) copy-start(f32[32]{0:T(128)} %param.25) | copy-start | bytes 388
  33.8 14.7 %copy-start.6 = (f32[4,256,256]{2,1,0:T(8,128)}, f32[4,256,256]{2,1,0:T(8,128)S(1)}, u32[]{:S(2)}) copy-start(f32[4,256,256]{2,1,0:T(8,128)S(1)} %fusion.7) | copy-start | bytes 3145732
  33.9 14.7 %collective-permute-start = (f32[4,3,2304]{2,1,0:T(4,128)S(1)}, f32[4,3,2304]{2,1,0:T(4,128)S(1)}, u32[]{:S(2)}, u32[]{:S(2)}) collective-permute-start(f32[4,3,2304]{2,1,0:T(4,128)S(1)} %pad_maximum_fusion.9), channel_id=1, source_target_pairs={{0,2},{2,4},{4,6},{6,8},{8,10},{10,12},{12,14},{14,16},{16,18},{18... | collective-permute-start | bytes 331784 | tf_op jit(solution)/shard_map/ppermute | solution.py:18
  39.1 9.4 %copy-start.45 = (f32[1,256]{1,0:T(1,128)}, f32[1,256]{1,0:T(1,128)S(1)}, u32[]{:S(2)}) copy-start(f32[1,256]{1,0:T(1,128)S(1)} %get-tuple-element.260) | copy-start | bytes 3076
  39.1 9.4 %copy-start.47 = (f32[1,256]{1,0:T(1,128)}, f32[1,256]{1,0:T(1,128)S(1)}, u32[]{:S(2)}) copy-start(f32[1,256]{1,0:T(1,128)S(1)} %get-tuple-element.261) | copy-start | bytes 3076
  39.2 9.4 %copy-start.49 = (f32[1,256]{1,0:T(1,128)}, f32[1,256]{1,0:T(1,128)S(1)}, u32[]{:S(2)}) copy-start(f32[1,256]{1,0:T(1,128)S(1)} %get-tuple-element.262) | copy-start | bytes 3076
  39.2 9.4 %copy-start.51 = (f32[1,256]{1,0:T(1,128)}, f32[1,256]{1,0:T(1,128)S(1)}, u32[]{:S(2)}) copy-start(f32[1,256]{1,0:T(1,128)S(1)} %get-tuple-element.263) | copy-start | bytes 3076
  39.2 7.2 copy-start.67
  39.2 9.4 copy-start.64
  43.7 7.5 copy-start.18
  43.9 8.1 copy-start.43
  44.6 7.3 copy-start.30
  44.6 7.3 copy-start.32
  44.7 7.3 copy-start.34
  44.7 7.3 copy-start.41
  48.5 24.5 %copy-start.24 = (f32[4,3,256]{2,1,0:T(4,128)}, f32[4,3,256]{2,1,0:T(4,128)S(1)}, u32[]{:S(2)}) copy-start(f32[4,3,256]{2,1,0:T(4,128)S(1)} %slice.279) | copy-start | bytes 36868
  173.3 27.4 %copy-start.42 = (f32[4,256]{1,0:T(4,128)S(1)}, f32[4,256]{1,0:T(4,128)}, u32[]{:S(2)}) copy-start(f32[4,256]{1,0:T(4,128)} %copy-done.41) | copy-start | bytes 12292
  173.3 28.1 %copy-start.21 = (bf16[2048,32]{0,1:T(8,128)(2,1)S(1)}, bf16[2048,32]{0,1:T(8,128)(2,1)}, u32[]{:S(2)}) copy-start(bf16[2048,32]{0,1:T(8,128)(2,1)} %param.24) | copy-start | bytes 393220
  198.8 3.7 collective-permute-start.1
  325.3 145.5 %copy-start.44 = (f32[4,32,1]{1,0,2:T(4,128)S(1)}, f32[4,32,1]{1,0,2:T(4,128)}, u32[]{:S(2)}) copy-start(f32[4,32,1]{1,0,2:T(4,128)} %copy-done.43) | copy-start | bytes 1540
  325.3 145.5 %copy-start.62 = (f32[4]{0:T(128)S(1)}, f32[4]{0:T(128)}, u32[]{:S(2)}) copy-start(f32[4]{0:T(128)} %slice_reduce_fusion.4) | copy-start | bytes 52
  464.3 8.5 copy-start.19
  464.3 11.6 %copy-start.7 = (f32[4,256,256]{2,1,0:T(8,128)S(1)}, f32[4,256,256]{2,1,0:T(8,128)}, u32[]{:S(2)}) copy-start(f32[4,256,256]{2,1,0:T(8,128)} %copy-done.6) | copy-start | bytes 3145732
  464.3 11.6 %copy-start.9 = (f32[4,256,256]{2,1,0:T(8,128)S(1)}, f32[4,256,256]{2,1,0:T(8,128)}, u32[]{:S(2)}) copy-start(f32[4,256,256]{2,1,0:T(8,128)} %get-tuple-element.233) | copy-start | bytes 3145732
  464.3 11.6 %copy-start.25 = (f32[4,3,256]{2,1,0:T(4,128)S(1)}, f32[4,3,256]{2,1,0:T(4,128)}, u32[]{:S(2)}) copy-start(f32[4,3,256]{2,1,0:T(4,128)} %copy-done.24) | copy-start | bytes 36868
  466.7 9.3 collective-permute-start.3
  479.5 8.1 copy-start.29
  479.5 7.5 collective-permute-start.4
  506.0 7.1 slice-start.2
  538.3 124.0 %collective-permute-start.5 = (f32[1024,2048]{1,0:T(8,128)}, f32[1024,2048]{1,0:T(8,128)}, u32[]{:S(2)}, u32[]{:S(2)}) collective-permute-start(f32[1024,2048]{1,0:T(8,128)} %bitcast_add_fusion), channel_id=1, source_target_pairs={{0,1},{1,0},{2,3},{3,2},{4,5},{5,4},{6,7},{7,6},{8,9},{9,8},{10,11... | collective-permute-start | bytes 25165832 | tf_op jit(solution)/shard_map/ppermute | solution.py:288
  539.1 6.7 copy-start.22
  545.9 10.4 %copy-start.68 = (f32[1024,384]{1,0:T(8,128)S(1)}, f32[1024,384]{1,0:T(8,128)}, u32[]{:S(2)}) copy-start(f32[1024,384]{1,0:T(8,128)} %fusion.50) | copy-start | bytes 4718596
  545.9 12.9 %copy-start.66 = (f32[32]{0:T(128)S(1)}, f32[32]{0:T(128)}, u32[]{:S(2)}) copy-start(f32[32]{0:T(128)} %get-tuple-element.244) | copy-start | bytes 388
  545.9 12.9 %copy-start.71 = (f32[32]{0:T(128)S(1)}, f32[32]{0:T(128)}, u32[]{:S(2)}) copy-start(f32[32]{0:T(128)} %param.26) | copy-start | bytes 388
  545.9 12.9 %copy-start.57 = (f32[256]{0:T(256)S(1)}, f32[256]{0:T(256)}, u32[]{:S(2)}) copy-start(f32[256]{0:T(256)} %get-tuple-element.220) | copy-start | bytes 3076
  545.9 12.9 %copy-start.58 = (f32[256]{0:T(256)S(1)}, f32[256]{0:T(256)}, u32[]{:S(2)}) copy-start(f32[256]{0:T(256)} %get-tuple-element.221) | copy-start | bytes 3076
  545.9 12.9 %copy-start.59 = (f32[256]{0:T(256)S(1)}, f32[256]{0:T(256)}, u32[]{:S(2)}) copy-start(f32[256]{0:T(256)} %get-tuple-element.222) | copy-start | bytes 3076
  545.9 12.9 %copy-start.60 = (f32[256]{0:T(256)S(1)}, f32[256]{0:T(256)}, u32[]{:S(2)}) copy-start(f32[256]{0:T(256)} %get-tuple-element.223) | copy-start | bytes 3076
  545.9 15.4 %copy-start.5 = (f32[4,256,256]{2,1,0:T(8,128)S(1)}, f32[4,256,256]{2,1,0:T(8,128)}, u32[]{:S(2)}) copy-start(f32[4,256,256]{2,1,0:T(8,128)} %scatter-add.4) | copy-start | bytes 3145732
  556.2 97.2 %collective-permute-start.2 = (f32[1024,1024]{1,0:T(8,128)}, f32[1024,1024]{1,0:T(8,128)}, u32[]{:S(2)}, u32[]{:S(2)}) collective-permute-start(f32[1024,1024]{1,0:T(8,128)} %fusion.10), channel_id=1, source_target_pairs={{0,1},{1,0},{2,3},{3,2},{4,5},{5,4},{6,7},{7,6},{8,9},{9,8},{10,11... | collective-permute-start | bytes 12582920 | tf_op jit(solution)/shard_map/ppermute | solution.py:288
  556.2 35.6 %collective-permute-start.9 = (f32[1024,384]{1,0:T(8,128)S(1)}, f32[1024,384]{1,0:T(8,128)}, u32[]{:S(2)}, u32[]{:S(2)}) collective-permute-start(f32[1024,384]{1,0:T(8,128)S(1)} %copy-done.68), channel_id=1, source_target_pairs={{0,8},{2,10},{4,12},{6,14},{8,0},{10,2},{12,4},{14,6},{16,24},{18,... | collective-permute-start | bytes 4718600 | tf_op jit(solution)/shard_map/ppermute | solution.py:288
  558.9 66.6 %collective-permute-start.8 = (f32[1024,384]{1,0:T(8,128)}, f32[1024,384]{1,0:T(8,128)}, u32[]{:S(2)}, u32[]{:S(2)}) collective-permute-start(f32[1024,384]{1,0:T(8,128)} %fusion.52), channel_id=1, source_target_pairs={{0,8},{2,10},{4,12},{6,14},{8,0},{10,2},{12,4},{14,6},{16,24},{18,... | collective-permute-start | bytes 4718600 | tf_op jit(solution)/shard_map/ppermute | solution.py:288
  559.3 70.2 %collective-permute-start.6 = (f32[1024,640]{1,0:T(8,128)}, f32[1024,640]{1,0:T(8,128)}, u32[]{:S(2)}, u32[]{:S(2)}) collective-permute-start(f32[1024,640]{1,0:T(8,128)} %fusion.32), channel_id=1, source_target_pairs={{0,2},{2,0},{4,6},{6,4},{8,10},{10,8},{12,14},{14,12},{16,18},{18,... | collective-permute-start | bytes 7864328 | tf_op jit(solution)/shard_map/ppermute | solution.py:288
  561.5 31.4 %copy-start.10 = (bf16[1024,1024]{1,0:T(8,128)(2,1)S(1)}, bf16[1024,1024]{1,0:T(8,128)(2,1)}, u32[]{:S(2)}) copy-start(bf16[1024,1024]{1,0:T(8,128)(2,1)} %get-tuple-element.122.refs_10_) | copy-start | bytes 6291460
  591.8 56.4 %collective-permute-start.7 = (f32[1024,640]{1,0:T(8,128)}, f32[1024,640]{1,0:T(8,128)}, u32[]{:S(2)}, u32[]{:S(2)}) collective-permute-start(f32[1024,640]{1,0:T(8,128)} %fusion.30), channel_id=1, source_target_pairs={{0,4},{2,6},{4,0},{6,2},{8,12},{10,14},{12,8},{14,10},{16,20},{18,... | collective-permute-start | bytes 7864328 | tf_op jit(solution)/shard_map/ppermute | solution.py:288
  601.7 23.8 %copy-start.13 = (bf16[1024,1024]{1,0:T(8,128)(2,1)S(1)}, bf16[1024,1024]{1,0:T(8,128)(2,1)}, u32[]{:S(2)}) copy-start(bf16[1024,1024]{1,0:T(8,128)(2,1)} %get-tuple-element.126.refs_12_) | copy-start | bytes 6291460
  629.5 18.7 %copy-start.12 = (bf16[1024,1024]{1,0:T(8,128)(2,1)S(1)}, bf16[1024,1024]{1,0:T(8,128)(2,1)}, u32[]{:S(2)}) copy-start(bf16[1024,1024]{1,0:T(8,128)(2,1)} %get-tuple-element.124.refs_11_) | copy-start | bytes 6291460
  629.5 23.9 %slice-start = ((s8[8388608]{0:T(1024)(128)(4,1)}), s8[4194304]{0:T(1024)(128)(4,1)S(1)}, s32[]{:S(2)}) async-start(s8[8388608]{0:T(1024)(128)(4,1)} %bitcast.139), calls=%async_computation | async-start | bytes 8388608
  634.8 18.6 %slice-start.1 = ((s8[8388608]{0:T(1024)(128)(4,1)}), s8[4194304]{0:T(1024)(128)(4,1)S(1)}, s32[]{:S(2)}) async-start(s8[8388608]{0:T(1024)(128)(4,1)} %bitcast.139), calls=%async_computation.1 | async-start | bytes 8388608
  653.4 8.9 copy-start.28
  653.4 8.9 copy-start.37
  653.4 8.9 copy-start.1
  662.3 7.7 copy-start.56
  662.3 7.7 copy-start.61
  910.2 6.8 copy-start.16
  910.2 6.8 copy-start.17
  915.2 20.6 %collective-permute-start.10 = (f32[2048,128]{1,0:T(8,128)S(1)}, f32[2048,128]{1,0:T(8,128)S(1)}, u32[]{:S(2)}, u32[]{:S(2)}) collective-permute-start(f32[2048,128]{1,0:T(8,128)S(1)} %bitcast.156), channel_id=1, source_target_pairs={{0,1},{1,0},{2,3},{3,2},{4,5},{5,4},{6,7},{7,6},{8,9},{9,8},{10,11... | collective-permute-start | bytes 3145736 | tf_op jit(solution)/shard_map/ppermute | solution.py:288
  (28 other events, 85.0 us)

commit v4 on v3

--- a/solution.py
+++ b/solution.py
@@ -56,14 +56,16 @@
 GROUP = 4
 
 
-def exchange_kernel(length, reverse, orders, jobs, part_ref, log_ref, *refs):
+def exchange_kernel(length, reverse, orders, jobs, tail, part_ref, log_ref, *refs):
     refs = list(refs)
     sources = [refs.pop(0) for _ in range(2 if orders else 0)]
-    job_refs = [[refs.pop(0) for _ in range(count)] for _, _, count in jobs]
+    job_refs = [[refs.pop(0) for _ in range(job[2])] for job in jobs]
     out_ref = refs.pop(0)
-    steps = []
-    for (make, parts, _), inputs in zip(jobs, job_refs):
-        steps += make(inputs, refs.pop(0), parts)
+    steps, made = [], []
+    for (make, plan, _, results), inputs in zip(jobs, job_refs):
+        made.append(refs.pop(0))
+        steps += make(inputs, made[-1], plan)
+    tail_ref = refs.pop(0) if tail is not None else None
     targets = [refs.pop(0) for _ in range(4 * len(orders))]
     (
         parts,
@@ -81,6 +83,7 @@
         given_recv,
         stage_sem,
         place_sem,
+        tail_sem,
         staged,
     ) = refs
     me = lax.axis_index("seq")
@@ -216,6 +219,17 @@
         for slot in range(3):
             given_copy(m, slot).start()
         out_ref[m, rank] = given[m, rank]
+    if tail is not None:
+        columns = part_columns(jobs[0][1])[tail]
+        bit = jobs[0][1][tail][0][0]
+        tail_copy = remote(
+            made[0].at[:, columns],
+            tail_ref,
+            tail_sem.at[0],
+            tail_sem.at[1],
+            me + (1 << bit) * (1 - 2 * lax.rem(me // (1 << bit), 2)),
+        )
+        tail_copy.start()
     for m in range(micro):
         for slot in range(3):
             given_copy(m, slot).wait()
@@ -224,11 +238,13 @@
         def _():
             edge_copy(m).wait_send()
 
+    if tail is not None:
+        tail_copy.wait()
     for copy in placed:
         copy.wait()
 
 
-def exchange(parts, logs, reverse, sources=(), orders=(), jobs=()):
+def exchange(parts, logs, reverse, sources=(), orders=(), jobs=(), tail=None):
     micro, heads, rows, columns = parts.shape
     quarter = heads // GROUP
     length = lax.axis_size("seq")
@@ -242,12 +258,17 @@
     vmem = pl.BlockSpec(memory_space=pltpu.VMEM)
     hbm = pl.BlockSpec(memory_space=pl.ANY)
     made = [jax.ShapeDtypeStruct(job[3], jnp.float32) for job in jobs]
+    if tail is not None:
+        made.append(
+            jax.ShapeDtypeStruct((jobs[0][3][0], sum(jobs[0][1][tail][1])), jnp.float32)
+        )
+    results = len(made)
     count = len(arranged)
     arranged = made + arranged
     job_inputs = [item for job in jobs for item in job[2]]
-    plans = tuple((job[0], job[1], len(job[2])) for job in jobs)
+    plans = tuple((job[0], job[1], len(job[2]), 1) for job in jobs)
     out, *arranged = pl.pallas_call(
-        functools.partial(exchange_kernel, length, reverse, orders, plans),
+        functools.partial(exchange_kernel, length, reverse, orders, plans, tail),
         out_shape=[jax.ShapeDtypeStruct(shape, jnp.float32)] + arranged,
         in_specs=[vmem] * 2 + [hbm] * (len(sources) + len(job_inputs)),
         out_specs=[vmem] + [hbm] * len(arranged),
@@ -267,6 +288,7 @@
             pltpu.SemaphoreType.DMA((micro, 3)),
             pltpu.SemaphoreType.DMA((2,)),
             pltpu.SemaphoreType.DMA((max(count, 1) * max(length // 2, 1),)),
+            pltpu.SemaphoreType.DMA((2,)),
             pltpu.VMEM((2,) + sources[0].shape if sources else (2, 16, 128), jnp.bfloat16),
         ],
         compiler_params=pltpu.CompilerParams(
@@ -280,7 +302,7 @@
         name="exchange_back" if reverse else "exchange",
     )(parts.reshape(shape), spread, *sources, *job_inputs)
     out = out.reshape(micro, heads, rows, columns)
-    return out, arranged[: len(jobs)], arranged[len(jobs) :]
+    return out, arranged[:results], arranged[results:]
 
 
 def xor_permute(value, axis, bit):
@@ -368,15 +390,23 @@
     return lax.dot_general(left, right, (TN, ((), ())), preferred_element_type=jnp.float32)
 
 
+def part_columns(parts):
+    first, columns = 0, []
+    for _, widths in parts:
+        columns.append(pl.ds(first, sum(widths)))
+        first += sum(widths)
+    return columns
+
+
 def product_steps(inputs, out_ref, parts):
-    lefts, right_ref, more = inputs[: len(parts)], inputs[len(parts)], inputs[len(parts) + 1 :]
-    steps, first = [], 0
-    for left_ref, (_, widths) in zip(lefts, parts):
-        steps.append(
-            functools.partial(product_step, left_ref, right_ref, more, out_ref, first, sum(widths))
-        )
-        first += sum(widths)
-    return steps
+    count = len(parts)
+    lefts, right_ref, more = inputs[:count], inputs[count], inputs[count + 1 :]
+    return [
+        functools.partial(
+            product_step, lefts[k], right_ref, more[k : k + 1], out_ref, columns.start, columns.size
+        )
+        for k, columns in enumerate(part_columns(parts))
+    ]
 
 
 def product_step(left_ref, right_ref, more, out_ref, first, width):
@@ -403,7 +433,7 @@
     )(
         left_ref,
         right_ref.at[:, columns],
-        *[item.at[:, columns] for item in more],
+        *more,
         out_ref.at[:, columns],
     )
 
@@ -436,41 +466,130 @@
     )(left_ref, right_ref.at[:, columns], out_ref.at[:, columns])
 
 
-def split_columns(array, parts):
-    pieces, first = [], 0
-    for _, widths in parts:
-        pieces.append(array[:, first : first + sum(widths)])
-        first += sum(widths)
-    return pieces
-
-
-def sent_products(lefts, right, parts):
+def share_steps(inputs, out_refs, parts):
+    left_ref, right_ref = inputs
+    share = right_ref.shape[0] // 2
+    mine = lax.axis_index("head") * share
     return [
-        product(lefts[2 * k], piece) for k, piece in enumerate(split_columns(right, parts))
+        functools.partial(share_step, left_ref, right_ref, out_ref, first, share)
+        for out_ref, first in zip(out_refs, (share - mine, mine))
     ]
 
 
-def send_parts(products, parts):
-    return [xor_permute(item, "seq", order[0]) for item, (order, _) in zip(products, parts)]
-
-
-def keep_parts(lefts, right, parts, arrived):
-    return [
-        product(lefts[2 * k + 1], piece) + arrived[k]
-        for k, piece in enumerate(split_columns(right, parts))
-    ]
-
-
-def finish_kernel(parts, kinds, bits, blocks, *refs):
+def share_step(left_ref, right_ref, out_ref, first, share):
+    rows, depth = left_ref.shape
+    tile = min(rows, 256)
+    width = min(share, 512)
+    chosen = right_ref.at[pl.ds(pl.multiple_of(first, share), share)]
+
+    def body(left, right, out):
+        out[...] = low_dot(left[...], right[...], NT)
+
+    pltpu.emit_pipeline(
+        body,
+        grid=(share // width, rows // tile),
+        in_specs=[
+            pl.BlockSpec((tile, depth), lambda j, i: (i, 0)),
+            pl.BlockSpec((width, depth), lambda j, i: (j, 0)),
+        ],
+        out_specs=[pl.BlockSpec((tile, width), lambda j, i: (i, j))],
+    )(left_ref, chosen, out_ref)
+
+
+def row_step(grad_ref, weight_ref, narrow_left_ref, narrow_right_ref, out_ref, first, rows):
+    depth, halves, width = weight_ref.shape
+    tile = min(depth, 256)
+
+    def inner(held, sem):
+        copy = pltpu.make_async_copy(grad_ref.at[:, pl.ds(first, rows)], held, sem)
+        copy.start()
+        copy.wait()
+
+        def body(weight, narrow_left, narrow_right, out):
+            turned_weight = jnp.swapaxes(weight[...], 0, 1)
+            total = low_dot(narrow_left[...], narrow_right[...], NT)
+            for half in range(halves):
+                total = total + low_dot(held[half], turned_weight[half], NT)
+            out[...] = total
+
+        pltpu.emit_pipeline(
+            body,
+            grid=(depth // tile,),
+            in_specs=[
+                pl.BlockSpec((tile, halves, width), lambda j: (j, 0, 0)),
+                pl.BlockSpec((rows, narrow_left_ref.shape[1]), lambda j: (0, 0)),
+                pl.BlockSpec((tile, narrow_left_ref.shape[1]), lambda j: (j, 0)),
+            ],
+            out_specs=[pl.BlockSpec((rows, tile), lambda j: (0, j))],
+        )(
+            weight_ref,
+            narrow_left_ref.at[pl.ds(first, rows)],
+            narrow_right_ref,
+            out_ref.at[pl.ds(first, rows)],
+        )
+
+    pl.run_scoped(
+        inner,
+        pltpu.VMEM((halves, rows, width), jnp.bfloat16),
+        pltpu.SemaphoreType.DMA,
+    )
+
+
+def token_step(
+    gain_ref, gain_sum, tokens_ref, cot_ref, rows_refs, kept_ref, other_ref, grad_ref, block_ref
+):
+    count, width = tokens_ref.shape
+    share = width // 2
+    tile = min(count, 128)
+    mine = lax.axis_index("head") == 0
+    gain_sum[...] = jnp.zeros_like(gain_sum)
+
+    def body(tokens, cot, own, other, kept, arrived, grad, block):
+        values = tokens[...].astype(jnp.float32)
+        pulls = own[...] + other[...]
+        scale = lax.rsqrt(jnp.mean(values * values, axis=1, keepdims=True) + EPSILON)
+        gained = pulls * gain_ref[...]
+        cross = jnp.sum(gained * values, axis=1, keepdims=True)
+        grad[...] = (
+            cot[...].astype(jnp.float32)
+            + gained * scale
+            - values * (scale * scale * scale * cross * (1.0 / width))
+        )
+        parts = (pulls * values * scale).reshape(tile // 8, 8, width)
+        gain_sum[...] = gain_sum[...] + jnp.sum(parts, axis=0)
+        residual = jnp.where(mine, values[:, :share], values[:, share:])
+        block[...] = (residual + kept[...] + arrived[...]).astype(jnp.bfloat16)
+
+    full = pl.BlockSpec((tile, width), lambda i: (i, 0))
+    half = pl.BlockSpec((tile, share), lambda i: (i, 0))
+    pltpu.emit_pipeline(
+        body,
+        grid=(count // tile,),
+        in_specs=[full] * 4 + [half] * 2,
+        out_specs=[full, half],
+    )(tokens_ref, cot_ref, *rows_refs, kept_ref, other_ref, grad_ref, block_ref)
+
+
+def finish_kernel(parts, mats, paired, bits, blocks, *refs):
     refs = list(refs)
     take = lambda count: [refs.pop(0) for _ in range(count)]
-    mats = len(kinds)
-    ins = [take(len(parts) + (2 if made else 0)) for made in kinds]
-    narrow_ref, vector_ref = take(2)
+    ins = [take(2 * len(parts) + 1) for _ in range(mats - 1)]
+    last_sent, last_kept = take(len(parts)), take(len(parts))
+    grad_ref, narrow_ref, vector_ref = take(3)
+    if paired:
+        weight_ref, gain_ref, tokens_ref, cot_ref = take(4)
+        narrow_left_ref, narrow_right_ref, gated_ref, out_weight_ref = take(4)
     outs = take(mats)
     gathered_ref, vector_out_ref = take(2)
-    made_refs = [take(1)[0] if made else None for made in kinds]
+    if paired:
+        token_grad_ref, block_ref, row_ref, row_other_ref = take(4)
+        share_sent_ref, share_kept_ref, share_other_ref = take(3)
+    sent_ref, arrived_ref = take(2)
+    made_refs = take(mats)
     me = lax.axis_index("seq")
+    last_right = grad_ref.at[grad_ref.shape[0] - 1]
+    columns_of = part_columns(parts)
+    ins.append(last_kept + [last_right] + [arrived_ref.at[:, columns] for columns in columns_of])
 
     def partner(bit):
         return me + (1 << bit) * (1 - 2 * lax.rem(me // (1 << bit), 2))
@@ -481,23 +600,20 @@
     for mat in range(mats):
         for piece in range(piece_count):
             wave, first = [], 0
-            for k, (order, widths) in enumerate(parts):
+            for order, widths in parts:
                 if widths[piece]:
-                    within = sum(widths[:piece])
+                    place = first + sum(widths[:piece])
                     keep = refs.pop(0)
                     recvs = take(bits - 1)
-                    source, start = ins[mat][k], within
-                    if kinds[mat]:
-                        source, start = made_refs[mat], first + within
                     wave.append(
-                        (chain_count, source, start, outs[mat], first + within, order[1:], keep, recvs)
+                        (chain_count, made_refs[mat], place, outs[mat], place, order[1:], keep, recvs)
                     )
                     chain_count += 1
                 first += sum(widths)
             waves.append(wave)
     narrow_order = parts[0][0]
     narrow = (chain_count, narrow_ref, 0, None, 0, narrow_order, refs.pop(0), take(bits))
-    vector_sums, vector_recvs, local_sem, send_sem, recv_sem = refs
+    vector_sums, vector_recvs, gain_sum, local_sem, send_sem, recv_sem = refs
 
     barrier = pltpu.get_barrier_semaphore()
     for bit in range(bits):
@@ -507,20 +623,49 @@
             device_id={"seq": partner(bit)},
             device_id_type=pl.DeviceIdType.MESH,
         )
-    pl.semaphore_wait(barrier, bits)
+    if paired:
+        pl.semaphore_signal(
+            barrier,
+            inc=1,
+            device_id={"head": 1 - lax.axis_index("head")},
+            device_id_type=pl.DeviceIdType.MESH,
+        )
+    pl.semaphore_wait(barrier, bits + (1 if paired else 0))
 
     numbers = {}
 
-    def remote(key, src, dst, bit):
+    def remote_to(key, src, dst, target):
         number = numbers.setdefault(key, len(numbers))
         return pltpu.make_async_remote_copy(
             src_ref=src,
             dst_ref=dst,
             send_sem=send_sem.at[number],
             recv_sem=recv_sem.at[number],
-            device_id={"seq": partner(bit)},
+            device_id=target,
             device_id_type=pl.DeviceIdType.MESH,
         )
+
+    def remote(key, src, dst, bit):
+        return remote_to(key, src, dst, {"seq": partner(bit)})
+
+    def first_copy(k):
+        region = (slice(None), columns_of[k])
+        return remote(("first", k), sent_ref.at[region], arrived_ref.at[region], parts[k][0][0])
+
+    def share_copy():
+        return remote_to(
+            "share", share_sent_ref, share_other_ref, {"head": 1 - lax.axis_index("head")}
+        )
+
+    def shares(part):
+        share_steps(
+            (gated_ref, out_weight_ref), (share_sent_ref, share_kept_ref), ()
+        )[part]()
+        if part == 0:
+            share_copy().start()
+
+    def row_copy():
+        return remote_to("row", row_ref, row_other_ref, {"head": 1 - lax.axis_index("head")})
 
     def local_copy(chain):
         number, source, first, _, _, _, keep, _ = chain
@@ -538,8 +683,21 @@
             region = keep.at[pl.ds(rows, rows)]
         return remote((number, phase), region, recvs[phase], order[phase])
 
-    def begin(wave):
-        for chain in wave:
+    made = set()
+
+    def make(mat):
+        if mat in made:
+            return
+        made.add(mat)
+        if mat == mats - 1:
+            for k in range(len(parts)):
+                first_copy(k).wait_recv()
+        for step in product_steps(ins[mat], made_refs[mat], parts):
+            step()
+
+    def begin(number):
+        make(number // piece_count)
+        for chain in waves[number]:
             chain_copy(chain, 0).start()
             local_copy(chain).start()
 
@@ -565,6 +723,14 @@
     def vector_copy(phase):
         return remote(("vector", phase), vector_sums.at[phase], vector_recvs.at[phase], phase)
 
+    def begin_vector():
+        vector_sums[0] = vector_ref[...]
+        if paired:
+            total = jnp.sum(gain_sum[...], axis=0, keepdims=True)
+            for place in range(total.shape[1] // 128):
+                vector_sums[0, place : place + 1, :] = total[:, place * 128 : place * 128 + 128]
+        vector_copy(0).start()
+
     def advance_vector(phase):
         vector_copy(phase).wait_recv()
         total = vector_sums[phase] + vector_recvs[phase]
@@ -583,8 +749,6 @@
             copies.append(remote(("gather", phase, high), region, region, bit))
         return copies
 
-    narrow_steps = []
-
     def narrow_halving(phase):
         advance(narrow, phase)
         if phase + 1 == bits:
@@ -599,32 +763,55 @@
             for copy in gather_copies(phase + 1):
                 copy.start()
 
-    for phase in range(bits):
-        narrow_steps.append(functools.partial(narrow_halving, phase))
-    for phase in range(bits):
-        narrow_steps.append(functools.partial(narrow_gather, phase))
-
-    vector_sums[0] = vector_ref[...]
-    vector_copy(0).start()
+    def rows(part):
+        count = row_ref.shape[0] // 2
+        row_step(
+            grad_ref, weight_ref, narrow_left_ref, narrow_right_ref, row_ref, part * count, count
+        )
+        if part == 1:
+            row_copy().start()
+
+    def token_rows():
+        row_copy().wait()
+        share_copy().wait()
+        token_step(
+            gain_ref,
+            gain_sum,
+            tokens_ref,
+            cot_ref,
+            (row_ref, row_other_ref),
+            share_kept_ref,
+            share_other_ref,
+            token_grad_ref,
+            block_ref,
+        )
+
+    narrow_steps = [functools.partial(narrow_halving, phase) for phase in range(bits)]
+    narrow_steps += [functools.partial(narrow_gather, phase) for phase in range(bits)]
+    fills = {}
+    vector_tick = 0
+    if paired:
+        fills = {
+            0: [functools.partial(rows, 0)],
+            1: [functools.partial(rows, 1), functools.partial(shares, 0)],
+            2: [functools.partial(shares, 1)],
+            3: [token_rows],
+        }
+        vector_tick = 4
+
     chain_copy(narrow, 0).start()
     local_copy(narrow).start()
-    makes = [
-        product_steps(items, made_refs[mat], parts) if kinds[mat] else []
-        for mat, items in enumerate(ins)
-    ]
+    sent_steps = product_steps(last_sent + [last_right], sent_ref, parts)
+    for k, step in enumerate(sent_steps):
+        step()
+        first_copy(k).start()
     begun = min(2, len(waves))
     for number in range(begun):
-        if number % piece_count == 0:
-            for step in makes[number // piece_count]:
-                step()
-        begin(waves[number])
-    ticks = len(waves) + bits - 2
+        begin(number)
     if len(waves) > begun:
-        for step in makes[begun // piece_count]:
-            step()
-    for tick in range(max(ticks, 2 * bits)):
-        if tick < bits:
-            advance_vector(tick)
+        make(begun // piece_count)
+    ticks = max(len(waves) + bits - 2, 2 * bits, vector_tick + bits)
+    for tick in range(ticks):
         if tick < len(narrow_steps):
             narrow_steps[tick]()
         for phase in range(bits - 1):
@@ -633,11 +820,17 @@
                 for chain in waves[number]:
                     advance(chain, phase)
                 if phase == 0 and number + 2 < len(waves):
-                    begin(waves[number + 2])
-                    ahead = number + 3
-                    if ahead < len(waves) and ahead % piece_count == 0:
-                        for step in makes[ahead // piece_count]:
-                            step()
+                    begin(number + 2)
+        if tick + 3 < len(waves):
+            make((tick + 3) // piece_count)
+        for step in fills.get(tick, ()):
+            step()
+        if tick == vector_tick:
+            begin_vector()
+        if 0 <= tick - vector_tick < bits:
+            advance_vector(tick - vector_tick)
+    for k in range(len(parts)):
+        first_copy(k).wait_send()
     for wave in waves:
         for chain in wave:
             for phase in range(bits - 1):
@@ -649,57 +842,73 @@
             copy.wait_send()
 
 
-def finish(parts, mats, narrow, vector):
+def finish(parts, mats, last_sent, last_kept, grad, narrow, vector, row_inputs):
     bits = axis_bits("seq")
     size = 1 << bits
-    kinds = tuple(len(mat) > len(parts) for mat in mats)
-    blocks = mats[-1][-1].shape[0] // (size // 2)
+    count = len(mats) + 1
+    paired = bool(row_inputs)
+    rows = last_kept[0].shape[1]
+    blocks = rows // (size // 2)
     columns = sum(sum(widths) for _, widths in parts)
     scratch, copies, chains = [], 0, 0
-    for _ in mats:
+    for _ in range(count):
         for piece in range(len(parts[0][1])):
             for _, widths in parts:
                 if widths[piece]:
-                    rows = blocks * size // 4
-                    scratch.append(pltpu.VMEM((rows, widths[piece]), jnp.float32))
+                    scratch.append(pltpu.VMEM((rows // 2, widths[piece]), jnp.float32))
                     for phase in range(bits - 1):
-                        scratch.append(pltpu.VMEM((rows >> phase, widths[piece]), jnp.float32))
+                        scratch.append(
+                            pltpu.VMEM(((rows // 2) >> phase, widths[piece]), jnp.float32)
+                        )
                     copies += bits - 1
                     chains += 1
-    rows = narrow.shape[0] // 2
-    scratch.append(pltpu.VMEM((rows, narrow.shape[1]), jnp.float32))
+    narrow_rows = narrow.shape[0] // 2
+    scratch.append(pltpu.VMEM((narrow_rows, narrow.shape[1]), jnp.float32))
     for phase in range(bits):
-        scratch.append(pltpu.VMEM((rows >> phase, narrow.shape[1]), jnp.float32))
-    copies += 2 * bits + size - 1
+        scratch.append(pltpu.VMEM((narrow_rows >> phase, narrow.shape[1]), jnp.float32))
+    copies += 2 * bits + size - 1 + len(parts) + 2
     scratch += [pltpu.VMEM((bits,) + vector.shape, jnp.float32)] * 2
     scratch += [
+        pltpu.VMEM((8, row_inputs[1].shape[1] if paired else 128), jnp.float32),
         pltpu.SemaphoreType.DMA((chains + 1,)),
         pltpu.SemaphoreType.DMA((copies,)),
         pltpu.SemaphoreType.DMA((copies,)),
     ]
-    shapes = [jax.ShapeDtypeStruct((blocks, columns), jnp.float32) for _ in mats]
+    vmem, hbm = pl.BlockSpec(memory_space=pltpu.VMEM), pl.BlockSpec(memory_space=pl.ANY)
+    shapes = [jax.ShapeDtypeStruct((blocks, columns), jnp.float32) for _ in range(count)]
     shapes.append(
         jax.ShapeDtypeStruct((size, narrow.shape[0] // size, narrow.shape[1]), jnp.float32)
     )
     shapes.append(jax.ShapeDtypeStruct(vector.shape, jnp.float32))
-    flat = [item for mat in mats for item in mat]
-    outputs = len(shapes)
-    made = sum(kinds)
-    shapes += [jax.ShapeDtypeStruct((blocks * size // 2, columns), jnp.float32)] * made
+    specs = [vmem] * len(shapes)
+    if paired:
+        tokens = row_inputs[2]
+        token_shape = jax.ShapeDtypeStruct(tokens.shape, jnp.float32)
+        block_shape = jax.ShapeDtypeStruct((tokens.shape[0], tokens.shape[1] // 2), jnp.bfloat16)
+        share_shape = jax.ShapeDtypeStruct(block_shape.shape, jnp.float32)
+        shapes += [token_shape, block_shape, token_shape, token_shape] + [share_shape] * 3
+    half = jax.ShapeDtypeStruct((rows, columns), jnp.float32)
+    shapes += [half] * (2 + count)
+    specs += [hbm] * (len(shapes) - len(specs))
+    flat = [item for mat in mats for item in mat] + last_sent + last_kept + [grad, narrow]
+    row_specs = [hbm, vmem] + [hbm] * 6 if paired else []
     results = pl.pallas_call(
-        functools.partial(finish_kernel, parts, kinds, bits, blocks),
+        functools.partial(finish_kernel, parts, count, paired, bits, blocks),
         out_shape=shapes,
-        in_specs=[pl.BlockSpec(memory_space=pl.ANY)] * (len(flat) + 1)
-        + [pl.BlockSpec(memory_space=pltpu.VMEM)],
-        out_specs=[pl.BlockSpec(memory_space=pltpu.VMEM)] * outputs
-        + [pl.BlockSpec(memory_space=pl.ANY)] * made,
+        in_specs=[hbm] * len(flat) + [vmem] + row_specs,
+        out_specs=specs,
         scratch_shapes=scratch,
         compiler_params=pltpu.CompilerParams(
             collective_id=2, has_side_effects=True, vmem_limit_bytes=FINISH_LIMIT
         ),
         name="finish",
-    )(*flat, narrow, vector)
-    return results[: outputs - 2], results[outputs - 2], results[outputs - 1]
+    )(*flat, vector, *row_inputs)
+    return (
+        results[:count],
+        results[count],
+        results[count + 1],
+        *(results[count + 2 : count + 4] if paired else ()),
+    )
 
 
 def head_gather(block):
@@ -816,6 +1025,52 @@
             * masks[shift - 1]
         )
     return total
+
+
+def project_kernel(tokens_ref, gain_ref, weight_ref, normed_ref, out_ref):
+    count = tokens_ref.shape[0]
+    slab = min(count, 64)
+
+    @pl.when(pl.program_id(0) == 0)
+    def _():
+        @pl.loop(0, count // slab)
+        def _(step):
+            cut = pl.ds(pl.multiple_of(step * slab, slab), slab)
+            values = tokens_ref[cut, :].astype(jnp.float32)
+            scale = lax.rsqrt(jnp.mean(values * values, axis=1, keepdims=True) + EPSILON)
+            normed_ref[cut, :] = (values * scale * gain_ref[...]).astype(jnp.bfloat16)
+
+    weight = jnp.swapaxes(weight_ref[...], 0, 1)
+    for half in range(weight.shape[0]):
+        out_ref[half] = low_dot(normed_ref[...], weight[half], NN)
+
+
+def project(tokens, gain, weight):
+    count, width = tokens.shape
+    _, halves, columns = weight.shape
+    tile = min(columns, 256)
+    return pl.pallas_call(
+        project_kernel,
+        grid=(columns // tile,),
+        in_specs=[
+            pl.BlockSpec((count, width), lambda j: (0, 0)),
+            pl.BlockSpec((1, width), lambda j: (0, 0)),
+            pl.BlockSpec((width, halves, tile), lambda j: (0, 0, j)),
+        ],
+        out_specs=[
+            pl.BlockSpec((count, width), lambda j: (0, 0)),
+            pl.BlockSpec((halves, count, tile), lambda j: (0, 0, j)),
+        ],
+        out_shape=[
+            jax.ShapeDtypeStruct((count, width), jnp.bfloat16),
+            jax.ShapeDtypeStruct((halves, count, columns), jnp.float32),
+        ],
+        compiler_params=pltpu.CompilerParams(vmem_limit_bytes=VMEM_LIMIT),
+        cost_estimate=pl.CostEstimate(
+            flops=2 * count * width * columns * halves, bytes_accessed=0, transcendentals=0
+        ),
+        name="project",
+    )(tokens, gain[None], weight)
 
 
 def front_kernel(
@@ -951,7 +1206,7 @@
 def back_kernel(
     head_dim,
     parts,
-    bits,
+    skipped,
     base_ref,
     starts_ref,
     x_ref,
@@ -981,13 +1236,10 @@
     pair_ref,
     grad_b_ref,
     grad_c_ref,
-    out_arrived_ref,
-    gate_arrived_ref,
-    ext,
-    moved,
-    send_sem,
-    recv_sem,
+    *refs,
 ):
+    refs = list(refs)
+    ext, moved, send_sem, recv_sem = refs[-4:]
     me = lax.axis_index("seq")
 
     def partner(bit):
@@ -995,24 +1247,19 @@
 
     def sends():
         copies = []
-        for source, target in (
-            (out_sent_ref, out_arrived_ref),
-            (gate_sent_ref, gate_arrived_ref),
-        ):
-            first = 0
-            for order, widths in parts:
-                columns = pl.ds(first, sum(widths))
-                first += sum(widths)
-                copies.append(
-                    pltpu.make_async_remote_copy(
-                        src_ref=source.at[:, columns],
-                        dst_ref=target.at[:, columns],
-                        send_sem=send_sem.at[len(copies)],
-                        recv_sem=recv_sem.at[len(copies)],
-                        device_id={"seq": partner(order[0])},
-                        device_id_type=pl.DeviceIdType.MESH,
+        for mat, source in enumerate((out_sent_ref, gate_sent_ref)):
+            for k, columns in enumerate(part_columns(parts)):
+                if (mat, k) not in skipped:
+                    copies.append(
+                        pltpu.make_async_remote_copy(
+                            src_ref=source.at[:, columns],
+                            dst_ref=refs[len(copies)],
+                            send_sem=send_sem.at[len(copies)],
+                            recv_sem=recv_sem.at[len(copies)],
+                            device_id={"seq": partner(parts[k][0][0])},
+                            device_id_type=pl.DeviceIdType.MESH,
+                        )
                     )
-                )
         return copies
 
     at_first = (pl.program_id(0) == 0) & (pl.program_id(1) == 0)
@@ -1240,11 +1487,9 @@
 
     flat = tokens.reshape(total, width).astype(jnp.float32)
     cot_flat = cotangent.reshape(total, width)
-    normed, norm_back = jax.vjp(rms_scale, flat, norm_gain)
-    normed_low = normed.astype(jnp.bfloat16)
-    gate_x = jnp.einsum(
-        "td,dkc->ktc", normed_low, in_weight, preferred_element_type=jnp.float32
-    ).reshape(2, micro, length, inner)
+    _, norm_back = jax.vjp(rms_scale, flat, norm_gain)
+    normed_low, gate_x = project(tokens.reshape(total, width), norm_gain, in_weight)
+    gate_x = gate_x.reshape(2, micro, length, inner)
     bc_pre = jnp.dot(normed_low, bc_weight, preferred_element_type=jnp.float32).reshape(
         micro, length, 2 * state_size
     )
@@ -1405,7 +1650,11 @@
     grad_gate_gain = jnp.sum(gate_rows[:, 0], axis=0)
 
     half_shape = (width // 2, inner)
-    outgoing, (out_sent, gate_sent), _ = exchange(
+    paired = head_count == 2
+    share = width // head_count
+    far = [k for k, (order, _) in enumerate(parts) if order[0] == 2 and len(parts) > 1]
+    skipped = {(0, far[0])} if far else set()
+    outgoing, (out_sent, gate_sent, *early), _ = exchange(
         device_grad.reshape(exchange_shape),
         exchange_log,
         True,
@@ -1413,6 +1662,7 @@
             (product_steps, parts, cot_parts[::2] + [normed_gate], half_shape),
             (product_steps, parts, normed_parts[::2] + [grad_gate_pre], half_shape),
         ],
+        tail=far[0] if far else None,
     )
     outgoing = outgoing.reshape(state_shape)
     (
@@ -1425,10 +1675,9 @@
         pairs,
         grad_b,
         grad_c,
-        out_arrived,
-        gate_arrived,
+        *arrivals,
     ) = blocked(
-        functools.partial(back_kernel, head_dim, parts, axis_bits("seq")),
+        functools.partial(back_kernel, head_dim, parts, skipped),
         "back",
         grid,
         [
@@ -1463,8 +1712,12 @@
             ((micro, heads, state_size), jnp.float32, (1, group, state_size), in_state),
             ((micro, length, state_size), jnp.float32, map_block, in_map),
             ((micro, length, state_size), jnp.float32, map_block, in_map),
-            (half_shape, jnp.float32, "any"),
-            (half_shape, jnp.float32, "any"),
+        ]
+        + [
+            ((width // 2, sum(widths)), jnp.float32, "any")
+            for mat in range(2)
+            for k, (_, widths) in enumerate(parts)
+            if (mat, k) not in skipped
         ],
         [
             pltpu.VMEM((length + 8, wide), jnp.float32),
@@ -1476,6 +1729,10 @@
         {17: 0},
         3,
     )
+    arrived = [
+        [early[0] if (mat, k) in skipped else arrivals.pop(0) for k in range(len(parts))]
+        for mat in range(2)
+    ]
     grad_bc = all_sum(jnp.concatenate([grad_b, grad_c], axis=-1), "head")
     kept = jnp.sum(pairs, axis=-1) * jnp.exp(device_log) * device_live[:, None]
     grad_decay = by_head(fading + kept[:, :, None])
@@ -1496,23 +1753,37 @@
     grad_bc_pre = grad_bc_ext[:, taps - 1 :].at[:, length - taps + 1 :].add(right_bc)
     bc_flat = grad_bc_pre.reshape(total, 2 * state_size)
     grad_gate_x = grad_gate_x.reshape(2, total, inner)
-    x_sent = sent_products(normed_parts, grad_gate_x[1], parts)
-    grad_gate_x, x_sent = lax.optimization_barrier((grad_gate_x, x_sent))
-    x_arrived = send_parts(x_sent, parts)
-
-    row_part = jnp.einsum(
-        "ktc,dkc->td", grad_gate_x, in_weight, preferred_element_type=jnp.float32
-    )
     bc_high, bc_rest = halves_of(bc_flat * (1.0 / head_count))
     delta_high, delta_rest = halves_of(grad_delta_pre.T)
     narrow_left = jnp.concatenate([bc_high, bc_rest, delta_high, delta_rest], axis=1)
     narrow_right = jnp.concatenate([bc_weight, bc_weight, dt_weight, dt_weight], axis=1)
-    row_part = row_part + lax.dot_general(
-        narrow_left, narrow_right, (NT, ((), ())), preferred_element_type=jnp.float32
-    )
-    row_grads = all_sum(row_part, "head")
-    grad_flat, grad_norm_gain = norm_back(row_grads)
-    grad_tokens = (cot_flat.astype(jnp.float32) + grad_flat).reshape(micro, length, width)
+    if paired:
+        row_inputs = (
+            in_weight,
+            norm_gain[None],
+            tokens.reshape(total, width),
+            cot_flat,
+            narrow_left,
+            narrow_right,
+            normed_gate,
+            out_weight,
+        )
+        gain_grad = jnp.zeros_like(norm_gain)
+    else:
+        row_inputs = ()
+        row_part = lax.dot_general(
+            narrow_left, narrow_right, (NT, ((), ())), preferred_element_type=jnp.float32
+        ) + jnp.einsum(
+            "ktc,dkc->td", grad_gate_x, in_weight, preferred_element_type=jnp.float32
+        )
+        grad_flat, gain_grad = norm_back(all_sum(row_part, "head"))
+        grad_tokens = cot_flat.astype(jnp.float32) + grad_flat
+        head_terms = lax.dot_general(
+            normed_gate, out_weight, (NT, ((), ())), preferred_element_type=jnp.float32
+        )
+        summed = lax.psum_scatter(head_terms, "head", scatter_dimension=1, tiled=True)
+        residual = lax.dynamic_slice_in_dim(flat, lax.axis_index("head") * share, share, 1)
+        block_out = (residual + summed).astype(jnp.bfloat16)
 
     share_bc = 2 * state_size // head_count
     own_bc = lax.dynamic_slice_in_dim(bc_flat, lax.axis_index("head") * share_bc, share_bc, 1)
@@ -1536,9 +1807,9 @@
     narrow = narrow.reshape(-1, narrow.shape[2])
 
     small = [
+        gain_grad,
         grad_bc_conv_weight,
         grad_bc_conv_bias,
-        grad_norm_gain,
         grad_dt_bias,
         grad_a_log,
         grad_d_skip,
@@ -1550,12 +1821,23 @@
     count = row.size
     row = jnp.pad(row, (0, -count % 1024)).reshape(-1, 128)
 
-    mats = [
-        keep_parts(normed_parts, grad_gate_x[1], parts, x_arrived),
-        cot_parts[1::2] + [normed_gate, out_arrived],
-        normed_parts[1::2] + [grad_gate_pre, gate_arrived],
-    ]
-    (x_block, grad_out_weight, gate_block), gathered, row = finish(parts, mats, narrow, row)
+    (grad_out_weight, gate_block, x_block), gathered, row, *token_grads = finish(
+        parts,
+        [
+            cot_parts[1::2] + [normed_gate] + arrived[0],
+            normed_parts[1::2] + [grad_gate_pre] + arrived[1],
+        ],
+        normed_parts[::2],
+        normed_parts[1::2],
+        grad_gate_x,
+        narrow,
+        row,
+        row_inputs,
+    )
+    if paired:
+        grad_tokens, block_out = token_grads
+    grad_tokens = grad_tokens.reshape(micro, length, width)
+    block_out = block_out.reshape(micro, length, share)
     grad_in_weight = jnp.stack([gate_block, x_block], axis=1)
     grad_bc_weight = head_gather(gathered[:, :row_count, :share_bc].reshape(width, share_bc))
     grad_dt_weight = gathered[:, row_count:narrow_rows, :128].reshape(width, heads)
@@ -1565,9 +1847,9 @@
         sizes.append(row[first : first + item.size].reshape(item.shape))
         first += item.size
     (
+        grad_norm_gain,
         grad_bc_conv_weight,
         grad_bc_conv_bias,
-        grad_norm_gain,
         grad_dt_bias,
         grad_a_log,
         grad_d_skip,
@@ -1576,27 +1858,6 @@
         grad_gate_gain,
     ) = sizes
 
-    share = width // head_count
-    if head_count == 2:
-        first = lax.axis_index("head") * share
-        own_rows = lax.dynamic_slice_in_dim(out_weight, first, share, 0)
-        other_rows = lax.dynamic_slice_in_dim(out_weight, share - first, share, 0)
-        summed = lax.dot_general(
-            normed_gate, own_rows, (NT, ((), ())), preferred_element_type=jnp.float32
-        ) + xor_permute(
-            lax.dot_general(
-                normed_gate, other_rows, (NT, ((), ())), preferred_element_type=jnp.float32
-            ),
-            "head",
-            0,
-        )
-    else:
-        head_terms = lax.dot_general(
-            normed_gate, out_weight, (NT, ((), ())), preferred_element_type=jnp.float32
-        )
-        summed = lax.psum_scatter(head_terms, "head", scatter_dimension=1, tiled=True)
-    residual = lax.dynamic_slice_in_dim(flat, lax.axis_index("head") * share, share, 1)
-    block_out = (residual + summed).astype(jnp.bfloat16).reshape(micro, length, share)
     return (
         block_out,
         grad_tokens,

time: 951 us -> 863 us (0.907)
  matrix products: 110 us -> 10 us
  Pallas kernels: 646 us -> 745 us
  waiting for transfers between devices: 66.7 us -> 5.33 us
  other arithmetic: 53.1 us -> 29.2 us
    pallas_call x1 -> x2, Pallas kernels: 239 us -> 350 us  [the longest x1 324 us: finish(): pl.pallas_call(functools.partial(finish_kernel, parts, count, paired, bit...]
    dot_general x5 -> x0, matrix products: 72.2 us -> none  [the longest x1 25.2 us: body(): jnp.einsum('ktc,dkc->td', grad_gate_x, in_weight, preferred_element_type=...]
    ppermute x9 -> x3, waiting for transfers between devices: 62.5 us -> 1.06 us  [xor_permute(): return lax.ppermute(value, axis, [(i, i ^ 1 << bit) for i in range(size)])]
    dot_general x10 -> x2, matrix products: 32.1 us -> 1.97 us  [product(): lax.dot_general(left, right, (TN, ((), ())), preferred_element_type=jnp.f...]
    pallas_call x4, Pallas kernels: 208 us -> 188 us  [blocked(): pl.pallas_call(kernel, grid=grid, in_specs=[spec(item) for item in ins],...]
    add x1 -> x0, other arithmetic: 13.1 us -> none  [body(): cot_flat.astype(jnp.float32) + grad_flat]
    reduce_sum x2 -> x0, other arithmetic: 10.9 us -> none  [the longest x1 7.65 us: rms_scale(): values * lax.rsqrt(jnp.mean(values * values, axis=-1, keepdims=True) + EP...]
  transfers between devices with their start and end apart: 11 -> 5, of which waited for: 4 -> 2; matrix products, arithmetic and copies ran while one was open for 10% -> 3% of each run, Pallas kernels for 0% -> 0%
where the time goes in v4:
time: 863 us; the launch traced here: 847 us
  Pallas kernels  745 us (86%)
  local copies, waits for them, and re-layouts  39 us (5%)
  other arithmetic  29.2 us (3%)
  starting transfers between devices  15.3 us (2%)
  matrix products  10 us (1%)
    pallas_call x1, Pallas kernels, finish(): pl.pallas_call(functools.partial(finish_kernel, parts, count, paired, bit...  324 us
    pallas_call x2, Pallas kernels, exchange(): pl.pallas_call(functools.partial(exchange_kernel, length, reverse, orders...  207 us
    pallas_call x4, Pallas kernels, blocked(): pl.pallas_call(kernel, grid=grid, in_specs=[spec(item) for item in ins],...  188 us
    pallas_call x1, Pallas kernels, project(): pl.pallas_call(project_kernel, grid=(columns // tile,), in_specs=[pl.Bloc...  26.7 us
  transfers between devices with their start and end apart: 5, of which 2 were waited for; matrix products, arithmetic and copies ran while one was open for 3% of the time, Pallas kernels for 0%

profile of v4, /device:TPU:1, one launch (start us, length us, event | category | flops | bytes accessed | tf_op | source)
XLA Modules:
  0.0 846.8 jit_solution(10025535257245906137)
XLA Ops:
  0.7 26.7 %project.1 = (bf16[1024,2048]{1,0:T(8,128)(2,1)}, f32[2,1024,2048]{2,1,0:T(8,128)}) custom-call(bf16[1024,2048]{1,0:T(8,128)(2,1)} %bitcast.124, f32[1,2048]{1,0:T(1,128)} %bitcast.155, bf16[2048,2,2048]{2,1,0:T(2,128)(2,1)} %refs_29_.1), custom_call_target="tpu_custom_call" | custom-call | flops 17179869184 | tf_op jit(solution)/shard_map/project/pallas_call | solution.py:1052
  27.4 1.0 slice_bitcast_fusion
  28.4 3.5 fusion.36
  32.0 4.0 collective-permute-start
  38.4 0.7 broadcast_in_dim_reshape.3.skip_ref
  39.3 2.3 pad_maximum_fusion.refs_34_
  41.7 4.3 broadcast_multiply_fusion.1
  46.9 0.7 broadcast_bitcast_fusion.log_ref
  47.7 0.8 bitcast_multiply_fusion.3
  49.2 1.7 multiply_convert_fusion
  50.9 0.9 fusion.31
  51.8 0.7 pad.38.halo_ref
  52.5 21.1 %front.1 = (bf16[4,256,2048]{2,1,0:T(8,128)(2,1)}, f32[4,2048,128]{2,1,0:T(8,128)}) custom-call(s32[1]{0:T(128)} %bitcast.base_ref, s32[4,3]{1,0:T(4,128)} %pad_add_fusion.2.starts_ref, f32[2,4,256,2048]{3,2,1,0:T(8,128)} %bitcast.162, f32[4,8,2048]{2,1,0:T(8,128)} %pad.38.halo_ref, f32[4,2048]{1,0:T(4,128)} %weight_ref.5, f32[1,2048]{1,0:T(1,128)} %bitcast.168, ...), custom_call_target="tpu_custom_call" | custom-call | flops 20000000000 | bytes 25862196 | tf_op jit(solution)/shard_map/front/pallas_call | solution.py:1428
  73.6 100.1 %exchange.1 = (f32[4,4,8,64,128]{4,3,2,1,0:T(8,128)}, f32[1024,2048]{1,0:T(8,128)}, bf16[1024,1024]{1,0:T(8,128)(2,1)}, bf16[1024,1024]{1,0:T(8,128)(2,1)}, bf16...) custom-call(f32[4,4,8,64,128]{4,3,2,1,0:T(8,128)} %bitcast.175, ...), custom_call_target="tpu_custom_call" | custom-call | flops 99999997952 | tf_op jit(solution)/shard_map/exchange/pallas_call | solution.py:270
  173.8 25.4 %mix.1 = (f32[4,256,2048]{2,1,0:T(8,128)}, f32[4,256,2]{2,1,0:T(8,128)}) custom-call(s32[1]{0:T(128)} %bitcast.base_ref, s32[4,3]{1,0:T(4,128)} %pad_add_fusion.2.starts_ref, bf16[4,256,2048]{2,1,0:T(8,128)(2,1)} %get-tuple-element.103.x_ref, bf16[4,256,128]{2,1,0:T(8,128)(2,1)} %get-tuple-element.252.b_ref, bf16[4,256,128]{2,1,0:T(8,128)(2,1)} %get-tuple-element.251.c_ref, ...), custom_call_target="tpu_custom_call" | custom-call | flops 24999999488 | bytes 42909748 | tf_op jit(solution)/shard_map/mix/pallas_call | solution.py:1428
  199.2 1.9 collective-permute-start.1
  201.2 0.7 slice_reduce_fusion.4
  201.9 1.1 collective-permute-done.1
  202.9 1.9 add.122.sums_ref
  204.8 22.3 %gate.1 = (bf16[4,256,2048]{2,1,0:T(8,128)(2,1)}, bf16[4,256,2048]{2,1,0:T(8,128)(2,1)}, bf16[2,4,256,2048]{3,2,1,0:T(8,128)(2,1)}, bf16[4,256,2048]{2,1,0:T(8,1...) custom-call(f32[4,256,2048]{2,1,0:T(8,128)} %get-tuple-element.106.mixed_ref, f32[2,4,256,2048]{3,2,1,0:T(8,128)} %bitcast.164, ...), custom_call_target="tpu_custom_call" | custom-call | flops 20000000000 | bytes 55197696 | tf_op jit(solution)/shard_map/gate/pallas_call | solution.py:1428
  227.1 106.8 %exchange_back.1 = (f32[4,4,8,64,128]{4,3,2,1,0:T(8,128)}, f32[1024,2048]{1,0:T(8,128)}, f32[1024,2048]{1,0:T(8,128)}, f32[1024,384]{1,0:T(8,128)}) custom-call(f32[4,4,8,64,128]{4,3,2,1,0:T(8,128)} %bitcast.176, f32[4,4,8,128]{3,2,1,0:T(8,128)} %broadcast_bitcast_fusion.log_ref, bf16[1024,1024]{1,0:T(8,128)(2,1)} %get-tuple-element.111.refs_0_, ...), custom_call_target="tpu_custom_call" | custom-call | flops 99999997952 | tf_op jit(solution)/shard_map/exchange_back/pallas_call | solution.py:270
  333.9 119.1 %back.1 = (bf16[2,4,256,2048]{3,2,1,0:T(8,128)(2,1)}, f32[4,8,2048]{2,1,0:T(8,128)}, f32[4,8,2048]{2,1,0:T(8,128)}, f32[4,8,2048]{2,1,0:T(8,128)}, f32[4,32,256]...) custom-call(s32[1]{0:T(128)} %bitcast.base_ref, ...), custom_call_target="tpu_custom_call", output_to_operand_aliasing={{0}: (17, {})} | custom-call | flops 80000000000 | bytes 44417076 | tf_op jit(solution)/shard_map/back/pallas_call | solution.py:1428
  453.1 1.0 reduce_sum.126
  454.2 0.9 reduce_sum.111
  455.3 1.0 slice.208
  456.3 1.9 constant_dynamic-update-slice_fusion.1
  458.2 0.8 constant_dynamic-update-slice_fusion
  459.0 5.7 collective-permute-start.2
  465.1 1.0 copy.103
  466.1 2.4 bitcast_convert_fusion
  468.7 1.0 slice_reduce_fusion
  469.7 0.7 subtract_convert_fusion.2
  470.6 2.3 multiply_reduce_fusion.3
  473.5 0.9 copy-done
  474.9 0.7 pad_maximum_fusion.12
  475.6 1.5 collective-permute-start.3
  477.1 1.1 slice.254
  478.9 4.3 collective-permute-done.3
  483.1 0.8 slice_add_fusion.1
  483.9 1.5 scatter-add.4
  485.4 1.2 constant_dynamic-slice_fusion
  486.6 1.1 subtract_convert_fusion.1
  487.8 1.1 multiply_convert_fusion.1
  488.9 0.8 copy-done.8
  489.7 1.0 fusion.13
  491.2 1.0 fusion.14
  492.4 0.8 copy.112
  493.3 1.1 slice.258
  494.6 2.5 pad_maximum_fusion.4
  497.2 1.7 dynamic_update_slice.3
  499.0 1.2 pad_maximum_fusion.5.refs_33_
  500.2 323.6 %finish.1 = (f32[128,2048]{1,0:T(8,128)}, f32[128,2048]{1,0:T(8,128)}, f32[128,2048]{1,0:T(8,128)}, f32[16,160,128]{2,1,0:T(8,128)}, f32[128,128]{1,0:T(8,128)},...) custom-call(bf16[1024,1024]{1,0:T(8,128)(2,1)} %get-tuple-element.99, ...), custom_call_target="tpu_custom_call" | custom-call | tf_op jit(solution)/shard_map/finish/pallas_call | solution.py:895
  823.8 1.0 slice.225
  824.9 1.4 slice.224
  827.9 1.0 copy.110
  828.9 2.3 collective-permute-start.4
  831.2 1.4 pad_maximum_fusion.1
  832.6 2.9 copy.109
  837.3 0.7 fusion.32
  838.1 1.5 pad_maximum_fusion.2
  839.6 1.0 copy-done.9
  840.6 1.3 copy.123
  841.9 3.4 copy.124
  845.3 1.0 copy.125
  (178 shorter events, 10.8 us)
Async XLA Ops:
  0.6 27.7 %copy-start.13 = (bf16[2048,256]{1,0:T(8,128)(2,1)S(1)}, bf16[2048,256]{1,0:T(8,128)(2,1)}, u32[]{:S(2)}) copy-start(bf16[2048,256]{1,0:T(8,128)(2,1)} %param.23) | copy-start | bytes 3145732
  28.4 8.9 %copy-start.53 = (f32[32]{0:T(128)S(1)}, f32[32]{0:T(128)}, u32[]{:S(2)}) copy-start(f32[32]{0:T(128)} %param.26) | copy-start | bytes 388
  28.4 8.9 %copy-start.45 = (s32[2,3]{1,0:T(2,128)S(1)}, s32[2,3]{1,0:T(2,128)}, u32[]{:S(2)}) copy-start(s32[2,3]{1,0:T(2,128)} %param.35) | copy-start | bytes 76
  28.4 9.5 %copy-start.46 = (f32[4,256]{1,0:T(4,128)S(1)}, f32[4,256]{1,0:T(4,128)}, u32[]{:S(2)}) copy-start(f32[4,256]{1,0:T(4,128)} %param.29) | copy-start | bytes 12292
  28.4 9.9 %copy-start.49 = (f32[32]{0:T(128)S(1)}, f32[32]{0:T(128)}, u32[]{:S(2)}) copy-start(f32[32]{0:T(128)} %param.31) | copy-start | bytes 388
  28.4 10.6 %copy-start.22 = (bf16[2048,32]{0,1:T(8,128)(2,1)S(1)}, bf16[2048,32]{0,1:T(8,128)(2,1)}, u32[]{:S(2)}) copy-start(bf16[2048,32]{0,1:T(8,128)(2,1)} %param.24) | copy-start | bytes 393220
  31.9 17.2 %copy-start.3 = (f32[1024,256]{1,0:T(8,128)}, f32[1024,256]{1,0:T(8,128)S(1)}, u32[]{:S(2)}) copy-start(f32[1024,256]{1,0:T(8,128)S(1)} %fusion.36) | copy-start | bytes 3145732
  32.0 17.1 %collective-permute-start = (f32[4,3,2304]{2,1,0:T(4,128)S(1)}, f32[4,3,2304]{2,1,0:T(4,128)S(1)}, u32[]{:S(2)}, u32[]{:S(2)}) collective-permute-start(f32[4,3,2304]{2,1,0:T(4,128)S(1)} %pad_maximum_fusion.11), channel_id=1, source_target_pairs={{0,2},{2,4},{4,6},{6,8},{8,10},{10,12},{12,14},{14,16},{16,18},{18... | collective-permute-start | bytes 331784 | tf_op jit(solution)/shard_map/ppermute | solution.py:18
  37.3 4.4 copy-start.50
  37.9 11.2 %copy-start.37 = (f32[1,256]{1,0:T(1,128)}, f32[1,256]{1,0:T(1,128)S(1)}, u32[]{:S(2)}) copy-start(f32[1,256]{1,0:T(1,128)S(1)} %get-tuple-element.268) | copy-start | bytes 3076
  37.9 11.2 %copy-start.39 = (f32[1,256]{1,0:T(1,128)}, f32[1,256]{1,0:T(1,128)S(1)}, u32[]{:S(2)}) copy-start(f32[1,256]{1,0:T(1,128)S(1)} %get-tuple-element.269) | copy-start | bytes 3076
  38.0 11.2 %copy-start.41 = (f32[1,256]{1,0:T(1,128)}, f32[1,256]{1,0:T(1,128)S(1)}, u32[]{:S(2)}) copy-start(f32[1,256]{1,0:T(1,128)S(1)} %get-tuple-element.270) | copy-start | bytes 3076
  38.0 11.2 %copy-start.43 = (f32[1,256]{1,0:T(1,128)}, f32[1,256]{1,0:T(1,128)S(1)}, u32[]{:S(2)}) copy-start(f32[1,256]{1,0:T(1,128)S(1)} %get-tuple-element.271) | copy-start | bytes 3076
  38.1 9.6 %copy-start.33 = (f32[4,256]{1,0:T(4,128)}, f32[4,256]{1,0:T(4,128)S(1)}, u32[]{:S(2)}) copy-start(f32[4,256]{1,0:T(4,128)S(1)} %get-tuple-element.263) | copy-start | bytes 12292
  38.1 11.1 %copy-start.26 = (f32[4,256]{1,0:T(4,128)}, f32[4,256]{1,0:T(4,128)S(1)}, u32[]{:S(2)}) copy-start(f32[4,256]{1,0:T(4,128)S(1)} %get-tuple-element.264) | copy-start | bytes 12292
  38.1 11.1 %copy-start.28 = (f32[4,256]{1,0:T(4,128)}, f32[4,256]{1,0:T(4,128)S(1)}, u32[]{:S(2)}) copy-start(f32[4,256]{1,0:T(4,128)S(1)} %get-tuple-element.265) | copy-start | bytes 12292
  38.1 11.1 %copy-start.30 = (f32[4,256]{1,0:T(4,128)}, f32[4,256]{1,0:T(4,128)S(1)}, u32[]{:S(2)}) copy-start(f32[4,256]{1,0:T(4,128)S(1)} %get-tuple-element.267) | copy-start | bytes 12292
  39.3 2.4 copy-start.52
  46.0 3.2 copy-start.48
  46.4 4.5 copy-start.17
  46.6 5.2 copy-start.19
  46.8 5.0 copy-start.35
  49.1 3.4 copy-start.20
  173.8 27.4 %copy-start.34 = (f32[4,256]{1,0:T(4,128)S(1)}, f32[4,256]{1,0:T(4,128)}, u32[]{:S(2)}) copy-start(f32[4,256]{1,0:T(4,128)} %copy-done.33) | copy-start | bytes 12292
  199.2 3.7 collective-permute-start.1
  453.0 5.2 copy-start.18
  453.0 11.6 %copy-start.36 = (f32[4,32,1]{1,0,2:T(4,128)S(1)}, f32[4,32,1]{1,0,2:T(4,128)}, u32[]{:S(2)}) copy-start(f32[4,32,1]{1,0,2:T(4,128)} %copy-done.35) | copy-start | bytes 1540
  453.0 11.6 %copy-start.47 = (f32[4]{0:T(128)S(1)}, f32[4]{0:T(128)}, u32[]{:S(2)}) copy-start(f32[4]{0:T(128)} %slice_reduce_fusion.4) | copy-start | bytes 52
  453.0 11.7 %copy-start.24 = (f32[4,32,256]{2,1,0:T(8,128)S(1)}, f32[4,32,256]{2,1,0:T(8,128)}, u32[]{:S(2)}) copy-start(f32[4,32,256]{2,1,0:T(8,128)} %get-tuple-element.142) | copy-start | bytes 393220
  453.1 12.0 %copy-start.23 = (f32[4,32,256]{2,1,0:T(8,128)S(1)}, f32[4,32,256]{2,1,0:T(8,128)}, u32[]{:S(2)}) copy-start(f32[4,32,256]{2,1,0:T(8,128)} %get-tuple-element.141) | copy-start | bytes 393220
  454.1 12.0 %copy-start.51 = (f32[32]{0:T(128)S(1)}, f32[32]{0:T(128)}, u32[]{:S(2)}) copy-start(f32[32]{0:T(128)} %copy-done.50) | copy-start | bytes 388
  459.0 11.5 %collective-permute-start.2 = (f32[4,256,256]{2,1,0:T(8,128)}, f32[4,256,256]{2,1,0:T(8,128)}, u32[]{:S(2)}, u32[]{:S(2)}) collective-permute-start(f32[4,256,256]{2,1,0:T(8,128)} %constant_dynamic-update-slice_fusion), channel_id=1, source_target_pairs={{0,1},{1,0},{2,3},{3,2},{4,5},{5,4},{6,7},{7,6},{8,9},{9,8},{10,11... | collective-permute-start | bytes 3145736 | tf_op jit(solution)/shard_map/ppermute | solution.py:310
  464.8 4.9 copy-start.54
  465.0 5.4 copy-start.4
  465.1 5.4 copy-start.7
  465.1 5.4 copy-start.21
  465.1 5.4 copy-start.27
  465.1 5.4 copy-start.29
  465.1 5.4 copy-start.31
  468.5 4.4 copy-start.1
  470.5 2.4 copy-start.38
  470.5 2.4 copy-start.40
  470.6 2.4 copy-start.42
  470.6 2.4 copy-start.44
  473.5 1.0 copy-start
  475.6 7.6 collective-permute-start.3
  483.9 3.8 copy-start.2
  485.4 2.4 copy-start.6
  487.7 2.0 copy-start.8
  489.7 1.6 copy-start.5
  494.3 2.9 copy-start.25
  494.3 4.6 copy-start.10
  494.3 4.6 copy-start.11
  494.4 4.6 copy-start.15
  494.4 4.6 copy-start.16
  823.8 2.4 copy-start.32
  824.9 6.3 copy-start.14
  828.9 9.1 %collective-permute-start.4 = (f32[2048,128]{1,0:T(8,128)S(1)}, f32[2048,128]{1,0:T(8,128)S(1)}, u32[]{:S(2)}, u32[]{:S(2)}) collective-permute-start(f32[2048,128]{1,0:T(8,128)S(1)} %bitcast.131), channel_id=1, source_target_pairs={{0,1},{1,0},{2,3},{3,2},{4,5},{5,4},{6,7},{7,6},{8,9},{9,8},{10,11... | collective-permute-start | bytes 3145736 | tf_op jit(solution)/shard_map/ppermute | solution.py:310
  832.6 9.3 %slice-start = ((s8[8388608]{0:T(1024)(128)(4,1)}), s8[4194304]{0:T(1024)(128)(4,1)S(1)}, s32[]{:S(2)}) async-start(s8[8388608]{0:T(1024)(128)(4,1)} %bitcast.117), calls=%async_computation | async-start | bytes 8388608
  838.0 4.0 slice-start.1
  838.1 2.5 copy-start.9
  841.9 3.4 copy-start.12

commit v5 on v4

--- a/solution.py
+++ b/solution.py
@@ -56,16 +56,14 @@
 GROUP = 4
 
 
-def exchange_kernel(length, reverse, orders, jobs, tail, part_ref, log_ref, *refs):
+def exchange_kernel(length, reverse, orders, jobs, part_ref, log_ref, *refs):
     refs = list(refs)
     sources = [refs.pop(0) for _ in range(2 if orders else 0)]
     job_refs = [[refs.pop(0) for _ in range(job[2])] for job in jobs]
     out_ref = refs.pop(0)
-    steps, made = [], []
-    for (make, plan, _, results), inputs in zip(jobs, job_refs):
-        made.append(refs.pop(0))
-        steps += make(inputs, made[-1], plan)
-    tail_ref = refs.pop(0) if tail is not None else None
+    steps = []
+    for (make, plan, _), inputs in zip(jobs, job_refs):
+        steps += make(inputs, refs.pop(0), plan)
     targets = [refs.pop(0) for _ in range(4 * len(orders))]
     (
         parts,
@@ -83,7 +81,6 @@
         given_recv,
         stage_sem,
         place_sem,
-        tail_sem,
         staged,
     ) = refs
     me = lax.axis_index("seq")
@@ -148,10 +145,15 @@
             log_ref.at[mate], logs.at[rank], log_send.at[slot], log_recv.at[slot], first + mate
         )
 
+    quarter = edge_in.shape[2]
+
+    def own_columns(place):
+        return pl.ds(pl.multiple_of(place * quarter, quarter), quarter)
+
     def part_copy(m, slot):
         mate = mates[slot]
         return remote(
-            part_ref.at[m, mate],
+            part_ref.at[m, :, own_columns(mate)],
             parts.at[m, rank],
             part_send.at[m, slot],
             part_recv.at[m, slot],
@@ -165,7 +167,7 @@
         mate = mates[slot]
         return remote(
             given.at[m, mate],
-            out_ref.at[m, rank],
+            out_ref.at[m, :, own_columns(rank)],
             given_send.at[m, slot],
             given_recv.at[m, slot],
             first + mate,
@@ -178,7 +180,7 @@
             part_copy(m, slot).start()
     logs[rank] = log_ref[rank]
     for m in range(micro):
-        parts[m, rank] = part_ref[m, rank]
+        parts[m, rank] = part_ref[m, :, own_columns(rank)]
 
     @pl.when(begins)
     def _():
@@ -196,8 +198,8 @@
             step()
         for slot in range(3):
             part_copy(m, slot).wait()
-        factors = [jnp.exp(logs[t, m])[:, None, :] for t in order]
-        whole = jnp.exp(logs[0, m] + logs[1, m] + logs[2, m] + logs[3, m])[:, None, :]
+        factors = [jnp.exp(logs[t, m : m + 1, :]) for t in order]
+        whole = jnp.exp(sum(logs[t, m : m + 1, :] for t in order))
         total = parts[m, order[0]]
         for t, factor in zip(order[1:], factors[1:]):
             total = total * factor + parts[m, t]
@@ -218,18 +220,7 @@
                 running = running * factor + parts[m, t]
         for slot in range(3):
             given_copy(m, slot).start()
-        out_ref[m, rank] = given[m, rank]
-    if tail is not None:
-        columns = part_columns(jobs[0][1])[tail]
-        bit = jobs[0][1][tail][0][0]
-        tail_copy = remote(
-            made[0].at[:, columns],
-            tail_ref,
-            tail_sem.at[0],
-            tail_sem.at[1],
-            me + (1 << bit) * (1 - 2 * lax.rem(me // (1 << bit), 2)),
-        )
-        tail_copy.start()
+        out_ref[m, :, own_columns(rank)] = given[m, rank]
     for m in range(micro):
         for slot in range(3):
             given_copy(m, slot).wait()
@@ -238,19 +229,16 @@
         def _():
             edge_copy(m).wait_send()
 
-    if tail is not None:
-        tail_copy.wait()
     for copy in placed:
         copy.wait()
 
 
-def exchange(parts, logs, reverse, sources=(), orders=(), jobs=(), tail=None):
-    micro, heads, rows, columns = parts.shape
-    quarter = heads // GROUP
+def exchange(parts, logs, reverse, sources=(), orders=(), jobs=()):
+    micro, rows, columns = parts.shape
+    quarter = columns // GROUP
     length = lax.axis_size("seq")
-    spread = jnp.broadcast_to(logs[:, :, None], (micro, heads, columns))
-    spread = spread.reshape(micro, GROUP, quarter, columns).transpose(1, 0, 2, 3)
-    shape = (micro, GROUP, quarter, rows, columns)
+    spread = logs.reshape(micro, GROUP, quarter).transpose(1, 0, 2)
+    shape = (micro, GROUP, rows, quarter)
     arranged = []
     for source in sources:
         half = jax.ShapeDtypeStruct((source.shape[0], source.shape[1] // 2), source.dtype)
@@ -258,25 +246,23 @@
     vmem = pl.BlockSpec(memory_space=pltpu.VMEM)
     hbm = pl.BlockSpec(memory_space=pl.ANY)
     made = [jax.ShapeDtypeStruct(job[3], jnp.float32) for job in jobs]
-    if tail is not None:
-        made.append(
-            jax.ShapeDtypeStruct((jobs[0][3][0], sum(jobs[0][1][tail][1])), jnp.float32)
-        )
     results = len(made)
     count = len(arranged)
     arranged = made + arranged
     job_inputs = [item for job in jobs for item in job[2]]
-    plans = tuple((job[0], job[1], len(job[2]), 1) for job in jobs)
+    plans = tuple((job[0], job[1], len(job[2])) for job in jobs)
+    smem = pl.BlockSpec(memory_space=pltpu.SMEM)
+    job_specs = [smem if item.dtype == jnp.int32 else hbm for item in job_inputs]
     out, *arranged = pl.pallas_call(
-        functools.partial(exchange_kernel, length, reverse, orders, plans, tail),
-        out_shape=[jax.ShapeDtypeStruct(shape, jnp.float32)] + arranged,
-        in_specs=[vmem] * 2 + [hbm] * (len(sources) + len(job_inputs)),
+        functools.partial(exchange_kernel, length, reverse, orders, plans),
+        out_shape=[jax.ShapeDtypeStruct(parts.shape, jnp.float32)] + arranged,
+        in_specs=[vmem] * 2 + [hbm] * len(sources) + job_specs,
         out_specs=[vmem] + [hbm] * len(arranged),
         scratch_shapes=[
             pltpu.VMEM(shape, jnp.float32),
-            pltpu.VMEM((GROUP, micro, quarter, columns), jnp.float32),
-            pltpu.VMEM((micro, quarter, rows, columns), jnp.float32),
-            pltpu.VMEM((micro, quarter, rows, columns), jnp.float32),
+            pltpu.VMEM((GROUP, micro, quarter), jnp.float32),
+            pltpu.VMEM((micro, rows, quarter), jnp.float32),
+            pltpu.VMEM((micro, rows, quarter), jnp.float32),
             pltpu.VMEM(shape, jnp.float32),
             pltpu.SemaphoreType.DMA((micro, 3)),
             pltpu.SemaphoreType.DMA((micro, 3)),
@@ -288,7 +274,6 @@
             pltpu.SemaphoreType.DMA((micro, 3)),
             pltpu.SemaphoreType.DMA((2,)),
             pltpu.SemaphoreType.DMA((max(count, 1) * max(length // 2, 1),)),
-            pltpu.SemaphoreType.DMA((2,)),
             pltpu.VMEM((2,) + sources[0].shape if sources else (2, 16, 128), jnp.bfloat16),
         ],
         compiler_params=pltpu.CompilerParams(
@@ -300,8 +285,7 @@
             flops=EXCHANGE_COST, bytes_accessed=0, transcendentals=0
         ),
         name="exchange_back" if reverse else "exchange",
-    )(parts.reshape(shape), spread, *sources, *job_inputs)
-    out = out.reshape(micro, heads, rows, columns)
+    )(parts, spread, *sources, *job_inputs)
     return out, arranged[:results], arranged[results:]
 
 
@@ -324,16 +308,23 @@
     return value
 
 
-def scatter_parts(columns, bits):
+def scatter_plans(columns, bits):
     if bits < 3 or columns % 2048:
-        return [(tuple(range(bits)), (columns,))]
+        return [[(tuple(range(bits)), (columns,))]] * 3
     rest = tuple(range(3, bits))
     unit = columns // 16
+    orders = ((0, 1, 2), (1, 0, 2), (2, 0, 1), (2, 1, 0))
+    shares = (
+        ((3, 3), (2, 3), (3, 0), (0, 2)),
+        ((3, 2), (3, 3), (3, 0), (0, 2)),
+        ((3, 2), (2, 3), (3, 0), (0, 3)),
+    )
     return [
-        ((0, 1, 2) + rest, (3 * unit, 2 * unit)),
-        ((1, 0, 2) + rest, (2 * unit, 3 * unit)),
-        ((2, 0, 1) + rest, (3 * unit, 0)),
-        ((2, 1, 0) + rest, (0, 3 * unit)),
+        [
+            (order + rest, tuple(unit * count for count in counts))
+            for order, counts in zip(orders, share)
+        ]
+        for share in shares
     ]
 
 
@@ -496,7 +487,7 @@
     )(left_ref, chosen, out_ref)
 
 
-def row_step(grad_ref, weight_ref, narrow_left_ref, narrow_right_ref, out_ref, first, rows):
+def row_step(grad_ref, weight_ref, narrow_ref, map_ref, step_ref, out_ref, first, rows):
     depth, halves, width = weight_ref.shape
     tile = min(depth, 256)
 
@@ -505,9 +496,15 @@
         copy.start()
         copy.wait()
 
-        def body(weight, narrow_left, narrow_right, out):
+        def body(weight, narrow, map_weight, step_weight, out):
             turned_weight = jnp.swapaxes(weight[...], 0, 1)
-            total = low_dot(narrow_left[...], narrow_right[...], NT)
+            maps = map_weight.shape[1]
+            high, rest = halves_of(narrow[...])
+            total = low_dot(high[:, :maps], map_weight[...], NT) + low_dot(
+                rest[:, :maps], map_weight[...], NT
+            )
+            total = total + low_dot(high[:, maps:], step_weight[...], NT)
+            total = total + low_dot(rest[:, maps:], step_weight[...], NT)
             for half in range(halves):
                 total = total + low_dot(held[half], turned_weight[half], NT)
             out[...] = total
@@ -517,14 +514,16 @@
             grid=(depth // tile,),
             in_specs=[
                 pl.BlockSpec((tile, halves, width), lambda j: (j, 0, 0)),
-                pl.BlockSpec((rows, narrow_left_ref.shape[1]), lambda j: (0, 0)),
-                pl.BlockSpec((tile, narrow_left_ref.shape[1]), lambda j: (j, 0)),
+                pl.BlockSpec((rows, narrow_ref.shape[1]), lambda j: (0, 0)),
+                pl.BlockSpec((tile, map_ref.shape[1]), lambda j: (j, 0)),
+                pl.BlockSpec((tile, step_ref.shape[1]), lambda j: (j, 0)),
             ],
             out_specs=[pl.BlockSpec((rows, tile), lambda j: (0, j))],
         )(
             weight_ref,
-            narrow_left_ref.at[pl.ds(first, rows)],
-            narrow_right_ref,
+            narrow_ref.at[pl.ds(first, rows)],
+            map_ref,
+            step_ref,
             out_ref.at[pl.ds(first, rows)],
         )
 
@@ -570,15 +569,16 @@
     )(tokens_ref, cot_ref, *rows_refs, kept_ref, other_ref, grad_ref, block_ref)
 
 
-def finish_kernel(parts, mats, paired, bits, blocks, *refs):
+def finish_kernel(plans, paired, bits, blocks, *refs):
     refs = list(refs)
+    mats, parts = len(plans), plans[-1]
     take = lambda count: [refs.pop(0) for _ in range(count)]
     ins = [take(2 * len(parts) + 1) for _ in range(mats - 1)]
     last_sent, last_kept = take(len(parts)), take(len(parts))
     grad_ref, narrow_ref, vector_ref = take(3)
     if paired:
         weight_ref, gain_ref, tokens_ref, cot_ref = take(4)
-        narrow_left_ref, narrow_right_ref, gated_ref, out_weight_ref = take(4)
+        narrow_row_ref, map_ref, step_ref, gated_ref, out_weight_ref = take(5)
     outs = take(mats)
     gathered_ref, vector_out_ref = take(2)
     if paired:
@@ -600,7 +600,7 @@
     for mat in range(mats):
         for piece in range(piece_count):
             wave, first = [], 0
-            for order, widths in parts:
+            for order, widths in plans[mat]:
                 if widths[piece]:
                     place = first + sum(widths[:piece])
                     keep = refs.pop(0)
@@ -611,7 +611,7 @@
                     chain_count += 1
                 first += sum(widths)
             waves.append(wave)
-    narrow_order = parts[0][0]
+    narrow_order = parts[min(1, len(parts) - 1)][0]
     narrow = (chain_count, narrow_ref, 0, None, 0, narrow_order, refs.pop(0), take(bits))
     vector_sums, vector_recvs, gain_sum, local_sem, send_sem, recv_sem = refs
 
@@ -692,7 +692,7 @@
         if mat == mats - 1:
             for k in range(len(parts)):
                 first_copy(k).wait_recv()
-        for step in product_steps(ins[mat], made_refs[mat], parts):
+        for step in product_steps(ins[mat], made_refs[mat], plans[mat]):
             step()
 
     def begin(number):
@@ -740,13 +740,20 @@
         else:
             vector_out_ref[...] = total
 
+    gather_bits = tuple(range(bits - 1, 1, -1)) + tuple(range(min(bits, 2)))
+
     def gather_copies(phase):
-        bit = bits - 1 - phase
+        free = gather_bits[:phase]
+        fixed = sum(
+            (1 << bit) * lax.rem(me // (1 << bit), 2) for bit in range(bits) if bit not in free
+        )
         copies = []
-        for high in range(1 << phase):
-            block = lax.rem(me, 2 << bit) + high * (2 << bit)
+        for number in range(1 << phase):
+            block = fixed + sum(
+                (1 << bit) * ((number >> place) & 1) for place, bit in enumerate(free)
+            )
             region = gathered_ref.at[block]
-            copies.append(remote(("gather", phase, high), region, region, bit))
+            copies.append(remote(("gather", phase, number), region, region, gather_bits[phase]))
         return copies
 
     def narrow_halving(phase):
@@ -766,7 +773,14 @@
     def rows(part):
         count = row_ref.shape[0] // 2
         row_step(
-            grad_ref, weight_ref, narrow_left_ref, narrow_right_ref, row_ref, part * count, count
+            grad_ref,
+            weight_ref,
+            narrow_row_ref,
+            map_ref,
+            step_ref,
+            row_ref,
+            part * count,
+            count,
         )
         if part == 1:
             row_copy().start()
@@ -842,18 +856,18 @@
             copy.wait_send()
 
 
-def finish(parts, mats, last_sent, last_kept, grad, narrow, vector, row_inputs):
+def finish(plans, mats, last_sent, last_kept, grad, narrow, vector, row_inputs):
     bits = axis_bits("seq")
     size = 1 << bits
-    count = len(mats) + 1
+    count, parts = len(plans), plans[-1]
     paired = bool(row_inputs)
     rows = last_kept[0].shape[1]
     blocks = rows // (size // 2)
     columns = sum(sum(widths) for _, widths in parts)
     scratch, copies, chains = [], 0, 0
-    for _ in range(count):
+    for plan in plans:
         for piece in range(len(parts[0][1])):
-            for _, widths in parts:
+            for _, widths in plan:
                 if widths[piece]:
                     scratch.append(pltpu.VMEM((rows // 2, widths[piece]), jnp.float32))
                     for phase in range(bits - 1):
@@ -891,9 +905,9 @@
     shapes += [half] * (2 + count)
     specs += [hbm] * (len(shapes) - len(specs))
     flat = [item for mat in mats for item in mat] + last_sent + last_kept + [grad, narrow]
-    row_specs = [hbm, vmem] + [hbm] * 6 if paired else []
+    row_specs = [hbm, vmem] + [hbm] * 7 if paired else []
     results = pl.pallas_call(
-        functools.partial(finish_kernel, parts, count, paired, bits, blocks),
+        functools.partial(finish_kernel, plans, paired, bits, blocks),
         out_shape=shapes,
         in_specs=[hbm] * len(flat) + [vmem] + row_specs,
         out_specs=specs,
@@ -922,6 +936,8 @@
 
 
 HEAD_GROUP = 8
+BROAD_GROUP = 32
+SLAB = 16
 VMEM_LIMIT = 56 * 1024 * 1024
 FAR = 1 << 30
 NN = ((1,), (0,))
@@ -968,9 +984,8 @@
 
 
 def map_dot(left, right):
-    high, low = halves_of(right)
     return low_dot(
-        jnp.concatenate([left, left], axis=1), jnp.concatenate([high, low], axis=1), NT
+        jnp.concatenate([left, left], axis=1), jnp.concatenate(halves_of(right), axis=0), NN
     )
 
 
@@ -978,14 +993,14 @@
     left_high, left_low = halves_of(left)
     right_high, right_low = halves_of(right)
     return (
-        low_dot(left_high, right_high, NN)
-        + low_dot(left_high, right_low, NN)
-        + low_dot(left_low, right_high, NN)
+        low_dot(left_high, right_high, NT)
+        + low_dot(left_high, right_low, NT)
+        + low_dot(left_low, right_high, NT)
     )
 
 
 def sigmoid(value):
-    return 1.0 / (1.0 + jnp.exp(-value))
+    return 0.5 + 0.5 * jnp.tanh(0.5 * value)
 
 
 def segment_of(places, starts_ref, micro):
@@ -1005,8 +1020,7 @@
     ]
 
 
-def pair_labels(count, base_ref, starts_ref):
-    micro = pl.program_id(0)
+def pair_labels(count, base_ref, starts_ref, micro):
     column = base_ref[0] + lax.broadcasted_iota(jnp.int32, (count, 1), 0)
     row = base_ref[0] + lax.broadcasted_iota(jnp.int32, (1, count), 1)
     return segment_of(column, starts_ref, micro) == segment_of(row, starts_ref, micro)
@@ -1027,7 +1041,9 @@
     return total
 
 
-def project_kernel(tokens_ref, gain_ref, weight_ref, normed_ref, out_ref):
+def project_kernel(
+    tokens_ref, gain_ref, weight_ref, map_ref, step_ref, normed_ref, out_ref, map_out_ref, step_out_ref
+):
     count = tokens_ref.shape[0]
     slab = min(count, 64)
 
@@ -1040,12 +1056,15 @@
             scale = lax.rsqrt(jnp.mean(values * values, axis=1, keepdims=True) + EPSILON)
             normed_ref[cut, :] = (values * scale * gain_ref[...]).astype(jnp.bfloat16)
 
+        map_out_ref[...] = low_dot(normed_ref[...], map_ref[...], NN)
+        step_out_ref[...] = low_dot(normed_ref[...], step_ref[...], NN)
+
     weight = jnp.swapaxes(weight_ref[...], 0, 1)
     for half in range(weight.shape[0]):
         out_ref[half] = low_dot(normed_ref[...], weight[half], NN)
 
 
-def project(tokens, gain, weight):
+def project(tokens, gain, weight, map_weight, step_weight):
     count, width = tokens.shape
     _, halves, columns = weight.shape
     tile = min(columns, 256)
@@ -1056,21 +1075,27 @@
             pl.BlockSpec((count, width), lambda j: (0, 0)),
             pl.BlockSpec((1, width), lambda j: (0, 0)),
             pl.BlockSpec((width, halves, tile), lambda j: (0, 0, j)),
+            pl.BlockSpec(map_weight.shape, lambda j: (0, 0)),
+            pl.BlockSpec(step_weight.shape, lambda j: (0, 0)),
         ],
         out_specs=[
             pl.BlockSpec((count, width), lambda j: (0, 0)),
             pl.BlockSpec((halves, count, tile), lambda j: (0, 0, j)),
+            pl.BlockSpec((count, map_weight.shape[1]), lambda j: (0, 0)),
+            pl.BlockSpec((count, step_weight.shape[1]), lambda j: (0, 0)),
         ],
         out_shape=[
             jax.ShapeDtypeStruct((count, width), jnp.bfloat16),
             jax.ShapeDtypeStruct((halves, count, columns), jnp.float32),
+            jax.ShapeDtypeStruct((count, map_weight.shape[1]), jnp.float32),
+            jax.ShapeDtypeStruct((count, step_weight.shape[1]), jnp.float32),
         ],
         compiler_params=pltpu.CompilerParams(vmem_limit_bytes=VMEM_LIMIT),
         cost_estimate=pl.CostEstimate(
             flops=2 * count * width * columns * halves, bytes_accessed=0, transcendentals=0
         ),
         name="project",
-    )(tokens, gain[None], weight)
+    )(tokens, gain[None], weight, map_weight, step_weight)
 
 
 def front_kernel(
@@ -1086,49 +1111,39 @@
     low_ref,
     state_ref,
     ext,
+    high_keep,
+    rest_keep,
 ):
     heads = tail_ref.shape[1]
-    weight = weight_ref[...]
-    masks = same_segment(x_ref.shape[2], base_ref, starts_ref, weight.shape[0])
-    total = conv_sum(ext, x_ref[0, 0], halo_ref[0], weight, bias_ref[...], masks)
-    act = (total * sigmoid(total)).astype(jnp.bfloat16)
-    low_ref[0] = act
+    count = x_ref.shape[2]
+    weight, bias = weight_ref[...], bias_ref[...]
+    masks = same_segment(count, base_ref, starts_ref, weight.shape[0])
     scale = turned(tail_ref[0], spread_matrix(heads, head_dim))
-    high, low = halves_of(act.astype(jnp.float32) * scale)
-    state_ref[0] = low_dot(high, b_ref[0], TN) + low_dot(low, b_ref[0], TN)
-
-
-def mix_kernel(
-    head_dim,
-    base_ref,
-    starts_ref,
-    x_ref,
-    b_ref,
-    c_ref,
-    run_ref,
-    step_ref,
-    carry_ref,
-    start_ref,
-    gate_ref,
-    cot_ref,
-    gain_ref,
-    skip_ref,
-    mixed_ref,
-    sums_ref,
-):
-    heads = step_ref.shape[1]
-    count = x_ref.shape[1]
+    ext[0:8, :] = halo_ref[0]
+    ext[8 : 8 + count, :] = x_ref[0, 0]
+    for top in range(0, count, SLAB):
+        cut = slice(top, top + SLAB)
+        total = bias + weight[0:1] * ext[8 + top : 8 + top + SLAB, :]
+        for shift in range(1, weight.shape[0]):
+            first = 8 - shift + top
+            total = (
+                total
+                + weight[shift : shift + 1] * ext[first : first + SLAB, :] * masks[shift - 1][cut]
+            )
+        act = (total * sigmoid(total)).astype(jnp.bfloat16)
+        low_ref[0, cut, :] = act
+        high, rest = halves_of(act.astype(jnp.float32) * scale[cut])
+        high_keep[cut, :] = high
+        rest_keep[cut, :] = rest
+    state_ref[0] = low_dot(b_ref[0], high_keep[...], TN) + low_dot(b_ref[0], rest_keep[...], TN)
+
+
+def intra_block(head_dim, valid, x, b, c, run_row, step_row, skip):
+    heads, count = run_row.shape
     spread = spread_matrix(heads, head_dim)
-    x = x_ref[0]
-    b, c = b_ref[0], c_ref[0]
-    rows = lax.broadcasted_iota(jnp.int32, (count, count), 0)
-    columns = lax.broadcasted_iota(jnp.int32, (count, count), 1)
-    valid = pair_labels(count, base_ref, starts_ref) & (rows >= columns)
     scores = jnp.where(valid, low_dot(c, b, NT), 0.0)
     wide = x.astype(jnp.float32)
-    scaled = (wide * turned(step_ref[0], spread)).astype(jnp.bfloat16)
-    inter = map_dot(c, start_ref[0]) * turned(carry_ref[0], spread)
-    run_row = run_ref[0]
+    scaled = (wide * turned(step_row, spread)).astype(jnp.bfloat16)
     run = turned(run_row, spread_matrix(heads, 1))
     pair = 2 * head_dim
     middle = count // 2
@@ -1141,72 +1156,177 @@
             strips = []
             for top, cut in ((0, middle), (middle, count)):
                 gap = run[top:cut, head : head + 1] - run_row[head : head + 1, :cut]
-                weights = jnp.exp(jnp.minimum(gap, 0.0)) * scores[top:cut, :cut]
+                weights = jnp.exp2(jnp.minimum(gap, 0.0)) * scores[top:cut, :cut]
                 strips.append(low_dot(weights, block[:cut], NN))
             halves.append(jnp.concatenate(strips, axis=0))
         results.append(jnp.where(lane < head_dim, halves[0], halves[1]))
-    mixed = jnp.concatenate(results, axis=1) + inter + skip_ref[...] * wide
-    mixed_ref[0] = mixed
-    gate = gate_ref[0, 0]
-    gated = mixed * (gate * sigmoid(gate))
-    square = jnp.sum(gated * gated, axis=1, keepdims=True)
-    cross = jnp.sum(cot_ref[0] * gain_ref[...] * gated, axis=1, keepdims=True)
-    both = jnp.concatenate([square, cross], axis=1)
-
-    @pl.when(pl.program_id(1) == 0)
-    def _():
-        sums_ref[0] = both
-
-    @pl.when(pl.program_id(1) > 0)
-    def _():
-        sums_ref[0] = sums_ref[0] + both
+    return jnp.concatenate(results, axis=1) + skip * wide
+
+
+def intra_steps(inputs, out_ref, head_dim):
+    return [
+        functools.partial(intra_step, inputs, out_ref, head_dim, micro)
+        for micro in range(out_ref.shape[0])
+    ]
+
+
+def intra_step(inputs, out_ref, head_dim, micro):
+    base_ref, starts_ref, x_ref, b_ref, c_ref, run_ref, step_ref, skip_ref = inputs
+    _, count, inner = x_ref.shape
+    heads = run_ref.shape[1]
+    group = min(HEAD_GROUP, heads)
+    wide = group * head_dim
+
+    def body(x, b, c, run, step, skip, out):
+        rows = lax.broadcasted_iota(jnp.int32, (count, count), 0)
+        columns = lax.broadcasted_iota(jnp.int32, (count, count), 1)
+        valid = pair_labels(count, base_ref, starts_ref, micro) & (rows >= columns)
+        out[...] = intra_block(
+            head_dim, valid, x[...], b[...], c[...], run[...], step[...], skip[...]
+        )
+
+    token = pl.BlockSpec((count, wide), lambda k: (0, k))
+    maps = pl.BlockSpec((count, b_ref.shape[2]), lambda k: (0, 0))
+    row = pl.BlockSpec((group, count), lambda k: (k, 0))
+    pltpu.emit_pipeline(
+        body,
+        grid=(inner // wide,),
+        in_specs=[token, maps, maps, row, row, pl.BlockSpec((1, wide), lambda k: (0, k))],
+        out_specs=[token],
+    )(
+        x_ref.at[micro],
+        b_ref.at[micro],
+        c_ref.at[micro],
+        run_ref.at[micro],
+        step_ref.at[micro],
+        skip_ref,
+        out_ref.at[micro],
+    )
 
 
 def gate_kernel(
     head_dim,
     full,
-    mixed_ref,
+    bits,
+    intra_ref,
+    c_ref,
+    carry_ref,
+    begin_ref,
     gate_ref,
     cot_ref,
-    sums_ref,
     gain_ref,
-    carry_ref,
-    c_ref,
     norm_ref,
     grad_gate_ref,
     both_ref,
     grad_mixed_ref,
     start_ref,
     rows_ref,
+    mixed_keep,
+    gate_keep,
+    cot_keep,
+    high_keep,
+    rest_keep,
+    both_keep,
+    sums,
+    sums_in,
+    send_sem,
+    recv_sem,
 ):
+    stage, micro, number = pl.program_id(0), pl.program_id(1), pl.program_id(2)
+    groups = pl.num_programs(2)
     heads = carry_ref.shape[1]
-    mixed, gate, cot, gain = mixed_ref[0], gate_ref[0, 0], cot_ref[0], gain_ref[...]
-    scale = lax.rsqrt(sums_ref[0, :, 0:1] / full + EPSILON)
-    sigma = sigmoid(gate)
-    act = gate * sigma
-    gated = mixed * act
-    unit = gated * scale
-    norm_ref[0] = (unit * gain).astype(jnp.bfloat16)
-    pull = scale * scale * scale * sums_ref[0, :, 1:2] / full
-    grad_gated = cot * gain * scale - gated * pull
-    grad_gate = (grad_gated * mixed * sigma * (1.0 + gate * (1.0 - sigma))).astype(jnp.bfloat16)
-    grad_gate_ref[0] = grad_gate
-    both_ref[0, 0] = grad_gate
-    grad_mixed = (grad_gated * act).astype(jnp.bfloat16)
-    grad_mixed_ref[0] = grad_mixed
-    carried = grad_mixed.astype(jnp.float32) * turned(
-        carry_ref[0], spread_matrix(heads, head_dim)
-    )
-    high, low = halves_of(carried)
-    start_ref[0] = low_dot(high, c_ref[0], TN) + low_dot(low, c_ref[0], TN)
-    gains = jnp.sum(cot * unit, axis=0, keepdims=True)
-    rows_ref[0] = jnp.concatenate([gains, jnp.zeros((7, gains.shape[1]), jnp.float32)], axis=0)
+    place = micro * groups + number
+    carry = turned(carry_ref[0], spread_matrix(heads, head_dim))
+    mine = lax.axis_index("head")
+
+    def partner(bit):
+        return {"head": mine + (1 << bit) * (1 - 2 * lax.rem(mine // (1 << bit), 2))}
+
+    @pl.when((stage == 0) & (place == 0))
+    def _():
+        barrier = pltpu.get_barrier_semaphore()
+        for bit in range(bits):
+            pl.semaphore_signal(
+                barrier, inc=1, device_id=partner(bit), device_id_type=pl.DeviceIdType.MESH
+            )
+        pl.semaphore_wait(barrier, bits)
+
+    @pl.when(stage == 0)
+    def _():
+        inter = map_dot(c_ref[0], begin_ref[0])
+        gain = gain_ref[...]
+        for top in range(0, inter.shape[0], SLAB):
+            cut = slice(top, top + SLAB)
+            mixed = intra_ref[0, cut, :] + inter[cut] * carry[cut]
+            gate, cot = gate_ref[0, 0, cut, :], cot_ref[0, cut, :]
+            mixed_keep[place, cut, :] = mixed
+            gate_keep[place, cut, :] = gate
+            cot_keep[place, cut, :] = cot
+            gated = mixed * (gate * sigmoid(gate))
+            square = jnp.sum(gated * gated, axis=1, keepdims=True)
+            cross = jnp.sum(cot * gain * gated, axis=1, keepdims=True)
+            lane = lax.broadcasted_iota(jnp.int32, (SLAB, 128), 1)
+            both_keep[cut, :] = jnp.where(lane == 0, square, jnp.where(lane == 1, cross, 0.0))
+
+        @pl.when(number == 0)
+        def _():
+            sums[0, micro] = both_keep[...]
+
+        @pl.when(number > 0)
+        def _():
+            sums[0, micro] = sums[0, micro] + both_keep[...]
+
+    @pl.when((stage == 1) & (place == 0))
+    def _():
+        for bit in range(bits):
+            copy = pltpu.make_async_remote_copy(
+                src_ref=sums.at[bit],
+                dst_ref=sums_in.at[bit],
+                send_sem=send_sem.at[bit],
+                recv_sem=recv_sem.at[bit],
+                device_id=partner(bit),
+                device_id_type=pl.DeviceIdType.MESH,
+            )
+            copy.start()
+            copy.wait()
+            sums[bit + 1] = sums[bit] + sums_in[bit]
+
+    @pl.when(stage == 1)
+    def _():
+        gain = gain_ref[...]
+        gains = jnp.zeros((8, gain.shape[1]), jnp.float32)
+        for top in range(0, carry.shape[0], SLAB):
+            cut = slice(top, top + SLAB)
+            mixed, gate = mixed_keep[place, cut, :], gate_keep[place, cut, :]
+            cot = cot_keep[place, cut, :]
+            total = sums[bits, micro, cut, :]
+            scale = lax.rsqrt(total[:, 0:1] / full + EPSILON)
+            pull = scale * scale * scale * total[:, 1:2] / full
+            sigma = sigmoid(gate)
+            act = gate * sigma
+            gated = mixed * act
+            unit = gated * scale
+            norm_ref[0, cut, :] = (unit * gain).astype(jnp.bfloat16)
+            grad_gated = cot * gain * scale - gated * pull
+            grad_gate = grad_gated * mixed * sigma * (1.0 + gate * (1.0 - sigma))
+            grad_gate = grad_gate.astype(jnp.bfloat16)
+            grad_gate_ref[0, cut, :] = grad_gate
+            both_ref[0, 0, cut, :] = grad_gate
+            grad_mixed = (grad_gated * act).astype(jnp.bfloat16)
+            grad_mixed_ref[0, cut, :] = grad_mixed
+            high, rest = halves_of(grad_mixed.astype(jnp.float32) * carry[cut])
+            high_keep[cut, :] = high
+            rest_keep[cut, :] = rest
+            parts = (cot * unit).reshape(SLAB // 8, 8, cot.shape[1])
+            gains = gains + jnp.sum(parts, axis=0)
+        c = c_ref[0]
+        start_ref[0] = low_dot(c, high_keep[...], TN) + low_dot(c, rest_keep[...], TN)
+        rows_ref[0] = gains
 
 
 def back_kernel(
     head_dim,
-    parts,
-    skipped,
+    plans,
     base_ref,
     starts_ref,
     x_ref,
@@ -1233,7 +1353,6 @@
     rows_ref,
     direct_ref,
     decay_ref,
-    pair_ref,
     grad_b_ref,
     grad_c_ref,
     *refs,
@@ -1247,26 +1366,25 @@
 
     def sends():
         copies = []
-        for mat, source in enumerate((out_sent_ref, gate_sent_ref)):
-            for k, columns in enumerate(part_columns(parts)):
-                if (mat, k) not in skipped:
-                    copies.append(
-                        pltpu.make_async_remote_copy(
-                            src_ref=source.at[:, columns],
-                            dst_ref=refs[len(copies)],
-                            send_sem=send_sem.at[len(copies)],
-                            recv_sem=recv_sem.at[len(copies)],
-                            device_id={"seq": partner(parts[k][0][0])},
-                            device_id_type=pl.DeviceIdType.MESH,
-                        )
+        for plan, source in zip(plans, (out_sent_ref, gate_sent_ref)):
+            for (order, _), columns in zip(plan, part_columns(plan)):
+                copies.append(
+                    pltpu.make_async_remote_copy(
+                        src_ref=source.at[:, columns],
+                        dst_ref=refs[len(copies)],
+                        send_sem=send_sem.at[len(copies)],
+                        recv_sem=recv_sem.at[len(copies)],
+                        device_id={"seq": partner(order[0])},
+                        device_id_type=pl.DeviceIdType.MESH,
                     )
+                )
         return copies
 
     at_first = (pl.program_id(0) == 0) & (pl.program_id(1) == 0)
     at_last = (pl.program_id(0) == pl.num_programs(0) - 1) & (
         pl.program_id(1) == pl.num_programs(1) - 1
     )
-    used = sorted({order[0] for order, _ in parts})
+    used = sorted({order[0] for order, _ in plans[0]})
 
     @pl.when(at_first)
     def _():
@@ -1289,7 +1407,9 @@
     x_wide, g_wide = x.astype(jnp.float32), g.astype(jnp.float32)
     rows = lax.broadcasted_iota(jnp.int32, (count, count), 0)
     columns = lax.broadcasted_iota(jnp.int32, (count, count), 1)
-    valid = pair_labels(count, base_ref, starts_ref) & (columns >= rows)
+    valid = pair_labels(count, base_ref, starts_ref, pl.program_id(0)) & (
+        columns >= rows
+    )
     scores = jnp.where(valid, low_dot(b, c, NT), 0.0)
     upto = (rows >= columns).astype(jnp.bfloat16)
     before = (rows < columns).astype(jnp.float32)
@@ -1322,7 +1442,7 @@
             strips, straddle = [], None
             for part, (top, cut) in enumerate(((0, middle), (middle, count))):
                 gap = run_row[head : head + 1, top:] - run[top:cut, head : head + 1]
-                fade = jnp.exp(jnp.minimum(gap, 0.0))
+                fade = jnp.exp2(jnp.minimum(gap, 0.0))
                 weights = fade * scores[top:cut, top:]
                 strips.append(low_dot(weights, g_block[top:], NN))
                 inner = low_dot(x_own[top:cut], g_own[top:], NT)
@@ -1360,8 +1480,6 @@
     decay_ref[0] = (
         jnp.concatenate(straddles, axis=0) + flow_later[:heads] + flow_sooner[heads:]
     )
-    pair_high, pair_low = halves_of(start * end)
-    pair_ref[0] = low_dot(spread, pair_high, NN) + low_dot(spread, pair_low, NN)
     grads_high, grads_low = halves_of(score_grad)
     grad_c = fine_dot(g_wide * carry, start) + low_dot(grads_high, b, TN) + low_dot(grads_low, b, TN)
     grad_b = fine_dot(scaled_wide * tail, end) + low_dot(grads_high, c, NN) + low_dot(grads_low, c, NN)
@@ -1401,6 +1519,7 @@
     edge_ref[0] = back[count:]
     sums.append(jnp.sum(grad_conv, axis=0, keepdims=True))
     sums.append(jnp.sum(g_wide * x_wide, axis=0, keepdims=True))
+    sums.append(jnp.sum(start * end, axis=0, keepdims=True))
     sums.append(jnp.zeros((8 - len(sums), pre.shape[1]), jnp.float32))
     rows_ref[0] = jnp.concatenate(sums, axis=0)
 
@@ -1413,7 +1532,7 @@
 def blocked(kernel, name, grid, ins, outs, scratch=(), micros=0, aliases=None, remote=None):
     moved = sum(item[0].size * item[0].dtype.itemsize for item in ins if item[1] != "any")
     moved += sum(
-        math.prod(item[2]) * grid[0] * grid[1] * jnp.dtype(item[1]).itemsize
+        math.prod(item[2]) * math.prod(grid) * jnp.dtype(item[1]).itemsize
         for item in outs
         if item[2] != "any"
     )
@@ -1488,14 +1607,12 @@
     flat = tokens.reshape(total, width).astype(jnp.float32)
     cot_flat = cotangent.reshape(total, width)
     _, norm_back = jax.vjp(rms_scale, flat, norm_gain)
-    normed_low, gate_x = project(tokens.reshape(total, width), norm_gain, in_weight)
+    normed_low, gate_x, bc_pre, delta_pre = project(
+        tokens.reshape(total, width), norm_gain, in_weight, bc_weight, dt_weight
+    )
     gate_x = gate_x.reshape(2, micro, length, inner)
-    bc_pre = jnp.dot(normed_low, bc_weight, preferred_element_type=jnp.float32).reshape(
-        micro, length, 2 * state_size
-    )
-    delta_pre = lax.dot_general(
-        dt_weight, normed_low, (((0,), (1,)), ((), ())), preferred_element_type=jnp.float32
-    )
+    bc_pre = bc_pre.reshape(micro, length, 2 * state_size)
+    delta_pre = delta_pre.T
     left = shifted(
         jnp.concatenate(
             [gate_x[1, :, length - taps + 1 :], bc_pre[:, length - taps + 1 :]], axis=-1
@@ -1531,6 +1648,7 @@
         precision=HIGHEST,
     )
     device_log = running[:, :, -1]
+    running_two = running * math.log2(math.e)
     live = (own_labels == before_labels[:, None]).astype(jnp.float32)
     last = (own_labels == own_labels[:, -1:]).astype(jnp.float32)
     carried = jnp.exp(running) * live[:, None]
@@ -1546,125 +1664,136 @@
     in_gate, in_x = lambda m, k: (0, m, 0, k), lambda m, k: (1, m, 0, k)
     row_block, in_row = (1, group, length), lambda m, k: (m, k, 0)
     map_block, in_map = (1, length, state_size), lambda m, k: (m, 0, 0)
-    state_block, in_state = (1, wide, state_size), lambda m, k: (m, k, 0)
+    state_block, in_state = (1, state_size, wide), in_token
     halo_block = (1, 8, wide)
     flat_block, in_flat = (1, wide), lambda m, k: (0, k)
     conv_item = (conv_weight, (taps, wide), in_flat)
     whole = (micro, length, inner)
-    state_shape = (micro, inner, state_size)
+    state_shape = (micro, state_size, inner)
     row_shape = (micro, heads, length)
 
+    broad_group = min(BROAD_GROUP, heads)
+    broad_groups, broad = heads // broad_group, broad_group * head_dim
+    broad_token, broad_half = (1, length, broad), (1, 1, length, broad)
+    broad_row, broad_state = (1, broad_group, length), (1, state_size, broad)
     x_low, device_state = blocked(
         functools.partial(front_kernel, head_dim),
         "front",
-        grid,
+        (micro, broad_groups),
         [
             base_item,
             starts_item,
-            (gate_x, half_block, in_x),
-            (halo, halo_block, in_token),
-            conv_item,
-            (conv_row, flat_block, in_flat),
+            (gate_x, broad_half, in_x),
+            (halo, (1, 8, broad), in_token),
+            (conv_weight, (taps, broad), in_flat),
+            (conv_row, (1, broad), in_flat),
             (b_low, map_block, in_map),
-            (tail * delta, row_block, in_row),
+            (tail * delta, broad_row, in_row),
         ],
         [
-            (whole, jnp.bfloat16, token_block, in_token),
-            (state_shape, jnp.float32, state_block, in_state),
+            (whole, jnp.bfloat16, broad_token, in_token),
+            (state_shape, jnp.float32, broad_state, in_state),
         ],
-        [pltpu.VMEM((length + 8, wide), jnp.float32)],
+        [
+            pltpu.VMEM((length + 8, broad), jnp.float32),
+            pltpu.VMEM((length, broad), jnp.bfloat16),
+            pltpu.VMEM((length, broad), jnp.bfloat16),
+        ],
         20,
     )
     exchange_log = jnp.where(device_live[:, None] > 0.0, device_log, DEAD)
-    exchange_shape = (micro, heads, head_dim, state_size)
-    parts = scatter_parts(inner, axis_bits("seq"))
+    exchange_log = jnp.repeat(exchange_log, head_dim, axis=1)
+    plans = scatter_plans(inner, axis_bits("seq"))
+    parts = plans[-1]
     orders = tuple(order for order, _ in parts)
     tiled = (width >> axis_bits("seq")) % 128 == 0
-    incoming, (grad_gate_n,), arranged = exchange(
-        device_state.reshape(exchange_shape),
+    incoming, (grad_gate_n, intra), arranged = exchange(
+        device_state,
         exchange_log,
         False,
         (cot_flat, normed_low) if tiled else (),
         orders if tiled else (),
-        [(plain_steps, (), (cot_flat, out_weight), (total, inner))],
+        [
+            (plain_steps, (), (cot_flat, out_weight), (total, inner)),
+            (
+                intra_steps,
+                head_dim,
+                (base[None], starts, x_low, b_low, c_low, running_two, delta, skip_row),
+                whole,
+            ),
+        ],
     )
     grad_gate_n = grad_gate_n.reshape(whole)
     if not tiled:
         arranged = arrange(cot_flat, orders) + arrange(normed_low, orders)
     cot_parts, normed_parts = arranged[: 2 * len(parts)], arranged[2 * len(parts) :]
-    incoming = incoming.reshape(state_shape)
-
-    mixed, sums = blocked(
-        functools.partial(mix_kernel, head_dim),
-        "mix",
-        grid,
+
+
+    def first_stage(index):
+        return lambda p, m, k: index(m + p * (micro - 1 - m), k + p * (broad_groups - 1 - k))
+
+    def second_stage(index):
+        return lambda p, m, k: index(m * p, k * p)
+
+    def both_stages(index):
+        return lambda p, m, k: index(m, k)
+
+    head_bits = axis_bits("head")
+    kept_shape = (micro * broad_groups, length, broad)
+    sums_shape = (micro, length, 128)
+    normed_gate, grad_gate_pre, grad_gate_x, grad_mixed, device_grad, gate_rows = blocked(
+        functools.partial(gate_kernel, head_dim, float(full_inner), head_bits),
+        "gate",
+        (2, micro, broad_groups),
         [
-            base_item,
-            starts_item,
-            (x_low, token_block, in_token),
-            (b_low, map_block, in_map),
-            (c_low, map_block, in_map),
-            (running, row_block, in_row),
-            (delta, row_block, in_row),
-            (carried, row_block, in_row),
-            (incoming, state_block, in_state),
-            (gate_x, half_block, in_gate),
-            (grad_gate_n, token_block, in_token),
-            (gain_row, flat_block, in_flat),
-            (skip_row, flat_block, in_flat),
+            (intra, broad_token, first_stage(in_token)),
+            (c_low, map_block, both_stages(in_map)),
+            (carried, broad_row, both_stages(in_row)),
+            (incoming, broad_state, first_stage(in_state)),
+            (gate_x, broad_half, first_stage(in_gate)),
+            (grad_gate_n, broad_token, first_stage(in_token)),
+            (gain_row, (1, broad), both_stages(in_flat)),
         ],
         [
-            (whole, jnp.float32, token_block, in_token),
-            ((micro, length, 2), jnp.float32, (1, length, 2), in_map),
-        ],
-        (),
-        25,
-    )
-    sums = all_sum(sums, "head")
-    normed_gate, grad_gate_pre, grad_gate_x, grad_mixed, device_grad, gate_rows = blocked(
-        functools.partial(gate_kernel, head_dim, float(full_inner)),
-        "gate",
-        grid,
-        [
-            (mixed, token_block, in_token),
-            (gate_x, half_block, in_gate),
-            (grad_gate_n, token_block, in_token),
-            (sums, (1, length, 2), in_map),
-            (gain_row, flat_block, in_flat),
-            (carried, row_block, in_row),
-            (c_low, map_block, in_map),
+            (whole, jnp.bfloat16, broad_token, second_stage(in_token)),
+            (whole, jnp.bfloat16, broad_token, second_stage(in_token)),
+            ((2,) + whole, jnp.bfloat16, broad_half, second_stage(in_gate)),
+            (whole, jnp.bfloat16, broad_token, second_stage(in_token)),
+            (state_shape, jnp.float32, broad_state, second_stage(in_state)),
+            ((micro, 8, inner), jnp.float32, (1, 8, broad), second_stage(in_token)),
         ],
         [
-            (whole, jnp.bfloat16, token_block, in_token),
-            (whole, jnp.bfloat16, token_block, in_token),
-            ((2,) + whole, jnp.bfloat16, half_block, in_gate),
-            (whole, jnp.bfloat16, token_block, in_token),
-            (state_shape, jnp.float32, state_block, in_state),
-            ((micro, 8, inner), jnp.float32, halo_block, in_token),
+            pltpu.VMEM(kept_shape, jnp.float32),
+            pltpu.VMEM(kept_shape, jnp.float32),
+            pltpu.VMEM(kept_shape, jnp.float32),
+            pltpu.VMEM((length, broad), jnp.bfloat16),
+            pltpu.VMEM((length, broad), jnp.bfloat16),
+            pltpu.VMEM((length, 128), jnp.float32),
+            pltpu.VMEM((head_bits + 1,) + sums_shape, jnp.float32),
+            pltpu.VMEM((head_bits,) + sums_shape, jnp.float32),
+            pltpu.SemaphoreType.DMA((head_bits,)),
+            pltpu.SemaphoreType.DMA((head_bits,)),
         ],
-        (),
-        20,
+        30,
+        None,
+        4,
     )
     normed_gate = normed_gate.reshape(total, inner)
     grad_gate_pre = grad_gate_pre.reshape(total, inner)
-    grad_gate_gain = jnp.sum(gate_rows[:, 0], axis=0)
+    grad_gate_gain = jnp.sum(gate_rows, axis=(0, 1))
 
     half_shape = (width // 2, inner)
     paired = head_count == 2
     share = width // head_count
-    far = [k for k, (order, _) in enumerate(parts) if order[0] == 2 and len(parts) > 1]
-    skipped = {(0, far[0])} if far else set()
-    outgoing, (out_sent, gate_sent, *early), _ = exchange(
-        device_grad.reshape(exchange_shape),
+    outgoing, (out_sent, gate_sent), _ = exchange(
+        device_grad,
         exchange_log,
         True,
         jobs=[
-            (product_steps, parts, cot_parts[::2] + [normed_gate], half_shape),
-            (product_steps, parts, normed_parts[::2] + [grad_gate_pre], half_shape),
+            (product_steps, plans[0], cot_parts[::2] + [normed_gate], half_shape),
+            (product_steps, plans[1], normed_parts[::2] + [grad_gate_pre], half_shape),
         ],
-        tail=far[0] if far else None,
-    )
-    outgoing = outgoing.reshape(state_shape)
+    )
     (
         grad_gate_x,
         edge,
@@ -1672,12 +1801,11 @@
         conv_rows,
         direct,
         fading,
-        pairs,
         grad_b,
         grad_c,
         *arrivals,
     ) = blocked(
-        functools.partial(back_kernel, head_dim, parts, skipped),
+        functools.partial(back_kernel, head_dim, plans),
         "back",
         grid,
         [
@@ -1687,7 +1815,7 @@
             (grad_mixed, token_block, in_token),
             (b_low, map_block, in_map),
             (c_low, map_block, in_map),
-            (running, row_block, in_row),
+            (running_two, row_block, in_row),
             (delta, row_block, in_row),
             (carried, row_block, in_row),
             (tail, row_block, in_row),
@@ -1709,15 +1837,13 @@
             ((micro, 8, inner), jnp.float32, halo_block, in_token),
             (row_shape, jnp.float32, row_block, in_row),
             (row_shape, jnp.float32, row_block, in_row),
-            ((micro, heads, state_size), jnp.float32, (1, group, state_size), in_state),
             ((micro, length, state_size), jnp.float32, map_block, in_map),
             ((micro, length, state_size), jnp.float32, map_block, in_map),
         ]
         + [
             ((width // 2, sum(widths)), jnp.float32, "any")
-            for mat in range(2)
-            for k, (_, widths) in enumerate(parts)
-            if (mat, k) not in skipped
+            for plan in plans[:2]
+            for _, widths in plan
         ],
         [
             pltpu.VMEM((length + 8, wide), jnp.float32),
@@ -1729,11 +1855,9 @@
         {17: 0},
         3,
     )
-    arrived = [
-        [early[0] if (mat, k) in skipped else arrivals.pop(0) for k in range(len(parts))]
-        for mat in range(2)
-    ]
+    arrived = [arrivals[: len(parts)], arrivals[len(parts) :]]
     grad_bc = all_sum(jnp.concatenate([grad_b, grad_c], axis=-1), "head")
+    pairs = conv_rows[:, taps + 2].reshape(micro, heads, head_dim)
     kept = jnp.sum(pairs, axis=-1) * jnp.exp(device_log) * device_live[:, None]
     grad_decay = by_head(fading + kept[:, :, None])
     grad_delta_pre, grad_dt_bias, grad_a_log = rate_back((by_head(direct), grad_decay))
@@ -1753,18 +1877,17 @@
     grad_bc_pre = grad_bc_ext[:, taps - 1 :].at[:, length - taps + 1 :].add(right_bc)
     bc_flat = grad_bc_pre.reshape(total, 2 * state_size)
     grad_gate_x = grad_gate_x.reshape(2, total, inner)
-    bc_high, bc_rest = halves_of(bc_flat * (1.0 / head_count))
-    delta_high, delta_rest = halves_of(grad_delta_pre.T)
-    narrow_left = jnp.concatenate([bc_high, bc_rest, delta_high, delta_rest], axis=1)
-    narrow_right = jnp.concatenate([bc_weight, bc_weight, dt_weight, dt_weight], axis=1)
+    grad_steps = grad_delta_pre.T
+    narrow_row = jnp.concatenate([bc_flat * (1.0 / head_count), grad_steps], axis=1)
     if paired:
         row_inputs = (
             in_weight,
             norm_gain[None],
             tokens.reshape(total, width),
             cot_flat,
-            narrow_left,
-            narrow_right,
+            narrow_row,
+            bc_weight,
+            dt_weight,
             normed_gate,
             out_weight,
         )
@@ -1772,7 +1895,11 @@
     else:
         row_inputs = ()
         row_part = lax.dot_general(
-            narrow_left, narrow_right, (NT, ((), ())), preferred_element_type=jnp.float32
+            narrow_row,
+            jnp.concatenate([bc_weight, dt_weight], axis=1),
+            (NT, ((), ())),
+            precision=HIGHEST,
+            preferred_element_type=jnp.float32,
         ) + jnp.einsum(
             "ktc,dkc->td", grad_gate_x, in_weight, preferred_element_type=jnp.float32
         )
@@ -1788,10 +1915,11 @@
     share_bc = 2 * state_size // head_count
     own_bc = lax.dynamic_slice_in_dim(bc_flat, lax.axis_index("head") * share_bc, share_bc, 1)
     across = share_bc + heads
-    narrow_high, narrow_rest = halves_of(jnp.concatenate([own_bc, grad_delta_pre.T], axis=1))
+    side = min(1, len(parts) - 1)
+    narrow_high, narrow_rest = halves_of(jnp.concatenate([own_bc, grad_steps], axis=1))
     both = jnp.concatenate([narrow_high, narrow_rest], axis=1)
     narrow = jnp.concatenate(
-        [product(normed_parts[1], both), product(normed_parts[0], both)], axis=0
+        [product(normed_parts[2 * side + 1], both), product(normed_parts[2 * side], both)], axis=0
     )
     narrow = narrow[:, :across] + narrow[:, across:]
     size = lax.axis_size("seq")
@@ -1822,7 +1950,7 @@
     row = jnp.pad(row, (0, -count % 1024)).reshape(-1, 128)
 
     (grad_out_weight, gate_block, x_block), gathered, row, *token_grads = finish(
-        parts,
+        plans,
         [
             cot_parts[1::2] + [normed_gate] + arrived[0],
             normed_parts[1::2] + [grad_gate_pre] + arrived[1],

time: 863 us -> 838 us (0.971)
  Pallas kernels: 745 us -> 734 us
    pallas_call x4 -> x3, Pallas kernels: 188 us -> 176 us  [blocked(): pl.pallas_call(kernel, grid=grid, in_specs=[spec(item) for item in ins],...]
    pallas_call x2, Pallas kernels: 207 us -> 198 us  [exchange(): pl.pallas_call(functools.partial(exchange_kernel, length, reverse, orders...]
    unnamed x125 -> x111, local copies, waits for them, and re-layouts: 15.5 us -> 18.2 us
  transfers between devices with their start and end apart: 5 -> 4, of which waited for: 2 -> 1; matrix products, arithmetic and copies ran while one was open for 3% -> 3% of each run, Pallas kernels for 0% -> 0%
where the time goes in v5:
time: 838 us; the launch traced here: 825 us
  Pallas kernels  734 us (88%)
  local copies, waits for them, and re-layouts  46.9 us (6%)
  other arithmetic  26.4 us (3%)
  starting transfers between devices  9.93 us (1%)
    pallas_call x1, Pallas kernels, finish(): pl.pallas_call(functools.partial(finish_kernel, plans, paired, bits, bloc...  331 us
    pallas_call x2, Pallas kernels, exchange(): pl.pallas_call(functools.partial(exchange_kernel, length, reverse, orders...  198 us
    pallas_call x3, Pallas kernels, blocked(): pl.pallas_call(kernel, grid=grid, in_specs=[spec(item) for item in ins],...  176 us
    pallas_call x1, Pallas kernels, project(): pl.pallas_call(project_kernel, grid=(columns // tile,), in_specs=[pl.Bloc...  29.6 us
    unnamed x111, local copies, waits for them, and re-layouts  18.2 us
  transfers between devices with their start and end apart: 4, of which 1 were waited for; matrix products, arithmetic and copies ran while one was open for 3% of the time, Pallas kernels for 0%

profile of v5, /device:TPU:1, one launch (start us, length us, event | category | flops | bytes accessed | tf_op | source)
XLA Modules:
  0.0 825.1 jit_solution(14743899010143716680)
XLA Ops:
  0.6 1.9 copy.91.step_ref.refs_35_
  2.6 29.6 %project.1 = (bf16[1024,2048]{1,0:T(8,128)(2,1)}, f32[2,1024,2048]{2,1,0:T(8,128)}, f32[1024,256]{1,0:T(8,128)}, f32[1024,32]{1,0:T(8,128)}) custom-call(bf16[1024,2048]{1,0:T(8,128)(2,1)} %bitcast.134, f32[1,2048]{1,0:T(1,128)} %bitcast.167, bf16[2048,2,2048]{2,1,0:T(2,128)(2,1)} %refs_29_.1, bf16[2048,256]{1,0:T(8,128)(2,1)} %refs_34_.1, ...), custom_call_target="tpu_custom_call" | custom-call | flops 17179869184 | tf_op jit(solution)/shard_map/project/pallas_call | solution.py:1071
  32.2 0.8 slice.236
  32.9 1.0 slice_bitcast_fusion
  33.9 3.9 collective-permute-start
  37.9 0.6 compare_reduce_fusion.1
  39.3 0.7 slice_reduce_fusion.4
  41.0 0.7 broadcast_in_dim_reshape.3.refs_11_.skip_ref
  41.7 1.4 broadcast_multiply_fusion.2
  44.8 0.8 exponential_multiply_fusion
  46.3 1.7 multiply_convert_fusion
  48.0 0.9 fusion.35
  48.9 0.7 pad.38.halo_ref
  49.7 14.4 %front.1 = (bf16[4,256,2048]{2,1,0:T(8,128)(2,1)}, f32[4,128,2048]{2,1,0:T(8,128)}) custom-call(s32[1]{0:T(128)} %bitcast.base_ref.refs_4_, s32[4,3]{1,0:T(4,128)} %pad_add_fusion.2.starts_ref.refs_5_, f32[2,4,256,2048]{3,2,1,0:T(8,128)} %bitcast.174, f32[4,8,2048]{2,1,0:T(8,128)} %pad.38.halo_ref, f32[4,2048]{1,0:T(4,128)} %weight_ref.5, ...), custom_call_target="tpu_custom_call" | custom-call | flops 20000000000 | bytes 25862196 | tf_op jit(solution)/shard_map/front/pallas_call | solution.py:1547
  64.1 99.9 %exchange.1 = (f32[4,128,2048]{2,1,0:T(8,128)}, f32[1024,2048]{1,0:T(8,128)}, f32[4,256,2048]{2,1,0:T(8,128)}, bf16[1024,1024]{1,0:T(8,128)(2,1)}, bf16[1024,102...) custom-call(f32[4,128,2048]{2,1,0:T(8,128)} %get-tuple-element.99.pa, ...), custom_call_target="tpu_custom_call" | custom-call | flops 99999997952 | tf_op jit(solution)/shard_map/exchange/pallas_call | solution.py:256
  164.0 30.5 %gate.1 = (bf16[4,256,2048]{2,1,0:T(8,128)(2,1)}, bf16[4,256,2048]{2,1,0:T(8,128)(2,1)}, bf16[2,4,256,2048]{3,2,1,0:T(8,128)(2,1)}, bf16[4,256,2048]{2,1,0:T(8,1...) custom-call(f32[4,256,2048]{2,1,0:T(8,128)} %get-tuple-element.106.intra_ref, ...), custom_call_target="tpu_custom_call" | custom-call | flops 30000001024 | bytes 80617472 | tf_op jit(solution)/shard_map/gate/pallas_call | solution.py:1547
  194.5 97.7 %exchange_back.1 = (f32[4,128,2048]{2,1,0:T(8,128)}, f32[1024,2048]{1,0:T(8,128)}, f32[1024,2048]{1,0:T(8,128)}) custom-call(f32[4,128,2048]{2,1,0:T(8,128)} %get-tuple-element.111.part_ref, f32[4,4,512]{2,1,0:T(4,128)} %bitcast.156, bf16[1024,1024]{1,0:T(8,128)(2,1)} %get-tuple-element.112.refs_0_, bf16[1024,1024]{1,0:T(8,128)(2,1)} %get-tuple-element.113.refs_1_, ...), custom_call_target="tpu_custom_call" | custom-call | flops 99999997952 | tf_op jit(solution)/shard_map/exchange_back/pallas_call | solution.py:256
  292.2 130.9 %back.1 = (bf16[2,4,256,2048]{3,2,1,0:T(8,128)(2,1)}, f32[4,8,2048]{2,1,0:T(8,128)}, f32[4,8,2048]{2,1,0:T(8,128)}, f32[4,8,2048]{2,1,0:T(8,128)}, f32[4,32,256]...) custom-call(s32[1]{0:T(128)} %bitcast.base_ref.refs_4_, ...), custom_call_target="tpu_custom_call", output_to_operand_aliasing={{0}: (17, {})} | custom-call | flops 80000000000 | bytes 44351540 | tf_op jit(solution)/shard_map/back/pallas_call | solution.py:1547
  423.1 1.0 reduce_sum.126
  426.1 0.6 reduce_sum.127
  426.7 1.1 constant_dynamic-update-slice_fusion.1
  427.9 2.2 collective-permute-start.1
  430.1 1.0 slice_reduce_fusion
  431.4 1.0 slice.208
  432.4 1.0 add_bitcast_fusion
  433.4 1.0 copy.98
  434.4 1.0 copy.97
  435.4 3.2 fusion.32
  439.3 2.7 multiply_reduce_fusion.3
  442.6 0.9 copy-done
  444.6 1.5 collective-permute-start.2
  446.1 1.1 slice.254
  447.2 0.9 concatenate.53
  448.1 0.6 pad_bitcast_fusion.refs_28_
  448.7 3.1 collective-permute-done.2
  451.8 0.8 slice_add_fusion.1
  452.6 1.5 scatter-add.4
  454.0 1.2 constant_dynamic-slice_fusion
  455.2 1.1 subtract_convert_fusion
  456.4 1.0 broadcast_multiply_fusion
  457.5 0.8 copy-done.10
  458.3 1.0 fusion.16
  459.9 1.0 fusion.17
  460.9 1.2 fusion.1
  462.1 1.8 copy.104
  463.9 1.1 slice.259
  465.0 1.1 slice.258
  466.1 1.2 pad_maximum_fusion.2.refs_33_
  468.2 1.2 pad_maximum_fusion.4
  469.4 1.7 dynamic_update_slice.3
  471.0 331.1 %finish.1 = (f32[128,2048]{1,0:T(8,128)}, f32[128,2048]{1,0:T(8,128)}, f32[128,2048]{1,0:T(8,128)}, f32[16,160,128]{2,1,0:T(8,128)}, f32[128,128]{1,0:T(8,128)},...) custom-call(bf16[1024,1024]{1,0:T(8,128)(2,1)} %get-tuple-element.10, ...), custom_call_target="tpu_custom_call" | custom-call | tf_op jit(solution)/shard_map/finish/pallas_call | solution.py:909
  802.2 1.0 slice.225
  803.2 1.4 slice.224
  805.3 0.6 reshape.260
  806.2 1.0 copy.103
  807.2 2.3 collective-permute-start.3
  809.5 1.4 pad_maximum_fusion
  811.0 2.9 copy.102
  815.6 0.7 fusion.36
  816.5 1.5 pad_maximum_fusion.1
  817.9 1.0 copy-done.11
  819.0 1.3 copy.117
  820.3 3.4 copy.118
  823.7 1.0 copy.119
  (158 shorter events, 12.2 us)
Async XLA Ops:
  2.6 36.0 %copy-start.39 = (s32[2,3]{1,0:T(2,128)S(1)}, s32[2,3]{1,0:T(2,128)}, u32[]{:S(2)}) copy-start(s32[2,3]{1,0:T(2,128)} %param.35) | copy-start | bytes 76
  2.6 38.2 %copy-start.46 = (f32[32]{0:T(128)S(1)}, f32[32]{0:T(128)}, u32[]{:S(2)}) copy-start(f32[32]{0:T(128)} %param.26) | copy-start | bytes 388
  2.6 38.3 %copy-start.40 = (f32[4,256]{1,0:T(4,128)S(1)}, f32[4,256]{1,0:T(4,128)}, u32[]{:S(2)}) copy-start(f32[4,256]{1,0:T(4,128)} %param.29) | copy-start | bytes 12292
  2.6 38.3 %copy-start.45 = (f32[32]{0:T(128)S(1)}, f32[32]{0:T(128)}, u32[]{:S(2)}) copy-start(f32[32]{0:T(128)} %param.31) | copy-start | bytes 388
  2.6 39.1 %copy-start.41 = (f32[32]{0:T(128)S(1)}, f32[32]{0:T(128)}, u32[]{:S(2)}) copy-start(f32[32]{0:T(128)} %param.25) | copy-start | bytes 388
  33.9 12.3 %collective-permute-start = (f32[4,3,2304]{2,1,0:T(4,128)S(1)}, f32[4,3,2304]{2,1,0:T(4,128)S(1)}, u32[]{:S(2)}, u32[]{:S(2)}) collective-permute-start(f32[4,3,2304]{2,1,0:T(4,128)S(1)} %pad_maximum_fusion.10), channel_id=1, source_target_pairs={{0,2},{2,4},{4,6},{6,8},{8,10},{10,12},{12,14},{14,16},{16,18},{18... | collective-permute-start | bytes 331784 | tf_op jit(solution)/shard_map/ppermute | solution.py:18
  39.2 7.0 copy-start.21
  39.2 7.0 copy-start.23
  39.2 7.0 copy-start.25
  40.8 2.3 copy-start.42
  40.9 5.4 copy-start.31
  40.9 5.4 copy-start.33
  40.9 5.4 copy-start.35
  40.9 5.4 copy-start.37
  41.7 4.6 copy-start.1
  41.7 4.6 copy-start.44
  43.7 5.2 copy-start.14
  43.9 5.0 copy-start.28
  46.2 3.4 copy-start.17
  292.2 132.6 %copy-start.16 = (f32[4,8,2048]{2,1,0:T(8,128)S(1)}, f32[4,8,2048]{2,1,0:T(8,128)}, u32[]{:S(2)}) copy-start(f32[4,8,2048]{2,1,0:T(8,128)} %get-tuple-element.145) | copy-start | bytes 786436
  423.1 4.7 copy-start.15
  423.1 9.2 %copy-start.29 = (f32[4,32,1]{1,0,2:T(4,128)S(1)}, f32[4,32,1]{1,0,2:T(4,128)}, u32[]{:S(2)}) copy-start(f32[4,32,1]{1,0,2:T(4,128)} %copy-done.28) | copy-start | bytes 1540
  423.1 9.2 %copy-start.43 = (f32[4]{0:T(128)S(1)}, f32[4]{0:T(128)}, u32[]{:S(2)}) copy-start(f32[4]{0:T(128)} %slice_reduce_fusion.4) | copy-start | bytes 52
  423.1 11.3 %copy-start.19 = (f32[4,32,256]{2,1,0:T(8,128)S(1)}, f32[4,32,256]{2,1,0:T(8,128)}, u32[]{:S(2)}) copy-start(f32[4,32,256]{2,1,0:T(8,128)} %get-tuple-element.142) | copy-start | bytes 393220
  427.9 11.3 %copy-start.2 = (f32[1024,256]{1,0:T(8,128)S(1)}, f32[1024,256]{1,0:T(8,128)}, u32[]{:S(2)}) copy-start(f32[1024,256]{1,0:T(8,128)} %get-tuple-element.97) | copy-start | bytes 3145732
  427.9 11.3 %copy-start.8 = (f32[4,256,256]{2,1,0:T(8,128)S(1)}, f32[4,256,256]{2,1,0:T(8,128)}, u32[]{:S(2)}) copy-start(f32[4,256,256]{2,1,0:T(8,128)} %get-tuple-element.241) | copy-start | bytes 3145732
  427.9 11.3 %copy-start.18 = (f32[4,3,256]{2,1,0:T(4,128)S(1)}, f32[4,3,256]{2,1,0:T(4,128)}, u32[]{:S(2)}) copy-start(f32[4,3,256]{2,1,0:T(4,128)} %copy-done.17) | copy-start | bytes 36868
  427.9 11.3 %collective-permute-start.1 = (f32[4,256,256]{2,1,0:T(8,128)S(1)}, f32[4,256,256]{2,1,0:T(8,128)}, u32[]{:S(2)}, u32[]{:S(2)}) collective-permute-start(f32[4,256,256]{2,1,0:T(8,128)S(1)} %constant_dynamic-update-slice_fusion), channel_id=1, source_target_pairs={{0,1},{1,0},{2,3},{3,2},{4,5},{5,4},{6,7},{7,6},{8,9},{9,8},{10,11... | collective-permute-start | bytes 3145736 | tf_op jit(solution)/shard_map/ppermute | solution.py:294
  434.4 4.3 copy-start.47
  434.4 4.8 copy-start.22
  434.4 4.8 copy-start.24
  434.4 4.8 copy-start.26
  439.3 2.8 copy-start.32
  439.3 2.8 copy-start.34
  439.3 2.8 copy-start.36
  439.3 2.8 copy-start.38
  442.5 1.0 copy-start
  444.6 2.6 copy-start.30
  444.6 7.2 collective-permute-start.2
  452.6 3.8 copy-start.4
  454.0 2.4 copy-start.5
  456.3 2.0 copy-start.10
  458.3 1.6 copy-start.3
  463.9 2.1 copy-start.6
  466.0 1.7 copy-start.7
  466.1 2.1 copy-start.9
  467.7 1.6 copy-start.20
  802.2 2.4 copy-start.27
  803.2 6.3 copy-start.13
  807.2 9.1 %collective-permute-start.3 = (f32[2048,128]{1,0:T(8,128)S(1)}, f32[2048,128]{1,0:T(8,128)S(1)}, u32[]{:S(2)}, u32[]{:S(2)}) collective-permute-start(f32[2048,128]{1,0:T(8,128)S(1)} %bitcast.141), channel_id=1, source_target_pairs={{0,1},{1,0},{2,3},{3,2},{4,5},{5,4},{6,7},{7,6},{8,9},{9,8},{10,11... | collective-permute-start | bytes 3145736 | tf_op jit(solution)/shard_map/ppermute | solution.py:294
  810.9 9.3 %slice-start = ((s8[8388608]{0:T(1024)(128)(4,1)}), s8[4194304]{0:T(1024)(128)(4,1)S(1)}, s32[]{:S(2)}) async-start(s8[8388608]{0:T(1024)(128)(4,1)} %bitcast.127), calls=%async_computation | async-start | bytes 8388608
  816.3 4.0 slice-start.1
  816.5 2.5 copy-start.11
  820.3 3.4 copy-start.12

commit v6 on v5

--- a/solution.py
+++ b/solution.py
@@ -56,14 +56,21 @@
 GROUP = 4
 
 
-def exchange_kernel(length, reverse, orders, jobs, part_ref, log_ref, *refs):
+def exchange_kernel(length, reverse, orders, jobs, head_dim, log_ref, *refs):
     refs = list(refs)
+    if head_dim:
+        front_ins = [refs.pop(0) for _ in range(8)]
+    else:
+        part_ref = refs.pop(0)
     sources = [refs.pop(0) for _ in range(2 if orders else 0)]
     job_refs = [[refs.pop(0) for _ in range(job[2])] for job in jobs]
     out_ref = refs.pop(0)
+    if head_dim:
+        low_ref = refs.pop(0)
     steps = []
     for (make, plan, _), inputs in zip(jobs, job_refs):
-        steps += make(inputs, refs.pop(0), plan)
+        more = [low_ref] if make is intra_steps else []
+        steps += make(inputs + more, refs.pop(0), plan)
     targets = [refs.pop(0) for _ in range(4 * len(orders))]
     (
         parts,
@@ -82,7 +89,10 @@
         stage_sem,
         place_sem,
         staged,
+        *front_keeps,
     ) = refs
+    if head_dim:
+        part_ref = front_keeps.pop(0)
     me = lax.axis_index("seq")
     bits = (length - 1).bit_length()
     placed = arrange_copies(bits, orders, me, staged, targets, place_sem)
@@ -100,7 +110,7 @@
         rank + 2 - 4 * (rank // 2),
         3 - rank,
     )
-    micro = part_ref.shape[0]
+    micro = parts.shape[0]
     planes = length // GROUP
     begins, ends = plane == 0, plane == planes - 1
     if reverse:
@@ -175,9 +185,46 @@
 
     for slot in range(3):
         log_copy(slot).start()
-    for m in range(micro):
+    def front_body(x, halo, weight, bias, b, tail, low):
+        m = pl.program_id(0)
+        front_kernel(
+            head_dim,
+            front_ins[0],
+            front_ins[1],
+            x,
+            halo,
+            weight,
+            bias,
+            b,
+            tail,
+            low,
+            part_ref.at[pl.ds(m, 1)],
+            *front_keeps,
+        )
         for slot in range(3):
             part_copy(m, slot).start()
+
+    if head_dim:
+        x_ref, halo_ref, weight_ref, bias_ref, b_ref, tail_ref = front_ins[2:]
+        by_micro = lambda shape: pl.BlockSpec((1,) + shape[1:], lambda m: (m, 0, 0))
+        fixed = lambda shape: pl.BlockSpec(shape, lambda m: (0, 0))
+        pltpu.emit_pipeline(
+            front_body,
+            grid=(micro,),
+            in_specs=[
+                pl.BlockSpec((1, 1) + x_ref.shape[2:], lambda m: (1, m, 0, 0)),
+                by_micro(halo_ref.shape),
+                fixed(weight_ref.shape),
+                fixed(bias_ref.shape),
+                by_micro(b_ref.shape),
+                by_micro(tail_ref.shape),
+            ],
+            out_specs=[by_micro(low_ref.shape)],
+        )(x_ref, halo_ref, weight_ref, bias_ref, b_ref, tail_ref, low_ref)
+    else:
+        for m in range(micro):
+            for slot in range(3):
+                part_copy(m, slot).start()
     logs[rank] = log_ref[rank]
     for m in range(micro):
         parts[m, rank] = part_ref[m, :, own_columns(rank)]
@@ -233,8 +280,13 @@
         copy.wait()
 
 
-def exchange(parts, logs, reverse, sources=(), orders=(), jobs=()):
-    micro, rows, columns = parts.shape
+def exchange(parts, logs, reverse, sources=(), orders=(), jobs=(), head_dim=0):
+    if head_dim:
+        state_shape = (parts[6].shape[0], parts[6].shape[2], parts[2].shape[3])
+        low_shape = parts[2].shape[1:]
+    else:
+        state_shape = parts.shape
+    micro, rows, columns = state_shape
     quarter = columns // GROUP
     length = lax.axis_size("seq")
     spread = logs.reshape(micro, GROUP, quarter).transpose(1, 0, 2)
@@ -254,10 +306,15 @@
     smem = pl.BlockSpec(memory_space=pltpu.SMEM)
     job_specs = [smem if item.dtype == jnp.int32 else hbm for item in job_inputs]
     out, *arranged = pl.pallas_call(
-        functools.partial(exchange_kernel, length, reverse, orders, plans),
-        out_shape=[jax.ShapeDtypeStruct(parts.shape, jnp.float32)] + arranged,
-        in_specs=[vmem] * 2 + [hbm] * len(sources) + job_specs,
-        out_specs=[vmem] + [hbm] * len(arranged),
+        functools.partial(exchange_kernel, length, reverse, orders, plans, head_dim),
+        out_shape=[jax.ShapeDtypeStruct(state_shape, jnp.float32)]
+        + ([jax.ShapeDtypeStruct(low_shape, jnp.bfloat16)] if head_dim else [])
+        + arranged,
+        in_specs=[vmem]
+        + ([smem, smem] + [hbm] * 6 if head_dim else [vmem])
+        + [hbm] * len(sources)
+        + job_specs,
+        out_specs=[vmem] + [hbm] * (len(arranged) + (1 if head_dim else 0)),
         scratch_shapes=[
             pltpu.VMEM(shape, jnp.float32),
             pltpu.VMEM((GROUP, micro, quarter), jnp.float32),
@@ -275,7 +332,17 @@
             pltpu.SemaphoreType.DMA((2,)),
             pltpu.SemaphoreType.DMA((max(count, 1) * max(length // 2, 1),)),
             pltpu.VMEM((2,) + sources[0].shape if sources else (2, 16, 128), jnp.bfloat16),
-        ],
+        ]
+        + (
+            [
+                pltpu.VMEM(state_shape, jnp.float32),
+                pltpu.VMEM((low_shape[1] + 8, columns), jnp.float32),
+                pltpu.VMEM(low_shape[1:], jnp.bfloat16),
+                pltpu.VMEM(low_shape[1:], jnp.bfloat16),
+            ]
+            if head_dim
+            else []
+        ),
         compiler_params=pltpu.CompilerParams(
             collective_id=1 if reverse else 0,
             has_side_effects=True,
@@ -285,7 +352,9 @@
             flops=EXCHANGE_COST, bytes_accessed=0, transcendentals=0
         ),
         name="exchange_back" if reverse else "exchange",
-    )(parts, spread, *sources, *job_inputs)
+    )(spread, *(parts if head_dim else (parts,)), *sources, *job_inputs)
+    if head_dim:
+        out = (out, arranged.pop(0))
     return out, arranged[:results], arranged[results:]
 
 
@@ -317,7 +386,7 @@
     shares = (
         ((3, 3), (2, 3), (3, 0), (0, 2)),
         ((3, 2), (3, 3), (3, 0), (0, 2)),
-        ((3, 2), (2, 3), (3, 0), (0, 3)),
+        ((4, 1), (2, 2), (3, 1), (2, 1)),
     )
     return [
         [
@@ -611,7 +680,7 @@
                     chain_count += 1
                 first += sum(widths)
             waves.append(wave)
-    narrow_order = parts[min(1, len(parts) - 1)][0]
+    narrow_order = parts[0][0]
     narrow = (chain_count, narrow_ref, 0, None, 0, narrow_order, refs.pop(0), take(bits))
     vector_sums, vector_recvs, gain_sum, local_sem, send_sem, recv_sem = refs
 
@@ -740,7 +809,7 @@
         else:
             vector_out_ref[...] = total
 
-    gather_bits = tuple(range(bits - 1, 1, -1)) + tuple(range(min(bits, 2)))
+    gather_bits = tuple(reversed(range(bits)))
 
     def gather_copies(phase):
         free = gather_bits[:phase]
@@ -1171,7 +1240,7 @@
 
 
 def intra_step(inputs, out_ref, head_dim, micro):
-    base_ref, starts_ref, x_ref, b_ref, c_ref, run_ref, step_ref, skip_ref = inputs
+    base_ref, starts_ref, b_ref, c_ref, run_ref, step_ref, skip_ref, x_ref = inputs
     _, count, inner = x_ref.shape
     heads = run_ref.shape[1]
     group = min(HEAD_GROUP, heads)
@@ -1676,39 +1745,14 @@
     broad_groups, broad = heads // broad_group, broad_group * head_dim
     broad_token, broad_half = (1, length, broad), (1, 1, length, broad)
     broad_row, broad_state = (1, broad_group, length), (1, state_size, broad)
-    x_low, device_state = blocked(
-        functools.partial(front_kernel, head_dim),
-        "front",
-        (micro, broad_groups),
-        [
-            base_item,
-            starts_item,
-            (gate_x, broad_half, in_x),
-            (halo, (1, 8, broad), in_token),
-            (conv_weight, (taps, broad), in_flat),
-            (conv_row, (1, broad), in_flat),
-            (b_low, map_block, in_map),
-            (tail * delta, broad_row, in_row),
-        ],
-        [
-            (whole, jnp.bfloat16, broad_token, in_token),
-            (state_shape, jnp.float32, broad_state, in_state),
-        ],
-        [
-            pltpu.VMEM((length + 8, broad), jnp.float32),
-            pltpu.VMEM((length, broad), jnp.bfloat16),
-            pltpu.VMEM((length, broad), jnp.bfloat16),
-        ],
-        20,
-    )
     exchange_log = jnp.where(device_live[:, None] > 0.0, device_log, DEAD)
     exchange_log = jnp.repeat(exchange_log, head_dim, axis=1)
     plans = scatter_plans(inner, axis_bits("seq"))
     parts = plans[-1]
     orders = tuple(order for order, _ in parts)
     tiled = (width >> axis_bits("seq")) % 128 == 0
-    incoming, (grad_gate_n, intra), arranged = exchange(
-        device_state,
+    (incoming, x_low), (grad_gate_n, intra), arranged = exchange(
+        (base[None], starts, gate_x, halo, conv_weight, conv_row, b_low, tail * delta),
         exchange_log,
         False,
         (cot_flat, normed_low) if tiled else (),
@@ -1718,10 +1762,11 @@
             (
                 intra_steps,
                 head_dim,
-                (base[None], starts, x_low, b_low, c_low, running_two, delta, skip_row),
+                (base[None], starts, b_low, c_low, running_two, delta, skip_row),
                 whole,
             ),
         ],
+        head_dim,
     )
     grad_gate_n = grad_gate_n.reshape(whole)
     if not tiled:
@@ -1915,7 +1960,7 @@
     share_bc = 2 * state_size // head_count
     own_bc = lax.dynamic_slice_in_dim(bc_flat, lax.axis_index("head") * share_bc, share_bc, 1)
     across = share_bc + heads
-    side = min(1, len(parts) - 1)
+    side = 0
     narrow_high, narrow_rest = halves_of(jnp.concatenate([own_bc, grad_steps], axis=1))
     both = jnp.concatenate([narrow_high, narrow_rest], axis=1)
     narrow = jnp.concatenate(

time: 838 us -> 833 us (level)
    pallas_call x3 -> x2, Pallas kernels: 176 us -> 166 us  [blocked(): pl.pallas_call(kernel, grid=grid, in_specs=[spec(item) for item in ins],...]
where the time goes in v6:
time: 833 us; the launch traced here: 819 us
  Pallas kernels  727 us (87%)
  local copies, waits for them, and re-layouts  46.9 us (6%)
  other arithmetic  26.4 us (3%)
  starting transfers between devices  11.1 us (1%)
    pallas_call x1, Pallas kernels, finish(): pl.pallas_call(functools.partial(finish_kernel, plans, paired, bits, bloc...  325 us
    pallas_call x2, Pallas kernels, exchange(): pl.pallas_call(functools.partial(exchange_kernel, length, reverse, orders...  205 us
    pallas_call x2, Pallas kernels, blocked(): pl.pallas_call(kernel, grid=grid, in_specs=[spec(item) for item in ins],...  166 us
    pallas_call x1, Pallas kernels, project(): pl.pallas_call(project_kernel, grid=(columns // tile,), in_specs=[pl.Bloc...  29.6 us
    unnamed x111, local copies, waits for them, and re-layouts  18.2 us
  transfers between devices with their start and end apart: 4, of which 1 were waited for; matrix products, arithmetic and copies ran while one was open for 3% of the time, Pallas kernels for 0%

profile of v6, /device:TPU:1, one launch (start us, length us, event | category | flops | bytes accessed | tf_op | source)
XLA Modules:
  0.0 819.1 jit_solution(15959106025512659918)
XLA Ops:
  0.6 1.9 copy.92.step_ref.refs_35_
  2.6 29.6 %project.1 = (bf16[1024,2048]{1,0:T(8,128)(2,1)}, f32[2,1024,2048]{2,1,0:T(8,128)}, f32[1024,256]{1,0:T(8,128)}, f32[1024,32]{1,0:T(8,128)}) custom-call(bf16[1024,2048]{1,0:T(8,128)(2,1)} %bitcast.134, f32[1,2048]{1,0:T(1,128)} %bitcast.167, bf16[2048,2,2048]{2,1,0:T(2,128)(2,1)} %refs_29_.1, bf16[2048,256]{1,0:T(8,128)(2,1)} %refs_34_.1, ...), custom_call_target="tpu_custom_call" | custom-call | flops 17179869184 | tf_op jit(solution)/shard_map/project/pallas_call | solution.py:1140
  32.2 0.8 slice.240
  32.9 1.0 slice_bitcast_fusion
  34.0 3.9 collective-permute-start
  37.9 0.6 compare_reduce_fusion
  39.3 0.7 slice_reduce_fusion.4
  41.0 0.7 broadcast_in_dim_reshape.3.refs_18_.skip_ref
  41.7 1.4 compare_select_fusion.2
  44.2 0.6 copy.109
  44.8 0.8 exponential_multiply_fusion
  46.4 1.7 multiply_convert_fusion
  48.1 0.9 fusion.35
  49.0 0.7 pad.38.refs_3_.halo_ref
  49.7 105.8 %exchange.1 = (f32[4,128,2048]{2,1,0:T(8,128)}, bf16[4,256,2048]{2,1,0:T(8,128)(2,1)}, f32[1024,2048]{1,0:T(8,128)}, f32[4,256,2048]{2,1,0:T(8,128)}, bf16[1024,...) custom-call(f32[4,4,512]{2,1,0:T(4,128)} %bitcast.155, ...), custom_call_target="tpu_custom_call" | custom-call | flops 99999997952 | tf_op jit(solution)/shard_map/exchange/pallas_call | solution.py:308
  155.6 30.1 %gate.1 = (bf16[4,256,2048]{2,1,0:T(8,128)(2,1)}, bf16[4,256,2048]{2,1,0:T(8,128)(2,1)}, bf16[2,4,256,2048]{3,2,1,0:T(8,128)(2,1)}, bf16[4,256,2048]{2,1,0:T(8,1...) custom-call(f32[4,256,2048]{2,1,0:T(8,128)} %get-tuple-element.103.intra_ref, ...), custom_call_target="tpu_custom_call" | custom-call | flops 30000001024 | bytes 80617472 | tf_op jit(solution)/shard_map/gate/pallas_call | solution.py:1616
  185.6 99.6 %exchange_back.1 = (f32[4,128,2048]{2,1,0:T(8,128)}, f32[1024,2048]{1,0:T(8,128)}, f32[1024,2048]{1,0:T(8,128)}) custom-call(f32[4,4,512]{2,1,0:T(4,128)} %bitcast.156, f32[4,128,2048]{2,1,0:T(8,128)} %get-tuple-element.109.refs_0_, bf16[1024,1024]{1,0:T(8,128)(2,1)} %get-tuple-element.110.refs_1_, bf16[1024,1024]{1,0:T(8,128)(2,1)} %get-tuple-element.111.refs_2_, ...), custom_call_target="tpu_custom_call" | custom-call | flops 99999997952 | tf_op jit(solution)/shard_map/exchange_back/pallas_call | solution.py:308
  285.2 136.4 %back.1 = (bf16[2,4,256,2048]{3,2,1,0:T(8,128)(2,1)}, f32[4,8,2048]{2,1,0:T(8,128)}, f32[4,8,2048]{2,1,0:T(8,128)}, f32[4,8,2048]{2,1,0:T(8,128)}, f32[4,32,256]...) custom-call(s32[1]{0:T(128)} %bitcast.8.refs_0_.refs_12_.base_ref, ...), custom_call_target="tpu_custom_call", output_to_operand_aliasing={{0}: (17, {})} | custom-call | flops 80000000000 | bytes 44351540 | tf_op jit(solution)/shard_map/back/pallas_call | solution.py:1616
  421.7 1.0 reduce_sum.126
  424.7 0.6 reduce_sum.127
  425.3 1.1 constant_dynamic-update-slice_fusion.1
  426.5 2.2 collective-permute-start.1
  428.7 1.0 slice_reduce_fusion
  429.9 1.0 slice.208
  431.0 1.0 add_bitcast_fusion
  432.0 1.0 copy.98
  433.0 1.0 copy.97
  434.0 3.2 fusion.32
  437.9 2.7 multiply_reduce_fusion.3
  441.1 0.9 copy-done
  443.2 1.5 collective-permute-start.2
  444.7 1.1 slice.254
  445.7 0.9 concatenate.53
  446.7 0.6 pad_bitcast_fusion.refs_28_
  447.3 3.1 collective-permute-done.2
  450.4 0.8 slice_add_fusion.1
  451.1 1.5 scatter-add.4
  452.6 1.2 constant_dynamic-slice_fusion
  453.8 1.1 subtract_convert_fusion
  455.0 1.0 broadcast_multiply_fusion
  456.0 0.8 copy-done.10
  456.9 1.0 fusion.16
  458.5 1.0 fusion.17
  459.5 1.2 fusion.1
  460.7 1.8 copy.104
  462.5 1.1 slice.259
  463.6 1.1 slice.258
  464.6 1.2 pad_maximum_fusion.2.refs_33_
  466.7 1.2 pad_maximum_fusion.4
  467.9 1.7 dynamic_update_slice.3
  469.6 325.5 %finish.1 = (f32[128,2048]{1,0:T(8,128)}, f32[128,2048]{1,0:T(8,128)}, f32[128,2048]{1,0:T(8,128)}, f32[16,160,128]{2,1,0:T(8,128)}, f32[128,128]{1,0:T(8,128)},...) custom-call(bf16[1024,1024]{1,0:T(8,128)(2,1)} %get-tuple-element.99, ...), custom_call_target="tpu_custom_call" | custom-call | tf_op jit(solution)/shard_map/finish/pallas_call | solution.py:978
  795.1 1.0 slice.225
  796.1 1.4 slice.224
  798.2 0.6 reshape.260
  799.1 1.0 copy.103
  800.1 3.4 collective-permute-start.3
  803.5 1.4 pad_maximum_fusion
  805.0 2.9 copy.102
  809.7 0.7 fusion.36
  810.5 1.5 pad_maximum_fusion.1
  811.9 1.0 copy-done.11
  813.0 1.3 copy.117
  814.3 3.4 copy.118
  817.7 1.0 copy.119
  (157 shorter events, 11.5 us)
Async XLA Ops:
  2.6 36.0 %copy-start.39 = (s32[2,3]{1,0:T(2,128)S(1)}, s32[2,3]{1,0:T(2,128)}, u32[]{:S(2)}) copy-start(s32[2,3]{1,0:T(2,128)} %param.35) | copy-start | bytes 76
  2.6 38.3 %copy-start.46 = (f32[32]{0:T(128)S(1)}, f32[32]{0:T(128)}, u32[]{:S(2)}) copy-start(f32[32]{0:T(128)} %param.26) | copy-start | bytes 388
  2.6 38.3 %copy-start.40 = (f32[4,256]{1,0:T(4,128)S(1)}, f32[4,256]{1,0:T(4,128)}, u32[]{:S(2)}) copy-start(f32[4,256]{1,0:T(4,128)} %param.29) | copy-start | bytes 12292
  2.6 38.3 %copy-start.45 = (f32[32]{0:T(128)S(1)}, f32[32]{0:T(128)}, u32[]{:S(2)}) copy-start(f32[32]{0:T(128)} %param.31) | copy-start | bytes 388
  2.6 39.1 %copy-start.41 = (f32[32]{0:T(128)S(1)}, f32[32]{0:T(128)}, u32[]{:S(2)}) copy-start(f32[32]{0:T(128)} %param.25) | copy-start | bytes 388
  34.0 12.3 %collective-permute-start = (f32[4,3,2304]{2,1,0:T(4,128)S(1)}, f32[4,3,2304]{2,1,0:T(4,128)S(1)}, u32[]{:S(2)}, u32[]{:S(2)}) collective-permute-start(f32[4,3,2304]{2,1,0:T(4,128)S(1)} %pad_maximum_fusion.10), channel_id=1, source_target_pairs={{0,2},{2,4},{4,6},{6,8},{8,10},{10,12},{12,14},{14,16},{16,18},{18... | collective-permute-start | bytes 331784 | tf_op jit(solution)/shard_map/ppermute | solution.py:18
  39.3 7.0 copy-start.21
  39.3 7.0 copy-start.23
  39.3 7.0 copy-start.25
  40.9 2.3 copy-start.42
  40.9 5.4 copy-start.31
  40.9 5.4 copy-start.33
  40.9 5.4 copy-start.35
  40.9 5.4 copy-start.37
  41.7 4.7 copy-start.1
  41.7 4.7 copy-start.44
  43.3 4.7 copy-start.14
  43.9 5.0 copy-start.28
  46.3 3.4 copy-start.17
  285.2 138.1 %copy-start.16 = (f32[4,8,2048]{2,1,0:T(8,128)S(1)}, f32[4,8,2048]{2,1,0:T(8,128)}, u32[]{:S(2)}) copy-start(f32[4,8,2048]{2,1,0:T(8,128)} %get-tuple-element.143) | copy-start | bytes 786436
  421.7 4.7 copy-start.15
  421.7 9.2 %copy-start.29 = (f32[4,32,1]{1,0,2:T(4,128)S(1)}, f32[4,32,1]{1,0,2:T(4,128)}, u32[]{:S(2)}) copy-start(f32[4,32,1]{1,0,2:T(4,128)} %copy-done.28) | copy-start | bytes 1540
  421.7 9.2 %copy-start.43 = (f32[4]{0:T(128)S(1)}, f32[4]{0:T(128)}, u32[]{:S(2)}) copy-start(f32[4]{0:T(128)} %slice_reduce_fusion.4) | copy-start | bytes 52
  421.7 11.3 %copy-start.19 = (f32[4,32,256]{2,1,0:T(8,128)S(1)}, f32[4,32,256]{2,1,0:T(8,128)}, u32[]{:S(2)}) copy-start(f32[4,32,256]{2,1,0:T(8,128)} %get-tuple-element.140) | copy-start | bytes 393220
  426.4 11.3 %copy-start.2 = (f32[1024,256]{1,0:T(8,128)S(1)}, f32[1024,256]{1,0:T(8,128)}, u32[]{:S(2)}) copy-start(f32[1024,256]{1,0:T(8,128)} %get-tuple-element.97) | copy-start | bytes 3145732
  426.5 11.3 %copy-start.8 = (f32[4,256,256]{2,1,0:T(8,128)S(1)}, f32[4,256,256]{2,1,0:T(8,128)}, u32[]{:S(2)}) copy-start(f32[4,256,256]{2,1,0:T(8,128)} %get-tuple-element.239) | copy-start | bytes 3145732
  426.5 11.3 %copy-start.18 = (f32[4,3,256]{2,1,0:T(4,128)S(1)}, f32[4,3,256]{2,1,0:T(4,128)}, u32[]{:S(2)}) copy-start(f32[4,3,256]{2,1,0:T(4,128)} %copy-done.17) | copy-start | bytes 36868
  426.5 11.3 %collective-permute-start.1 = (f32[4,256,256]{2,1,0:T(8,128)S(1)}, f32[4,256,256]{2,1,0:T(8,128)}, u32[]{:S(2)}, u32[]{:S(2)}) collective-permute-start(f32[4,256,256]{2,1,0:T(8,128)S(1)} %constant_dynamic-update-slice_fusion), channel_id=1, source_target_pairs={{0,1},{1,0},{2,3},{3,2},{4,5},{5,4},{6,7},{7,6},{8,9},{9,8},{10,11... | collective-permute-start | bytes 3145736 | tf_op jit(solution)/shard_map/ppermute | solution.py:363
  433.0 4.3 copy-start.47
  433.0 4.8 copy-start.22
  433.0 4.8 copy-start.24
  433.0 4.8 copy-start.26
  437.8 2.8 copy-start.32
  437.8 2.8 copy-start.34
  437.8 2.8 copy-start.36
  437.9 2.8 copy-start.38
  441.1 1.0 copy-start
  443.1 2.6 copy-start.30
  443.2 7.2 collective-permute-start.2
  451.1 3.8 copy-start.4
  452.6 2.4 copy-start.5
  454.9 2.0 copy-start.10
  456.9 1.6 copy-start.3
  462.5 2.1 copy-start.6
  464.6 1.7 copy-start.7
  464.6 2.1 copy-start.9
  466.3 1.6 copy-start.20
  795.1 2.4 copy-start.27
  796.1 7.4 copy-start.13
  800.1 10.2 %collective-permute-start.3 = (f32[2048,128]{1,0:T(8,128)S(1)}, f32[2048,128]{1,0:T(8,128)S(1)}, u32[]{:S(2)}, u32[]{:S(2)}) collective-permute-start(f32[2048,128]{1,0:T(8,128)S(1)} %bitcast.141), channel_id=1, source_target_pairs={{0,1},{1,0},{2,3},{3,2},{4,5},{5,4},{6,7},{7,6},{8,9},{9,8},{10,11... | collective-permute-start | bytes 3145736 | tf_op jit(solution)/shard_map/ppermute | solution.py:363
  805.0 9.3 %slice-start = ((s8[8388608]{0:T(1024)(128)(4,1)}), s8[4194304]{0:T(1024)(128)(4,1)S(1)}, s32[]{:S(2)}) async-start(s8[8388608]{0:T(1024)(128)(4,1)} %bitcast.127), calls=%async_computation | async-start | bytes 8388608
  810.3 4.0 slice-start.1
  810.5 2.5 copy-start.11
  814.3 3.4 copy-start.12

commit v7 on v6

--- a/solution.py
+++ b/solution.py
@@ -1681,7 +1681,7 @@
     )
     gate_x = gate_x.reshape(2, micro, length, inner)
     bc_pre = bc_pre.reshape(micro, length, 2 * state_size)
-    delta_pre = delta_pre.T
+    delta_pre = delta_pre.reshape(micro, length, heads).transpose(0, 2, 1)
     left = shifted(
         jnp.concatenate(
             [gate_x[1, :, length - taps + 1 :], bc_pre[:, length - taps + 1 :]], axis=-1
@@ -1702,13 +1702,6 @@
     b_low, c_low = bc_low[..., :state_size], bc_low[..., state_size:]
     (delta, decay), rate_back = jax.vjp(step_sizes, delta_pre, dt_bias, a_log)
 
-    def by_micro(array):
-        return array.reshape(heads, micro, length).transpose(1, 0, 2)
-
-    def by_head(array):
-        return array.transpose(1, 0, 2).reshape(heads, total)
-
-    delta, decay = by_micro(delta), by_micro(decay)
     order = jnp.arange(length)
     running = jnp.einsum(
         "mhj,ji->mhi",
@@ -1904,8 +1897,7 @@
     grad_bc = all_sum(jnp.concatenate([grad_b, grad_c], axis=-1), "head")
     pairs = conv_rows[:, taps + 2].reshape(micro, heads, head_dim)
     kept = jnp.sum(pairs, axis=-1) * jnp.exp(device_log) * device_live[:, None]
-    grad_decay = by_head(fading + kept[:, :, None])
-    grad_delta_pre, grad_dt_bias, grad_a_log = rate_back((by_head(direct), grad_decay))
+    grad_delta_pre, grad_dt_bias, grad_a_log = rate_back((direct, fading + kept[:, :, None]))
     conv_rows = jnp.sum(conv_rows, axis=0)
     grad_conv_weight, grad_conv_bias = conv_rows[:taps], conv_rows[taps]
     grad_d_skip = jnp.sum(conv_rows[taps + 1].reshape(heads, head_dim), axis=-1)
@@ -1922,7 +1914,7 @@
     grad_bc_pre = grad_bc_ext[:, taps - 1 :].at[:, length - taps + 1 :].add(right_bc)
     bc_flat = grad_bc_pre.reshape(total, 2 * state_size)
     grad_gate_x = grad_gate_x.reshape(2, total, inner)
-    grad_steps = grad_delta_pre.T
+    grad_steps = grad_delta_pre.transpose(0, 2, 1).reshape(total, heads)
     narrow_row = jnp.concatenate([bc_flat * (1.0 / head_count), grad_steps], axis=1)
     if paired:
         row_inputs = (

time: 833 us -> 835 us (level)
    unnamed x111 -> x105, local copies, waits for them, and re-layouts: 18.2 us -> 19.7 us
where the time goes in v7:
time: 835 us; the launch traced here: 821 us
  Pallas kernels  727 us (87%)
  local copies, waits for them, and re-layouts  50.3 us (6%)
  other arithmetic  24.8 us (3%)
  starting transfers between devices  11 us (1%)
    pallas_call x1, Pallas kernels, finish(): pl.pallas_call(functools.partial(finish_kernel, plans, paired, bits, bloc...  326 us
    pallas_call x2, Pallas kernels, exchange(): pl.pallas_call(functools.partial(exchange_kernel, length, reverse, orders...  205 us
    pallas_call x2, Pallas kernels, blocked(): pl.pallas_call(kernel, grid=grid, in_specs=[spec(item) for item in ins],...  166 us
    pallas_call x1, Pallas kernels, project(): pl.pallas_call(project_kernel, grid=(columns // tile,), in_specs=[pl.Bloc...  29.6 us
    unnamed x105, local copies, waits for them, and re-layouts  19.7 us
  transfers between devices with their start and end apart: 4, of which 1 were waited for; matrix products, arithmetic and copies ran while one was open for 3% of the time, Pallas kernels for 0%

profile of v7, /device:TPU:1, one launch (start us, length us, event | category | flops | bytes accessed | tf_op | source)
XLA Modules:
  0.0 821.0 jit_solution(13100570379817732715)
XLA Ops:
  0.6 1.9 copy.86.step_ref.refs_35_
  2.6 29.6 %project.1 = (bf16[1024,2048]{1,0:T(8,128)(2,1)}, f32[2,1024,2048]{2,1,0:T(8,128)}, f32[1024,256]{1,0:T(8,128)}, f32[1024,32]{1,0:T(8,128)}) custom-call(bf16[1024,2048]{1,0:T(8,128)(2,1)} %bitcast.116, f32[1,2048]{1,0:T(1,128)} %bitcast.146, bf16[2048,2,2048]{2,1,0:T(2,128)(2,1)} %refs_29_.1, bf16[2048,256]{1,0:T(8,128)(2,1)} %refs_34_.1, ...), custom_call_target="tpu_custom_call" | custom-call | flops 17179869184 | tf_op jit(solution)/shard_map/project/pallas_call | solution.py:1140
  32.2 0.9 slice.240
  33.0 1.0 slice_bitcast_fusion
  34.1 3.9 collective-permute-start
  38.0 0.6 compare_reduce_fusion
  39.4 0.7 slice_reduce_fusion.4
  41.1 0.7 broadcast_in_dim_reshape.3.refs_18_.skip_ref
  41.8 1.2 copy.88
  44.4 1.0 fusion.31
  46.1 1.7 multiply_convert_fusion
  47.8 0.9 fusion.35
  48.7 0.7 pad.38.refs_3_.halo_ref
  49.5 105.9 %exchange.1 = (f32[4,128,2048]{2,1,0:T(8,128)}, bf16[4,256,2048]{2,1,0:T(8,128)(2,1)}, f32[1024,2048]{1,0:T(8,128)}, f32[4,256,2048]{2,1,0:T(8,128)}, bf16[1024,...) custom-call(f32[4,4,512]{2,1,0:T(4,128)} %bitcast.134, ...), custom_call_target="tpu_custom_call" | custom-call | flops 99999997952 | tf_op jit(solution)/shard_map/exchange/pallas_call | solution.py:308
  155.3 30.0 %gate.1 = (bf16[4,256,2048]{2,1,0:T(8,128)(2,1)}, bf16[4,256,2048]{2,1,0:T(8,128)(2,1)}, bf16[2,4,256,2048]{3,2,1,0:T(8,128)(2,1)}, bf16[4,256,2048]{2,1,0:T(8,1...) custom-call(f32[4,256,2048]{2,1,0:T(8,128)} %get-tuple-element.103.intra_ref, ...), custom_call_target="tpu_custom_call" | custom-call | flops 30000001024 | bytes 80617472 | tf_op jit(solution)/shard_map/gate/pallas_call | solution.py:1616
  185.3 99.4 %exchange_back.1 = (f32[4,128,2048]{2,1,0:T(8,128)}, f32[1024,2048]{1,0:T(8,128)}, f32[1024,2048]{1,0:T(8,128)}) custom-call(f32[4,4,512]{2,1,0:T(4,128)} %bitcast.135, f32[4,128,2048]{2,1,0:T(8,128)} %get-tuple-element.109.refs_0_, bf16[1024,1024]{1,0:T(8,128)(2,1)} %get-tuple-element.110.refs_1_, bf16[1024,1024]{1,0:T(8,128)(2,1)} %get-tuple-element.111.refs_2_, ...), custom_call_target="tpu_custom_call" | custom-call | flops 99999997952 | tf_op jit(solution)/shard_map/exchange_back/pallas_call | solution.py:308
  284.8 136.4 %back.1 = (bf16[2,4,256,2048]{3,2,1,0:T(8,128)(2,1)}, f32[4,8,2048]{2,1,0:T(8,128)}, f32[4,8,2048]{2,1,0:T(8,128)}, f32[4,8,2048]{2,1,0:T(8,128)}, f32[4,32,256]...) custom-call(s32[1]{0:T(128)} %bitcast.7.refs_0_.refs_12_.base_ref, ...), custom_call_target="tpu_custom_call", output_to_operand_aliasing={{0}: (17, {})} | custom-call | flops 80000000000 | bytes 44351540 | tf_op jit(solution)/shard_map/back/pallas_call | solution.py:1616
  421.2 1.6 reduce_sum.126
  422.9 1.2 constant_dynamic-update-slice_fusion.1
  424.1 1.1 constant_dynamic-update-slice_fusion
  425.2 2.2 collective-permute-start.1
  428.7 1.4 copy.102
  430.0 1.5 fusion.38
  432.3 1.0 slice_reduce_fusion
  433.5 1.0 slice.208
  434.5 0.8 fusion.28
  435.3 1.8 fusion.32
  437.1 1.0 copy.91
  438.1 1.2 negate_multiply_fusion
  439.4 2.8 multiply_reduce_fusion.3
  442.7 0.9 copy-done
  444.8 1.5 collective-permute-start.2
  446.3 1.1 slice.254
  447.4 0.9 concatenate.53
  448.3 0.6 pad_bitcast_fusion.refs_28_
  448.9 3.2 collective-permute-done.2
  452.1 0.8 slice_add_fusion.1
  452.9 1.5 scatter-add.4
  454.4 1.2 constant_dynamic-slice_fusion
  455.5 1.1 subtract_convert_fusion
  456.8 1.0 broadcast_multiply_fusion
  457.8 0.8 copy-done.10
  458.7 1.0 fusion.7
  460.2 1.0 fusion.8
  461.2 1.2 fusion.1
  462.5 1.8 copy.99
  464.3 1.1 slice.259
  465.3 1.1 slice.258
  466.4 1.2 pad_maximum_fusion.2.refs_33_
  468.5 1.2 pad_maximum_fusion.4
  469.7 1.7 dynamic_update_slice.3
  471.4 325.6 %finish.1 = (f32[128,2048]{1,0:T(8,128)}, f32[128,2048]{1,0:T(8,128)}, f32[128,2048]{1,0:T(8,128)}, f32[16,160,128]{2,1,0:T(8,128)}, f32[128,128]{1,0:T(8,128)},...) custom-call(bf16[1024,1024]{1,0:T(8,128)(2,1)} %get-tuple-element.99, ...), custom_call_target="tpu_custom_call" | custom-call | tf_op jit(solution)/shard_map/finish/pallas_call | solution.py:978
  797.0 1.0 slice.225
  798.0 1.4 slice.224
  801.0 1.0 copy.96
  802.0 3.4 collective-permute-start.3
  805.4 1.4 pad_maximum_fusion
  806.9 2.9 copy.95
  811.5 0.7 fusion.36
  812.4 1.5 pad_maximum_fusion.1
  813.8 1.0 copy-done.11
  814.9 1.3 copy.112
  816.2 3.4 copy.113
  819.6 1.0 copy.114
  (147 shorter events, 11.9 us)
Async XLA Ops:
  2.6 36.1 %copy-start.38 = (s32[2,3]{1,0:T(2,128)S(1)}, s32[2,3]{1,0:T(2,128)}, u32[]{:S(2)}) copy-start(s32[2,3]{1,0:T(2,128)} %param.35) | copy-start | bytes 76
  2.6 38.4 %copy-start.44 = (f32[32]{0:T(128)S(1)}, f32[32]{0:T(128)}, u32[]{:S(2)}) copy-start(f32[32]{0:T(128)} %param.26) | copy-start | bytes 388
  2.6 38.4 %copy-start.39 = (f32[4,256]{1,0:T(4,128)S(1)}, f32[4,256]{1,0:T(4,128)}, u32[]{:S(2)}) copy-start(f32[4,256]{1,0:T(4,128)} %param.29) | copy-start | bytes 12292
  2.6 38.4 %copy-start.42 = (f32[32]{0:T(128)S(1)}, f32[32]{0:T(128)}, u32[]{:S(2)}) copy-start(f32[32]{0:T(128)} %param.31) | copy-start | bytes 388
  2.6 40.4 %copy-start.40 = (f32[32]{0:T(128)S(1)}, f32[32]{0:T(128)}, u32[]{:S(2)}) copy-start(f32[32]{0:T(128)} %param.25) | copy-start | bytes 388
  32.2 13.9 %copy-start.1 = (f32[1024,256]{1,0:T(8,128)S(1)}, f32[1024,256]{1,0:T(8,128)}, u32[]{:S(2)}) copy-start(f32[1024,256]{1,0:T(8,128)} %get-tuple-element.97) | copy-start | bytes 3145732
  32.2 13.9 %copy-start.41 = (f32[256]{0:T(256)S(1)}, f32[256]{0:T(256)}, u32[]{:S(2)}) copy-start(f32[256]{0:T(256)} %param.30) | copy-start | bytes 3076
  34.1 12.0 %collective-permute-start = (f32[4,3,2304]{2,1,0:T(4,128)S(1)}, f32[4,3,2304]{2,1,0:T(4,128)S(1)}, u32[]{:S(2)}, u32[]{:S(2)}) collective-permute-start(f32[4,3,2304]{2,1,0:T(4,128)S(1)} %pad_maximum_fusion.10), channel_id=1, source_target_pairs={{0,2},{2,4},{4,6},{6,8},{8,10},{10,12},{12,14},{14,16},{16,18},{18... | collective-permute-start | bytes 331784 | tf_op jit(solution)/shard_map/ppermute | solution.py:18
  39.4 8.4 %copy-start.21 = (f32[4,256]{1,0:T(4,128)}, f32[4,256]{1,0:T(4,128)S(1)}, u32[]{:S(2)}) copy-start(f32[4,256]{1,0:T(4,128)S(1)} %get-tuple-element.260) | copy-start | bytes 12292
  39.4 8.4 %copy-start.23 = (f32[4,256]{1,0:T(4,128)}, f32[4,256]{1,0:T(4,128)S(1)}, u32[]{:S(2)}) copy-start(f32[4,256]{1,0:T(4,128)S(1)} %get-tuple-element.261) | copy-start | bytes 12292
  39.4 8.4 %copy-start.25 = (f32[4,256]{1,0:T(4,128)}, f32[4,256]{1,0:T(4,128)S(1)}, u32[]{:S(2)}) copy-start(f32[4,256]{1,0:T(4,128)S(1)} %get-tuple-element.262) | copy-start | bytes 12292
  41.0 2.5 copy-start.43
  41.0 6.7 copy-start.30
  41.0 6.7 copy-start.32
  41.0 6.7 copy-start.34
  41.0 6.7 copy-start.36
  43.0 4.8 copy-start.12
  43.6 5.1 copy-start.28
  46.1 3.4 copy-start.18
  421.2 6.8 copy-start.16
  421.2 14.0 %copy-start.13 = (f32[4,256,32]{1,2,0:T(8,128)S(1)}, f32[4,256,32]{1,2,0:T(8,128)}, u32[]{:S(2)}) copy-start(f32[4,256,32]{1,2,0:T(8,128)} %copy-done.12) | copy-start | bytes 393220
  422.9 4.5 copy-start.17
  422.9 16.4 %copy-start.2 = (f32[1024,256]{1,0:T(8,128)S(1)}, f32[1024,256]{1,0:T(8,128)}, u32[]{:S(2)}) copy-start(f32[1024,256]{1,0:T(8,128)} %get-tuple-element.97) | copy-start | bytes 3145732
  422.9 16.4 %copy-start.8 = (f32[4,256,256]{2,1,0:T(8,128)S(1)}, f32[4,256,256]{2,1,0:T(8,128)}, u32[]{:S(2)}) copy-start(f32[4,256,256]{2,1,0:T(8,128)} %get-tuple-element.239) | copy-start | bytes 3145732
  422.9 16.4 %copy-start.19 = (f32[4,3,256]{2,1,0:T(4,128)S(1)}, f32[4,3,256]{2,1,0:T(4,128)}, u32[]{:S(2)}) copy-start(f32[4,3,256]{2,1,0:T(4,128)} %copy-done.18) | copy-start | bytes 36868
  425.2 14.1 %collective-permute-start.1 = (f32[4,256,256]{2,1,0:T(8,128)S(1)}, f32[4,256,256]{2,1,0:T(8,128)}, u32[]{:S(2)}, u32[]{:S(2)}) collective-permute-start(f32[4,256,256]{2,1,0:T(8,128)S(1)} %constant_dynamic-update-slice_fusion), channel_id=1, source_target_pairs={{0,1},{1,0},{2,3},{3,2},{4,5},{5,4},{6,7},{7,6},{8,9},{9,8},{10,11... | collective-permute-start | bytes 3145736 | tf_op jit(solution)/shard_map/ppermute | solution.py:363
  439.3 2.9 copy-start.22
  439.3 2.9 copy-start.24
  439.3 2.9 copy-start.26
  439.3 2.9 copy-start.31
  439.3 2.9 copy-start.33
  439.3 2.9 copy-start.35
  439.4 2.9 copy-start.37
  442.7 1.0 copy-start
  444.8 2.6 copy-start.29
  444.8 7.4 collective-permute-start.2
  452.9 3.8 copy-start.4
  454.4 2.4 copy-start.5
  456.7 2.0 copy-start.10
  458.6 1.6 copy-start.3
  464.3 2.1 copy-start.6
  466.4 1.7 copy-start.7
  466.4 2.1 copy-start.9
  468.1 1.6 copy-start.20
  797.0 2.4 copy-start.27
  798.0 7.4 copy-start.15
  802.0 10.2 %collective-permute-start.3 = (f32[2048,128]{1,0:T(8,128)S(1)}, f32[2048,128]{1,0:T(8,128)S(1)}, u32[]{:S(2)}, u32[]{:S(2)}) collective-permute-start(f32[2048,128]{1,0:T(8,128)S(1)} %bitcast.123), channel_id=1, source_target_pairs={{0,1},{1,0},{2,3},{3,2},{4,5},{5,4},{6,7},{7,6},{8,9},{9,8},{10,11... | collective-permute-start | bytes 3145736 | tf_op jit(solution)/shard_map/ppermute | solution.py:363
  806.8 9.3 %slice-start = ((s8[8388608]{0:T(1024)(128)(4,1)}), s8[4194304]{0:T(1024)(128)(4,1)S(1)}, s32[]{:S(2)}) async-start(s8[8388608]{0:T(1024)(128)(4,1)} %bitcast.109), calls=%async_computation | async-start | bytes 8388608
  812.2 4.0 slice-start.1
  812.4 2.5 copy-start.11
  816.2 3.4 copy-start.14
